TPU v7x, 128 devices: a whole 4x4x4 slice. The times are simulated.
128 devices in a mesh: seq: 32 (over y, z, core), head: 4 (over x).
Axes of the slice: x: 4, y: 4, z: 4, core: 2. Of those that a mesh axis runs over, the one named last changes fastest.
Arguments:
- query: bfloat16 [8192, 2048], P('seq', 'head'), may hold values from -6 to 6
- key: bfloat16 [8192, 2048], P('seq', 'head'), may hold values from -6 to 6
- value: bfloat16 [8192, 4096], P('seq', 'head'), may hold values from -6 to 6
- beta: float32 [32, 8192], P('head', 'seq'), may hold values from 0 to 1, as said below
- decay: float32 [32, 8192], P('head', 'seq'), may hold values from -1 to 0, as said below
- wo_start: bfloat16 [2048, 4096], P('seq', 'head'), may hold values from -0.09375 to 0.09375
- wo_end: bfloat16 [2048, 4096], P('seq', 'head'), may hold values from -0.09375 to 0.09375
- curve_index: int32 [1], replicated, may hold values from 0 to 256
- cotangent: bfloat16 [8192, 2048], P('seq', 'head'), may hold values from -6 to 6
Outputs:
- mixed: bfloat16 [8192, 2048], P('seq', 'head')
- grad_query: float32 [8192, 2048], P('seq', 'head')
- grad_key: float32 [8192, 2048], P('seq', 'head')
- grad_value: float32 [8192, 4096], P('seq', 'head')
- grad_beta: float32 [32, 8192], P('head', 'seq')
- grad_decay: float32 [32, 8192], P('head', 'seq')
- grad_wo_start: float32 [2048, 4096], P('seq', 'head')
- grad_wo_end: float32 [2048, 4096], P('seq', 'head')
Inputs may be any that keep to these rules, and one draw needn't show every extreme that they name: beta lies strictly between 0 and 1. decay is negative: each token's gate exp(decay) lies strictly between 0 and 1.
All inputs are finite; a program needn't handle non-finite values.
Results may differ from a plain program's by a relative error of at most 0.02.
Values may be sent and summed in bfloat16 or wider, within the bound.
No kernel may reach another device: no remote copies, remote signals or barrier semaphores. Data moves between devices by JAX's collectives and lax.ppermute only.
A program may use at most 192 MiB of HBM per device.

v0:
```python
import jax
import jax.numpy as jnp
from jax import lax
from jax.sharding import PartitionSpec as P

DK = 128
DV = 128
SPAN_LOG = 7
CURVE_POINTS = 257


norm_eps = 1e-06


def carried_in(part, axis, combine, identity, reverse):
    count = lax.axis_size(axis)
    place = lax.axis_index(axis)
    ahead = count - 1 - place if reverse else place
    gathered = jax.tree.map(lambda a: lax.all_gather(a, axis), part)
    state = jax.tree.map(lambda a, e: jnp.zeros_like(a) + jnp.asarray(e, a.dtype), part, identity)

    def one(step, state):
        source = count - 1 - step if reverse else step
        return combine(
            state, jax.tree.map(lambda a: lax.dynamic_index_in_dim(a, source, 0, False), gathered)
        )

    return lax.fori_loop(0, ahead, one, state)


def matmul_high(left, right):
    return jnp.matmul(left, right, precision=lax.Precision.HIGHEST)


def flip_last(matrix):
    return jnp.swapaxes(matrix, -1, -2)


def gram_low(left, right):
    return lax.dot_general(
        left.astype(jnp.bfloat16),
        right.astype(jnp.bfloat16),
        (((2,), (2,)), ((0,), (0,))),
        preferred_element_type=jnp.float32,
    )


def unit_inverse(lower):
    size = lower.shape[-1]
    negated = -lower
    result = jnp.eye(size, dtype=lower.dtype) + negated
    power = negated
    for level in range(size.bit_length() - 2):
        power = matmul_high(power, power)
        result = result + matmul_high(result, power)
    return result


def span_parts(queries, keys, values, betas, decays):
    size = queries.shape[1]
    cumulative = jnp.cumsum(decays, axis=-1)
    growth = jnp.exp(cumulative)
    row_ids = lax.broadcasted_iota(jnp.int32, (size, size), 0)
    col_ids = lax.broadcasted_iota(jnp.int32, (size, size), 1)
    inclusive = row_ids >= col_ids
    strict = row_ids > col_ids
    spread = cumulative[:, :, None] - cumulative[:, None, :]
    ratio = jnp.where(inclusive, jnp.exp(jnp.minimum(spread, 0.0)), 0.0)
    lower = jnp.where(strict, betas[:, :, None] * gram_low(keys, keys) * ratio, 0.0)
    inverse = unit_inverse(lower)
    weights = matmul_high(inverse, (betas * growth)[:, :, None] * keys)
    written = matmul_high(inverse, betas[:, :, None] * values)
    attend = jnp.where(inclusive, gram_low(queries, keys) * ratio, 0.0)
    tail = jnp.exp(cumulative[:, -1:] - cumulative)[:, :, None] * keys
    return (growth, attend, weights, written, tail)


def span_step(carry, pieces):
    local_state, prefix = carry
    queries, keys, values, betas, decays = pieces
    growth, attend, weights, written, tail = span_parts(queries, keys, values, betas, decays)
    update = written - matmul_high(weights, flip_last(local_state))
    output = growth[:, :, None] * matmul_high(queries, flip_last(local_state)) + matmul_high(
        attend, update
    )
    reach = growth[:, :, None] * queries - matmul_high(attend, weights)
    carried = matmul_high(reach, flip_last(prefix))
    last_growth = growth[:, -1][:, None, None]
    new_state = last_growth * local_state + matmul_high(flip_last(update), tail)
    identity = jnp.eye(prefix.shape[-1], dtype=prefix.dtype)
    step_map = last_growth * identity - matmul_high(flip_last(weights), tail)
    new_prefix = matmul_high(prefix, step_map)
    return ((new_state, new_prefix), (output, carried))


def local_pass(query, key, value, beta, decay):
    tokens = query.shape[0]
    heads = beta.shape[0]
    key_heads = key.shape[1] // DK
    group = heads // key_heads
    size = 2**SPAN_LOG
    blocks = tokens // size
    keyed = key.reshape(tokens, key_heads, DK)
    keyed = keyed * lax.rsqrt(jnp.sum(keyed * keyed, axis=-1, keepdims=True) + norm_eps)
    key_full = jnp.repeat(keyed, group, axis=1)
    query_full = jnp.repeat(query.reshape(tokens, key_heads, DK), group, axis=1)
    value_full = value.reshape(tokens, heads, DV)

    def arrange(array):
        return array.reshape(blocks, size, heads, array.shape[-1]).transpose(0, 2, 1, 3)

    def arrange_rates(array):
        return array.reshape(heads, blocks, size).transpose(1, 0, 2)

    advance = jax.checkpoint(span_step)
    initial = (
        jnp.zeros((heads, DV, DK), jnp.float32),
        jnp.broadcast_to(jnp.eye(DK, dtype=jnp.float32), (heads, DK, DK)),
    )
    finals, outputs = lax.scan(
        advance,
        initial,
        (
            arrange(query_full),
            arrange(key_full),
            arrange(value_full),
            arrange_rates(beta),
            arrange_rates(decay),
        ),
    )
    output_local = outputs[0].transpose(1, 0, 2, 3).reshape(heads, tokens, DV)
    carried = outputs[1].transpose(1, 0, 2, 3).reshape(heads, tokens, DK)
    return (output_local, carried, finals[1], finals[0])


def compose(earlier, later):
    return (matmul_high(earlier[0], later[0]), matmul_high(earlier[1], later[0]) + later[1])


def body(query, key, value, beta, decay, wo_start, wo_end, curve_index, cotangent):
    position = curve_index[0].astype(jnp.float32) / (CURVE_POINTS - 1)
    weight_local = (
        (1.0 - position) * wo_start.astype(jnp.float32) + position * wo_end.astype(jnp.float32)
    ).astype(jnp.bfloat16)
    weight_full = lax.all_gather(weight_local, "seq", axis=0, tiled=True)
    inputs = (
        query.astype(jnp.float32),
        key.astype(jnp.float32),
        value.astype(jnp.float32),
        beta,
        decay,
    )
    (output_local, carried, transition, offset), pullback = jax.vjp(local_pass, *inputs)
    heads = beta.shape[0]
    tokens = query.shape[0]
    identity = (
        jnp.broadcast_to(jnp.eye(DK, dtype=jnp.float32), transition.shape),
        jnp.zeros_like(offset),
    )
    incoming = carried_in((transition, offset), "seq", compose, identity, False)[1]
    heads_out = output_local + jnp.einsum(
        "hlk,hvk->hlv", carried, incoming, precision=lax.Precision.HIGHEST
    )
    scale = lax.rsqrt(jnp.mean(heads_out * heads_out, axis=-1, keepdims=True) + norm_eps)
    normalized_rows = (
        (heads_out * scale).transpose(1, 0, 2).reshape(tokens, heads * DV).astype(jnp.bfloat16)
    )
    partial_out = lax.dot_general(
        normalized_rows, weight_full, (((1,), (1,)), ((), ())), preferred_element_type=jnp.float32
    )
    mixed = lax.psum_scatter(partial_out, "head", scatter_dimension=1, tiled=True).astype(
        jnp.bfloat16
    )
    grad_full = lax.all_gather(cotangent, "head", axis=1, tiled=True)
    grad_normed = jnp.dot(grad_full, weight_full, preferred_element_type=jnp.float32)
    grad_weight = lax.psum_scatter(
        lax.dot_general(
            grad_full, normalized_rows, (((0,), (0,)), ((), ())), preferred_element_type=jnp.float32
        ).astype(jnp.bfloat16),
        "seq",
        scatter_dimension=0,
        tiled=True,
    ).astype(jnp.float32)
    grad_grouped = grad_normed.reshape(tokens, heads, DV).transpose(1, 0, 2)
    inner = jnp.mean(grad_grouped * heads_out, axis=-1, keepdims=True)
    grad_heads = scale * grad_grouped - scale * scale * scale * heads_out * inner
    direct = jnp.einsum("hlv,hlk->hvk", grad_heads, carried, precision=lax.Precision.HIGHEST)
    later = carried_in((flip_last(transition), direct), "seq", compose, identity, True)[1]
    grad_carried = jnp.einsum("hlv,hvk->hlk", grad_heads, incoming, precision=lax.Precision.HIGHEST)
    grad_transition = jnp.einsum("hvk,hvj->hkj", incoming, later, precision=lax.Precision.HIGHEST)
    grad_query, grad_key, grad_value, grad_beta, grad_decay = pullback(
        (grad_heads, grad_carried, grad_transition, later)
    )
    return (
        mixed,
        grad_query,
        grad_key,
        grad_value,
        grad_beta,
        grad_decay,
        (1.0 - position) * grad_weight,
        position * grad_weight,
    )


def solution(mesh):
    return jax.shard_map(
        body,
        mesh=mesh,
        in_specs=(
            P("seq", "head"),
            P("seq", "head"),
            P("seq", "head"),
            P("head", "seq"),
            P("head", "seq"),
            P("seq", "head"),
            P("seq", "head"),
            P(),
            P("seq", "head"),
        ),
        out_specs=(
            P("seq", "head"),
            P("seq", "head"),
            P("seq", "head"),
            P("seq", "head"),
            P("head", "seq"),
            P("head", "seq"),
            P("seq", "head"),
            P("seq", "head"),
        ),
        check_vma=False,
    )
```

profile of v0, /device:TPU:0, one launch (start us, length us, event | category | flops | bytes accessed | tf_op | source)
XLA Modules:
  0.0 935.4 jit_solution(11956972027494796517)
XLA Ops:
  20.2 48.7 %while.79 = (s32[]{:T(128)}, f32[8,128,128]{2,1,0:T(8,128)S(1)}, f32[8,128,128]{1,2,0:T(8,128)S(1)}, f32[2,8,128,128]{3,2,1,0:T(8,128)}, f32[2,8,128,128]{3,2,0,...) while((s32[]{:T(128)}, f32[8,128,128]{2,1,0:T(8,128)S(1)}, ...), condition=%wide.region_3.4_spmd.clone.clone, body=%wide.region_1.3_spmd.clone.clone.sunk | while | flops 4501177344 | bytes 64036888 | solution.py:120
  32.7 2.3 convolution_multiply_fusion.5
  37.1 2.1 convolution_subtract_fusion.17
  56.9 2.3 convolution_multiply_fusion.5
  61.3 2.1 convolution_subtract_fusion.17
  74.2 11.5 %all-gather.11.cloned.1.call-done = bf16[2048,1024]{1,0:T(8,128)(2,1)} async-done(((bf16[64,1024]{1,0:T(8,128)(2,1)}), bf16[2048,1024]{1,0:T(8,128)(2,1)}) %all-gather.11.cloned.1.call-update) | async-done | bytes 4194320 | tf_op jit(solution)/shard_map/all_gather | solution.py:145
  85.7 4.8 fusion.176
  90.5 70.0 %all-gather.15.cloned.1.call-done = f32[256,128,128]{2,1,0:T(8,128)} async-done(((f32[8,128,128]{2,1,0:T(8,128)}), f32[256,128,128]{2,1,0:T(8,128)}) %all-gather.15.cloned.1.call-update) | async-done | bytes 16777232 | tf_op jit(solution)/shard_map/all_gather | solution.py:19
  160.4 74.7 %all-gather.17.cloned.1.call-done = f32[256,128,128]{2,1,0:T(8,128)} async-done(((f32[8,128,128]{2,1,0:T(8,128)}), f32[256,128,128]{2,1,0:T(8,128)}) %all-gather.17.cloned.1.call-update) | async-done | bytes 16777232 | tf_op jit(solution)/shard_map/all_gather | solution.py:19
  235.3 3.2 multiply_reduce_fusion.8
  238.8 2.6 fusion.175
  241.5 4.4 convert_bitcast_fusion.1
  245.9 6.4 copy.879
  253.2 3.2 fusion.177
  260.9 2.2 copy.796
  263.2 112.8 %reduce-scatter.5.cloned.1.call-done = f32[256,512]{1,0:T(8,128)} async-done(((f32[256,2048]{1,0:T(8,128)}), f32[256,512]{1,0:T(8,128)}) %reduce-scatter.5.cloned.1.call-update) | async-done | bytes 524304 | tf_op jit(solution)/shard_map/reduce_scatter | solution.py:171
  377.8 84.1 %reduce-scatter.7.cloned.1.call-done = bf16[64,1024]{1,0:T(8,128)(2,1)} async-done(((bf16[2048,1024]{1,0:T(8,128)(2,1)}), bf16[64,1024]{1,0:T(8,128)(2,1)}) %reduce-scatter.7.cloned.1.call-update) | async-done | bytes 131088 | tf_op jit(solution)/shard_map/reduce_scatter | solution.py:176
  463.6 72.3 %all-gather.19.cloned.1.call-done = f32[256,128,128]{2,1,0:T(8,128)} async-done(((f32[8,128,128]{2,1,0:T(8,128)}), f32[256,128,128]{2,1,0:T(8,128)}) %all-gather.19.cloned.1.call-update) | async-done | bytes 16777232 | tf_op jit(solution)/shard_map/all_gather | solution.py:19
  535.9 74.9 %all-gather.21.cloned.1.call-done = f32[256,128,128]{2,1,0:T(8,128)} async-done(((f32[8,128,128]{2,1,0:T(8,128)}), f32[256,128,128]{2,1,0:T(8,128)}) %all-gather.21.cloned.1.call-update) | async-done | bytes 16777232 | tf_op jit(solution)/shard_map/all_gather | solution.py:19
  610.8 106.2 %while.77 = (s32[]{:T(128)}, f32[8,128,128]{1,2,0:T(8,128)S(1)}, s32[]{:T(128)}, f32[32,8,128,128]{3,2,1,0:T(8,128)}, f32[32,8,128,128]{3,2,1,0:T(8,128)}, /*index=5*/s32[]{:T(128)}, s32[]{:T(128)}, s32[]{:T(128)}, s32[]{:T(128)}) while((s32[]{:T(128)}, f32[8,128,128]{1,2,0:T(8,128)S(1)}, s32[]{:T(128)}, f32[32,8,128,128]{3,2,1,0:T(8,128)}, ...), condition=%wide.region_10.11_spmd, body=%wide.region_9.10_spmd.sunk | while | flops 201457664 | bytes 5243027 | solution.py:28
  612.2 2.1 fusion.572
  615.6 2.1 fusion.572
  619.1 2.1 fusion.572
  622.5 2.1 fusion.572
  625.9 2.1 fusion.572
  629.3 2.1 fusion.572
  632.8 2.1 fusion.572
  636.2 2.1 fusion.572
  639.6 2.1 fusion.572
  643.0 2.1 fusion.572
  646.5 2.1 fusion.572
  649.9 2.1 fusion.572
  653.3 2.1 fusion.572
  656.7 2.1 fusion.572
  660.2 2.1 fusion.572
  663.6 2.1 fusion.572
  667.0 2.1 fusion.572
  670.5 2.1 fusion.572
  673.9 2.1 fusion.572
  677.3 2.1 fusion.572
  680.7 2.1 fusion.572
  684.2 2.1 fusion.572
  687.6 2.1 fusion.572
  691.0 2.1 fusion.572
  694.4 2.1 fusion.572
  697.9 2.1 fusion.572
  701.3 2.1 fusion.572
  704.7 2.1 fusion.572
  708.1 2.1 fusion.572
  711.6 2.1 fusion.572
  715.0 2.1 fusion.572
  724.0 196.9 %while.78 = (s32[]{:T(128)}, f32[8,128,128]{2,1,0:T(8,128)}, f32[8,128,128]{2,1,0:T(8,128)}, f32[2,8,128,128]{3,2,0,1:T(8,128)}, f32[2,8,128,128]{3,2,0,1:T(8,12...) while((s32[]{:T(128)}, f32[8,128,128]{2,1,0:T(8,128)}, ...), condition=%wide.region_25.26_spmd, body=%wide.region_11.25_spmd.sunk | while | flops 12707636224 | bytes 179910064 | solution.py:120
  725.8 2.3 dynamic-slice_bitcast_fusion.21
  731.9 2.1 fusion.719
  785.3 2.5 fusion.736
  789.8 2.3 multiply_reduce_fusion.19
  802.2 2.1 copy.918
  815.2 2.2 convolution_add_fusion.101
  823.2 2.3 dynamic-slice_bitcast_fusion.21
  829.2 2.1 fusion.719
  882.6 2.5 fusion.736
  887.1 2.3 multiply_reduce_fusion.19
  899.5 2.1 copy.918
  912.5 2.2 convolution_add_fusion.101
  (546 shorter events, 286.2 us)
Async XLA Ops:
  7.2 67.0 %all-gather.13.cloned.1.call-start = ((), (), s32[]{:S(2)}) async-start(), calls=%async_computation.4 | async-start | bytes 1310720 | tf_op jit(solution)/shard_map/all_gather | solution.py:174
  7.9 77.8 %all-gather.11.cloned.1.call-start = ((), (), s32[]{:S(2)}) async-start(), calls=%async_computation.2 | async-start | bytes 4325376 | tf_op jit(solution)/shard_map/all_gather | solution.py:145
  10.3 150.1 %all-gather.15.cloned.1.call-start = ((), (), s32[]{:S(2)}) async-start(), calls=%async_computation.5 | async-start | bytes 17301504 | tf_op jit(solution)/shard_map/all_gather | solution.py:19
  11.6 5.0 copy-start.33
  12.4 4.1 copy-start.20
  15.4 4.8 copy-start.31
  15.4 4.8 copy-start.32
  31.4 5.0 copy-start.26
  32.7 6.6 copy-start.16
  36.4 4.9 copy-start.18
  37.1 5.3 copy-start.27
  55.7 5.0 copy-start.26
  56.9 6.6 copy-start.16
  60.6 4.9 copy-start.18
  61.3 5.3 copy-start.27
  69.0 21.5 %copy-start.15 = (f32[8,128,128]{1,2,0:T(8,128)}, f32[8,128,128]{1,2,0:T(8,128)S(1)}, u32[]{:S(2)}) copy-start(f32[8,128,128]{1,2,0:T(8,128)S(1)} %get-tuple-element.673) | copy-start | bytes 1572868
  70.1 165.1 %all-gather.17.cloned.1.call-start = ((), (), s32[]{:S(2)}) async-start(), calls=%async_computation.6 | async-start | bytes 17301504 | tf_op jit(solution)/shard_map/all_gather | solution.py:19
  70.7 305.3 %reduce-scatter.5.cloned.1.call-start = ((), (), s32[]{:S(2)}) async-start(), calls=%async_computation.3 | async-start | bytes 2621440 | tf_op jit(solution)/shard_map/reduce_scatter | solution.py:171
  235.2 3.3 copy-start.21
  235.2 3.5 copy-start.42
  241.4 220.4 %reduce-scatter.7.cloned.1.call-start = ((), (), s32[]{:S(2)}) async-start(), calls=%async_computation.9 | async-start | bytes 4325376 | tf_op jit(solution)/shard_map/reduce_scatter | solution.py:176
  252.4 283.5 %all-gather.19.cloned.1.call-start = ((), (), s32[]{:S(2)}) async-start(), calls=%async_computation.7 | async-start | bytes 17301504 | tf_op jit(solution)/shard_map/all_gather | solution.py:19
  253.1 357.6 %all-gather.21.cloned.1.call-start = ((), (), s32[]{:S(2)}) async-start(), calls=%async_computation.8 | async-start | bytes 17301504 | tf_op jit(solution)/shard_map/all_gather | solution.py:19
  724.0 198.3 %copy-start.34 = (f32[256,4]{0,1:T(4,128)S(1)}, f32[256,4]{0,1:T(4,128)}, u32[]{:S(2)}) copy-start(f32[256,4]{0,1:T(4,128)} %copy-done.33) | copy-start | bytes 12292
  724.0 199.8 %copy-start.36 = (f32[256,4]{0,1:T(4,128)S(1)}, f32[256,4]{0,1:T(4,128)}, u32[]{:S(2)}) copy-start(f32[256,4]{0,1:T(4,128)} %copy-done.35) | copy-start | bytes 12292
  724.1 4.0 copy-start.7
  725.8 20.1 %copy-start.3 = (f32[8,128,128]{2,1,0:T(8,128)}, f32[8,128,128]{2,1,0:T(8,128)S(1)}, u32[]{:S(2)}) copy-start(f32[8,128,128]{2,1,0:T(8,128)S(1)} %get-tuple-element.1581) | copy-start | bytes 1572868 | tf_op jit(solution)/shard_map/transpose(jvp())/while
  734.2 51.0 %copy-start = (f32[8,128,128]{2,1,0:T(8,128)}, f32[8,128,128]{2,1,0:T(8,128)S(1)}, u32[]{:S(2)}) copy-start(f32[8,128,128]{2,1,0:T(8,128)S(1)} %fusion.718) | copy-start | bytes 1572868 | tf_op jit(solution)/shard_map/transpose(jvp())/while
  741.0 3.3 copy-start.22
  743.0 4.2 copy-start.11
  743.0 4.2 copy-start.13
  744.3 4.7 copy-start.9
  750.2 30.8 %copy-start.5 = (f32[8,128,128]{1,2,0:T(8,128)}, f32[8,128,128]{1,2,0:T(8,128)S(1)}, u32[]{:S(2)}) copy-start(f32[8,128,128]{1,2,0:T(8,128)S(1)} %fusion.717) | copy-start | bytes 1572868 | tf_op jit(solution)/shard_map/transpose(jvp())/while
  775.7 6.4 copy-start.4
  785.3 6.9 copy-start.6
  792.1 6.2 copy-start.37
  804.3 4.2 copy-start.12
  804.3 5.7 copy-start.1
  807.0 5.2 copy-start.14
  808.5 4.9 copy-start.10
  812.1 8.3 copy-start.40
  812.1 8.9 copy-start.8
  812.2 8.9 copy-start.38
  821.5 4.0 copy-start.7
  823.2 20.1 %copy-start.3 = (f32[8,128,128]{2,1,0:T(8,128)}, f32[8,128,128]{2,1,0:T(8,128)S(1)}, u32[]{:S(2)}) copy-start(f32[8,128,128]{2,1,0:T(8,128)S(1)} %get-tuple-element.1581) | copy-start | bytes 1572868 | tf_op jit(solution)/shard_map/transpose(jvp())/while
  831.6 51.0 %copy-start = (f32[8,128,128]{2,1,0:T(8,128)}, f32[8,128,128]{2,1,0:T(8,128)S(1)}, u32[]{:S(2)}) copy-start(f32[8,128,128]{2,1,0:T(8,128)S(1)} %fusion.718) | copy-start | bytes 1572868 | tf_op jit(solution)/shard_map/transpose(jvp())/while
  838.4 3.3 copy-start.22
  840.3 4.2 copy-start.11
  840.3 4.2 copy-start.13
  841.7 4.6 copy-start.9
  847.5 30.8 %copy-start.5 = (f32[8,128,128]{1,2,0:T(8,128)}, f32[8,128,128]{1,2,0:T(8,128)S(1)}, u32[]{:S(2)}) copy-start(f32[8,128,128]{1,2,0:T(8,128)S(1)} %fusion.717) | copy-start | bytes 1572868 | tf_op jit(solution)/shard_map/transpose(jvp())/while
  873.0 6.4 copy-start.4
  882.6 6.8 copy-start.6
  889.4 6.3 copy-start.37
  901.6 4.2 copy-start.12
  901.6 5.8 copy-start.1
  904.3 5.2 copy-start.14
  905.8 4.9 copy-start.10
  909.4 8.3 copy-start.40
  909.5 8.9 copy-start.8
  909.5 8.9 copy-start.38
  920.8 4.8 copy-start.39
  920.8 3.1 copy-start.29
  920.8 4.2 copy-start.24
  (13 other events, 23.0 us)
Sparse Core Ops, SparseCore 0:
  9.7 26.3 all-gather.12
  38.9 46.7 all-gather.10
  88.5 71.8 all-gather.14
  163.1 71.9 all-gather.16
  241.6 134.3 reduce-scatter.4
  379.9 81.8 reduce-scatter.6
  464.1 71.7 all-gather.18
  538.8 71.9 all-gather.20
where the time goes:
time: 954 us; the launch traced here: 935 us
  waiting for transfers between devices  502 us (53%)
  matrix products  280 us (29%)
  local copies, waits for them, and re-layouts  105 us (11%)
  other arithmetic  25.4 us (3%)
  between operations  15.6 us (2%)
    all_gather x4, waiting for transfers between devices, carried_in(): gathered = jax.tree.map(lambda a: lax.all_gather(a, axis), part)  292 us
    dot_general x199, matrix products, matmul_high(): return jnp.matmul(left, right, precision=lax.Precision.HIGHEST)  246 us
    reduce_scatter x1, waiting for transfers between devices, body(): lax.psum_scatter(partial_out, 'head', scatter_dimension=1, tiled=True)  113 us
    reduce_scatter x1, waiting for transfers between devices, body(): lax.psum_scatter(lax.dot_general(grad_full, normalized_rows, (((0,), (0,)...  84.1 us
    dynamic_slice x62, local copies, waits for them, and re-layouts, one(): lax.dynamic_index_in_dim(a, source, 0, False)  39.6 us
  transfers between devices with their start and end apart: 8, of which 7 were waited for; matrix products, arithmetic and copies ran while one was open for 10% of the time, Pallas kernels for 0%

commit v1 on v0

v1 whole, which is shorter than its diff:
```python
import jax
import jax.numpy as jnp
from jax import lax
from jax.experimental import pallas as pl
from jax.experimental.pallas import tpu as pltpu
from jax.sharding import Mesh, PartitionSpec as P

DK = 128
CURVE_POINTS = 257
EPS = 1e-06
NY, NZ, NC, NH = 4, 4, 2, 4
SEG = NZ * NC
TOK = 256
HALF = 128
KEYS = 4
ROWS = 272
BF = jnp.bfloat16
F32 = jnp.float32
RING = ("y", "z", "c")
INTERPRET = False


def dot(left, right, dims):
    return lax.dot_general(
        left.astype(BF), right.astype(BF), (dims, ((), ())), preferred_element_type=F32
    )


def mm(left, right):
    return dot(left, right, ((1,), (0,)))


def mm_nt(left, right):
    return dot(left, right, ((1,), (1,)))


def mm_tn(left, right):
    return dot(left, right, ((0,), (0,)))


def iota(shape, dim):
    return lax.broadcasted_iota(jnp.int32, shape, dim)


def lane_sum(array):
    return jnp.sum(array, axis=1, keepdims=True)


def call(kernel, out_shape, grid, in_specs, out_specs, args, flops, scratch=(), prefetch=None):
    bytes_moved = sum(a.size * a.dtype.itemsize for a in (*args, *out_shape))
    spec = dict(grid=grid, in_specs=in_specs, out_specs=out_specs, scratch_shapes=list(scratch))
    extra = {}
    if prefetch is None:
        extra = spec
    else:
        extra = dict(grid_spec=pltpu.PrefetchScalarGridSpec(num_scalar_prefetch=1, **spec))
        args = (prefetch, *args)
    return pl.pallas_call(
        kernel,
        out_shape=out_shape,
        compiler_params=pltpu.CompilerParams(vmem_limit_bytes=48 * 2**20),
        cost_estimate=pl.CostEstimate(
            flops=flops, bytes_accessed=bytes_moved, transcendentals=0
        ),
        interpret=INTERPRET,
        **extra,
    )(*args)


def shape(*dims, dtype=F32):
    return jax.ShapeDtypeStruct(dims, dtype)


def whole(array):
    return pl.BlockSpec(array.shape, lambda *_: (0,) * len(array.shape))


def heads_spec(rows, cols):
    return pl.BlockSpec((2, rows, cols), lambda j: (j, 0, 0))


def lead_spec(rows, cols):
    return pl.BlockSpec((1, rows, cols), lambda j: (j, 0, 0))


def wide_spec(cols):
    return pl.BlockSpec((TOK, cols), lambda j: (0, j))


def unit_keys(key_block):
    raw = key_block.astype(F32)
    rate = lax.rsqrt(lane_sum(raw * raw) + EPS)
    return raw * rate, rate


def prefix_lanes(array):
    size = array.shape[1]
    lane = iota(array.shape, 1)
    step = 1
    while step < size:
        array = array + jnp.where(lane >= step, pltpu.roll(array, step, 1), 0.0)
        step *= 2
    return array


def suffix_lanes(array):
    size = array.shape[1]
    lane = iota(array.shape, 1)
    step = 1
    while step < size:
        array = array + jnp.where(lane < size - step, pltpu.roll(array, size - step, 1), 0.0)
        step *= 2
    return array


def invert_blocks(lowers):
    row, col = iota((HALF, HALF), 0), iota((HALF, HALF), 1)
    apart = row ^ col
    eye = jnp.where(row == col, 1.0, 0.0)
    found = [eye - jnp.where(apart < 2, low, 0.0) for low in lowers]
    size = 2
    while size < HALF:
        mask = (apart >= size) & (apart < 2 * size)
        offs = [jnp.where(mask, low, 0.0).astype(BF) for low in lowers]
        lows = [x.astype(BF) for x in found]
        halfway = [mm(x, off) for x, off in zip(lows, offs)]
        found = [f - mm(m, x) for f, m, x in zip(found, halfway, lows)]
        size *= 2
    return found


def pre_kernel(k_ref, v_ref, beta_ref, decay_ref, pay_ref, x_ref, wu_ref, c_ref, cols_ref):
    j = pl.program_id(0)

    @pl.when(j == 0)
    def _():
        c_ref[...] = prefix_lanes(decay_ref[...])

    unit, _ = unit_keys(k_ref[...])
    low = unit.astype(BF)
    gram = mm_nt(low, low)
    rows = [c_ref[pl.ds(2 * j + a, 1), :] for a in range(2)]
    rates = [beta_ref[pl.ds(2 * j + a, 1), :] for a in range(2)]
    sub = iota((8, TOK), 0)
    packed = jnp.zeros((8, TOK), F32)
    for place, line in enumerate((*rows, *rates)):
        packed = jnp.where(sub == place, line, packed)
    cols = jnp.transpose(jnp.concatenate([packed, jnp.zeros((HALF - 8, TOK), F32)], axis=0))
    cols_ref[0] = cols
    strict = iota((TOK, TOK), 0) > iota((TOK, TOK), 1)
    lowers = []
    for a in range(2):
        ratio = jnp.exp(jnp.minimum(cols[:, a : a + 1] - rows[a], 0.0))
        lowers.append(jnp.where(strict, cols[:, 2 + a : 3 + a] * gram * ratio, 0.0))
    found = invert_blocks(
        [low[b * HALF : (b + 1) * HALF, b * HALF : (b + 1) * HALF] for low in lowers for b in (0, 1)]
    )
    for a in range(2):
        first, second = found[2 * a].astype(BF), found[2 * a + 1].astype(BF)
        corner = -mm(mm(second, lowers[a][HALF:, :HALF]), first)
        inverse = jnp.concatenate(
            [
                jnp.concatenate([first, jnp.zeros((HALF, HALF), BF)], axis=1),
                jnp.concatenate([corner.astype(BF), second], axis=1),
            ],
            axis=0,
        )
        x_ref[a] = inverse
        c_col, beta_col = cols[:, a : a + 1], cols[:, 2 + a : 3 + a]
        value = v_ref[:, a * DK : (a + 1) * DK].astype(F32)
        right = jnp.concatenate(
            [(beta_col * jnp.exp(c_col) * unit).astype(BF), (beta_col * value).astype(BF)], axis=1
        )
        wu = mm(inverse, right).astype(BF)
        wu_ref[a] = wu
        end = c_col[TOK - 1 : TOK, :]
        tail = (jnp.exp(end - c_col) * unit).astype(BF)
        pay_ref[a, : 2 * DK, :] = mm_tn(wu, tail).astype(BF)
        gate = jnp.broadcast_to(jnp.exp(end), (16, DK))
        one = gate.astype(BF)
        two = (gate - one.astype(F32)).astype(BF)
        three = (gate - one.astype(F32) - two.astype(F32)).astype(BF)
        place = iota((16, DK), 0)
        pay_ref[a, 2 * DK :, :] = jnp.where(
            place == 0,
            one.astype(F32),
            jnp.where(
                place == 1, two.astype(F32), jnp.where(place == 2, three.astype(F32), 0.0)
            ),
        ).astype(BF)


def gate_of(block):
    return jnp.sum(block[2 * DK :, :].astype(F32), axis=0, keepdims=True)


def pre_pass(key, value, beta, decay):
    heads = 2 * KEYS
    return call(
        pre_kernel,
        (
            shape(heads, ROWS, DK, dtype=BF),
            shape(heads, TOK, TOK, dtype=BF),
            shape(heads, TOK, 2 * DK, dtype=BF),
            shape(heads, TOK),
            shape(KEYS, TOK, DK),
        ),
        (KEYS,),
        [wide_spec(DK), wide_spec(2 * DK), whole(beta), whole(decay)],
        (
            heads_spec(ROWS, DK),
            heads_spec(TOK, TOK),
            heads_spec(TOK, 2 * DK),
            whole(decay),
            lead_spec(TOK, DK),
        ),
        (key, value, beta, decay),
        2 * 10**9,
    )


def attend_kernel(q_ref, k_ref, c_ref, cols_ref, x_ref, wu_ref, p_ref, car_ref, out_ref, xz_ref):
    j = pl.program_id(0)
    unit, _ = unit_keys(k_ref[...])
    query = q_ref[...]
    gram = mm_nt(query, unit)
    cols = cols_ref[0]
    inclusive = iota((TOK, TOK), 0) >= iota((TOK, TOK), 1)
    for a in range(2):
        c_col = cols[:, a : a + 1]
        ratio = jnp.exp(jnp.minimum(c_col - c_ref[pl.ds(2 * j + a, 1), :], 0.0))
        attend = jnp.where(inclusive, gram * ratio, 0.0).astype(BF)
        p_ref[a] = attend
        both = mm(attend, wu_ref[a])
        car_ref[a] = (jnp.exp(c_col) * query.astype(F32) - both[:, :DK]).astype(BF)
        out_ref[a] = both[:, DK:]
        tail = jnp.exp(c_col[TOK - 1 : TOK, :] - c_col) * unit
        xz_ref[a] = mm_tn(x_ref[a], tail).astype(BF)


def attend_pass(query, key, cums, cols, inverse, wu):
    heads = 2 * KEYS
    return call(
        attend_kernel,
        (
            shape(heads, TOK, TOK, dtype=BF),
            shape(heads, TOK, DK, dtype=BF),
            shape(heads, TOK, DK),
            shape(heads, TOK, DK, dtype=BF),
        ),
        (KEYS,),
        [
            wide_spec(DK),
            wide_spec(DK),
            whole(cums),
            lead_spec(TOK, DK),
            heads_spec(TOK, TOK),
            heads_spec(TOK, 2 * DK),
        ],
        (
            heads_spec(TOK, TOK),
            heads_spec(TOK, DK),
            heads_spec(TOK, DK),
            heads_spec(TOK, DK),
        ),
        (query, key, cums, cols, inverse, wu),
        10**9,
    )


def prefix_kernel(pay_ref, nx_ref, bx_ref, gx_ref, tot_ref):
    both = jnp.zeros((2 * DK, DK), F32)
    gate = jnp.ones((1, DK), F32)
    for i in range(SEG):
        nx_ref[i] = both[:DK].astype(BF)
        bx_ref[i] = both[DK:]
        gx_ref[i : i + 1, :] = gate
        block = pay_ref[i]
        step_gate = gate_of(block)
        moved = block[:DK].astype(F32)
        both = (
            step_gate * both
            - mm(both, block[:DK])
            + jnp.concatenate([gate * moved, block[DK : 2 * DK].astype(F32)], axis=0)
        )
        gate = gate * step_gate
    tot_ref[: 2 * DK, :] = both.astype(BF)
    full = jnp.broadcast_to(gate, (16, DK))
    one = full.astype(BF)
    two = (full - one.astype(F32)).astype(BF)
    three = (full - one.astype(F32) - two.astype(F32)).astype(BF)
    place = iota((16, DK), 0)
    tot_ref[2 * DK :, :] = jnp.where(
        place == 0,
        one.astype(F32),
        jnp.where(place == 1, two.astype(F32), jnp.where(place == 2, three.astype(F32), 0.0)),
    ).astype(BF)


def prefix_pass(pay):
    outs = (
        shape(SEG, DK, DK, dtype=BF),
        shape(SEG, DK, DK),
        shape(SEG, DK),
        shape(ROWS, DK, dtype=BF),
    )
    return call(
        prefix_kernel, outs, (1,), [whole(pay)], tuple(whole(o) for o in outs), (pay,), 10**8
    )


def suffix_kernel(pay_ref, ns_ref, gs_ref):
    later = jnp.zeros((DK, DK), F32)
    gate = jnp.ones((1, DK), F32)
    for i in reversed(range(SEG)):
        ns_ref[i] = later.astype(BF)
        gs_ref[i : i + 1, :] = gate
        block = pay_ref[i]
        step_gate = gate_of(block)
        moved = block[:DK]
        later = step_gate * later + gate * moved.astype(F32) - mm(moved, later)
        gate = gate * step_gate


def suffix_pass(pay):
    outs = (shape(SEG, DK, DK, dtype=BF), shape(SEG, DK))
    return call(
        suffix_kernel, outs, (1,), [whole(pay)], tuple(whole(o) for o in outs), (pay,), 10**8
    )


def enter_kernel(place_ref, one_ref, two_ref, three_ref, nx_ref, bx_ref, gx_ref, s_ref):
    here = place_ref[1]
    state = jnp.zeros((DK, DK), F32)
    for back, ref in ((3, three_ref), (2, two_ref), (1, one_ref)):
        block = ref[...]
        moved = (
            gate_of(block) * state - mm(state, block[:DK]) + block[DK : 2 * DK].astype(F32)
        )
        state = jnp.where(here >= back, moved, state)
    for i in range(SEG):
        s_ref[i] = (gx_ref[i : i + 1, :] * state - mm(state, nx_ref[i]) + bx_ref[i]).astype(BF)


def enter_pass(place, totals, nx, bx, gx):
    out = shape(SEG, DK, DK, dtype=BF)
    args = (*totals, nx, bx, gx)
    return call(
        enter_kernel,
        (out,),
        (1,),
        [whole(a) for a in args],
        (whole(out),),
        args,
        10**8,
        prefetch=place,
    )[0]


def norm_kernel(s_ref, car_ref, loc_ref, gn_ref, norm_ref, do_ref, dir_ref):
    for a in range(2):
        carried = car_ref[a]
        head = loc_ref[a] + mm_nt(carried, s_ref[a])
        scale = lax.rsqrt(lane_sum(head * head) * (1.0 / DK) + EPS)
        normed = head * scale
        norm_ref[:, a * DK : (a + 1) * DK] = normed.astype(BF)
        grad = gn_ref[:, a * DK : (a + 1) * DK]
        inner = lane_sum(grad * normed) * (1.0 / DK)
        back = (scale * (grad - normed * inner)).astype(BF)
        do_ref[a] = back
        dir_ref[a] = mm_tn(back, carried).astype(BF)


def norm_pass(state, carried, local, grad_normed):
    heads = 2 * KEYS
    return call(
        norm_kernel,
        (
            shape(TOK, heads * DK, dtype=BF),
            shape(heads, TOK, DK, dtype=BF),
            shape(heads, DK, DK, dtype=BF),
        ),
        (KEYS,),
        [heads_spec(DK, DK), heads_spec(TOK, DK), heads_spec(TOK, DK), wide_spec(2 * DK)],
        (wide_spec(2 * DK), heads_spec(TOK, DK), heads_spec(DK, DK)),
        (state, carried, local, grad_normed),
        10**8,
    )


def middle_kernel(
    q_ref, k_ref, v_ref, c_ref, cols_ref, s_ref, do_ref, p_ref, x_ref, wu_ref,
    dq_ref, u_ref, dk_ref, e_ref, y_ref, dcc_ref, dcr_ref,
):
    j = pl.program_id(0)
    unit, _ = unit_keys(k_ref[...])
    low = unit.astype(BF)
    query = q_ref[...]
    wide = query.astype(F32)
    cols = cols_ref[0]
    inclusive = iota((TOK, TOK), 0) >= iota((TOK, TOK), 1)
    lane = iota((TOK, DK), 1)
    sub = iota((8, TOK), 0)
    down = jnp.zeros((TOK, DK), F32)
    across = jnp.zeros((8, TOK), F32)
    pair_sum = jnp.zeros((TOK, TOK), F32)
    grad_query = jnp.zeros((TOK, DK), F32)
    for a in range(2):
        c_col = cols[:, a : a + 1]
        growth = jnp.exp(c_col)
        state, back, attend = s_ref[a], do_ref[a], p_ref[a]
        update = (wu_ref[a, :, DK:].astype(F32) - mm_nt(wu_ref[a, :, :DK], state)).astype(BF)
        u_ref[a] = update
        pairs = mm_nt(back, update)
        ratio = jnp.exp(jnp.minimum(c_col - c_ref[pl.ds(2 * j + a, 1), :], 0.0))
        pair_sum += jnp.where(inclusive, pairs * ratio, 0.0)
        shares = pairs * attend.astype(F32)
        reached = growth * mm(back, state)
        grad_query += reached
        down = jnp.where(lane == a, lane_sum(shares) + lane_sum(reached * wide), down)
        across = jnp.where(sub == a, -jnp.sum(shares, axis=0, keepdims=True), across)
        e_ref[a] = mm_tn(x_ref[a], mm_tn(attend, back))
        value = v_ref[:, a * DK : (a + 1) * DK].astype(F32)
        y_ref[a] = (value - growth * mm_nt(low, state)).astype(BF)
    pair_low = pair_sum.astype(BF)
    dq_ref[...] = grad_query + mm(pair_low, low)
    dk_ref[...] = mm_tn(pair_low, query)
    dcc_ref[0] = down
    dcr_ref[0] = across


def middle_pass(query, key, value, cums, cols, state, back, attend, inverse, wu):
    heads = 2 * KEYS
    return call(
        middle_kernel,
        (
            shape(TOK, KEYS * DK),
            shape(heads, TOK, DK, dtype=BF),
            shape(TOK, KEYS * DK),
            shape(heads, TOK, DK),
            shape(heads, TOK, DK, dtype=BF),
            shape(KEYS, TOK, DK),
            shape(KEYS, 8, TOK),
        ),
        (KEYS,),
        [
            wide_spec(DK),
            wide_spec(DK),
            wide_spec(2 * DK),
            whole(cums),
            lead_spec(TOK, DK),
            heads_spec(DK, DK),
            heads_spec(TOK, DK),
            heads_spec(TOK, TOK),
            heads_spec(TOK, TOK),
            heads_spec(TOK, 2 * DK),
        ],
        (
            wide_spec(DK),
            heads_spec(TOK, DK),
            wide_spec(DK),
            heads_spec(TOK, DK),
            heads_spec(TOK, DK),
            lead_spec(TOK, DK),
            lead_spec(8, TOK),
        ),
        (query, key, value, cums, cols, state, back, attend, inverse, wu),
        2 * 10**9,
    )


def later_kernel(pay_ref, dir_ref, d_ref, tot_ref):
    total = jnp.zeros((DK, DK), F32)
    for i in reversed(range(SEG)):
        d_ref[i] = total
        block = pay_ref[i]
        total = gate_of(block) * total - mm_nt(total, block[:DK]) + dir_ref[i].astype(F32)
    tot_ref[...] = total.astype(BF)


def later_pass(pay, direct):
    outs = (shape(SEG, DK, DK), shape(DK, DK, dtype=BF))
    args = (pay, direct)
    return call(
        later_kernel,
        outs,
        (1,),
        [whole(a) for a in args],
        tuple(whole(o) for o in outs),
        args,
        10**8,
    )


def leave_kernel(
    place_ref, one_ref, two_ref, three_ref, g1_ref, g2_ref, g3_ref, ns_ref, gs_ref, d_ref, g_ref
):
    here = place_ref[1]
    total = jnp.zeros((DK, DK), F32)
    for ahead, ref, grad in ((3, one_ref, g3_ref), (2, two_ref, g2_ref), (1, three_ref, g1_ref)):
        block = ref[...]
        moved = gate_of(block) * total - mm_nt(total, block[:DK]) + grad[...].astype(F32)
        total = jnp.where(here + ahead < NY, moved, total)
    for i in range(SEG):
        g_ref[i] = (gs_ref[i : i + 1, :] * total - mm_nt(total, ns_ref[i]) + d_ref[i]).astype(BF)


def leave_pass(place, totals, grads, ns, gs, directs):
    out = shape(SEG, DK, DK, dtype=BF)
    args = (*totals, *grads, ns, gs, directs)
    return call(
        leave_kernel,
        (out,),
        (1,),
        [whole(a) for a in args],
        (whole(out),),
        args,
        10**8,
        prefetch=place,
    )[0]


def last_kernel(
    k_ref, c_ref, cols_ref, s_ref, g_ref, e_ref, y_ref, u_ref, xz_ref, dk0_ref, dcc_ref, dcr_ref,
    dv_ref, dk_ref, db_ref, dd_ref,
):
    j = pl.program_id(0)
    unit, rate = unit_keys(k_ref[...])
    low = unit.astype(BF)
    gram = mm_nt(low, low)
    cols = cols_ref[0]
    strict = iota((TOK, TOK), 0) > iota((TOK, TOK), 1)
    last = iota((TOK, 1), 0) == TOK - 1
    lane = iota((TOK, DK), 1)
    down = jnp.zeros((TOK, DK), F32)
    pair_sum = jnp.zeros((TOK, TOK), F32)
    grad_key = dk0_ref[...]
    across = []
    for a in range(2):
        c_col, beta_col = cols[:, a : a + 1], cols[:, 2 + a : 3 + a]
        growth = jnp.exp(c_col)
        end = c_col[TOK - 1 : TOK, :]
        state, later, update = s_ref[a], g_ref[a], u_ref[a]
        error = e_ref[a] + mm_nt(xz_ref[a], later)
        ratio = jnp.exp(jnp.minimum(c_col - c_ref[pl.ds(2 * j + a, 1), :], 0.0))
        pairs = jnp.where(strict, -mm_nt(error, update) * ratio, 0.0)
        shares = pairs * gram
        row_share = lane_sum(shares)
        across.append(jnp.sum(beta_col * shares, axis=0, keepdims=True))
        pair_sum += beta_col * pairs
        grad_value = beta_col * error
        dv_ref[:, a * DK : (a + 1) * DK] = grad_value
        reached = growth * mm(grad_value, state)
        tail = jnp.exp(end - c_col) * mm(update, later)
        grad_key += tail - reached
        tail_share = lane_sum(tail * unit)
        gate_share = jnp.exp(end) * jnp.sum(
            lane_sum(state.astype(F32) * later.astype(F32)), axis=0, keepdims=True
        )
        total = jnp.sum(tail_share, axis=0, keepdims=True) + gate_share
        grad_cum = beta_col * row_share - lane_sum(reached * unit) - tail_share
        grad_cum += jnp.where(last, total, 0.0)
        grad_beta = row_share + lane_sum(error * y_ref[a].astype(F32))
        down = jnp.where(lane == a, grad_cum, jnp.where(lane == 2 + a, grad_beta, down))
    pair_low = pair_sum.astype(BF)
    grad_key += mm(pair_low, low) + mm_tn(pair_low, low)
    dk_ref[...] = rate * (grad_key - unit * lane_sum(unit * grad_key))
    turned = jnp.transpose(down + jnp.where(lane < 2, dcc_ref[0], 0.0))[:8]
    sub = iota((8, TOK), 0)
    cum = turned + dcr_ref[0]
    for a in range(2):
        cum = jnp.where(sub == a, cum - across[a], cum)
    decayed = suffix_lanes(cum)
    for a in range(2):
        mine = sub == 2 * j + a
        dd_ref[...] = jnp.where(mine, decayed[a : a + 1], dd_ref[...])
        db_ref[...] = jnp.where(mine, turned[2 + a : 3 + a], db_ref[...])


def last_pass(key, cums, cols, state, later, error, y, update, xz, dk0, dcc, dcr):
    heads = 2 * KEYS
    return call(
        last_kernel,
        (
            shape(TOK, heads * DK),
            shape(TOK, KEYS * DK),
            shape(heads, TOK),
            shape(heads, TOK),
        ),
        (KEYS,),
        [
            wide_spec(DK),
            whole(cums),
            lead_spec(TOK, DK),
            heads_spec(DK, DK),
            heads_spec(DK, DK),
            heads_spec(TOK, DK),
            heads_spec(TOK, DK),
            heads_spec(TOK, DK),
            heads_spec(TOK, DK),
            wide_spec(DK),
            lead_spec(TOK, DK),
            lead_spec(8, TOK),
        ],
        (wide_spec(2 * DK), wide_spec(DK), whole(cums), whole(cums)),
        (key, cums, cols, state, later, error, y, update, xz, dk0, dcc, dcr),
        2 * 10**9,
    )


def back_kernel(place_ref, cot_ref, w_ref, out_ref):
    part = mm(cot_ref[0], w_ref[...])

    @pl.when(pl.program_id(0) == 0)
    def _():
        out_ref[...] = part

    @pl.when(pl.program_id(0) > 0)
    def _():
        out_ref[...] += part


def back_pass(place, cot, weight):
    depth, wide = cot.shape[2], weight.shape[1]
    out = shape(TOK, wide)
    return call(
        back_kernel,
        (out,),
        (NH,),
        [
            pl.BlockSpec((1, TOK, depth), lambda k, place: (k, 0, 0)),
            pl.BlockSpec((depth, wide), lambda k, place: ((place[0] + k) % NH, 0)),
        ],
        (whole(out),),
        (cot, weight),
        2 * TOK * NH * depth * wide,
        prefetch=place,
    )[0]


def mix_kernel(place_ref, norm_ref, w_ref, out_ref):
    out_ref[0] = mm_nt(norm_ref[...], w_ref[...]).astype(BF)


def mix_pass(place, normed, weight):
    depth = weight.shape[0] // NH
    out = shape(NH, TOK, depth, dtype=BF)
    return call(
        mix_kernel,
        (out,),
        (NH,),
        [
            whole(normed),
            pl.BlockSpec((depth, weight.shape[1]), lambda k, place: ((place[0] + k) % NH, 0)),
        ],
        (pl.BlockSpec((1, TOK, depth), lambda k, place: (k, 0, 0)),),
        (normed, weight),
        2 * TOK * weight.size,
        prefetch=place,
    )[0]


def outer_kernel(place_ref, cot_ref, norm_ref, mine_ref, other_ref):
    here, core = place_ref[2], place_ref[3]
    rows = mine_ref.shape[2]
    for k in range(NZ):
        start = pl.multiple_of(((here + k) % NZ) * 2 * rows, 2 * rows)
        part = mm_tn(cot_ref[0, :, pl.ds(start, 2 * rows)], norm_ref[...]).astype(BF)
        first = core == 0
        mine_ref[0, k] = jnp.where(first, part[:rows], part[rows:])
        other_ref[0, k] = jnp.where(first, part[rows:], part[:rows])


def outer_pass(place, cot, normed):
    rows = cot.shape[2] // (NZ * NC)
    out = shape(NY, NZ, rows, normed.shape[1], dtype=BF)
    spec = pl.BlockSpec((1, NZ, rows, normed.shape[1]), lambda k, place: (k, 0, 0, 0))
    return call(
        outer_kernel,
        (out, out),
        (NY,),
        [
            pl.BlockSpec(
                (1, TOK, cot.shape[2]), lambda k, place: ((place[1] + k - place[0] + NH) % NH, 0, 0)
            ),
            whole(normed),
        ],
        (spec, spec),
        (cot, normed),
        2 * cot.size * normed.shape[1],
        prefetch=place,
    )


def shift(array, axis, count, step):
    return lax.ppermute(array, axis, [(i, (i + step) % count) for i in range(count)])


def scatter_stage(parts, axis, count):
    total = parts[0].astype(F32)
    moved = [shift(parts[k].astype(BF), axis, count, k) for k in range(1, count)]
    for part in moved:
        total = total + part.astype(F32)
    return total


def body(query, key, value, beta, decay, wo_start, wo_end, curve_index, cotangent):
    place = jnp.stack([lax.axis_index(a) for a in ("head", "y", "z", "c")]).astype(jnp.int32)
    position = curve_index[0].astype(F32) / (CURVE_POINTS - 1)
    weight_local = (
        (1.0 - position) * wo_start.astype(F32) + position * wo_end.astype(F32)
    ).astype(BF)
    weight = lax.all_gather(weight_local, RING, axis=0, tiled=True)
    cot = jnp.stack([cotangent] + [shift(cotangent, "head", NH, -k) for k in range(1, NH)])

    pay, inverse, wu, cums, cols = pre_pass(key, value, beta, decay)
    pays = lax.all_to_all(pay, ("z", "c"), 0, 0, tiled=True)
    attend, carried, local, xz = attend_pass(query, key, cums, cols, inverse, wu)
    nx, bx, gx, total = prefix_pass(pays)
    totals = [shift(total, "y", NY, k) for k in range(1, NY)]
    ns, gs = suffix_pass(pays)
    states = enter_pass(place, totals, nx, bx, gx)
    state = lax.all_to_all(states, ("z", "c"), 0, 0, tiled=True)
    grad_normed = back_pass(place, cot, weight)
    normed, back, direct = norm_pass(state, carried, local, grad_normed)

    directs = lax.all_to_all(direct, ("z", "c"), 0, 0, tiled=True)
    mine, other = outer_pass(place, cot, normed)
    got = lax.ppermute(other, "c", [(0, 1), (1, 0)])
    grad_query, update, dk0, error, y, dcc, dcr = middle_pass(
        query, key, value, cums, cols, state, back, attend, inverse, wu
    )
    mixes = mix_pass(place, normed, weight)
    mixed = scatter_stage([mixes[k] for k in range(NH)], "head", NH).astype(BF)
    suffixes, grad_total = later_pass(pays, directs)
    grads = [shift(grad_total, "y", NY, -k) for k in range(1, NY)]
    laters = leave_pass(place, totals, grads, ns, gs, suffixes)
    later = lax.all_to_all(laters, ("z", "c"), 0, 0, tiled=True)

    pair = mine.astype(F32) + got.astype(F32)
    wide = pair.shape[-1] // 2
    left, right = pair[..., :wide], pair[..., wide:]
    left = scatter_stage([left[:, k] for k in range(NZ)], "z", NZ)
    right = scatter_stage([right[k] for k in range(NY)], "y", NY)
    left = scatter_stage([left[k] for k in range(NY)], "y", NY)
    right = scatter_stage([right[k] for k in range(NZ)], "z", NZ)
    grad_weight = jnp.concatenate([left, right], axis=-1)

    grad_value, grad_key, grad_beta, grad_decay = last_pass(
        key, cums, cols, state, later, error, y, update, xz, dk0, dcc, dcr
    )
    return (
        mixed,
        grad_query,
        grad_key,
        grad_value,
        grad_beta,
        grad_decay,
        (1.0 - position) * grad_weight,
        position * grad_weight,
    )


def solution(mesh):
    fine = Mesh(mesh.devices.reshape(NY, NZ, NC, NH), ("y", "z", "c", "head"))
    rows, flipped = P(RING, "head"), P("head", RING)
    return jax.shard_map(
        body,
        mesh=fine,
        in_specs=(rows, rows, rows, flipped, flipped, rows, rows, P(), rows),
        out_specs=(rows, rows, rows, rows, flipped, flipped, rows, rows),
        check_vma=False,
    )
```

time: 954 us -> 199 us (0.21); the launches traced: 935 us -> 198 us
  waiting for transfers between devices: 502 us -> 37.3 us
  matrix products: 280 us -> 0 us
  local copies, waits for them, and re-layouts: 105 us -> 30.9 us
  Pallas kernels: 0 us -> 53.6 us
  starting transfers between devices: 0.32 us -> 51.4 us
  other arithmetic: 25.4 us -> 9.39 us
    all_gather x6 -> x1, waiting for transfers between devices: 303 us -> 0.02 us  [body(): weight = lax.all_gather(weight_local, RING, axis=0, tiled=True)]
    dot_general x222 -> x0, matrix products: 280 us -> none  [the longest x199 246 us: matmul_high(): return jnp.matmul(left, right, precision=lax.Precision.HIGHEST)]
    reduce_scatter x2 -> x0, waiting for transfers between devices: 197 us -> none  [the longest x1 113 us: body(): lax.psum_scatter(partial_out, 'head', scatter_dimension=1, tiled=True)]
    pallas_call x0 -> x13, Pallas kernels: none -> 53.6 us  [call(): pl.pallas_call(kernel, out_shape=out_shape, compiler_params=pltpu.Compile...]
    dynamic_slice x66 -> x0, local copies, waits for them, and re-layouts: 40.1 us -> none  [the longest x62 39.6 us: one(): lax.dynamic_index_in_dim(a, source, 0, False)]
    ppermute x0 -> x25, starting transfers between devices: none -> 34.9 us  [the longest x24 34.9 us: shift(): lax.ppermute(array, axis, [(i, (i + step) % count) for i in range(count)])]
    ppermute x0 -> x25, waiting for transfers between devices: none -> 22.5 us  [the longest x24 22.5 us: shift(): lax.ppermute(array, axis, [(i, (i + step) % count) for i in range(count)])]
    all_to_all x0 -> x4, starting transfers between devices: none -> 16.4 us  [the longest x1 5.4 us: body(): pays = lax.all_to_all(pay, ('z', 'c'), 0, 0, tiled=True)]
  transfers between devices with their start and end apart: 8 -> 30, of which waited for: 7 -> 12; matrix products, arithmetic and copies ran while one was open for 10% -> 2% of each run, Pallas kernels for 0% -> 23%
where the time goes in v1:
time: 199 us; the launch traced here: 198 us
  Pallas kernels  53.6 us (27%)
  starting transfers between devices  51.4 us (26%)
  waiting for transfers between devices  37.3 us (19%)
  local copies, waits for them, and re-layouts  30.9 us (16%)
  between operations  15 us (8%)
  other arithmetic  9.39 us (5%)
    pallas_call x13, Pallas kernels, call(): pl.pallas_call(kernel, out_shape=out_shape, compiler_params=pltpu.Compile...  53.6 us
    ppermute x24, starting transfers between devices, shift(): lax.ppermute(array, axis, [(i, (i + step) % count) for i in range(count)])  34.9 us
    unnamed x84, local copies, waits for them, and re-layouts  29.8 us
    ppermute x24, waiting for transfers between devices, shift(): lax.ppermute(array, axis, [(i, (i + step) % count) for i in range(count)])  22.5 us
    all_to_all x1, waiting for transfers between devices, body(): later = lax.all_to_all(laters, ('z', 'c'), 0, 0, tiled=True)  5.48 us
    all_to_all x1, starting transfers between devices, body(): pays = lax.all_to_all(pay, ('z', 'c'), 0, 0, tiled=True)  5.4 us
    all_to_all x1, waiting for transfers between devices, body(): pays = lax.all_to_all(pay, ('z', 'c'), 0, 0, tiled=True)  5.04 us
    all_to_all x1, starting transfers between devices, body(): state = lax.all_to_all(states, ('z', 'c'), 0, 0, tiled=True)  4.02 us
  transfers between devices with their start and end apart: 30, of which 12 were waited for; matrix products, arithmetic and copies ran while one was open for 2% of the time, Pallas kernels for 23%

profile of v1, /device:TPU:0, one launch (start us, length us, event | category | flops | bytes accessed | tf_op | source)
XLA Modules:
  0.0 197.6 jit_solution(8598901167525642739)
XLA Ops:
  7.9 1.7 add_convert_fusion
  9.6 1.0 copy-done.11
  13.0 13.0 %shard_map.152 = (bf16[8,272,128]{2,1,0:T(8,128)(2,1)}, bf16[8,256,256]{2,1,0:T(8,128)(2,1)S(1)}, bf16[8,256,256]{2,1,0:T(8,128)(2,1)S(1)}, f32[8,256]{1,0:T(8,128)S(1)}, f32[4,256,128]{2,1,0:T(8,128)S(1)}) custom-call(bf16[256,512]{1,0:T(8,128)(2,1)S(1)} %copy-done.17, bf16[256,1024]{1,0:T(8,128)(2,1)S(1)} %copy-done.11, f32[8,256]{1,0:T(8,128)S(1)} %copy-done.21, ...), custom_call_target="tpu_custom_call" | custom-call | flops 2000000000 | bytes 3989504 | tf_op jit(solution)/shard_map/pallas_call | solution.py:58
  26.0 1.0 copy-done.24
  27.7 5.4 %all-to-all-start = ((bf16[8,272,128]{2,1,0:T(8,128)(2,1)}), bf16[8,272,128]{2,1,0:T(8,128)(2,1)S(1)}, u32[]{:S(2)}, u32[]{:S(2)}) async-start(bf16[8,272,128]{2,1,0:T(8,128)(2,1)} %get-tuple-element.41), calls=%async_computation | async-start | bytes 1114112 | tf_op jit(solution)/shard_map/all_to_all | solution.py:717
  33.1 1.5 collective-permute-start.5
  34.6 2.7 %collective-permute-start.4 = (bf16[256,512]{1,0:T(8,128)(2,1)}, bf16[256,512]{1,0:T(8,128)(2,1)}, u32[]{:S(2)}, u32[]{:S(2)}) collective-permute-start(bf16[256,512]{1,0:T(8,128)(2,1)} %param.17), channel_id=1, source_target_pairs={{0,2},{1,3},{2,0},{3,1},{4,6},{5,7},{6,4},{7,5},{8,10},{9,11},{10,... | collective-permute-start | bytes 786440 | tf_op jit(solution)/shard_map/ppermute | solution.py:696
  37.4 1.4 collective-permute-start.3
  38.8 5.0 %all-to-all-done.pay_ref = bf16[8,272,128]{2,1,0:T(8,128)(2,1)S(1)} async-done(((bf16[8,272,128]{2,1,0:T(8,128)(2,1)}), bf16[8,272,128]{2,1,0:T(8,128)(2,1)S(1)}, u32[]{:S(2)}, u32[]{:S(2)}) %all-to-all-start) | async-done | bytes 557088 | tf_op jit(solution)/shard_map/all_to_all | solution.py:717
  43.8 1.0 shard_map.153
  44.8 1.6 collective-permute-start
  46.6 2.9 %collective-permute-start.1 = (bf16[272,128]{1,0:T(8,128)(2,1)S(1)}, bf16[272,128]{1,0:T(8,128)(2,1)S(1)}, u32[]{:S(2)}, u32[]{:S(2)}) collective-permute-start(bf16[272,128]{1,0:T(8,128)(2,1)S(1)} %get-tuple-element.42), channel_id=1, source_target_pairs={{0,64},{32,96},{64,0},{96,32},{1,65},{33,97},{65,1},{97,33},{2,66}... | collective-permute-start | bytes 208904 | tf_op jit(solution)/shard_map/ppermute | solution.py:696
  49.5 2.4 %collective-permute-done.one_ref = bf16[272,128]{1,0:T(8,128)(2,1)S(1)} collective-permute-done((bf16[272,128]{1,0:T(8,128)(2,1)S(1)}, bf16[272,128]{1,0:T(8,128)(2,1)S(1)}, u32[]{:S(2)}, u32[]{:S(2)}) %collective-permute-start) | collective-permute-done | bytes 69664 | tf_op jit(solution)/shard_map/ppermute | solution.py:696
  51.9 1.0 collective-permute-start.2
  52.9 1.0 copy-done.27
  53.9 3.7 %shard_map.155 = (bf16[8,256,256]{2,1,0:T(8,128)(2,1)S(1)}, bf16[8,256,128]{2,1,0:T(8,128)(2,1)S(1)}, f32[8,256,128]{2,1,0:T(8,128)S(1)}, bf16[8,256,128]{2,1,0:T(8,128)(2,1)S(1)}) custom-call(bf16[256,512]{1,0:T(8,128)(2,1)S(1)} %copy-done.15, bf16[256,512]{1,0:T(8,128)(2,1)S(1)} %copy-done.18, f32[8,256]{1,0:T(8,128)S(1)} %get-tuple-element.46.c_ref, ...), custom_call_target="tpu_custom_call" | custom-call | flops 1000000000 | bytes 6299648 | tf_op jit(solution)/shard_map/pallas_call | solution.py:58
  57.7 1.0 copy-done.2
  60.3 1.8 shard_map.154
  62.1 4.0 %all-to-all-start.1 = ((bf16[8,128,128]{2,1,0:T(8,128)(2,1)}), bf16[8,128,128]{2,1,0:T(8,128)(2,1)S(1)}, u32[]{:S(2)}, u32[]{:S(2)}) async-start(bf16[8,128,128]{2,1,0:T(8,128)(2,1)} %shard_map.154), calls=%async_computation.1 | async-start | bytes 524288 | tf_op jit(solution)/shard_map/all_to_all | solution.py:723
  66.2 1.3 pad_maximum_fusion.cot_ref
  67.6 4.7 %shard_map.156.gn_ref = f32[256,1024]{1,0:T(8,128)S(1)} custom-call(s32[4]{0:T(128)S(1)} %pad_add_fusion.place_ref, bf16[4,256,512]{2,1,0:T(8,128)(2,1)S(1)} %pad_maximum_fusion.cot_ref, bf16[2048,1024]{1,0:T(8,128)(2,1)} %all-gather.2.cloned.1.call-done.w_ref), custom_call_target="tpu_custom_call" | custom-call | flops 1073741824 | bytes 6291456 | tf_op jit(solution)/shard_map/pallas_call | solution.py:58
  72.3 1.4 all-to-all-done.1.s_ref
  73.7 1.2 copy-done.3
  74.9 1.0 copy-done.5
  76.0 3.8 %shard_map.157 = (bf16[256,1024]{1,0:T(8,128)(2,1)S(1)}, bf16[8,256,128]{2,1,0:T(8,128)(2,1)S(1)}, bf16[8,128,128]{2,1,0:T(8,128)(2,1)S(1)}) custom-call(bf16[8,128,128]{2,1,0:T(8,128)(2,1)S(1)} %all-to-all-done.1.s_ref, bf16[8,256,128]{2,1,0:T(8,128)(2,1)S(1)} %copy-done.5, f32[8,256,128]{2,1,0:T(8,128)S(1)} %copy-done.3, f32[256,1024]{1,0:T(8,128)S(1)} %shard_map.156.gn_ref), custom_call_target="tpu_custom_call" | custom-call | flops 100000000 | bytes 4194304 | tf_op jit(solution)/shard_map/pallas_call | solution.py:58
  81.3 3.7 %shard_map.164 = (bf16[4,4,64,1024]{3,2,1,0:T(8,128)(2,1)S(1)}, bf16[4,4,64,1024]{3,2,1,0:T(8,128)(2,1)}) custom-call(s32[4]{0:T(128)S(1)} %pad_add_fusion.place_ref, bf16[4,256,512]{2,1,0:T(8,128)(2,1)S(1)} %pad_maximum_fusion.cot_ref, bf16[256,1024]{1,0:T(8,128)(2,1)S(1)} %get-tuple-element.52.norm_ref), custom_call_target="tpu_custom_call" | custom-call | flops 1073741824 | bytes 5767168 | tf_op jit(solution)/shard_map/pallas_call | solution.py:58
  85.0 1.3 copy-done.1
  86.3 3.6 %all-to-all-start.2 = ((bf16[8,128,128]{2,1,0:T(8,128)(2,1)}), bf16[8,128,128]{2,1,0:T(8,128)(2,1)S(1)}, u32[]{:S(2)}, u32[]{:S(2)}) async-start(bf16[8,128,128]{2,1,0:T(8,128)(2,1)} %copy-done.10), calls=%async_computation.2 | async-start | bytes 524288 | tf_op jit(solution)/shard_map/all_to_all | solution.py:727
  89.9 2.2 %copy-done = bf16[2048,1024]{1,0:T(8,128)(2,1)S(1)} copy-done((bf16[2048,1024]{1,0:T(8,128)(2,1)S(1)}, bf16[2048,1024]{1,0:T(8,128)(2,1)}, u32[]{:S(2)}) %copy-start) | copy-done | bytes 4194328
  92.1 2.5 %shard_map.158 = bf16[4,256,512]{2,1,0:T(8,128)(2,1)S(1)} custom-call(s32[4]{0:T(128)S(1)} %pad_add_fusion.place_ref, bf16[256,1024]{1,0:T(8,128)(2,1)S(1)} %get-tuple-element.52.norm_ref, bf16[2048,1024]{1,0:T(8,128)(2,1)S(1)} %copy-done), custom_call_target="tpu_custom_call" | custom-call | flops 1073741824 | bytes 5767168 | tf_op jit(solution)/shard_map/pallas_call | solution.py:58
  94.6 2.8 %all-to-all-done.2.dir_ref = bf16[8,128,128]{2,1,0:T(8,128)(2,1)S(1)} async-done(((bf16[8,128,128]{2,1,0:T(8,128)(2,1)}), bf16[8,128,128]{2,1,0:T(8,128)(2,1)S(1)}, u32[]{:S(2)}, u32[]{:S(2)}) %all-to-all-start.2) | async-done | bytes 262176 | tf_op jit(solution)/shard_map/all_to_all | solution.py:727
  97.4 1.0 shard_map.160
  98.4 1.2 collective-permute-start.9
  100.5 3.2 %collective-permute-start.8 = (bf16[256,512]{1,0:T(8,128)(2,1)}, bf16[256,512]{1,0:T(8,128)(2,1)}, u32[]{:S(2)}, u32[]{:S(2)}) collective-permute-start(bf16[256,512]{1,0:T(8,128)(2,1)} %get-tuple-element.85), channel_id=1, source_target_pairs={{0,3},{1,0},{2,1},{3,2},{4,7},{5,4},{6,5},{7,6},{8,11},{9,8},{10,9... | collective-permute-start | bytes 786440 | tf_op jit(solution)/shard_map/ppermute | solution.py:696
  104.1 1.1 collective-permute-start.6
  105.2 1.0 collective-permute-start.10
  107.2 3.7 %collective-permute-done.10.g2_ref = bf16[128,128]{1,0:T(8,128)(2,1)S(1)} collective-permute-done((bf16[128,128]{1,0:T(8,128)(2,1)S(1)}, bf16[128,128]{1,0:T(8,128)(2,1)S(1)}, u32[]{:S(2)}, u32[]{:S(2)}) %collective-permute-start.10) | collective-permute-done | bytes 32800 | tf_op jit(solution)/shard_map/ppermute | solution.py:696
  111.2 1.0 copy-done.14
  113.2 1.0 copy-done.28
  114.3 6.2 %shard_map.159 = (f32[256,512]{1,0:T(8,128)}, bf16[8,256,128]{2,1,0:T(8,128)(2,1)S(1)}, f32[256,512]{1,0:T(8,128)S(1)}, f32[8,256,128]{2,1,0:T(8,128)S(1)}, bf16...) custom-call(bf16[256,512]{1,0:T(8,128)(2,1)S(1)} %copy-done.16, ...), custom_call_target="tpu_custom_call" | custom-call | flops 2000000000 | bytes 9216000 | tf_op jit(solution)/shard_map/pallas_call | solution.py:58
  120.4 1.0 copy-done.32
  124.7 1.9 shard_map.162
  126.7 3.4 %all-to-all-start.3 = ((bf16[8,128,128]{2,1,0:T(8,128)(2,1)}), bf16[8,128,128]{2,1,0:T(8,128)(2,1)S(1)}, u32[]{:S(2)}, u32[]{:S(2)}) async-start(bf16[8,128,128]{2,1,0:T(8,128)(2,1)} %shard_map.162), calls=%async_computation.3 | async-start | bytes 524288 | tf_op jit(solution)/shard_map/all_to_all | solution.py:738
  130.1 1.9 fusion.8
  132.1 5.5 %all-to-all-done.3.g_ref = bf16[8,128,128]{2,1,0:T(8,128)(2,1)S(1)} async-done(((bf16[8,128,128]{2,1,0:T(8,128)(2,1)}), bf16[8,128,128]{2,1,0:T(8,128)(2,1)S(1)}, u32[]{:S(2)}, u32[]{:S(2)}) %all-to-all-start.3) | async-done | bytes 262176 | tf_op jit(solution)/shard_map/all_to_all | solution.py:738
  137.5 1.0 copy-done.31
  138.6 1.2 copy-done.33
  139.8 1.0 copy-done.35
  140.9 1.0 copy-done.37
  141.9 1.0 copy-done.39
  142.9 1.0 copy-done.41
  144.0 9.3 %shard_map.163 = (f32[256,1024]{1,0:T(8,128)}, f32[256,512]{1,0:T(8,128)}, f32[8,256]{1,0:T(8,128)}, f32[8,256]{1,0:T(8,128)}) custom-call(bf16[256,512]{1,0:T(8,128)(2,1)S(1)} %copy-done.20, f32[8,256]{1,0:T(8,128)S(1)} %get-tuple-element.46.c_ref, f32[4,256,128]{2,1,0:T(8,128)S(1)} %copy-done.29, bf16[8,128,128]{2,1,0:T(8,128)(2,1)S(1)} %all-to-all-done.1.s_ref, ...), custom_call_target="tpu_custom_call" | custom-call | flops 2000000000 | bytes 6610944 | tf_op jit(solution)/shard_map/pallas_call | solution.py:58
  153.2 3.2 %convert_add_fusion = f32[4,4,64,1024]{3,2,1,0:T(8,128)S(1)} fusion(bf16[4,4,64,1024]{3,2,1,0:T(8,128)(2,1)} %collective-permute-done.12, bf16[4,4,64,1024]{3,2,1,0:T(8,128)(2,1)} %copy-done.1), kind=kLoop, calls=%fused_computation | loop fusion | flops 3145728 | bytes 8388608 | tf_op jit(solution)/shard_map/add | solution.py:740
  156.5 3.0 %collective-permute-start.21 = (bf16[4,64,512]{2,1,0:T(8,128)(2,1)S(1)}, bf16[4,64,512]{2,1,0:T(8,128)(2,1)S(1)}, u32[]{:S(2)}, u32[]{:S(2)}) collective-permute-start(bf16[4,64,512]{2,1,0:T(8,128)(2,1)S(1)} %get-tuple-element.82), channel_id=1, source_target_pairs={{0,96},{32,0},{64,32},{96,64},{1,97},{33,1},{65,33},{97,65},{2,98}... | collective-permute-start | bytes 786440 | tf_op jit(solution)/shard_map/ppermute | solution.py:696
  160.6 1.2 collective-permute-start.15
  161.8 1.5 collective-permute-start.14
  163.3 7.0 %collective-permute-done.21 = bf16[4,64,512]{2,1,0:T(8,128)(2,1)S(1)} collective-permute-done((bf16[4,64,512]{2,1,0:T(8,128)(2,1)S(1)}, bf16[4,64,512]{2,1,0:T(8,128)(2,1)S(1)}, u32[]{:S(2)}, u32[]{:S(2)}) %collective-permute-start.21) | collective-permute-done | bytes 262176 | tf_op jit(solution)/shard_map/ppermute | solution.py:696
  170.9 2.8 %collective-permute-done.19 = bf16[4,64,512]{2,1,0:T(8,128)(2,1)S(1)} collective-permute-done((bf16[4,64,512]{2,1,0:T(8,128)(2,1)S(1)}, bf16[4,64,512]{2,1,0:T(8,128)(2,1)S(1)}, u32[]{:S(2)}, u32[]{:S(2)}) %collective-permute-start.19) | collective-permute-done | bytes 262176 | tf_op jit(solution)/shard_map/ppermute | solution.py:696
  173.9 1.2 collective-permute-start.24
  175.2 1.5 collective-permute-start.23
  176.7 1.3 collective-permute-done.13
  178.1 5.6 %collective-permute-start.18 = (bf16[64,512]{1,0:T(8,128)(2,1)S(1)}, bf16[64,512]{1,0:T(8,128)(2,1)S(1)}, u32[]{:S(2)}, u32[]{:S(2)}) collective-permute-start(bf16[64,512]{1,0:T(8,128)(2,1)S(1)} %get-tuple-element.90), channel_id=1, source_target_pairs={{0,96},{32,0},{64,32},{96,64},{1,97},{33,1},{65,33},{97,65},{2,98}... | collective-permute-start | bytes 196616 | tf_op jit(solution)/shard_map/ppermute | solution.py:696
  184.7 1.5 collective-permute-done.18
  186.2 3.4 %collective-permute-done.17 = bf16[64,512]{1,0:T(8,128)(2,1)S(1)} collective-permute-done((bf16[64,512]{1,0:T(8,128)(2,1)S(1)}, bf16[64,512]{1,0:T(8,128)(2,1)S(1)}, u32[]{:S(2)}, u32[]{:S(2)}) %collective-permute-start.17) | collective-permute-done | bytes 65568 | tf_op jit(solution)/shard_map/ppermute | solution.py:696
  (109 shorter events, 17.5 us)
Async XLA Ops:
  7.2 60.4 %all-gather.2.cloned.1.call-start = ((), (), s32[]{:S(2)}) async-start(), calls=%async_computation.4 | async-start | bytes 4325376 | tf_op jit(solution)/shard_map/all_gather | solution.py:713
  9.6 1.0 copy-start.11
  10.6 0.9 copy-start.17
  13.0 40.0 %copy-start.15 = (bf16[256,512]{1,0:T(8,128)(2,1)S(1)}, bf16[256,512]{1,0:T(8,128)(2,1)}, u32[]{:S(2)}) copy-start(bf16[256,512]{1,0:T(8,128)(2,1)} %q_ref.3) | copy-start | bytes 786436
  13.0 40.0 %copy-start.18 = (bf16[256,512]{1,0:T(8,128)(2,1)S(1)}, bf16[256,512]{1,0:T(8,128)(2,1)}, u32[]{:S(2)}) copy-start(bf16[256,512]{1,0:T(8,128)(2,1)} %k_ref.7) | copy-start | bytes 786436
  26.0 1.0 copy-start.24
  27.7 38.4 %copy-start.23 = (bf16[8,256,256]{2,1,0:T(8,128)(2,1)}, bf16[8,256,256]{2,1,0:T(8,128)(2,1)S(1)}, u32[]{:S(2)}) copy-start(bf16[8,256,256]{2,1,0:T(8,128)(2,1)S(1)} %get-tuple-element.48.x_ref) | copy-start | bytes 3145732
  27.7 16.1 %all-to-all-start = ((bf16[8,272,128]{2,1,0:T(8,128)(2,1)}), bf16[8,272,128]{2,1,0:T(8,128)(2,1)S(1)}, u32[]{:S(2)}, u32[]{:S(2)}) async-start(bf16[8,272,128]{2,1,0:T(8,128)(2,1)} %get-tuple-element.41), calls=%async_computation | async-start | bytes 1114112 | tf_op jit(solution)/shard_map/all_to_all | solution.py:717
  33.1 33.0 %collective-permute-start.5 = (bf16[256,512]{1,0:T(8,128)(2,1)}, bf16[256,512]{1,0:T(8,128)(2,1)}, u32[]{:S(2)}, u32[]{:S(2)}) collective-permute-start(bf16[256,512]{1,0:T(8,128)(2,1)} %param.17), channel_id=1, source_target_pairs={{0,1},{1,2},{2,3},{3,0},{4,5},{5,6},{6,7},{7,4},{8,9},{9,10},{10,1... | collective-permute-start | bytes 786440 | tf_op jit(solution)/shard_map/ppermute | solution.py:696
  34.6 31.5 %collective-permute-start.4 = (bf16[256,512]{1,0:T(8,128)(2,1)}, bf16[256,512]{1,0:T(8,128)(2,1)}, u32[]{:S(2)}, u32[]{:S(2)}) collective-permute-start(bf16[256,512]{1,0:T(8,128)(2,1)} %param.17), channel_id=1, source_target_pairs={{0,2},{1,3},{2,0},{3,1},{4,6},{5,7},{6,4},{7,5},{8,10},{9,11},{10,... | collective-permute-start | bytes 786440 | tf_op jit(solution)/shard_map/ppermute | solution.py:696
  37.4 28.8 %collective-permute-start.3 = (bf16[256,512]{1,0:T(8,128)(2,1)}, bf16[256,512]{1,0:T(8,128)(2,1)}, u32[]{:S(2)}, u32[]{:S(2)}) collective-permute-start(bf16[256,512]{1,0:T(8,128)(2,1)} %param.17), channel_id=1, source_target_pairs={{0,3},{1,0},{2,1},{3,2},{4,7},{5,4},{6,5},{7,6},{8,11},{9,8},{10,9... | collective-permute-start | bytes 786440 | tf_op jit(solution)/shard_map/ppermute | solution.py:696
  44.8 7.1 %collective-permute-start = (bf16[272,128]{1,0:T(8,128)(2,1)S(1)}, bf16[272,128]{1,0:T(8,128)(2,1)S(1)}, u32[]{:S(2)}, u32[]{:S(2)}) collective-permute-start(bf16[272,128]{1,0:T(8,128)(2,1)S(1)} %get-tuple-element.42), channel_id=1, source_target_pairs={{0,32},{32,64},{64,96},{96,0},{1,33},{33,65},{65,97},{97,1},{2,34}... | collective-permute-start | bytes 208904 | tf_op jit(solution)/shard_map/ppermute | solution.py:696
  46.6 13.7 %collective-permute-start.1 = (bf16[272,128]{1,0:T(8,128)(2,1)S(1)}, bf16[272,128]{1,0:T(8,128)(2,1)S(1)}, u32[]{:S(2)}, u32[]{:S(2)}) collective-permute-start(bf16[272,128]{1,0:T(8,128)(2,1)S(1)} %get-tuple-element.42), channel_id=1, source_target_pairs={{0,64},{32,96},{64,0},{96,32},{1,65},{33,97},{65,1},{97,33},{2,66}... | collective-permute-start | bytes 208904 | tf_op jit(solution)/shard_map/ppermute | solution.py:696
  51.9 8.3 %collective-permute-start.2 = (bf16[272,128]{1,0:T(8,128)(2,1)S(1)}, bf16[272,128]{1,0:T(8,128)(2,1)S(1)}, u32[]{:S(2)}, u32[]{:S(2)}) collective-permute-start(bf16[272,128]{1,0:T(8,128)(2,1)S(1)} %get-tuple-element.42), channel_id=1, source_target_pairs={{0,96},{32,0},{64,32},{96,64},{1,97},{33,1},{65,33},{97,65},{2,98}... | collective-permute-start | bytes 208904 | tf_op jit(solution)/shard_map/ppermute | solution.py:696
  52.9 1.0 copy-start.27
  57.7 1.0 copy-start.2
  60.3 7.3 %copy-start.25 = (bf16[8,256,256]{2,1,0:T(8,128)(2,1)}, bf16[8,256,256]{2,1,0:T(8,128)(2,1)S(1)}, u32[]{:S(2)}) copy-start(bf16[8,256,256]{2,1,0:T(8,128)(2,1)S(1)} %get-tuple-element.54.p_ref) | copy-start | bytes 3145732
  60.3 5.9 %copy-start.6 = (bf16[272,128]{1,0:T(8,128)(2,1)}, bf16[272,128]{1,0:T(8,128)(2,1)S(1)}, u32[]{:S(2)}) copy-start(bf16[272,128]{1,0:T(8,128)(2,1)S(1)} %collective-permute-done.1.two_ref) | copy-start | bytes 208900
  60.3 5.9 %copy-start.8 = (bf16[272,128]{1,0:T(8,128)(2,1)}, bf16[272,128]{1,0:T(8,128)(2,1)S(1)}, u32[]{:S(2)}) copy-start(bf16[272,128]{1,0:T(8,128)(2,1)S(1)} %collective-permute-done.2.three_ref) | copy-start | bytes 208900
  62.1 11.6 %all-to-all-start.1 = ((bf16[8,128,128]{2,1,0:T(8,128)(2,1)}), bf16[8,128,128]{2,1,0:T(8,128)(2,1)S(1)}, u32[]{:S(2)}, u32[]{:S(2)}) async-start(bf16[8,128,128]{2,1,0:T(8,128)(2,1)} %shard_map.154), calls=%async_computation.1 | async-start | bytes 524288 | tf_op jit(solution)/shard_map/all_to_all | solution.py:723
  73.7 1.2 copy-start.3
  74.9 1.0 copy-start.5
  85.0 1.3 copy-start.1
  86.3 67.0 %collective-permute-start.12 = (bf16[4,4,64,1024]{3,2,1,0:T(8,128)(2,1)}, bf16[4,4,64,1024]{3,2,1,0:T(8,128)(2,1)}, u32[]{:S(2)}, u32[]{:S(2)}) collective-permute-start(bf16[4,4,64,1024]{3,2,1,0:T(8,128)(2,1)} %get-tuple-element.73), channel_id=1, source_target_pairs={{0,4},{4,0},{1,5},{5,1},{2,6},{6,2},{3,7},{7,3},{8,12},{12,8},{9,1... | collective-permute-start | bytes 6291464 | tf_op jit(solution)/shard_map/ppermute | solution.py:729
  86.3 11.1 %all-to-all-start.2 = ((bf16[8,128,128]{2,1,0:T(8,128)(2,1)}), bf16[8,128,128]{2,1,0:T(8,128)(2,1)S(1)}, u32[]{:S(2)}, u32[]{:S(2)}) async-start(bf16[8,128,128]{2,1,0:T(8,128)(2,1)} %copy-done.10), calls=%async_computation.2 | async-start | bytes 524288 | tf_op jit(solution)/shard_map/all_to_all | solution.py:727
  89.9 2.2 %copy-start = (bf16[2048,1024]{1,0:T(8,128)(2,1)S(1)}, bf16[2048,1024]{1,0:T(8,128)(2,1)}, u32[]{:S(2)}) copy-start(bf16[2048,1024]{1,0:T(8,128)(2,1)} %all-gather.2.cloned.1.call-done.w_ref) | copy-start | bytes 12582916
  92.0 19.2 %copy-start.12 = (bf16[256,1024]{1,0:T(8,128)(2,1)S(1)}, bf16[256,1024]{1,0:T(8,128)(2,1)}, u32[]{:S(2)}) copy-start(bf16[256,1024]{1,0:T(8,128)(2,1)} %v_ref.3) | copy-start | bytes 1572868
  92.0 19.2 %copy-start.16 = (bf16[256,512]{1,0:T(8,128)(2,1)S(1)}, bf16[256,512]{1,0:T(8,128)(2,1)}, u32[]{:S(2)}) copy-start(bf16[256,512]{1,0:T(8,128)(2,1)} %q_ref.3) | copy-start | bytes 786436
  98.4 6.8 %collective-permute-start.9 = (bf16[128,128]{1,0:T(8,128)(2,1)S(1)}, bf16[128,128]{1,0:T(8,128)(2,1)S(1)}, u32[]{:S(2)}, u32[]{:S(2)}) collective-permute-start(bf16[128,128]{1,0:T(8,128)(2,1)S(1)} %get-tuple-element.57), channel_id=1, source_target_pairs={{0,96},{32,0},{64,32},{96,64},{1,97},{33,1},{65,33},{97,65},{2,98}... | collective-permute-start | bytes 98312 | tf_op jit(solution)/shard_map/ppermute | solution.py:696
  100.5 24.2 %copy-start.7 = (bf16[272,128]{1,0:T(8,128)(2,1)S(1)}, bf16[272,128]{1,0:T(8,128)(2,1)}, u32[]{:S(2)}) copy-start(bf16[272,128]{1,0:T(8,128)(2,1)} %copy-done.6) | copy-start | bytes 208900
  100.5 24.2 %copy-start.9 = (bf16[272,128]{1,0:T(8,128)(2,1)S(1)}, bf16[272,128]{1,0:T(8,128)(2,1)}, u32[]{:S(2)}) copy-start(bf16[272,128]{1,0:T(8,128)(2,1)} %copy-done.8) | copy-start | bytes 208900
  100.5 29.5 %collective-permute-start.8 = (bf16[256,512]{1,0:T(8,128)(2,1)}, bf16[256,512]{1,0:T(8,128)(2,1)}, u32[]{:S(2)}, u32[]{:S(2)}) collective-permute-start(bf16[256,512]{1,0:T(8,128)(2,1)} %get-tuple-element.85), channel_id=1, source_target_pairs={{0,3},{1,0},{2,1},{3,2},{4,7},{5,4},{6,5},{7,6},{8,11},{9,8},{10,9... | collective-permute-start | bytes 786440 | tf_op jit(solution)/shard_map/ppermute | solution.py:696
  103.7 26.4 %collective-permute-start.7 = (bf16[256,512]{1,0:T(8,128)(2,1)}, bf16[256,512]{1,0:T(8,128)(2,1)}, u32[]{:S(2)}, u32[]{:S(2)}) collective-permute-start(bf16[256,512]{1,0:T(8,128)(2,1)} %get-tuple-element.86), channel_id=1, source_target_pairs={{0,2},{1,3},{2,0},{3,1},{4,6},{5,7},{6,4},{7,5},{8,10},{9,11},{10,... | collective-permute-start | bytes 786440 | tf_op jit(solution)/shard_map/ppermute | solution.py:696
  104.1 26.0 %collective-permute-start.6 = (bf16[256,512]{1,0:T(8,128)(2,1)}, bf16[256,512]{1,0:T(8,128)(2,1)}, u32[]{:S(2)}, u32[]{:S(2)}) collective-permute-start(bf16[256,512]{1,0:T(8,128)(2,1)} %get-tuple-element.84), channel_id=1, source_target_pairs={{0,1},{1,2},{2,3},{3,0},{4,5},{5,6},{6,7},{7,4},{8,9},{9,10},{10,1... | collective-permute-start | bytes 786440 | tf_op jit(solution)/shard_map/ppermute | solution.py:696
  105.2 5.6 %collective-permute-start.10 = (bf16[128,128]{1,0:T(8,128)(2,1)S(1)}, bf16[128,128]{1,0:T(8,128)(2,1)S(1)}, u32[]{:S(2)}, u32[]{:S(2)}) collective-permute-start(bf16[128,128]{1,0:T(8,128)(2,1)S(1)} %get-tuple-element.57), channel_id=1, source_target_pairs={{0,64},{32,96},{64,0},{96,32},{1,65},{33,97},{65,1},{97,33},{2,66}... | collective-permute-start | bytes 98312 | tf_op jit(solution)/shard_map/ppermute | solution.py:696
  110.9 13.8 %collective-permute-start.11 = (bf16[128,128]{1,0:T(8,128)(2,1)S(1)}, bf16[128,128]{1,0:T(8,128)(2,1)S(1)}, u32[]{:S(2)}, u32[]{:S(2)}) collective-permute-start(bf16[128,128]{1,0:T(8,128)(2,1)S(1)} %get-tuple-element.57), channel_id=1, source_target_pairs={{0,32},{32,64},{64,96},{96,0},{1,33},{33,65},{65,97},{97,1},{2,34}... | collective-permute-start | bytes 98312 | tf_op jit(solution)/shard_map/ppermute | solution.py:696
  111.2 1.0 copy-start.14
  112.3 0.9 copy-start.19
  113.2 1.0 copy-start.28
  114.2 23.3 %copy-start.20 = (bf16[256,512]{1,0:T(8,128)(2,1)S(1)}, bf16[256,512]{1,0:T(8,128)(2,1)}, u32[]{:S(2)}) copy-start(bf16[256,512]{1,0:T(8,128)(2,1)} %k_ref.7) | copy-start | bytes 786436
  114.2 23.3 %copy-start.29 = (f32[4,256,128]{2,1,0:T(8,128)S(1)}, f32[4,256,128]{2,1,0:T(8,128)}, u32[]{:S(2)}) copy-start(f32[4,256,128]{2,1,0:T(8,128)} %copy-done.26) | copy-start | bytes 1572868
  120.4 1.0 copy-start.32
  121.4 0.8 copy-start.34
  122.2 0.9 copy-start.36
  123.1 0.8 copy-start.38
  126.7 10.9 %all-to-all-start.3 = ((bf16[8,128,128]{2,1,0:T(8,128)(2,1)}), bf16[8,128,128]{2,1,0:T(8,128)(2,1)S(1)}, u32[]{:S(2)}, u32[]{:S(2)}) async-start(bf16[8,128,128]{2,1,0:T(8,128)(2,1)} %shard_map.162), calls=%async_computation.3 | async-start | bytes 524288 | tf_op jit(solution)/shard_map/all_to_all | solution.py:738
  137.5 1.0 copy-start.31
  138.6 1.2 copy-start.33
  139.8 1.0 copy-start.35
  140.8 1.0 copy-start.37
  141.9 1.0 copy-start.39
  142.9 1.0 copy-start.41
  156.5 13.8 %collective-permute-start.21 = (bf16[4,64,512]{2,1,0:T(8,128)(2,1)S(1)}, bf16[4,64,512]{2,1,0:T(8,128)(2,1)S(1)}, u32[]{:S(2)}, u32[]{:S(2)}) collective-permute-start(bf16[4,64,512]{2,1,0:T(8,128)(2,1)S(1)} %get-tuple-element.82), channel_id=1, source_target_pairs={{0,96},{32,0},{64,32},{96,64},{1,97},{33,1},{65,33},{97,65},{2,98}... | collective-permute-start | bytes 786440 | tf_op jit(solution)/shard_map/ppermute | solution.py:696
  159.5 11.4 %collective-permute-start.20 = (bf16[4,64,512]{2,1,0:T(8,128)(2,1)S(1)}, bf16[4,64,512]{2,1,0:T(8,128)(2,1)S(1)}, u32[]{:S(2)}, u32[]{:S(2)}) collective-permute-start(bf16[4,64,512]{2,1,0:T(8,128)(2,1)S(1)} %get-tuple-element.83), channel_id=1, source_target_pairs={{0,64},{32,96},{64,0},{96,32},{1,65},{33,97},{65,1},{97,33},{2,66}... | collective-permute-start | bytes 786440 | tf_op jit(solution)/shard_map/ppermute | solution.py:696
  159.5 14.2 %collective-permute-start.19 = (bf16[4,64,512]{2,1,0:T(8,128)(2,1)S(1)}, bf16[4,64,512]{2,1,0:T(8,128)(2,1)S(1)}, u32[]{:S(2)}, u32[]{:S(2)}) collective-permute-start(bf16[4,64,512]{2,1,0:T(8,128)(2,1)S(1)} %get-tuple-element.81), channel_id=1, source_target_pairs={{0,32},{32,64},{64,96},{96,0},{1,33},{33,65},{65,97},{97,1},{2,34}... | collective-permute-start | bytes 786440 | tf_op jit(solution)/shard_map/ppermute | solution.py:696
  160.6 16.0 %collective-permute-start.15 = (bf16[4,64,512]{2,1,0:T(8,128)(2,1)S(1)}, bf16[4,64,512]{2,1,0:T(8,128)(2,1)S(1)}, u32[]{:S(2)}, u32[]{:S(2)}) collective-permute-start(bf16[4,64,512]{2,1,0:T(8,128)(2,1)S(1)} %get-tuple-element.79), channel_id=1, source_target_pairs={{0,24},{8,0},{16,8},{24,16},{1,25},{9,1},{17,9},{25,17},{2,26},{10... | collective-permute-start | bytes 786440 | tf_op jit(solution)/shard_map/ppermute | solution.py:696
  161.8 14.8 %collective-permute-start.14 = (bf16[4,64,512]{2,1,0:T(8,128)(2,1)S(1)}, bf16[4,64,512]{2,1,0:T(8,128)(2,1)S(1)}, u32[]{:S(2)}, u32[]{:S(2)}) collective-permute-start(bf16[4,64,512]{2,1,0:T(8,128)(2,1)S(1)} %get-tuple-element.80), channel_id=1, source_target_pairs={{0,16},{8,24},{16,0},{24,8},{1,17},{9,25},{17,1},{25,9},{2,18},{10... | collective-permute-start | bytes 786440 | tf_op jit(solution)/shard_map/ppermute | solution.py:696
  170.3 7.6 %collective-permute-start.13 = (bf16[4,64,512]{2,1,0:T(8,128)(2,1)S(1)}, bf16[4,64,512]{2,1,0:T(8,128)(2,1)S(1)}, u32[]{:S(2)}, u32[]{:S(2)}) collective-permute-start(bf16[4,64,512]{2,1,0:T(8,128)(2,1)S(1)} %get-tuple-element.78), channel_id=1, source_target_pairs={{0,8},{8,16},{16,24},{24,0},{1,9},{9,17},{17,25},{25,1},{2,10},{10... | collective-permute-start | bytes 786440 | tf_op jit(solution)/shard_map/ppermute | solution.py:696
  173.9 9.7 %collective-permute-start.24 = (bf16[64,512]{1,0:T(8,128)(2,1)S(1)}, bf16[64,512]{1,0:T(8,128)(2,1)S(1)}, u32[]{:S(2)}, u32[]{:S(2)}) collective-permute-start(bf16[64,512]{1,0:T(8,128)(2,1)S(1)} %get-tuple-element.93), channel_id=1, source_target_pairs={{0,24},{8,0},{16,8},{24,16},{1,25},{9,1},{17,9},{25,17},{2,26},{10... | collective-permute-start | bytes 196616 | tf_op jit(solution)/shard_map/ppermute | solution.py:696
  175.2 9.4 %collective-permute-start.23 = (bf16[64,512]{1,0:T(8,128)(2,1)S(1)}, bf16[64,512]{1,0:T(8,128)(2,1)S(1)}, u32[]{:S(2)}, u32[]{:S(2)}) collective-permute-start(bf16[64,512]{1,0:T(8,128)(2,1)S(1)} %get-tuple-element.94), channel_id=1, source_target_pairs={{0,16},{8,24},{16,0},{24,8},{1,17},{9,25},{17,1},{25,9},{2,18},{10... | collective-permute-start | bytes 196616 | tf_op jit(solution)/shard_map/ppermute | solution.py:696
  176.7 8.0 %collective-permute-start.22 = (bf16[64,512]{1,0:T(8,128)(2,1)S(1)}, bf16[64,512]{1,0:T(8,128)(2,1)S(1)}, u32[]{:S(2)}, u32[]{:S(2)}) collective-permute-start(bf16[64,512]{1,0:T(8,128)(2,1)S(1)} %get-tuple-element.92), channel_id=1, source_target_pairs={{0,8},{8,16},{16,24},{24,0},{1,9},{9,17},{17,25},{25,1},{2,10},{10... | collective-permute-start | bytes 196616 | tf_op jit(solution)/shard_map/ppermute | solution.py:696
  178.1 8.1 %collective-permute-start.18 = (bf16[64,512]{1,0:T(8,128)(2,1)S(1)}, bf16[64,512]{1,0:T(8,128)(2,1)S(1)}, u32[]{:S(2)}, u32[]{:S(2)}) collective-permute-start(bf16[64,512]{1,0:T(8,128)(2,1)S(1)} %get-tuple-element.90), channel_id=1, source_target_pairs={{0,96},{32,0},{64,32},{96,64},{1,97},{33,1},{65,33},{97,65},{2,98}... | collective-permute-start | bytes 196616 | tf_op jit(solution)/shard_map/ppermute | solution.py:696
  183.7 5.9 %collective-permute-start.17 = (bf16[64,512]{1,0:T(8,128)(2,1)S(1)}, bf16[64,512]{1,0:T(8,128)(2,1)S(1)}, u32[]{:S(2)}, u32[]{:S(2)}) collective-permute-start(bf16[64,512]{1,0:T(8,128)(2,1)S(1)} %get-tuple-element.91), channel_id=1, source_target_pairs={{0,64},{32,96},{64,0},{96,32},{1,65},{33,97},{65,1},{97,33},{2,66}... | collective-permute-start | bytes 196616 | tf_op jit(solution)/shard_map/ppermute | solution.py:696
  183.7 6.2 %collective-permute-start.16 = (bf16[64,512]{1,0:T(8,128)(2,1)S(1)}, bf16[64,512]{1,0:T(8,128)(2,1)S(1)}, u32[]{:S(2)}, u32[]{:S(2)}) collective-permute-start(bf16[64,512]{1,0:T(8,128)(2,1)S(1)} %get-tuple-element.89), channel_id=1, source_target_pairs={{0,32},{32,64},{64,96},{96,0},{1,33},{33,65},{65,97},{97,1},{2,34}... | collective-permute-start | bytes 196616 | tf_op jit(solution)/shard_map/ppermute | solution.py:696
  (8 other events, 6.1 us)
Sparse Core Ops, SparseCore 0:
  10.8 50.5 all-gather.1

commit v2 on v1

--- a/solution.py
+++ b/solution.py
@@ -46,9 +46,16 @@
     return jnp.sum(array, axis=1, keepdims=True)
 
 
-def call(kernel, out_shape, grid, in_specs, out_specs, args, flops, scratch=(), prefetch=None):
+def call(kernel, out_shape, grid, in_specs, out_specs, args, flops, prefetch=None, after=()):
+    count = len(args) + (prefetch is not None)
+
+    def run(*refs):
+        kernel(*refs[:count], *refs[count + len(after) :])
+
+    in_specs = [*in_specs, *(pl.BlockSpec(memory_space=pl.ANY) for _ in after)]
     bytes_moved = sum(a.size * a.dtype.itemsize for a in (*args, *out_shape))
-    spec = dict(grid=grid, in_specs=in_specs, out_specs=out_specs, scratch_shapes=list(scratch))
+    args = (*args, *after)
+    spec = dict(grid=grid, in_specs=in_specs, out_specs=out_specs)
     extra = {}
     if prefetch is None:
         extra = spec
@@ -56,13 +63,14 @@
         extra = dict(grid_spec=pltpu.PrefetchScalarGridSpec(num_scalar_prefetch=1, **spec))
         args = (prefetch, *args)
     return pl.pallas_call(
-        kernel,
+        run,
         out_shape=out_shape,
-        compiler_params=pltpu.CompilerParams(vmem_limit_bytes=48 * 2**20),
+        compiler_params=pltpu.CompilerParams(vmem_limit_bytes=60 * 2**20),
         cost_estimate=pl.CostEstimate(
             flops=flops, bytes_accessed=bytes_moved, transcendentals=0
         ),
         interpret=INTERPRET,
+        name=kernel.__name__,
         **extra,
     )(*args)
 
@@ -429,7 +437,7 @@
     dcr_ref[0] = across
 
 
-def middle_pass(query, key, value, cums, cols, state, back, attend, inverse, wu):
+def middle_pass(query, key, value, cums, cols, state, back, attend, inverse, wu, after):
     heads = 2 * KEYS
     return call(
         middle_kernel,
@@ -466,6 +474,7 @@
         ),
         (query, key, value, cums, cols, state, back, attend, inverse, wu),
         2 * 10**9,
+        after=after,
     )
 
 
@@ -478,7 +487,7 @@
     tot_ref[...] = total.astype(BF)
 
 
-def later_pass(pay, direct):
+def later_pass(pay, direct, after):
     outs = (shape(SEG, DK, DK), shape(DK, DK, dtype=BF))
     args = (pay, direct)
     return call(
@@ -489,6 +498,7 @@
         tuple(whole(o) for o in outs),
         args,
         10**8,
+        after=after,
     )
 
 
@@ -505,7 +515,7 @@
         g_ref[i] = (gs_ref[i : i + 1, :] * total - mm_nt(total, ns_ref[i]) + d_ref[i]).astype(BF)
 
 
-def leave_pass(place, totals, grads, ns, gs, directs):
+def leave_pass(place, totals, grads, ns, gs, directs, after):
     out = shape(SEG, DK, DK, dtype=BF)
     args = (*totals, *grads, ns, gs, directs)
     return call(
@@ -517,6 +527,7 @@
         args,
         10**8,
         prefetch=place,
+        after=after,
     )[0]
 
 
@@ -577,7 +588,7 @@
         db_ref[...] = jnp.where(mine, turned[2 + a : 3 + a], db_ref[...])
 
 
-def last_pass(key, cums, cols, state, later, error, y, update, xz, dk0, dcc, dcr):
+def last_pass(key, cums, cols, state, later, error, y, update, xz, dk0, dcc, dcr, after):
     heads = 2 * KEYS
     return call(
         last_kernel,
@@ -605,6 +616,7 @@
         (wide_spec(2 * DK), wide_spec(DK), whole(cums), whole(cums)),
         (key, cums, cols, state, later, error, y, update, xz, dk0, dcc, dcr),
         2 * 10**9,
+        after=after,
     )
 
 
@@ -642,7 +654,7 @@
     out_ref[0] = mm_nt(norm_ref[...], w_ref[...]).astype(BF)
 
 
-def mix_pass(place, normed, weight):
+def mix_pass(place, normed, weight, after):
     depth = weight.shape[0] // NH
     out = shape(NH, TOK, depth, dtype=BF)
     return call(
@@ -657,6 +669,7 @@
         (normed, weight),
         2 * TOK * weight.size,
         prefetch=place,
+        after=after,
     )[0]
 
 
@@ -698,9 +711,8 @@
 
 def scatter_stage(parts, axis, count):
     total = parts[0].astype(F32)
-    moved = [shift(parts[k].astype(BF), axis, count, k) for k in range(1, count)]
-    for part in moved:
-        total = total + part.astype(F32)
+    for k in range(1, count):
+        total = total + shift(parts[k], axis, count, k).astype(F32)
     return total
 
 
@@ -727,28 +739,28 @@
     directs = lax.all_to_all(direct, ("z", "c"), 0, 0, tiled=True)
     mine, other = outer_pass(place, cot, normed)
     got = lax.ppermute(other, "c", [(0, 1), (1, 0)])
-    grad_query, update, dk0, error, y, dcc, dcr = middle_pass(
-        query, key, value, cums, cols, state, back, attend, inverse, wu
-    )
-    mixes = mix_pass(place, normed, weight)
-    mixed = scatter_stage([mixes[k] for k in range(NH)], "head", NH).astype(BF)
-    suffixes, grad_total = later_pass(pays, directs)
-    grads = [shift(grad_total, "y", NY, -k) for k in range(1, NY)]
-    laters = leave_pass(place, totals, grads, ns, gs, suffixes)
-    later = lax.all_to_all(laters, ("z", "c"), 0, 0, tiled=True)
-
     pair = mine.astype(F32) + got.astype(F32)
     wide = pair.shape[-1] // 2
-    left, right = pair[..., :wide], pair[..., wide:]
-    left = scatter_stage([left[:, k] for k in range(NZ)], "z", NZ)
-    right = scatter_stage([right[k] for k in range(NY)], "y", NY)
+    left = [pair[:, k, :, :wide].astype(BF) for k in range(NZ)]
+    right = [pair[k, :, :, wide:].astype(BF) for k in range(NY)]
+    grad_query, update, dk0, error, y, dcc, dcr = middle_pass(
+        query, key, value, cums, cols, state, back, attend, inverse, wu, (left[0],)
+    )
+    suffixes, grad_total = later_pass(pays, directs, (*left, *right))
+    grads = [shift(grad_total, "y", NY, -k) for k in range(1, NY)]
+    mixes = mix_pass(place, normed, weight, (grad_total,))
+    mixed = scatter_stage([mixes[k] for k in range(NH)], "head", NH).astype(BF)
+    laters = leave_pass(place, totals, grads, ns, gs, suffixes, (dk0,))
+    later = lax.all_to_all(laters, ("z", "c"), 0, 0, tiled=True)
+    left = scatter_stage(left, "z", NZ).astype(BF)
+    right = scatter_stage(right, "y", NY).astype(BF)
+
+    grad_value, grad_key, grad_beta, grad_decay = last_pass(
+        key, cums, cols, state, later, error, y, update, xz, dk0, dcc, dcr, (left, right)
+    )
     left = scatter_stage([left[k] for k in range(NY)], "y", NY)
     right = scatter_stage([right[k] for k in range(NZ)], "z", NZ)
     grad_weight = jnp.concatenate([left, right], axis=-1)
-
-    grad_value, grad_key, grad_beta, grad_decay = last_pass(
-        key, cums, cols, state, later, error, y, update, xz, dk0, dcc, dcr
-    )
     return (
         mixed,
         grad_query,

time: 199 us -> 189 us (0.950)
  waiting for transfers between devices: 37.3 us -> 15.4 us
  Pallas kernels: 53.6 us -> 74.5 us
  local copies, waits for them, and re-layouts: 30.9 us -> 11.3 us
  starting transfers between devices: 51.4 us -> 57.6 us
  other arithmetic: 9.39 us -> 12.7 us
    unnamed x84 -> x36, local copies, waits for them, and re-layouts: 29.8 us -> 4.23 us
    pallas_call x13, Pallas kernels: 53.6 us -> 74.5 us  [call(): pl.pallas_call(run, out_shape=out_shape, compiler_params=pltpu.CompilerPa...]
    ppermute x24, waiting for transfers between devices: 22.5 us -> 9.36 us  [shift(): lax.ppermute(array, axis, [(i, (i + step) % count) for i in range(count)])]
    all_to_all x1, waiting for transfers between devices: 5.48 us -> 0.01 us  [body(): later = lax.all_to_all(laters, ('z', 'c'), 0, 0, tiled=True)]
    ppermute x24, starting transfers between devices: 34.9 us -> 40.2 us  [shift(): lax.ppermute(array, axis, [(i, (i + step) % count) for i in range(count)])]
    pallas_call x0 -> x1, local copies, waits for them, and re-layouts: none -> 3.12 us  [call(): pl.pallas_call(run, out_shape=out_shape, compiler_params=pltpu.CompilerPa...]
    another operation x2 -> x1, other arithmetic: 0.28 us -> 3.32 us
    all_to_all x1, waiting for transfers between devices: 2.82 us -> 0.01 us  [body(): directs = lax.all_to_all(direct, ('z', 'c'), 0, 0, tiled=True)]
  transfers between devices with their start and end apart: 30 -> 30, of which waited for: 12 -> 5; matrix products, arithmetic and copies ran while one was open for 2% -> 7% of each run, Pallas kernels for 23% -> 34%
where the time goes in v2:
time: 189 us; the launch traced here: 187 us
  Pallas kernels  74.5 us (39%)
  starting transfers between devices  57.6 us (30%)
  waiting for transfers between devices  15.4 us (8%)
  between operations  14.9 us (8%)
  other arithmetic  12.7 us (7%)
  local copies, waits for them, and re-layouts  11.3 us (6%)
    pallas_call x13, Pallas kernels, call(): pl.pallas_call(run, out_shape=out_shape, compiler_params=pltpu.CompilerPa...  74.5 us
    ppermute x24, starting transfers between devices, shift(): lax.ppermute(array, axis, [(i, (i + step) % count) for i in range(count)])  40.2 us
    ppermute x24, waiting for transfers between devices, shift(): lax.ppermute(array, axis, [(i, (i + step) % count) for i in range(count)])  9.36 us
    all_to_all x1, waiting for transfers between devices, body(): pays = lax.all_to_all(pay, ('z', 'c'), 0, 0, tiled=True)  5.6 us
    all_to_all x1, starting transfers between devices, body(): pays = lax.all_to_all(pay, ('z', 'c'), 0, 0, tiled=True)  5.41 us
    all_to_all x1, starting transfers between devices, body(): directs = lax.all_to_all(direct, ('z', 'c'), 0, 0, tiled=True)  4.49 us
    unnamed x36, local copies, waits for them, and re-layouts  4.23 us
    all_to_all x1, starting transfers between devices, body(): later = lax.all_to_all(laters, ('z', 'c'), 0, 0, tiled=True)  4.05 us
  transfers between devices with their start and end apart: 30, of which 5 were waited for; matrix products, arithmetic and copies ran while one was open for 7% of the time, Pallas kernels for 34%

profile of v2, /device:TPU:0, one launch (start us, length us, event | category | flops | bytes accessed | tf_op | source)
XLA Modules:
  0.0 186.5 jit_solution(1033239266645315054)
XLA Ops:
  7.2 0.0 all-gather.2.cloned.1.call-start
  7.9 1.7 add_convert_fusion.3
  9.6 13.9 %pre_kernel.1 = (bf16[8,272,128]{2,1,0:T(8,128)(2,1)}, bf16[8,256,256]{2,1,0:T(8,128)(2,1)}, bf16[8,256,256]{2,1,0:T(8,128)(2,1)}, f32[8,256]{1,0:T(8,128)}, f32[4,256,128]{2,1,0:T(8,128)}) custom-call(bf16[256,512]{1,0:T(8,128)(2,1)} %refs_0_.7, bf16[256,1024]{1,0:T(8,128)(2,1)} %refs_2_.3, f32[8,256]{1,0:T(8,128)} %refs_2_.2, f32[8,256]{1,0:T(8,128)} %refs_3_.1), custom_call_target="tpu_custom_call" | custom-call | flops 2000000000 | bytes 3989504 | tf_op jit(solution)/shard_map/pre_kernel/pallas_call | solution.py:65
  23.5 5.4 %all-to-all-start = ((bf16[8,272,128]{2,1,0:T(8,128)(2,1)}), bf16[8,272,128]{2,1,0:T(8,128)(2,1)S(1)}, u32[]{:S(2)}, u32[]{:S(2)}) async-start(bf16[8,272,128]{2,1,0:T(8,128)(2,1)} %get-tuple-element.41), calls=%async_computation | async-start | bytes 1114112 | tf_op jit(solution)/shard_map/all_to_all | solution.py:729
  28.9 1.6 collective-permute-start.5
  30.5 2.7 %collective-permute-start.4 = (bf16[256,512]{1,0:T(8,128)(2,1)S(1)}, bf16[256,512]{1,0:T(8,128)(2,1)S(1)}, u32[]{:S(2)}, u32[]{:S(2)}) collective-permute-start(bf16[256,512]{1,0:T(8,128)(2,1)S(1)} %copy-done.14), channel_id=1, source_target_pairs={{0,2},{1,3},{2,0},{3,1},{4,6},{5,7},{6,4},{7,5},{8,10},{9,11},{10,... | collective-permute-start | bytes 786440 | tf_op jit(solution)/shard_map/ppermute | solution.py:709
  33.2 1.4 collective-permute-start.3
  34.6 5.6 %all-to-all-done.refs_0_ = bf16[8,272,128]{2,1,0:T(8,128)(2,1)S(1)} async-done(((bf16[8,272,128]{2,1,0:T(8,128)(2,1)}), bf16[8,272,128]{2,1,0:T(8,128)(2,1)S(1)}, u32[]{:S(2)}, u32[]{:S(2)}) %all-to-all-start) | async-done | bytes 557088 | tf_op jit(solution)/shard_map/all_to_all | solution.py:729
  40.2 0.8 copy-done
  41.0 2.8 %prefix_kernel.1 = (bf16[8,128,128]{2,1,0:T(8,128)(2,1)}, f32[8,128,128]{2,1,0:T(8,128)}, f32[8,128]{1,0:T(8,128)}, bf16[272,128]{1,0:T(8,128)(2,1)}) custom-call(bf16[8,272,128]{2,1,0:T(8,128)(2,1)} %copy-done), custom_call_target="tpu_custom_call" | custom-call | flops 100000000 | bytes 1417216 | tf_op jit(solution)/shard_map/prefix_kernel/pallas_call | solution.py:65
  43.8 1.4 collective-permute-start
  45.2 0.6 pad_add_fusion.refs_0_
  45.8 2.8 %collective-permute-start.1 = (bf16[272,128]{1,0:T(8,128)(2,1)}, bf16[272,128]{1,0:T(8,128)(2,1)S(1)}, u32[]{:S(2)}, u32[]{:S(2)}) collective-permute-start(bf16[272,128]{1,0:T(8,128)(2,1)} %get-tuple-element.42), channel_id=1, source_target_pairs={{0,64},{32,96},{64,0},{96,32},{1,65},{33,97},{65,1},{97,33},{2,66}... | collective-permute-start | bytes 208904 | tf_op jit(solution)/shard_map/ppermute | solution.py:709
  48.7 2.7 %collective-permute-done.refs_1_ = bf16[272,128]{1,0:T(8,128)(2,1)S(1)} collective-permute-done((bf16[272,128]{1,0:T(8,128)(2,1)}, bf16[272,128]{1,0:T(8,128)(2,1)S(1)}, u32[]{:S(2)}, u32[]{:S(2)}) %collective-permute-start) | collective-permute-done | bytes 69664 | tf_op jit(solution)/shard_map/ppermute | solution.py:709
  51.4 1.7 collective-permute-start.2
  53.1 5.1 %attend_kernel.1 = (bf16[8,256,256]{2,1,0:T(8,128)(2,1)}, bf16[8,256,128]{2,1,0:T(8,128)(2,1)}, f32[8,256,128]{2,1,0:T(8,128)}, bf16[8,256,128]{2,1,0:T(8,128)(2,1)}) custom-call(bf16[256,512]{1,0:T(8,128)(2,1)} %refs_0_.6, bf16[256,512]{1,0:T(8,128)(2,1)} %refs_0_.7, f32[8,256]{1,0:T(8,128)} %get-tuple-element.46.refs_2_.refs_3_.refs_1_, ...), custom_call_target="tpu_custom_call" | custom-call | flops 1000000000 | bytes 6299648 | tf_op jit(solution)/shard_map/attend_kernel/pallas_call | solution.py:65
  58.2 0.6 copy-done.12
  58.9 3.2 %enter_kernel.1 = bf16[8,128,128]{2,1,0:T(8,128)(2,1)} custom-call(s32[4]{0:T(128)} %pad_add_fusion.refs_0_, bf16[272,128]{1,0:T(8,128)(2,1)} %copy-done.11, bf16[272,128]{1,0:T(8,128)(2,1)} %copy-done.12, bf16[272,128]{1,0:T(8,128)(2,1)} %copy-done.13, bf16[8,128,128]{2,1,0:T(8,128)(2,1)} %get-tuple-element.43.refs_4_, ...), custom_call_target="tpu_custom_call" | custom-call | flops 100000000 | bytes 1261568 | tf_op jit(solution)/shard_map/enter_kernel/pallas_call | solution.py:65
  62.0 3.4 %all-to-all-start.1 = ((bf16[8,128,128]{2,1,0:T(8,128)(2,1)}), bf16[8,128,128]{2,1,0:T(8,128)(2,1)S(1)}, u32[]{:S(2)}, u32[]{:S(2)}) async-start(bf16[8,128,128]{2,1,0:T(8,128)(2,1)} %enter_kernel.1), calls=%async_computation.1 | async-start | bytes 524288 | tf_op jit(solution)/shard_map/all_to_all | solution.py:735
  65.5 1.1 pad_maximum_fusion.refs_1_
  66.6 6.0 %back_kernel.1.refs_3_ = f32[256,1024]{1,0:T(8,128)} custom-call(s32[4]{0:T(128)} %pad_add_fusion.refs_0_, bf16[4,256,512]{2,1,0:T(8,128)(2,1)} %pad_maximum_fusion.refs_1_, bf16[2048,1024]{1,0:T(8,128)(2,1)} %all-gather.2.cloned.1.call-done.refs_2_), custom_call_target="tpu_custom_call" | custom-call | flops 1073741824 | bytes 6291456 | tf_op jit(solution)/shard_map/back_kernel/pallas_call | solution.py:65
  72.6 0.4 all-to-all-done.1.refs_0_.refs_5_.refs_3_
  72.9 0.7 copy-done.10
  73.6 5.7 %norm_kernel.1 = (bf16[256,1024]{1,0:T(8,128)(2,1)}, bf16[8,256,128]{2,1,0:T(8,128)(2,1)}, bf16[8,128,128]{2,1,0:T(8,128)(2,1)}) custom-call(bf16[8,128,128]{2,1,0:T(8,128)(2,1)} %copy-done.10, bf16[8,256,128]{2,1,0:T(8,128)(2,1)} %get-tuple-element.50.refs_1_, f32[8,256,128]{2,1,0:T(8,128)} %get-tuple-element.51.refs_2_, f32[256,1024]{1,0:T(8,128)} %back_kernel.1.refs_3_), custom_call_target="tpu_custom_call" | custom-call | flops 100000000 | bytes 4194304 | tf_op jit(solution)/shard_map/norm_kernel/pallas_call | solution.py:65
  79.4 5.8 %outer_kernel.1 = (bf16[4,4,64,1024]{3,2,1,0:T(8,128)(2,1)}, bf16[4,4,64,1024]{3,2,1,0:T(8,128)(2,1)}) custom-call(s32[4]{0:T(128)} %pad_add_fusion.refs_0_, bf16[4,256,512]{2,1,0:T(8,128)(2,1)} %pad_maximum_fusion.refs_1_, bf16[256,1024]{1,0:T(8,128)(2,1)} %get-tuple-element.52.refs_2_.refs_1_), custom_call_target="tpu_custom_call" | custom-call | flops 1073741824 | bytes 5767168 | tf_op jit(solution)/shard_map/outer_kernel/pallas_call | solution.py:65
  85.1 3.1 %copy.18 = bf16[4,4,64,1024]{3,2,0,1:T(8,128)(2,1)} copy(bf16[4,4,64,1024]{3,2,1,0:T(8,128)(2,1)} %get-tuple-element.55) | data formatting | bytes 4194304 | tf_op jit(solution)/shard_map/outer_kernel/pallas_call | solution.py:65
  88.3 2.7 %suffix_kernel.1 = (bf16[8,128,128]{2,1,0:T(8,128)(2,1)}, f32[8,128]{1,0:T(8,128)}) custom-call(bf16[8,272,128]{2,1,0:T(8,128)(2,1)} %copy-done), custom_call_target="tpu_custom_call" | custom-call | flops 100000000 | bytes 823296 | tf_op jit(solution)/shard_map/suffix_kernel/pallas_call | solution.py:65
  91.0 4.5 %all-to-all-start.2 = ((bf16[8,128,128]{2,1,0:T(8,128)(2,1)}), bf16[8,128,128]{2,1,0:T(8,128)(2,1)S(1)}, u32[]{:S(2)}, u32[]{:S(2)}) async-start(bf16[8,128,128]{2,1,0:T(8,128)(2,1)} %get-tuple-element.53), calls=%async_computation.2 | async-start | bytes 524288 | tf_op jit(solution)/shard_map/all_to_all | solution.py:739
  95.5 1.4 copy-done.1
  96.8 3.3 %add_convert_fusion = bf16[4,4,64,1024]{3,2,0,1:T(8,128)(2,1)S(1)} fusion(bf16[4,4,64,1024]{3,2,0,1:T(8,128)(2,1)} %copy-done.1, bf16[4,4,64,1024]{3,2,1,0:T(8,128)(2,1)} %get-tuple-element.54), kind=kLoop, calls=%fused_computation | loop fusion | flops 4194304 | bytes 6291456 | tf_op jit(solution)/shard_map/convert.10
  100.2 1.0 slice_bitcast_fusion.4
  101.2 1.2 collective-permute-start.18
  102.3 1.0 slice_bitcast_fusion.8
  103.3 0.7 copy-done.4
  104.0 2.8 %later_kernel.1 = (f32[8,128,128]{2,1,0:T(8,128)}, bf16[128,128]{1,0:T(8,128)(2,1)}) custom-call(bf16[8,272,128]{2,1,0:T(8,128)(2,1)} %copy-done, bf16[8,128,128]{2,1,0:T(8,128)(2,1)} %copy-done.4, bf16[4,64,512]{2,1,0:T(8,128)(2,1)} %get-tuple-element.83.refs_2_.refs_10_, bf16[4,64,512]{2,1,0:T(8,128)(2,1)} %get-tuple-element.82.refs_3_, ...), custom_call_target="tpu_custom_call" | custom-call | flops 100000000 | bytes 1376256 | tf_op jit(solution)/shard_map/later_kernel/pallas_call | solution.py:65
  106.9 0.9 collective-permute-start.10
  107.7 2.0 %collective-permute-start.11 = (bf16[128,128]{1,0:T(8,128)(2,1)}, bf16[128,128]{1,0:T(8,128)(2,1)S(1)}, u32[]{:S(2)}, u32[]{:S(2)}) collective-permute-start(bf16[128,128]{1,0:T(8,128)(2,1)} %get-tuple-element.56.refs_3_), channel_id=1, source_target_pairs={{0,64},{32,96},{64,0},{96,32},{1,65},{33,97},{65,1},{97,33},{2,66}... | collective-permute-start | bytes 98312 | tf_op jit(solution)/shard_map/ppermute | solution.py:709
  109.8 3.3 %collective-permute-start.17 = (bf16[4,64,512]{2,1,0:T(8,128)(2,1)S(1)}, bf16[4,64,512]{2,1,0:T(8,128)(2,1)}, u32[]{:S(2)}, u32[]{:S(2)}) collective-permute-start(bf16[4,64,512]{2,1,0:T(8,128)(2,1)S(1)} %copy-done.9), channel_id=1, source_target_pairs={{0,64},{32,96},{64,0},{96,32},{1,65},{33,97},{65,1},{97,33},{2,66}... | collective-permute-start | bytes 786440 | tf_op jit(solution)/shard_map/ppermute | solution.py:709
  113.0 6.8 %middle_kernel.1 = (f32[256,512]{1,0:T(8,128)}, bf16[8,256,128]{2,1,0:T(8,128)(2,1)}, f32[256,512]{1,0:T(8,128)}, f32[8,256,128]{2,1,0:T(8,128)}, bf16[8,256,128...) custom-call(bf16[256,512]{1,0:T(8,128)(2,1)} %refs_0_.6, bf16[256,512]{1,0:T(8,128)(2,1)} %refs_0_.7, ...), custom_call_target="tpu_custom_call" | custom-call | flops 2000000000 | bytes 9216000 | tf_op jit(solution)/shard_map/middle_kernel/pallas_call | solution.py:65
  119.9 0.9 collective-permute-start.16
  120.8 3.3 %collective-permute-start.15 = (bf16[4,64,512]{2,1,0:T(8,128)(2,1)S(1)}, bf16[4,64,512]{2,1,0:T(8,128)(2,1)}, u32[]{:S(2)}, u32[]{:S(2)}) collective-permute-start(bf16[4,64,512]{2,1,0:T(8,128)(2,1)S(1)} %copy-done.7), channel_id=1, source_target_pairs={{0,24},{8,0},{16,8},{24,16},{1,25},{9,1},{17,9},{25,17},{2,26},{10... | collective-permute-start | bytes 786440 | tf_op jit(solution)/shard_map/ppermute | solution.py:709
  124.1 0.9 collective-permute-start.14
  125.1 0.9 collective-permute-start.13
  125.9 5.7 %mix_kernel.1 = bf16[4,256,512]{2,1,0:T(8,128)(2,1)} custom-call(s32[4]{0:T(128)} %pad_add_fusion.refs_0_, bf16[256,1024]{1,0:T(8,128)(2,1)} %get-tuple-element.52.refs_2_.refs_1_, bf16[2048,1024]{1,0:T(8,128)(2,1)} %all-gather.2.cloned.1.call-done.refs_2_, bf16[128,128]{1,0:T(8,128)(2,1)} %get-tuple-element.56.refs_3_), custom_call_target="tpu_custom_call" | custom-call | flops 1073741824 | bytes 5767168 | tf_op jit(solution)/shard_map/mix_kernel/pallas_call | solution.py:65
  131.6 2.0 %slice_bitcast_fusion.2 = (bf16[256,512]{1,0:T(8,128)(2,1)}, bf16[256,512]{1,0:T(8,128)(2,1)}, bf16[256,512]{1,0:T(8,128)(2,1)}) fusion(bf16[4,256,512]{2,1,0:T(8,128)(2,1)} %mix_kernel.1), kind=kLoop, calls=%fused_computation.10 | loop fusion | bytes 1572864 | tf_op jit(solution)/shard_map/squeeze | solution.py:752
  133.6 3.4 %leave_kernel.1 = bf16[8,128,128]{2,1,0:T(8,128)(2,1)} custom-call(s32[4]{0:T(128)} %pad_add_fusion.refs_0_, bf16[272,128]{1,0:T(8,128)(2,1)} %copy-done.11, bf16[272,128]{1,0:T(8,128)(2,1)} %copy-done.12, bf16[272,128]{1,0:T(8,128)(2,1)} %copy-done.13, bf16[128,128]{1,0:T(8,128)(2,1)} %copy-done.15, bf16[128,128]{1,0:T(8,128)(2,1)} %copy-done.16, ...), custom_call_target="tpu_custom_call" | custom-call | flops 100000000 | bytes 1359872 | tf_op jit(solution)/shard_map/leave_kernel/pallas_call | solution.py:65
  137.0 4.0 %all-to-all-start.3 = ((bf16[8,128,128]{2,1,0:T(8,128)(2,1)}), bf16[8,128,128]{2,1,0:T(8,128)(2,1)}, u32[]{:S(2)}, u32[]{:S(2)}) async-start(bf16[8,128,128]{2,1,0:T(8,128)(2,1)} %leave_kernel.1), calls=%async_computation.3 | async-start | bytes 524288 | tf_op jit(solution)/shard_map/all_to_all | solution.py:754
  141.1 2.7 %collective-permute-start.9 = (bf16[256,512]{1,0:T(8,128)(2,1)}, bf16[256,512]{1,0:T(8,128)(2,1)S(1)}, u32[]{:S(2)}, u32[]{:S(2)}) collective-permute-start(bf16[256,512]{1,0:T(8,128)(2,1)} %get-tuple-element.85), channel_id=1, source_target_pairs={{0,3},{1,0},{2,1},{3,2},{4,7},{5,4},{6,5},{7,6},{8,11},{9,8},{10,9... | collective-permute-start | bytes 786440 | tf_op jit(solution)/shard_map/ppermute | solution.py:709
  143.8 0.9 collective-permute-start.8
  144.7 0.9 collective-permute-start.7
  145.5 1.6 add_convert_fusion.1
  147.2 3.1 %collective-permute-start.24 = (bf16[64,512]{1,0:T(8,128)(2,1)S(1)}, bf16[64,512]{1,0:T(8,128)(2,1)S(1)}, u32[]{:S(2)}, u32[]{:S(2)}) collective-permute-start(bf16[64,512]{1,0:T(8,128)(2,1)S(1)} %get-tuple-element.93), channel_id=1, source_target_pairs={{0,24},{8,0},{16,8},{24,16},{1,25},{9,1},{17,9},{25,17},{2,26},{10... | collective-permute-start | bytes 196616 | tf_op jit(solution)/shard_map/ppermute | solution.py:709
  150.4 0.8 collective-permute-start.23
  151.2 4.6 %collective-permute-done.9 = bf16[256,512]{1,0:T(8,128)(2,1)S(1)} collective-permute-done((bf16[256,512]{1,0:T(8,128)(2,1)}, bf16[256,512]{1,0:T(8,128)(2,1)S(1)}, u32[]{:S(2)}, u32[]{:S(2)}) %collective-permute-start.9) | collective-permute-done | bytes 262176 | tf_op jit(solution)/shard_map/ppermute | solution.py:709
  155.8 1.7 collective-permute-start.22
  157.5 2.3 %collective-permute-start.21 = (bf16[64,512]{1,0:T(8,128)(2,1)S(1)}, bf16[64,512]{1,0:T(8,128)(2,1)S(1)}, u32[]{:S(2)}, u32[]{:S(2)}) collective-permute-start(bf16[64,512]{1,0:T(8,128)(2,1)S(1)} %get-tuple-element.90), channel_id=1, source_target_pairs={{0,96},{32,0},{64,32},{96,64},{1,97},{33,1},{65,33},{97,65},{2,98}... | collective-permute-start | bytes 196616 | tf_op jit(solution)/shard_map/ppermute | solution.py:709
  159.8 0.2 collective-permute-start.20
  160.0 1.8 fusion.2
  161.8 10.6 %last_kernel.1 = (f32[256,1024]{1,0:T(8,128)}, f32[256,512]{1,0:T(8,128)}, f32[8,256]{1,0:T(8,128)}, f32[8,256]{1,0:T(8,128)}) custom-call(bf16[256,512]{1,0:T(8,128)(2,1)} %refs_0_.7, f32[8,256]{1,0:T(8,128)} %get-tuple-element.46.refs_2_.refs_3_.refs_1_, f32[4,256,128]{2,1,0:T(8,128)} %get-tuple-element.47.refs_3_.refs_4_.refs_2_, ...), custom_call_target="tpu_custom_call" | custom-call | flops 2000000000 | bytes 6610944 | tf_op jit(solution)/shard_map/last_kernel/pallas_call | solution.py:65
  172.4 2.6 %collective-permute-start.19 = (bf16[64,512]{1,0:T(8,128)(2,1)S(1)}, bf16[64,512]{1,0:T(8,128)(2,1)S(1)}, u32[]{:S(2)}, u32[]{:S(2)}) collective-permute-start(bf16[64,512]{1,0:T(8,128)(2,1)S(1)} %get-tuple-element.89), channel_id=1, source_target_pairs={{0,32},{32,64},{64,96},{96,0},{1,33},{33,65},{65,97},{97,1},{2,34}... | collective-permute-start | bytes 196616 | tf_op jit(solution)/shard_map/ppermute | solution.py:709
  175.0 0.9 fusion.6
  175.9 2.0 %collective-permute-done.19 = bf16[64,512]{1,0:T(8,128)(2,1)S(1)} collective-permute-done((bf16[64,512]{1,0:T(8,128)(2,1)S(1)}, bf16[64,512]{1,0:T(8,128)(2,1)S(1)}, u32[]{:S(2)}, u32[]{:S(2)}) %collective-permute-start.19) | collective-permute-done | bytes 65568 | tf_op jit(solution)/shard_map/ppermute | solution.py:709
  177.9 0.9 fusion.8
  178.8 0.9 fusion.3
  (61 shorter events, 0.2 us)
Async XLA Ops:
  7.2 59.4 %all-gather.2.cloned.1.call-start = ((), (), s32[]{:S(2)}) async-start(), calls=%async_computation.4 | async-start | bytes 4325376 | tf_op jit(solution)/shard_map/all_gather | solution.py:725
  9.6 19.3 %copy-start.14 = (bf16[256,512]{1,0:T(8,128)(2,1)S(1)}, bf16[256,512]{1,0:T(8,128)(2,1)}, u32[]{:S(2)}) copy-start(bf16[256,512]{1,0:T(8,128)(2,1)} %param.17) | copy-start | bytes 786436
  23.5 16.7 %all-to-all-start = ((bf16[8,272,128]{2,1,0:T(8,128)(2,1)}), bf16[8,272,128]{2,1,0:T(8,128)(2,1)S(1)}, u32[]{:S(2)}, u32[]{:S(2)}) async-start(bf16[8,272,128]{2,1,0:T(8,128)(2,1)} %get-tuple-element.41), calls=%async_computation | async-start | bytes 1114112 | tf_op jit(solution)/shard_map/all_to_all | solution.py:729
  28.9 36.6 %collective-permute-start.5 = (bf16[256,512]{1,0:T(8,128)(2,1)S(1)}, bf16[256,512]{1,0:T(8,128)(2,1)S(1)}, u32[]{:S(2)}, u32[]{:S(2)}) collective-permute-start(bf16[256,512]{1,0:T(8,128)(2,1)S(1)} %copy-done.14), channel_id=1, source_target_pairs={{0,1},{1,2},{2,3},{3,0},{4,5},{5,6},{6,7},{7,4},{8,9},{9,10},{10,1... | collective-permute-start | bytes 786440 | tf_op jit(solution)/shard_map/ppermute | solution.py:709
  30.5 35.0 %collective-permute-start.4 = (bf16[256,512]{1,0:T(8,128)(2,1)S(1)}, bf16[256,512]{1,0:T(8,128)(2,1)S(1)}, u32[]{:S(2)}, u32[]{:S(2)}) collective-permute-start(bf16[256,512]{1,0:T(8,128)(2,1)S(1)} %copy-done.14), channel_id=1, source_target_pairs={{0,2},{1,3},{2,0},{3,1},{4,6},{5,7},{6,4},{7,5},{8,10},{9,11},{10,... | collective-permute-start | bytes 786440 | tf_op jit(solution)/shard_map/ppermute | solution.py:709
  33.2 32.3 %collective-permute-start.3 = (bf16[256,512]{1,0:T(8,128)(2,1)S(1)}, bf16[256,512]{1,0:T(8,128)(2,1)S(1)}, u32[]{:S(2)}, u32[]{:S(2)}) collective-permute-start(bf16[256,512]{1,0:T(8,128)(2,1)S(1)} %copy-done.14), channel_id=1, source_target_pairs={{0,3},{1,0},{2,1},{3,2},{4,7},{5,4},{6,5},{7,6},{8,11},{9,8},{10,9... | collective-permute-start | bytes 786440 | tf_op jit(solution)/shard_map/ppermute | solution.py:709
  40.2 0.8 copy-start
  43.8 7.5 %collective-permute-start = (bf16[272,128]{1,0:T(8,128)(2,1)}, bf16[272,128]{1,0:T(8,128)(2,1)S(1)}, u32[]{:S(2)}, u32[]{:S(2)}) collective-permute-start(bf16[272,128]{1,0:T(8,128)(2,1)} %get-tuple-element.42), channel_id=1, source_target_pairs={{0,32},{32,64},{64,96},{96,0},{1,33},{33,65},{65,97},{97,1},{2,34}... | collective-permute-start | bytes 208904 | tf_op jit(solution)/shard_map/ppermute | solution.py:709
  45.8 12.4 %collective-permute-start.1 = (bf16[272,128]{1,0:T(8,128)(2,1)}, bf16[272,128]{1,0:T(8,128)(2,1)S(1)}, u32[]{:S(2)}, u32[]{:S(2)}) collective-permute-start(bf16[272,128]{1,0:T(8,128)(2,1)} %get-tuple-element.42), channel_id=1, source_target_pairs={{0,64},{32,96},{64,0},{96,32},{1,65},{33,97},{65,1},{97,33},{2,66}... | collective-permute-start | bytes 208904 | tf_op jit(solution)/shard_map/ppermute | solution.py:709
  51.4 6.9 %copy-start.11 = (bf16[272,128]{1,0:T(8,128)(2,1)}, bf16[272,128]{1,0:T(8,128)(2,1)S(1)}, u32[]{:S(2)}) copy-start(bf16[272,128]{1,0:T(8,128)(2,1)S(1)} %collective-permute-done.refs_1_) | copy-start | bytes 208900
  51.4 6.8 %collective-permute-start.2 = (bf16[272,128]{1,0:T(8,128)(2,1)}, bf16[272,128]{1,0:T(8,128)(2,1)S(1)}, u32[]{:S(2)}, u32[]{:S(2)}) collective-permute-start(bf16[272,128]{1,0:T(8,128)(2,1)} %get-tuple-element.42), channel_id=1, source_target_pairs={{0,96},{32,0},{64,32},{96,64},{1,97},{33,1},{65,33},{97,65},{2,98}... | collective-permute-start | bytes 208904 | tf_op jit(solution)/shard_map/ppermute | solution.py:709
  58.2 0.6 copy-start.12
  58.2 0.6 copy-start.13
  62.0 10.9 %all-to-all-start.1 = ((bf16[8,128,128]{2,1,0:T(8,128)(2,1)}), bf16[8,128,128]{2,1,0:T(8,128)(2,1)S(1)}, u32[]{:S(2)}, u32[]{:S(2)}) async-start(bf16[8,128,128]{2,1,0:T(8,128)(2,1)} %enter_kernel.1), calls=%async_computation.1 | async-start | bytes 524288 | tf_op jit(solution)/shard_map/all_to_all | solution.py:735
  72.9 0.7 copy-start.10
  88.2 7.2 %collective-permute-start.6 = (bf16[4,4,64,1024]{3,2,0,1:T(8,128)(2,1)}, bf16[4,4,64,1024]{3,2,0,1:T(8,128)(2,1)S(1)}, u32[]{:S(2)}, u32[]{:S(2)}) collective-permute-start(bf16[4,4,64,1024]{3,2,0,1:T(8,128)(2,1)} %copy.18), channel_id=1, source_target_pairs={{0,4},{4,0},{1,5},{5,1},{2,6},{6,2},{3,7},{7,3},{8,12},{12,8},{9,1... | collective-permute-start | bytes 6291464 | tf_op jit(solution)/shard_map/ppermute | solution.py:741
  91.0 12.4 %all-to-all-start.2 = ((bf16[8,128,128]{2,1,0:T(8,128)(2,1)}), bf16[8,128,128]{2,1,0:T(8,128)(2,1)S(1)}, u32[]{:S(2)}, u32[]{:S(2)}) async-start(bf16[8,128,128]{2,1,0:T(8,128)(2,1)} %get-tuple-element.53), calls=%async_computation.2 | async-start | bytes 524288 | tf_op jit(solution)/shard_map/all_to_all | solution.py:739
  95.5 1.4 copy-start.1
  101.1 8.6 %copy-start.9 = (bf16[4,64,512]{2,1,0:T(8,128)(2,1)S(1)}, bf16[4,64,512]{2,1,0:T(8,128)(2,1)}, u32[]{:S(2)}) copy-start(bf16[4,64,512]{2,1,0:T(8,128)(2,1)} %get-tuple-element.79.refs_8_) | copy-start | bytes 786436
  101.2 23.9 %collective-permute-start.18 = (bf16[4,64,512]{2,1,0:T(8,128)(2,1)}, bf16[4,64,512]{2,1,0:T(8,128)(2,1)}, u32[]{:S(2)}, u32[]{:S(2)}) collective-permute-start(bf16[4,64,512]{2,1,0:T(8,128)(2,1)} %get-tuple-element.76.refs_9_), channel_id=1, source_target_pairs={{0,96},{32,0},{64,32},{96,64},{1,97},{33,1},{65,33},{97,65},{2,98}... | collective-permute-start | bytes 786440 | tf_op jit(solution)/shard_map/ppermute | solution.py:709
  103.3 0.7 copy-start.4
  106.9 13.0 %collective-permute-start.10 = (bf16[128,128]{1,0:T(8,128)(2,1)}, bf16[128,128]{1,0:T(8,128)(2,1)S(1)}, u32[]{:S(2)}, u32[]{:S(2)}) collective-permute-start(bf16[128,128]{1,0:T(8,128)(2,1)} %get-tuple-element.56.refs_3_), channel_id=1, source_target_pairs={{0,96},{32,0},{64,32},{96,64},{1,97},{33,1},{65,33},{97,65},{2,98}... | collective-permute-start | bytes 98312 | tf_op jit(solution)/shard_map/ppermute | solution.py:709
  107.7 13.1 %collective-permute-start.11 = (bf16[128,128]{1,0:T(8,128)(2,1)}, bf16[128,128]{1,0:T(8,128)(2,1)S(1)}, u32[]{:S(2)}, u32[]{:S(2)}) collective-permute-start(bf16[128,128]{1,0:T(8,128)(2,1)} %get-tuple-element.56.refs_3_), channel_id=1, source_target_pairs={{0,64},{32,96},{64,0},{96,32},{1,65},{33,97},{65,1},{97,33},{2,66}... | collective-permute-start | bytes 98312 | tf_op jit(solution)/shard_map/ppermute | solution.py:709
  109.8 14.4 %collective-permute-start.12 = (bf16[128,128]{1,0:T(8,128)(2,1)}, bf16[128,128]{1,0:T(8,128)(2,1)S(1)}, u32[]{:S(2)}, u32[]{:S(2)}) collective-permute-start(bf16[128,128]{1,0:T(8,128)(2,1)} %get-tuple-element.56.refs_3_), channel_id=1, source_target_pairs={{0,32},{32,64},{64,96},{96,0},{1,33},{33,65},{65,97},{97,1},{2,34}... | collective-permute-start | bytes 98312 | tf_op jit(solution)/shard_map/ppermute | solution.py:709
  109.8 31.3 %collective-permute-start.17 = (bf16[4,64,512]{2,1,0:T(8,128)(2,1)S(1)}, bf16[4,64,512]{2,1,0:T(8,128)(2,1)}, u32[]{:S(2)}, u32[]{:S(2)}) collective-permute-start(bf16[4,64,512]{2,1,0:T(8,128)(2,1)S(1)} %copy-done.9), channel_id=1, source_target_pairs={{0,64},{32,96},{64,0},{96,32},{1,65},{33,97},{65,1},{97,33},{2,66}... | collective-permute-start | bytes 786440 | tf_op jit(solution)/shard_map/ppermute | solution.py:709
  113.0 6.9 %copy-start.8 = (bf16[4,64,512]{2,1,0:T(8,128)(2,1)S(1)}, bf16[4,64,512]{2,1,0:T(8,128)(2,1)}, u32[]{:S(2)}) copy-start(bf16[4,64,512]{2,1,0:T(8,128)(2,1)} %get-tuple-element.77.refs_7_) | copy-start | bytes 786436
  113.0 7.8 %copy-start.7 = (bf16[4,64,512]{2,1,0:T(8,128)(2,1)S(1)}, bf16[4,64,512]{2,1,0:T(8,128)(2,1)}, u32[]{:S(2)}) copy-start(bf16[4,64,512]{2,1,0:T(8,128)(2,1)} %get-tuple-element.80.refs_5_) | copy-start | bytes 786436
  113.0 11.1 %copy-start.6 = (bf16[4,64,512]{2,1,0:T(8,128)(2,1)S(1)}, bf16[4,64,512]{2,1,0:T(8,128)(2,1)}, u32[]{:S(2)}) copy-start(bf16[4,64,512]{2,1,0:T(8,128)(2,1)} %get-tuple-element.81.refs_4_) | copy-start | bytes 786436
  113.0 12.0 %copy-start.5 = (bf16[4,64,512]{2,1,0:T(8,128)(2,1)S(1)}, bf16[4,64,512]{2,1,0:T(8,128)(2,1)}, u32[]{:S(2)}) copy-start(bf16[4,64,512]{2,1,0:T(8,128)(2,1)} %get-tuple-element.82.refs_3_) | copy-start | bytes 786436
  119.9 11.7 %copy-start.15 = (bf16[128,128]{1,0:T(8,128)(2,1)}, bf16[128,128]{1,0:T(8,128)(2,1)S(1)}, u32[]{:S(2)}) copy-start(bf16[128,128]{1,0:T(8,128)(2,1)S(1)} %collective-permute-done.10.refs_4_) | copy-start | bytes 98308
  119.9 23.9 %collective-permute-start.16 = (bf16[4,64,512]{2,1,0:T(8,128)(2,1)S(1)}, bf16[4,64,512]{2,1,0:T(8,128)(2,1)}, u32[]{:S(2)}, u32[]{:S(2)}) collective-permute-start(bf16[4,64,512]{2,1,0:T(8,128)(2,1)S(1)} %copy-done.8), channel_id=1, source_target_pairs={{0,32},{32,64},{64,96},{96,0},{1,33},{33,65},{65,97},{97,1},{2,34}... | collective-permute-start | bytes 786440 | tf_op jit(solution)/shard_map/ppermute | solution.py:709
  120.8 10.8 %copy-start.16 = (bf16[128,128]{1,0:T(8,128)(2,1)}, bf16[128,128]{1,0:T(8,128)(2,1)S(1)}, u32[]{:S(2)}) copy-start(bf16[128,128]{1,0:T(8,128)(2,1)S(1)} %collective-permute-done.11.refs_5_) | copy-start | bytes 98308
  120.8 23.9 %collective-permute-start.15 = (bf16[4,64,512]{2,1,0:T(8,128)(2,1)S(1)}, bf16[4,64,512]{2,1,0:T(8,128)(2,1)}, u32[]{:S(2)}, u32[]{:S(2)}) collective-permute-start(bf16[4,64,512]{2,1,0:T(8,128)(2,1)S(1)} %copy-done.7), channel_id=1, source_target_pairs={{0,24},{8,0},{16,8},{24,16},{1,25},{9,1},{17,9},{25,17},{2,26},{10... | collective-permute-start | bytes 786440 | tf_op jit(solution)/shard_map/ppermute | solution.py:709
  124.1 7.5 %copy-start.17 = (bf16[128,128]{1,0:T(8,128)(2,1)}, bf16[128,128]{1,0:T(8,128)(2,1)S(1)}, u32[]{:S(2)}) copy-start(bf16[128,128]{1,0:T(8,128)(2,1)S(1)} %collective-permute-done.12.refs_6_) | copy-start | bytes 98308
  124.1 21.4 %collective-permute-start.14 = (bf16[4,64,512]{2,1,0:T(8,128)(2,1)S(1)}, bf16[4,64,512]{2,1,0:T(8,128)(2,1)}, u32[]{:S(2)}, u32[]{:S(2)}) collective-permute-start(bf16[4,64,512]{2,1,0:T(8,128)(2,1)S(1)} %copy-done.6), channel_id=1, source_target_pairs={{0,16},{8,24},{16,0},{24,8},{1,17},{9,25},{17,1},{25,9},{2,18},{10... | collective-permute-start | bytes 786440 | tf_op jit(solution)/shard_map/ppermute | solution.py:709
  125.1 20.5 %collective-permute-start.13 = (bf16[4,64,512]{2,1,0:T(8,128)(2,1)S(1)}, bf16[4,64,512]{2,1,0:T(8,128)(2,1)}, u32[]{:S(2)}, u32[]{:S(2)}) collective-permute-start(bf16[4,64,512]{2,1,0:T(8,128)(2,1)S(1)} %copy-done.5), channel_id=1, source_target_pairs={{0,8},{8,16},{16,24},{24,0},{1,9},{9,17},{17,25},{25,1},{2,10},{10... | collective-permute-start | bytes 786440 | tf_op jit(solution)/shard_map/ppermute | solution.py:709
  137.0 24.8 %all-to-all-start.3 = ((bf16[8,128,128]{2,1,0:T(8,128)(2,1)}), bf16[8,128,128]{2,1,0:T(8,128)(2,1)}, u32[]{:S(2)}, u32[]{:S(2)}) async-start(bf16[8,128,128]{2,1,0:T(8,128)(2,1)} %leave_kernel.1), calls=%async_computation.3 | async-start | bytes 524288 | tf_op jit(solution)/shard_map/all_to_all | solution.py:754
  141.1 14.7 %collective-permute-start.9 = (bf16[256,512]{1,0:T(8,128)(2,1)}, bf16[256,512]{1,0:T(8,128)(2,1)S(1)}, u32[]{:S(2)}, u32[]{:S(2)}) collective-permute-start(bf16[256,512]{1,0:T(8,128)(2,1)} %get-tuple-element.85), channel_id=1, source_target_pairs={{0,3},{1,0},{2,1},{3,2},{4,7},{5,4},{6,5},{7,6},{8,11},{9,8},{10,9... | collective-permute-start | bytes 786440 | tf_op jit(solution)/shard_map/ppermute | solution.py:709
  143.8 13.7 %collective-permute-start.8 = (bf16[256,512]{1,0:T(8,128)(2,1)}, bf16[256,512]{1,0:T(8,128)(2,1)S(1)}, u32[]{:S(2)}, u32[]{:S(2)}) collective-permute-start(bf16[256,512]{1,0:T(8,128)(2,1)} %get-tuple-element.86), channel_id=1, source_target_pairs={{0,2},{1,3},{2,0},{3,1},{4,6},{5,7},{6,4},{7,5},{8,10},{9,11},{10,... | collective-permute-start | bytes 786440 | tf_op jit(solution)/shard_map/ppermute | solution.py:709
  144.7 15.2 %collective-permute-start.7 = (bf16[256,512]{1,0:T(8,128)(2,1)}, bf16[256,512]{1,0:T(8,128)(2,1)S(1)}, u32[]{:S(2)}, u32[]{:S(2)}) collective-permute-start(bf16[256,512]{1,0:T(8,128)(2,1)} %get-tuple-element.84), channel_id=1, source_target_pairs={{0,1},{1,2},{2,3},{3,0},{4,5},{5,6},{6,7},{7,4},{8,9},{9,10},{10,1... | collective-permute-start | bytes 786440 | tf_op jit(solution)/shard_map/ppermute | solution.py:709
  147.2 14.6 %copy-start.2 = (bf16[4,64,512]{2,1,0:T(8,128)(2,1)}, bf16[4,64,512]{2,1,0:T(8,128)(2,1)S(1)}, u32[]{:S(2)}) copy-start(bf16[4,64,512]{2,1,0:T(8,128)(2,1)S(1)} %get-tuple-element.75.refs_12_) | copy-start | bytes 786436
  147.2 14.6 %copy-start.3 = (bf16[4,64,512]{2,1,0:T(8,128)(2,1)}, bf16[4,64,512]{2,1,0:T(8,128)(2,1)S(1)}, u32[]{:S(2)}) copy-start(bf16[4,64,512]{2,1,0:T(8,128)(2,1)S(1)} %get-tuple-element.74.refs_13_) | copy-start | bytes 786436
  147.2 25.1 %collective-permute-start.24 = (bf16[64,512]{1,0:T(8,128)(2,1)S(1)}, bf16[64,512]{1,0:T(8,128)(2,1)S(1)}, u32[]{:S(2)}, u32[]{:S(2)}) collective-permute-start(bf16[64,512]{1,0:T(8,128)(2,1)S(1)} %get-tuple-element.93), channel_id=1, source_target_pairs={{0,24},{8,0},{16,8},{24,16},{1,25},{9,1},{17,9},{25,17},{2,26},{10... | collective-permute-start | bytes 196616 | tf_op jit(solution)/shard_map/ppermute | solution.py:709
  150.4 24.7 %collective-permute-start.23 = (bf16[64,512]{1,0:T(8,128)(2,1)S(1)}, bf16[64,512]{1,0:T(8,128)(2,1)S(1)}, u32[]{:S(2)}, u32[]{:S(2)}) collective-permute-start(bf16[64,512]{1,0:T(8,128)(2,1)S(1)} %get-tuple-element.94), channel_id=1, source_target_pairs={{0,16},{8,24},{16,0},{24,8},{1,17},{9,25},{17,1},{25,9},{2,18},{10... | collective-permute-start | bytes 196616 | tf_op jit(solution)/shard_map/ppermute | solution.py:709
  155.8 19.2 %collective-permute-start.22 = (bf16[64,512]{1,0:T(8,128)(2,1)S(1)}, bf16[64,512]{1,0:T(8,128)(2,1)S(1)}, u32[]{:S(2)}, u32[]{:S(2)}) collective-permute-start(bf16[64,512]{1,0:T(8,128)(2,1)S(1)} %get-tuple-element.92), channel_id=1, source_target_pairs={{0,8},{8,16},{16,24},{24,0},{1,9},{9,17},{17,25},{25,1},{2,10},{10... | collective-permute-start | bytes 196616 | tf_op jit(solution)/shard_map/ppermute | solution.py:709
  157.5 18.4 %collective-permute-start.21 = (bf16[64,512]{1,0:T(8,128)(2,1)S(1)}, bf16[64,512]{1,0:T(8,128)(2,1)S(1)}, u32[]{:S(2)}, u32[]{:S(2)}) collective-permute-start(bf16[64,512]{1,0:T(8,128)(2,1)S(1)} %get-tuple-element.90), channel_id=1, source_target_pairs={{0,96},{32,0},{64,32},{96,64},{1,97},{33,1},{65,33},{97,65},{2,98}... | collective-permute-start | bytes 196616 | tf_op jit(solution)/shard_map/ppermute | solution.py:709
  159.8 16.1 %collective-permute-start.20 = (bf16[64,512]{1,0:T(8,128)(2,1)S(1)}, bf16[64,512]{1,0:T(8,128)(2,1)S(1)}, u32[]{:S(2)}, u32[]{:S(2)}) collective-permute-start(bf16[64,512]{1,0:T(8,128)(2,1)S(1)} %get-tuple-element.91), channel_id=1, source_target_pairs={{0,64},{32,96},{64,0},{96,32},{1,65},{33,97},{65,1},{97,33},{2,66}... | collective-permute-start | bytes 196616 | tf_op jit(solution)/shard_map/ppermute | solution.py:709
  172.4 5.5 %collective-permute-start.19 = (bf16[64,512]{1,0:T(8,128)(2,1)S(1)}, bf16[64,512]{1,0:T(8,128)(2,1)S(1)}, u32[]{:S(2)}, u32[]{:S(2)}) collective-permute-start(bf16[64,512]{1,0:T(8,128)(2,1)S(1)} %get-tuple-element.89), channel_id=1, source_target_pairs={{0,32},{32,64},{64,96},{96,0},{1,33},{33,65},{65,97},{97,1},{2,34}... | collective-permute-start | bytes 196616 | tf_op jit(solution)/shard_map/ppermute | solution.py:709
Sparse Core Ops, SparseCore 0:
  10.8 50.6 all-gather.1

commit v3 on v2

v3 whole, which is shorter than its diff:
```python
import jax
import jax.numpy as jnp
from jax import lax
from jax.experimental import pallas as pl
from jax.experimental.pallas import tpu as pltpu
from jax.sharding import Mesh, PartitionSpec as P

DK = 128
DV = 128
CURVE_POINTS = 257
EPS = 1e-06
NY, NZ, NC, NH = 4, 4, 2, 4
TOK = 256
HALF = 128
KEYS = 4
ROWS = 272
GROUP = 4
VMEM = 14 * 2**20
SHORT = 10**6
LONG = 5 * 10**9
BF = jnp.bfloat16
F32 = jnp.float32
RING = ("y", "z", "c")
INTERPRET = False


def dot(left, right, dims):
    return lax.dot_general(
        left.astype(BF), right.astype(BF), (dims, ((), ())), preferred_element_type=F32
    )


def mm(left, right):
    return dot(left, right, ((1,), (0,)))


def mm_nt(left, right):
    return dot(left, right, ((1,), (1,)))


def mm_tn(left, right):
    return dot(left, right, ((0,), (0,)))


def iota(shape, dim):
    return lax.broadcasted_iota(jnp.int32, shape, dim)


def lane_sum(array):
    return jnp.sum(array, axis=1, keepdims=True)


def call(
    kernel, out_shape, grid, in_specs, out_specs, args, flops, prefetch=None, after=(), vmem=VMEM
):
    count = len(args) + (prefetch is not None)

    def run(*refs):
        kernel(*refs[:count], *refs[count + len(after) :])

    in_specs = [*in_specs, *(pl.BlockSpec(memory_space=pl.ANY) for _ in after)]
    args = (*args, *after)
    spec = dict(grid=grid, in_specs=in_specs, out_specs=out_specs)
    extra = {}
    if prefetch is None:
        extra = spec
    else:
        extra = dict(grid_spec=pltpu.PrefetchScalarGridSpec(num_scalar_prefetch=1, **spec))
        args = (prefetch, *args)
    return pl.pallas_call(
        run,
        out_shape=out_shape,
        compiler_params=pltpu.CompilerParams(vmem_limit_bytes=vmem),
        cost_estimate=pl.CostEstimate(flops=flops, bytes_accessed=1, transcendentals=0),
        interpret=INTERPRET,
        name=kernel.__name__,
        **extra,
    )(*args)


def shape(*dims, dtype=F32):
    return jax.ShapeDtypeStruct(dims, dtype)


def whole(array):
    return pl.BlockSpec(array.shape, lambda *_: (0,) * len(array.shape))


def heads_spec(rows, cols):
    return pl.BlockSpec((GROUP, rows, cols), lambda s, place: (s, 0, 0))


def lead_spec(rows, cols):
    return pl.BlockSpec((2, rows, cols), lambda s, place: (s, 0, 0))


def half_of(step, place):
    return (1 - place[3] + step) % 2


def key_head(i, place_ref):
    return 2 * half_of(pl.program_id(0), place_ref) + i


def wide_spec(cols):
    return pl.BlockSpec((TOK, 2 * cols), lambda s, place: (0, half_of(s, place)))


def gate_parts(gate):
    full = jnp.broadcast_to(gate, (16, DK))
    one = full.astype(BF)
    two = (full - one.astype(F32)).astype(BF)
    three = (full - one.astype(F32) - two.astype(F32)).astype(BF)
    place = iota((16, DK), 0)
    parts = jnp.where(place == 0, one.astype(F32), 0.0)
    parts = jnp.where(place == 1, two.astype(F32), parts)
    return jnp.where(place == 2, three.astype(F32), parts).astype(BF)


def gate_of(block):
    return jnp.sum(block[2 * DK :, :].astype(F32), axis=0, keepdims=True)


def unit_keys(key_block):
    raw = key_block.astype(F32)
    rate = lax.rsqrt(lane_sum(raw * raw) + EPS)
    return raw * rate, rate


def prefix_lanes(array):
    size = array.shape[1]
    lane = iota(array.shape, 1)
    step = 1
    while step < size:
        array = array + jnp.where(lane >= step, pltpu.roll(array, step, 1), 0.0)
        step *= 2
    return array


def suffix_lanes(array):
    size = array.shape[1]
    lane = iota(array.shape, 1)
    step = 1
    while step < size:
        array = array + jnp.where(lane < size - step, pltpu.roll(array, size - step, 1), 0.0)
        step *= 2
    return array


def invert_blocks(lowers):
    row, col = iota((HALF, HALF), 0), iota((HALF, HALF), 1)
    apart = row ^ col
    eye = jnp.where(row == col, 1.0, 0.0)
    found = [eye - jnp.where(apart < 2, low, 0.0) for low in lowers]
    size = 2
    while size < HALF:
        mask = (apart >= size) & (apart < 2 * size)
        offs = [jnp.where(mask, low, 0.0).astype(BF) for low in lowers]
        lows = [x.astype(BF) for x in found]
        halfway = [mm(x, off) for x, off in zip(lows, offs)]
        found = [f - mm(m, x) for f, m, x in zip(found, halfway, lows)]
        size *= 2
    return found


def pre_kernel(
    place_ref, k_ref, v_ref, beta_ref, decay_ref, sent_ref, kept_ref, x_ref, wu_ref, c_ref, cols_ref
):
    step = pl.program_id(0)

    @pl.when(step == 0)
    def _():
        c_ref[...] = prefix_lanes(decay_ref[...])

    strict = iota((TOK, TOK), 0) > iota((TOK, TOK), 1)
    sub = iota((8, TOK), 0)
    units, columns, lowers = [], [], []
    for i in range(2):
        j = key_head(i, place_ref)
        unit, _ = unit_keys(k_ref[:, i * DK : (i + 1) * DK])
        low = unit.astype(BF)
        gram = mm_nt(low, low)
        rows = [c_ref[pl.ds(2 * j + a, 1), :] for a in range(2)]
        rates = [beta_ref[pl.ds(2 * j + a, 1), :] for a in range(2)]
        packed = jnp.zeros((8, TOK), F32)
        for spot, line in enumerate((*rows, *rates)):
            packed = jnp.where(sub == spot, line, packed)
        cols = jnp.transpose(jnp.concatenate([packed, jnp.zeros((HALF - 8, TOK), F32)], axis=0))
        cols_ref[i] = cols
        units.append(unit)
        columns.append(cols)
        for a in range(2):
            ratio = jnp.exp(jnp.minimum(cols[:, a : a + 1] - rows[a], 0.0))
            lowers.append(jnp.where(strict, cols[:, 2 + a : 3 + a] * gram * ratio, 0.0))
    found = invert_blocks(
        [low[b * HALF : (b + 1) * HALF, b * HALF : (b + 1) * HALF] for low in lowers for b in (0, 1)]
    )
    for h in range(GROUP):
        i, a = h // 2, h % 2
        unit, cols = units[i], columns[i]
        first, second = found[2 * h].astype(BF), found[2 * h + 1].astype(BF)
        corner = -mm(mm(second, lowers[h][HALF:, :HALF]), first)
        inverse = jnp.concatenate(
            [
                jnp.concatenate([first, jnp.zeros((HALF, HALF), BF)], axis=1),
                jnp.concatenate([corner.astype(BF), second], axis=1),
            ],
            axis=0,
        )
        x_ref[h] = inverse
        c_col, beta_col = cols[:, a : a + 1], cols[:, 2 + a : 3 + a]
        value = v_ref[:, h * DK : (h + 1) * DK].astype(F32)
        right = jnp.concatenate(
            [(beta_col * jnp.exp(c_col) * unit).astype(BF), (beta_col * value).astype(BF)], axis=1
        )
        wu = mm(inverse, right).astype(BF)
        wu_ref[h] = wu
        end = c_col[TOK - 1 : TOK, :]
        moved = mm_tn(wu, jnp.exp(end - c_col) * unit).astype(BF)
        gate = gate_parts(jnp.exp(end))

        @pl.when(step == 0)
        def _():
            sent_ref[h, : 2 * DK, :] = moved
            sent_ref[h, 2 * DK :, :] = gate

        @pl.when(step == 1)
        def _():
            kept_ref[h, : 2 * DK, :] = moved
            kept_ref[h, 2 * DK :, :] = gate


def pre_pass(place, key, value, beta, decay):
    heads = 2 * KEYS
    pay = shape(GROUP, ROWS, DK, dtype=BF)

    return call(
        pre_kernel,
        (
            pay,
            pay,
            shape(heads, TOK, TOK, dtype=BF),
            shape(heads, TOK, 2 * DK, dtype=BF),
            shape(heads, TOK),
            shape(KEYS, TOK, DK),
        ),
        (2,),
        [wide_spec(DK), wide_spec(2 * DK), whole(beta), whole(decay)],
        (
            whole(pay),
            whole(pay),
            heads_spec(TOK, TOK),
            heads_spec(TOK, 2 * DK),
            whole(decay),
            lead_spec(TOK, DK),
        ),
        (key, value, beta, decay),
        SHORT,
        prefetch=place,
    )


def attend_kernel(
    place_ref, q_ref, k_ref, c_ref, cols_ref, x_ref, wu_ref, p_ref, car_ref, out_ref, xz_ref
):
    inclusive = iota((TOK, TOK), 0) >= iota((TOK, TOK), 1)
    for i in range(2):
        j = key_head(i, place_ref)
        unit, _ = unit_keys(k_ref[:, i * DK : (i + 1) * DK])
        query = q_ref[:, i * DK : (i + 1) * DK]
        gram = mm_nt(query, unit)
        cols = cols_ref[i]
        for a in range(2):
            h = 2 * i + a
            c_col = cols[:, a : a + 1]
            ratio = jnp.exp(jnp.minimum(c_col - c_ref[pl.ds(2 * j + a, 1), :], 0.0))
            attend = jnp.where(inclusive, gram * ratio, 0.0).astype(BF)
            p_ref[h] = attend
            both = mm(attend, wu_ref[h])
            car_ref[h] = (jnp.exp(c_col) * query.astype(F32) - both[:, :DK]).astype(BF)
            out_ref[h] = both[:, DK:]
            tail = jnp.exp(c_col[TOK - 1 : TOK, :] - c_col) * unit
            xz_ref[h] = mm_tn(x_ref[h], tail).astype(BF)


def attend_pass(place, query, key, cums, cols, inverse, wu):
    heads = 2 * KEYS
    return call(
        attend_kernel,
        (
            shape(heads, TOK, TOK, dtype=BF),
            shape(heads, TOK, DK, dtype=BF),
            shape(heads, TOK, DK),
            shape(heads, TOK, DK, dtype=BF),
        ),
        (2,),
        [
            wide_spec(DK),
            wide_spec(DK),
            whole(cums),
            lead_spec(TOK, DK),
            heads_spec(TOK, TOK),
            heads_spec(TOK, 2 * DK),
        ],
        (
            heads_spec(TOK, TOK),
            heads_spec(TOK, DK),
            heads_spec(TOK, DK),
            heads_spec(TOK, DK),
        ),
        (query, key, cums, cols, inverse, wu),
        LONG,
        prefetch=place,
    )


def single(kernel, outs, args, place, after=(), cost=SHORT):
    return call(
        kernel,
        outs,
        (1,),
        [whole(a) for a in args],
        tuple(whole(o) for o in outs),
        args,
        cost,
        prefetch=place,
        after=after,
    )


def pair_kernel(place_ref, kept_ref, got_ref, *out_refs):
    z, core = place_ref[2], place_ref[3]
    for k in range(NZ):
        head = (z + k) % NZ
        kept, got = kept_ref[head], got_ref[head]
        early, late = jnp.where(core == 0, kept, got), jnp.where(core == 0, got, kept)
        early_gate, late_gate = gate_of(early), gate_of(late)
        moved = late[:DK].astype(F32)
        out_refs[k][: 2 * DK, :] = (
            late_gate * early[: 2 * DK].astype(F32)
            - mm(early[: 2 * DK], late[:DK])
            + jnp.concatenate([early_gate * moved, late[DK : 2 * DK].astype(F32)], axis=0)
        ).astype(BF)
        out_refs[k][2 * DK :, :] = gate_parts(early_gate * late_gate)


def pair_pass(place, kept, got):
    return single(pair_kernel, (shape(ROWS, DK, dtype=BF),) * NZ, (kept, got), place)


def prefix_kernel(place_ref, *refs):
    parts, (row_ref, nx_ref, bx_ref, gx_ref, tot_ref) = refs[:NZ], refs[NZ:]
    z = place_ref[2]
    for k in range(NZ):
        row_ref[(z - k + NZ) % NZ] = parts[k][...]
    both = jnp.zeros((2 * DK, DK), F32)
    gate = jnp.ones((1, DK), F32)
    for i in range(NZ):
        nx_ref[i] = both[:DK].astype(BF)
        bx_ref[i] = both[DK:]
        gx_ref[i : i + 1, :] = gate
        block = row_ref[i]
        step_gate = gate_of(block)
        moved = block[:DK].astype(F32)
        both = (
            step_gate * both
            - mm(both, block[:DK])
            + jnp.concatenate([gate * moved, block[DK : 2 * DK].astype(F32)], axis=0)
        )
        gate = gate * step_gate
    tot_ref[: 2 * DK, :] = both.astype(BF)
    tot_ref[2 * DK :, :] = gate_parts(gate)


def prefix_pass(place, parts, after):
    outs = (
        shape(NZ, ROWS, DK, dtype=BF),
        shape(NZ, DK, DK, dtype=BF),
        shape(NZ, DK, DK),
        shape(8, DK),
        shape(ROWS, DK, dtype=BF),
    )
    return single(prefix_kernel, outs, parts, place, after)


def suffix_kernel(place_ref, row_ref, ns_ref, gs_ref):
    later = jnp.zeros((DK, DK), F32)
    gate = jnp.ones((1, DK), F32)
    for i in reversed(range(NZ)):
        ns_ref[i] = later.astype(BF)
        gs_ref[i : i + 1, :] = gate
        block = row_ref[i]
        step_gate = gate_of(block)
        moved = block[:DK]
        later = step_gate * later + gate * moved.astype(F32) - mm(moved, later)
        gate = gate * step_gate


def suffix_pass(place, row):
    return single(suffix_kernel, (shape(NZ, DK, DK, dtype=BF), shape(8, DK)), (row,), place, cost=LONG)


def enter_kernel(place_ref, one_ref, two_ref, three_ref, nx_ref, bx_ref, gx_ref, *out_refs):
    here, z = place_ref[1], place_ref[2]
    state = jnp.zeros((DK, DK), F32)
    for back, ref in ((3, three_ref), (2, two_ref), (1, one_ref)):
        block = ref[...]
        moved = gate_of(block) * state - mm(state, block[:DK]) + block[DK : 2 * DK].astype(F32)
        state = jnp.where(here >= back, moved, state)
    for k in range(NZ):
        i = (z + k) % NZ
        out_refs[k][...] = gx_ref[pl.ds(i, 1), :] * state - mm(state, nx_ref[i]) + bx_ref[i]


def enter_pass(place, totals, nx, bx, gx, after):
    outs = (shape(DK, DK),) * NZ
    return single(enter_kernel, outs, (*totals, nx, bx, gx), place, after)


def split_kernel(place_ref, *refs):
    states, (kept_ref, got_ref, own_ref, send_ref) = refs[:NZ], refs[NZ:]
    z, first = place_ref[2], place_ref[3] == 0
    for k in range(NZ):
        head = (z - k + NZ) % NZ
        early = jnp.where(first, kept_ref[head], got_ref[head])
        state = states[k][...]
        moved = (
            gate_of(early) * state - mm(state, early[:DK]) + early[DK : 2 * DK].astype(F32)
        )
        own_ref[head] = jnp.where(first, state, moved)
        send_ref[head] = jnp.where(first, moved, state)


def split_pass(place, states, kept, got, after):
    outs = (shape(GROUP, DK, DK),) * 2
    return single(split_kernel, outs, (*states, kept, got), place, after)


def two_parts(array):
    high = array.astype(BF)
    return high, (array - high.astype(F32)).astype(BF)


def select(theirs_ref, mine_ref, h):
    return jnp.where(pl.program_id(0) == 0, theirs_ref[h], mine_ref[h])


def norm_kernel(
    place_ref, got_ref, own_ref, car_ref, loc_ref, gn_ref,
    norm_ref, s_ref, do_ref, sent_ref, kept_ref,
):
    first = pl.program_id(0) == 0
    for h in range(GROUP):
        state, carried = select(got_ref, own_ref, h).astype(BF), car_ref[h]
        s_ref[h] = state
        head = loc_ref[h] + mm_nt(carried, state)
        scale = lax.rsqrt(lane_sum(head * head) * (1.0 / DK) + EPS)
        normed = head * scale
        norm_ref[:, h * DK : (h + 1) * DK] = normed.astype(BF)
        grad = gn_ref[:, h * DK : (h + 1) * DK]
        inner = lane_sum(grad * normed) * (1.0 / DK)
        back = scale * (grad - normed * inner)
        do_ref[h] = back
        both = mm_tn(jnp.concatenate(two_parts(back), axis=1), carried)
        direct = both[:DV] + both[DV:]

        @pl.when(first)
        def _():
            sent_ref[h] = direct

        @pl.when(jnp.logical_not(first))
        def _():
            kept_ref[h] = direct


def norm_pass(place, got, own, carried, local, grad_normed):
    heads = 2 * KEYS
    half = shape(GROUP, DK, DK)
    return call(
        norm_kernel,
        (
            shape(TOK, heads * DK, dtype=BF),
            shape(heads, DK, DK, dtype=BF),
            shape(heads, TOK, DK),
            half,
            half,
        ),
        (2,),
        [
            whole(got),
            whole(own),
            heads_spec(TOK, DK),
            heads_spec(TOK, DK),
            wide_spec(2 * DK),
        ],
        (wide_spec(2 * DK), heads_spec(DK, DK), heads_spec(TOK, DK), whole(half), whole(half)),
        (got, own, carried, local, grad_normed),
        SHORT,
        prefetch=place,
    )


def middle_kernel(
    place_ref, q_ref, k_ref, v_ref, c_ref, cols_ref, s_ref, do_ref, p_ref, x_ref, wu_ref,
    dq_ref, u_ref, dk_ref, e_ref, y_ref, dcc_ref, dcr_ref,
):
    inclusive = iota((TOK, TOK), 0) >= iota((TOK, TOK), 1)
    lane = iota((TOK, DK), 1)
    sub = iota((8, TOK), 0)
    for i in range(2):
        j = key_head(i, place_ref)
        unit, _ = unit_keys(k_ref[:, i * DK : (i + 1) * DK])
        low = unit.astype(BF)
        query = q_ref[:, i * DK : (i + 1) * DK]
        wide = query.astype(F32)
        cols = cols_ref[i]
        down = jnp.zeros((TOK, DK), F32)
        across = jnp.zeros((8, TOK), F32)
        pair_sum = jnp.zeros((TOK, TOK), F32)
        grad_query = jnp.zeros((TOK, DK), F32)
        for a in range(2):
            h = 2 * i + a
            c_col = cols[:, a : a + 1]
            growth = jnp.exp(c_col)
            state, attend = s_ref[h], p_ref[h]
            back, rest = two_parts(do_ref[h])
            update = (wu_ref[h, :, DK:].astype(F32) - mm_nt(wu_ref[h, :, :DK], state)).astype(BF)
            u_ref[h] = update
            pairs = mm_nt(back, update) + mm_nt(rest, update)
            ratio = jnp.exp(jnp.minimum(c_col - c_ref[pl.ds(2 * j + a, 1), :], 0.0))
            pair_sum += jnp.where(inclusive, pairs * ratio, 0.0)
            shares = pairs * attend.astype(F32)
            reached = growth * (mm(back, state) + mm(rest, state))
            grad_query += reached
            down = jnp.where(lane == a, lane_sum(shares) + lane_sum(reached * wide), down)
            across = jnp.where(sub == a, -jnp.sum(shares, axis=0, keepdims=True), across)
            e_ref[h] = mm_tn(x_ref[h], mm_tn(attend, back))
            value = v_ref[:, h * DK : (h + 1) * DK].astype(F32)
            y_ref[h] = (value - growth * mm_nt(low, state)).astype(BF)
        pair_low = pair_sum.astype(BF)
        dq_ref[:, i * DK : (i + 1) * DK] = grad_query + mm(pair_low, low)
        dk_ref[:, i * DK : (i + 1) * DK] = mm_tn(pair_low, query)
        dcc_ref[i] = down
        dcr_ref[i] = across


def middle_pass(place, query, key, value, cums, cols, state, back, attend, inverse, wu):
    heads = 2 * KEYS
    return call(
        middle_kernel,
        (
            shape(TOK, KEYS * DK),
            shape(heads, TOK, DK, dtype=BF),
            shape(TOK, KEYS * DK),
            shape(heads, TOK, DK),
            shape(heads, TOK, DK, dtype=BF),
            shape(KEYS, TOK, DK),
            shape(KEYS, 8, TOK),
        ),
        (2,),
        [
            wide_spec(DK),
            wide_spec(DK),
            wide_spec(2 * DK),
            whole(cums),
            lead_spec(TOK, DK),
            heads_spec(DK, DK),
            heads_spec(TOK, DK),
            heads_spec(TOK, TOK),
            heads_spec(TOK, TOK),
            heads_spec(TOK, 2 * DK),
        ],
        (
            wide_spec(DK),
            heads_spec(TOK, DK),
            wide_spec(DK),
            heads_spec(TOK, DK),
            heads_spec(TOK, DK),
            lead_spec(TOK, DK),
            lead_spec(8, TOK),
        ),
        (query, key, value, cums, cols, state, back, attend, inverse, wu),
        2 * LONG,
        prefetch=place,
    )


def join_kernel(place_ref, kept_ref, got_ref, dkept_ref, dgot_ref, *out_refs):
    z, first = place_ref[2], place_ref[3] == 0
    for k in range(NZ):
        head = (z + k) % NZ
        early = jnp.where(first, kept_ref[head], got_ref[head])
        before = jnp.where(first, dkept_ref[head], dgot_ref[head])
        after = jnp.where(first, dgot_ref[head], dkept_ref[head])
        out_refs[k][...] = gate_of(early) * after - mm_nt(after, early[:DK]) + before


def join_pass(place, kept, got, dkept, dgot, after):
    outs = (shape(DK, DK),) * NZ
    return single(join_kernel, outs, (kept, got, dkept, dgot), place, after)


def later_kernel(place_ref, *refs):
    parts, (row_ref, d_ref, tot_ref, line_ref) = refs[:NZ], refs[NZ:]
    z = place_ref[2]
    for k in range(NZ):
        line_ref[(z - k + NZ) % NZ] = parts[k][...]
    total = jnp.zeros((DK, DK), F32)
    for i in reversed(range(NZ)):
        d_ref[i] = total
        block = row_ref[i]
        total = gate_of(block) * total - mm_nt(total, block[:DK]) + line_ref[i]
    tot_ref[...] = total


def later_pass(place, parts, row, after):
    outs = (shape(NZ, DK, DK), shape(DK, DK), shape(NZ, DK, DK))
    return single(later_kernel, outs, (*parts, row), place, after)


def leave_kernel(
    place_ref, one_ref, two_ref, three_ref, g1_ref, g2_ref, g3_ref, ns_ref, gs_ref, d_ref, *out_refs
):
    here, z = place_ref[1], place_ref[2]
    total = jnp.zeros((DK, DK), F32)
    for ahead, ref, grad in ((3, one_ref, g3_ref), (2, two_ref, g2_ref), (1, three_ref, g1_ref)):
        block = ref[...]
        moved = gate_of(block) * total - mm_nt(total, block[:DK]) + grad[...]
        total = jnp.where(here + ahead < NY, moved, total)
    for k in range(NZ):
        i = (z + k) % NZ
        out_refs[k][...] = gs_ref[pl.ds(i, 1), :] * total - mm_nt(total, ns_ref[i]) + d_ref[i]


def leave_pass(place, totals, grads, ns, gs, directs, after):
    outs = (shape(DK, DK),) * NZ
    return single(leave_kernel, outs, (*totals, *grads, ns, gs, directs), place, after)


def part_kernel(place_ref, *refs):
    grads, (kept_ref, got_ref, dkept_ref, dgot_ref, own_ref, send_ref) = refs[:NZ], refs[NZ:]
    z, first = place_ref[2], place_ref[3] == 0
    for k in range(NZ):
        head = (z - k + NZ) % NZ
        late = jnp.where(first, got_ref[head], kept_ref[head])
        direct = jnp.where(first, dgot_ref[head], dkept_ref[head])
        grad = grads[k][...]
        moved = gate_of(late) * grad - mm_nt(grad, late[:DK]) + direct
        own_ref[head] = jnp.where(first, moved, grad)
        send_ref[head] = jnp.where(first, grad, moved)


def part_pass(place, grads, kept, got, dkept, dgot, after):
    outs = (shape(GROUP, DK, DK),) * 2
    return single(part_kernel, outs, (*grads, kept, got, dkept, dgot), place, after)


def last_kernel(
    place_ref, k_ref, c_ref, cols_ref, s_ref, ggot_ref, gown_ref, e_ref, y_ref, u_ref, xz_ref,
    dk0_ref, dcc_ref, dcr_ref, dv_ref, dk_ref, db_ref, dd_ref,
):
    strict = iota((TOK, TOK), 0) > iota((TOK, TOK), 1)
    last = iota((TOK, 1), 0) == TOK - 1
    lane = iota((TOK, DK), 1)
    sub = iota((8, TOK), 0)
    for i in range(2):
        j = key_head(i, place_ref)
        unit, rate = unit_keys(k_ref[:, i * DK : (i + 1) * DK])
        low = unit.astype(BF)
        gram = mm_nt(low, low)
        cols = cols_ref[i]
        down = jnp.zeros((TOK, DK), F32)
        pair_sum = jnp.zeros((TOK, TOK), F32)
        grad_key = dk0_ref[:, i * DK : (i + 1) * DK]
        across = []
        for a in range(2):
            h = 2 * i + a
            c_col, beta_col = cols[:, a : a + 1], cols[:, 2 + a : 3 + a]
            growth = jnp.exp(c_col)
            end = c_col[TOK - 1 : TOK, :]
            state, later, update = s_ref[h], select(ggot_ref, gown_ref, h), u_ref[h]
            error = e_ref[h] + mm_nt(xz_ref[h], later)
            ratio = jnp.exp(jnp.minimum(c_col - c_ref[pl.ds(2 * j + a, 1), :], 0.0))
            pairs = jnp.where(strict, -mm_nt(error, update) * ratio, 0.0)
            shares = pairs * gram
            row_share = lane_sum(shares)
            across.append(jnp.sum(beta_col * shares, axis=0, keepdims=True))
            pair_sum += beta_col * pairs
            grad_value = beta_col * error
            dv_ref[:, h * DK : (h + 1) * DK] = grad_value
            reached = growth * mm(grad_value, state)
            tail = jnp.exp(end - c_col) * mm(update, later)
            grad_key += tail - reached
            tail_share = lane_sum(tail * unit)
            gate_share = jnp.exp(end) * jnp.sum(
                lane_sum(state.astype(F32) * later.astype(F32)), axis=0, keepdims=True
            )
            total = jnp.sum(tail_share, axis=0, keepdims=True) + gate_share
            grad_cum = beta_col * row_share - lane_sum(reached * unit) - tail_share
            grad_cum += jnp.where(last, total, 0.0)
            grad_beta = row_share + lane_sum(error * y_ref[h].astype(F32))
            down = jnp.where(lane == a, grad_cum, jnp.where(lane == 2 + a, grad_beta, down))
        pair_low = pair_sum.astype(BF)
        grad_key += mm(pair_low, low) + mm_tn(pair_low, low)
        dk_ref[:, i * DK : (i + 1) * DK] = rate * (grad_key - unit * lane_sum(unit * grad_key))
        turned = jnp.transpose(down + jnp.where(lane < 2, dcc_ref[i], 0.0))[:8]
        cum = turned + dcr_ref[i]
        for a in range(2):
            cum = jnp.where(sub == a, cum - across[a], cum)
        decayed = suffix_lanes(cum)
        for a in range(2):
            dd_ref[pl.ds(2 * j + a, 1), :] = decayed[a : a + 1]
            db_ref[pl.ds(2 * j + a, 1), :] = turned[2 + a : 3 + a]


def last_pass(place, key, cums, cols, state, got, own, error, y, update, xz, dk0, dcc, dcr, after):
    heads = 2 * KEYS
    return call(
        last_kernel,
        (
            shape(TOK, heads * DK),
            shape(TOK, KEYS * DK),
            shape(heads, TOK),
            shape(heads, TOK),
        ),
        (2,),
        [
            wide_spec(DK),
            whole(cums),
            lead_spec(TOK, DK),
            heads_spec(DK, DK),
            whole(got),
            whole(own),
            heads_spec(TOK, DK),
            heads_spec(TOK, DK),
            heads_spec(TOK, DK),
            heads_spec(TOK, DK),
            wide_spec(DK),
            lead_spec(TOK, DK),
            lead_spec(8, TOK),
        ],
        (wide_spec(2 * DK), wide_spec(DK), whole(cums), whole(cums)),
        (key, cums, cols, state, got, own, error, y, update, xz, dk0, dcc, dcr),
        2 * LONG,
        prefetch=place,
        after=after,
    )


def back_kernel(place_ref, cot_ref, w_ref, out_ref):
    part = mm(cot_ref[0], w_ref[...])

    @pl.when(pl.program_id(0) == 0)
    def _():
        out_ref[...] = part

    @pl.when(pl.program_id(0) > 0)
    def _():
        out_ref[...] += part


def back_pass(place, cot, weight, after):
    depth, wide = cot.shape[2], weight.shape[1]
    out = shape(TOK, wide)
    return call(
        back_kernel,
        (out,),
        (NH,),
        [
            pl.BlockSpec((1, TOK, depth), lambda k, place: (k, 0, 0)),
            pl.BlockSpec((depth, wide), lambda k, place: ((place[0] + k) % NH, 0)),
        ],
        (whole(out),),
        (cot, weight),
        LONG,
        prefetch=place,
        after=after,
    )[0]


def mix_kernel(place_ref, norm_ref, w_ref, out_ref):
    out_ref[0] = mm_nt(norm_ref[...], w_ref[...]).astype(BF)


def mix_pass(place, normed, weight, after):
    depth = weight.shape[0] // NH
    out = shape(NH, TOK, depth, dtype=BF)
    return call(
        mix_kernel,
        (out,),
        (NH,),
        [
            whole(normed),
            pl.BlockSpec((depth, weight.shape[1]), lambda k, place: ((place[0] + k) % NH, 0)),
        ],
        (pl.BlockSpec((1, TOK, depth), lambda k, place: (k, 0, 0)),),
        (normed, weight),
        LONG,
        prefetch=place,
        after=after,
    )[0]


def outer_kernel(place_ref, cot_ref, norm_ref, mine_ref, other_ref):
    here, core = place_ref[2], place_ref[3]
    rows = mine_ref.shape[2]
    for k in range(NZ):
        start = pl.multiple_of(((here + k) % NZ) * 2 * rows, 2 * rows)
        part = mm_tn(cot_ref[0, :, pl.ds(start, 2 * rows)], norm_ref[...]).astype(BF)
        first = core == 0
        mine_ref[0, k] = jnp.where(first, part[:rows], part[rows:])
        other_ref[0, k] = jnp.where(first, part[rows:], part[:rows])


def outer_pass(place, cot, normed, after):
    rows = cot.shape[2] // (NZ * NC)
    out = shape(NY, NZ, rows, normed.shape[1], dtype=BF)
    spec = pl.BlockSpec((1, NZ, rows, normed.shape[1]), lambda k, place: (k, 0, 0, 0))
    return call(
        outer_kernel,
        (out, out),
        (NY,),
        [
            pl.BlockSpec(
                (1, TOK, cot.shape[2]), lambda k, place: ((place[1] + k - place[0] + NH) % NH, 0, 0)
            ),
            whole(normed),
        ],
        (spec, spec),
        (cot, normed),
        LONG,
        prefetch=place,
        after=after,
    )


def blend_kernel(place_ref, mine_ref, other_ref, *out_refs):
    for y in range(NY):
        for z in range(NZ):
            total = mine_ref[y, z].astype(F32) + other_ref[y, z].astype(F32)
            out_refs[z][y] = total.astype(BF)


def blend_pass(place, mine, other, after):
    outs = (shape(NY, *mine.shape[2:], dtype=BF),) * NZ
    return single(blend_kernel, outs, (mine, other), place, after, LONG)


def sum_kernel(place_ref, *refs):
    for y in range(NY):
        refs[NZ + y][...] = sum(refs[z][y].astype(F32) for z in range(NZ)).astype(BF)


def sum_pass(place, parts, after):
    outs = (shape(*parts[0].shape[1:], dtype=BF),) * NY
    return single(sum_kernel, outs, parts, place, after)


def shift(array, axis, count, step):
    return lax.ppermute(array, axis, [(i, (i + step) % count) for i in range(count)])


def spread(parts, axis, count, sign=1):
    return [parts[0]] + [shift(parts[k], axis, count, sign * k) for k in range(1, count)]


def scatter_stage(parts, axis, count):
    return sum(part.astype(F32) for part in spread(parts, axis, count))


def swap(array):
    return lax.ppermute(array, "c", [(0, 1), (1, 0)])


def body(query, key, value, beta, decay, wo_start, wo_end, curve_index, cotangent):
    place = jnp.stack([lax.axis_index(a) for a in ("head", "y", "z", "c")]).astype(jnp.int32)
    position = curve_index[0].astype(F32) / (CURVE_POINTS - 1)
    weight_local = (
        (1.0 - position) * wo_start.astype(F32) + position * wo_end.astype(F32)
    ).astype(BF)
    weight = lax.all_gather(weight_local, RING, axis=0, tiled=True)
    cot = jnp.stack([cotangent] + [shift(cotangent, "head", NH, -k) for k in range(1, NH)])

    sent, kept, inverse, wu, cums, cols = pre_pass(place, key, value, beta, decay)
    got = swap(sent)
    parts = spread(pair_pass(place, kept, got), "z", NZ)
    attend, carried, local, xz = attend_pass(place, query, key, cums, cols, inverse, wu)
    row, nx, bx, gx, total = prefix_pass(place, parts, (xz,))
    totals = [shift(total, "y", NY, k) for k in range(1, NY)]
    ns, gs = suffix_pass(place, row)
    states = spread(enter_pass(place, totals, nx, bx, gx, (ns,)), "z", NZ)
    grad_normed = back_pass(place, cot, weight, (ns,))
    own, send = split_pass(place, states, kept, got, (grad_normed,))
    normed, state, back, dsent, dkept = norm_pass(
        place, swap(send), own, carried, local, grad_normed
    )

    dgot = swap(dsent)
    grad_parts = spread(join_pass(place, kept, got, dkept, dgot, ()), "z", NZ)
    mine, other = outer_pass(place, cot, normed, (dgot,))
    theirs = swap(other)
    suffixes, grad_total, _ = later_pass(place, grad_parts, row, ())
    grads = [shift(grad_total, "y", NY, -k) for k in range(1, NY)]
    grad_query, update, dk0, error, y, dcc, dcr = middle_pass(
        place, query, key, value, cums, cols, state, back, attend, inverse, wu
    )
    laters = spread(leave_pass(place, totals, grads, ns, gs, suffixes, (dk0,)), "z", NZ)
    sums = spread(blend_pass(place, mine, theirs, (grad_total,)), "z", NZ)
    gown, gsend = part_pass(place, laters, kept, got, dkept, dgot, (sums[0],))
    ggot = swap(gsend)

    grad_value, grad_key, grad_beta, grad_decay = last_pass(
        place, key, cums, cols, state, ggot, gown, error, y, update, xz, dk0, dcc, dcr, ()
    )
    mixes = mix_pass(place, normed, weight, (grad_beta,))
    mixed = scatter_stage([mixes[k] for k in range(NH)], "head", NH).astype(BF)
    sums = sum_pass(place, sums, (grad_beta,))
    grad_weight = scatter_stage(sums, "y", NY)
    return (
        mixed,
        grad_query,
        grad_key,
        grad_value,
        grad_beta,
        grad_decay,
        (1.0 - position) * grad_weight,
        position * grad_weight,
    )


def solution(mesh):
    fine = Mesh(mesh.devices.reshape(NY, NZ, NC, NH), ("y", "z", "c", "head"))
    rows, flipped = P(RING, "head"), P("head", RING)
    return jax.shard_map(
        body,
        mesh=fine,
        in_specs=(rows, rows, rows, flipped, flipped, rows, rows, P(), rows),
        out_specs=(rows, rows, rows, rows, flipped, flipped, rows, rows),
        check_vma=False,
    )
```

time: 189 us -> 156 us (0.83)
  Pallas kernels: 74.5 us -> 53 us
  waiting for transfers between devices: 15.4 us -> 23.7 us
  other arithmetic: 12.7 us -> 4.62 us
  starting transfers between devices: 57.6 us -> 49.8 us
  local copies, waits for them, and re-layouts: 11.3 us -> 8.93 us
    pallas_call x13 -> x19, Pallas kernels: 74.5 us -> 53 us  [call(): pl.pallas_call(run, out_shape=out_shape, compiler_params=pltpu.CompilerPa...]
    all_to_all x4 -> x0, starting transfers between devices: 17.4 us -> none  [the longest x1 5.41 us: body(): pays = lax.all_to_all(pay, ('z', 'c'), 0, 0, tiled=True)]
    ppermute x24 -> x30, waiting for transfers between devices: 9.36 us -> 20.8 us  [shift(): lax.ppermute(array, axis, [(i, (i + step) % count) for i in range(count)])]
    ppermute x24 -> x30, starting transfers between devices: 40.2 us -> 48.9 us  [shift(): lax.ppermute(array, axis, [(i, (i + step) % count) for i in range(count)])]
    all_to_all x4 -> x0, waiting for transfers between devices: 5.97 us -> none  [the longest x1 5.6 us: body(): pays = lax.all_to_all(pay, ('z', 'c'), 0, 0, tiled=True)]
    unnamed x36 -> x56, local copies, waits for them, and re-layouts: 4.23 us -> 8.88 us
    another operation x1 -> x0, other arithmetic: 3.32 us -> none
    pallas_call x1 -> x0, local copies, waits for them, and re-layouts: 3.12 us -> none  [call(): pl.pallas_call(run, out_shape=out_shape, compiler_params=pltpu.CompilerPa...]
  transfers between devices with their start and end apart: 30 -> 36, of which waited for: 5 -> 17; matrix products, arithmetic and copies ran while one was open for 7% -> 1% of each run, Pallas kernels for 34% -> 27%
where the time goes in v3:
time: 156 us; the launch traced here: 155 us
  Pallas kernels  53 us (34%)
  starting transfers between devices  49.8 us (32%)
  waiting for transfers between devices  23.7 us (15%)
  between operations  15.1 us (10%)
  local copies, waits for them, and re-layouts  8.93 us (6%)
  other arithmetic  4.62 us (3%)
    pallas_call x19, Pallas kernels, call(): pl.pallas_call(run, out_shape=out_shape, compiler_params=pltpu.CompilerPa...  53 us
    ppermute x30, starting transfers between devices, shift(): lax.ppermute(array, axis, [(i, (i + step) % count) for i in range(count)])  48.9 us
    ppermute x30, waiting for transfers between devices, shift(): lax.ppermute(array, axis, [(i, (i + step) % count) for i in range(count)])  20.8 us
    unnamed x56, local copies, waits for them, and re-layouts  8.88 us
  transfers between devices with their start and end apart: 36, of which 17 were waited for; matrix products, arithmetic and copies ran while one was open for 1% of the time, Pallas kernels for 27%

profile of v3, /device:TPU:0, one launch (start us, length us, event | category | flops | bytes accessed | tf_op | source)
XLA Modules:
  0.0 155.2 jit_solution(11927107718255109508)
XLA Ops:
  7.9 1.7 %add_convert_fusion = bf16[64,1024]{1,0:T(8,128)(2,1)} fusion(bf16[64,1024]{1,0:T(8,128)(2,1)} %param.15, bf16[64,1024]{1,0:T(8,128)(2,1)} %param.14, f32[]{:T(128)} %bitcast.8, f32[]{:T(128)S(6)} %sub.4), kind=kLoop, calls=%fused_computation.10 | loop fusion | flops 393216 | bytes 393224 | tf_op jit(solution)/shard_map/convert_element_type | solution.py:880
  9.6 2.9 %collective-permute-start.10 = (bf16[256,512]{1,0:T(8,128)(2,1)}, bf16[256,512]{1,0:T(8,128)(2,1)S(1)}, u32[]{:S(2)}, u32[]{:S(2)}) collective-permute-start(bf16[256,512]{1,0:T(8,128)(2,1)} %param.17), channel_id=1, source_target_pairs={{0,3},{1,0},{2,1},{3,2},{4,7},{5,4},{6,5},{7,6},{8,11},{9,8},{10,9... | collective-permute-start | bytes 786440 | tf_op jit(solution)/shard_map/ppermute | solution.py:860
  12.5 2.3 %collective-permute-start.11 = (bf16[256,512]{1,0:T(8,128)(2,1)}, bf16[256,512]{1,0:T(8,128)(2,1)S(1)}, u32[]{:S(2)}, u32[]{:S(2)}) collective-permute-start(bf16[256,512]{1,0:T(8,128)(2,1)} %param.17), channel_id=1, source_target_pairs={{0,2},{1,3},{2,0},{3,1},{4,6},{5,7},{6,4},{7,5},{8,10},{9,11},{10,... | collective-permute-start | bytes 786440 | tf_op jit(solution)/shard_map/ppermute | solution.py:860
  14.8 1.0 copy-done
  15.9 0.9 copy-done.6
  16.8 0.7 copy-done.10
  17.5 0.7 copy-done.11
  18.2 10.4 %pre_kernel.1 = (bf16[4,272,128]{2,1,0:T(8,128)(2,1)S(1)}, bf16[4,272,128]{2,1,0:T(8,128)(2,1)S(1)}, bf16[8,256,256]{2,1,0:T(8,128)(2,1)S(1)}, bf16[8,256,256]{2...) custom-call(s32[4]{0:T(128)S(1)} %pad_add_fusion.refs_0_, bf16[256,512]{1,0:T(8,128)(2,1)S(1)} %copy-done.6, ...), custom_call_target="tpu_custom_call" | custom-call | flops 1000000 | bytes 1 | tf_op jit(solution)/shard_map/pre_kernel/pallas_call | solution.py:70
  28.8 1.1 copy-done.21
  29.9 2.6 %attend_kernel.1 = (bf16[8,256,256]{2,1,0:T(8,128)(2,1)S(1)}, bf16[8,256,128]{2,1,0:T(8,128)(2,1)S(1)}, f32[8,256,128]{2,1,0:T(8,128)S(1)}, bf16[8,256,128]{2,1,0:T(8,128)(2,1)S(1)}) custom-call(s32[4]{0:T(128)S(1)} %pad_add_fusion.refs_0_, bf16[256,512]{1,0:T(8,128)(2,1)S(1)} %copy-done.21, bf16[256,512]{1,0:T(8,128)(2,1)S(1)} %copy-done.6, ...), custom_call_target="tpu_custom_call" | custom-call | flops 5000000000 | bytes 1 | tf_op jit(solution)/shard_map/attend_kernel/pallas_call | solution.py:70
  32.6 0.8 pair_kernel.1
  33.4 2.0 %collective-permute-start.1 = (bf16[272,128]{1,0:T(8,128)(2,1)S(1)}, bf16[272,128]{1,0:T(8,128)(2,1)S(1)}, u32[]{:S(2)}, u32[]{:S(2)}) collective-permute-start(bf16[272,128]{1,0:T(8,128)(2,1)S(1)} %get-tuple-element.76), channel_id=1, source_target_pairs={{0,8},{8,16},{16,24},{24,0},{1,9},{9,17},{17,25},{25,1},{2,10},{10... | collective-permute-start | bytes 208904 | tf_op jit(solution)/shard_map/ppermute | solution.py:860
  35.4 3.6 %collective-permute-start.2 = (bf16[272,128]{1,0:T(8,128)(2,1)S(1)}, bf16[272,128]{1,0:T(8,128)(2,1)S(1)}, u32[]{:S(2)}, u32[]{:S(2)}) collective-permute-start(bf16[272,128]{1,0:T(8,128)(2,1)S(1)} %get-tuple-element.77), channel_id=1, source_target_pairs={{0,16},{8,24},{16,0},{24,8},{1,17},{9,25},{17,1},{25,9},{2,18},{10... | collective-permute-start | bytes 208904 | tf_op jit(solution)/shard_map/ppermute | solution.py:860
  39.0 1.0 collective-permute-start.3
  40.0 0.7 copy-done.26
  40.8 1.2 pad_maximum_fusion.refs_1_
  42.0 0.9 collective-permute-done.2.refs_3_
  43.3 1.1 prefix_kernel.1
  44.4 3.1 %collective-permute-start.6 = (bf16[272,128]{1,0:T(8,128)(2,1)S(1)}, bf16[272,128]{1,0:T(8,128)(2,1)S(1)}, u32[]{:S(2)}, u32[]{:S(2)}) collective-permute-start(bf16[272,128]{1,0:T(8,128)(2,1)S(1)} %get-tuple-element.84), channel_id=1, source_target_pairs={{0,96},{32,0},{64,32},{96,64},{1,97},{33,1},{65,33},{97,65},{2,98}... | collective-permute-start | bytes 208904 | tf_op jit(solution)/shard_map/ppermute | solution.py:860
  48.1 1.0 collective-permute-start.4
  49.1 0.9 suffix_kernel.1
  50.6 4.0 %collective-permute-done.5.refs_2_ = bf16[272,128]{1,0:T(8,128)(2,1)S(1)} collective-permute-done((bf16[272,128]{1,0:T(8,128)(2,1)S(1)}, bf16[272,128]{1,0:T(8,128)(2,1)S(1)}, u32[]{:S(2)}, u32[]{:S(2)}) %collective-permute-start.5) | collective-permute-done | bytes 69664 | tf_op jit(solution)/shard_map/ppermute | solution.py:860
  54.6 0.7 collective-permute-done.4.refs_1_
  55.4 1.7 %enter_kernel.1 = (f32[128,128]{1,0:T(8,128)S(1)}, f32[128,128]{1,0:T(8,128)}, f32[128,128]{1,0:T(8,128)}, f32[128,128]{1,0:T(8,128)}) custom-call(s32[4]{0:T(128)S(1)} %pad_add_fusion.refs_0_, bf16[272,128]{1,0:T(8,128)(2,1)S(1)} %collective-permute-done.4.refs_1_, bf16[272,128]{1,0:T(8,128)(2,1)S(1)} %collective-permute-done.5.refs_2_, ...), custom_call_target="tpu_custom_call" | custom-call | flops 1000000 | bytes 1 | tf_op jit(solution)/shard_map/enter_kernel/pallas_call | solution.py:70
  57.7 1.2 collective-permute-start.7
  58.9 2.9 %collective-permute-start.8 = (f32[128,128]{1,0:T(8,128)}, f32[128,128]{1,0:T(8,128)}, u32[]{:S(2)}, u32[]{:S(2)}) collective-permute-start(f32[128,128]{1,0:T(8,128)} %get-tuple-element.92), channel_id=1, source_target_pairs={{0,16},{8,24},{16,0},{24,8},{1,17},{9,25},{17,1},{25,9},{2,18},{10... | collective-permute-start | bytes 196616 | tf_op jit(solution)/shard_map/ppermute | solution.py:860
  62.4 2.2 %copy-done.13 = bf16[2048,1024]{1,0:T(8,128)(2,1)S(1)} copy-done((bf16[2048,1024]{1,0:T(8,128)(2,1)S(1)}, bf16[2048,1024]{1,0:T(8,128)(2,1)}, u32[]{:S(2)}) %copy-start.13) | copy-done | bytes 4194328
  64.6 2.7 %back_kernel.1.refs_7_.refs_5_ = f32[256,1024]{1,0:T(8,128)S(1)} custom-call(s32[4]{0:T(128)S(1)} %pad_add_fusion.refs_0_, bf16[4,256,512]{2,1,0:T(8,128)(2,1)S(1)} %pad_maximum_fusion.refs_1_, bf16[2048,1024]{1,0:T(8,128)(2,1)S(1)} %copy-done.13, bf16[4,128,128]{2,1,0:T(8,128)(2,1)S(1)} %get-tuple-element.89.refs_7_.refs_3_), custom_call_target="tpu_custom_call" | custom-call | flops 5000000000 | bytes 1 | tf_op jit(solution)/shard_map/back_kernel/pallas_call | solution.py:70
  67.3 1.6 %split_kernel.1 = (f32[4,128,128]{2,1,0:T(8,128)S(1)}, f32[4,128,128]{2,1,0:T(8,128)S(1)}) custom-call(s32[4]{0:T(128)S(1)} %pad_add_fusion.refs_0_, f32[128,128]{1,0:T(8,128)S(1)} %copy-done.9, f32[128,128]{1,0:T(8,128)} %collective-permute-done.7.refs_2_, f32[128,128]{1,0:T(8,128)} %collective-permute-done.8.refs_3_, ...), custom_call_target="tpu_custom_call" | custom-call | flops 1000000 | bytes 1 | tf_op jit(solution)/shard_map/split_kernel/pallas_call | solution.py:70
  69.1 1.5 collective-permute-done.13.refs_1_
  70.6 5.4 %norm_kernel.1 = (bf16[256,1024]{1,0:T(8,128)(2,1)S(1)}, bf16[8,128,128]{2,1,0:T(8,128)(2,1)S(1)}, f32[8,256,128]{2,1,0:T(8,128)S(1)}, f32[4,128,128]{2,1,0:T(8,128)S(1)}, f32[4,128,128]{2,1,0:T(8,128)S(1)}) custom-call(s32[4]{0:T(128)S(1)} %pad_add_fusion.refs_0_, f32[4,128,128]{2,1,0:T(8,128)S(1)} %collective-permute-done.13.refs_1_, ...), custom_call_target="tpu_custom_call" | custom-call | flops 1000000 | bytes 1 | tf_op jit(solution)/shard_map/norm_kernel/pallas_call | solution.py:70
  76.4 1.4 collective-permute-done.14.refs_4_.refs_3_.refs_8_
  77.9 2.6 %outer_kernel.1 = (bf16[4,4,64,1024]{3,2,1,0:T(8,128)(2,1)S(1)}, bf16[4,4,64,1024]{3,2,1,0:T(8,128)(2,1)S(1)}) custom-call(s32[4]{0:T(128)S(1)} %pad_add_fusion.refs_0_, bf16[4,256,512]{2,1,0:T(8,128)(2,1)S(1)} %pad_maximum_fusion.refs_1_, bf16[256,1024]{1,0:T(8,128)(2,1)S(1)} %get-tuple-element.98.refs_2_.refs_1_, ...), custom_call_target="tpu_custom_call" | custom-call | flops 5000000000 | bytes 1 | tf_op jit(solution)/shard_map/outer_kernel/pallas_call | solution.py:70
  80.6 0.8 join_kernel.1
  81.4 1.5 collective-permute-start.15
  82.9 0.9 collective-permute-start.16
  83.9 1.8 %collective-permute-start.17 = (f32[128,128]{1,0:T(8,128)S(1)}, f32[128,128]{1,0:T(8,128)S(1)}, u32[]{:S(2)}, u32[]{:S(2)}) collective-permute-start(f32[128,128]{1,0:T(8,128)S(1)} %get-tuple-element.105), channel_id=1, source_target_pairs={{0,24},{8,0},{16,8},{24,16},{1,25},{9,1},{17,9},{25,17},{2,26},{10... | collective-permute-start | bytes 196616 | tf_op jit(solution)/shard_map/ppermute | solution.py:860
  85.7 1.4 collective-permute-done.15.refs_2_
  87.1 1.6 %collective-permute-done.16.refs_3_ = f32[128,128]{1,0:T(8,128)S(1)} collective-permute-done((f32[128,128]{1,0:T(8,128)S(1)}, f32[128,128]{1,0:T(8,128)S(1)}, u32[]{:S(2)}, u32[]{:S(2)}) %collective-permute-start.16) | collective-permute-done | bytes 65568 | tf_op jit(solution)/shard_map/ppermute | solution.py:860
  89.1 1.3 later_kernel.1
  90.6 3.5 %collective-permute-start.19 = (f32[128,128]{1,0:T(8,128)S(1)}, f32[128,128]{1,0:T(8,128)S(1)}, u32[]{:S(2)}, u32[]{:S(2)}) collective-permute-start(f32[128,128]{1,0:T(8,128)S(1)} %get-tuple-element.106.refs_3_), channel_id=1, source_target_pairs={{0,64},{32,96},{64,0},{96,32},{1,65},{33,97},{65,1},{97,33},{2,66}... | collective-permute-start | bytes 196616 | tf_op jit(solution)/shard_map/ppermute | solution.py:860
  94.4 4.7 %middle_kernel.1 = (f32[256,512]{1,0:T(8,128)}, bf16[8,256,128]{2,1,0:T(8,128)(2,1)S(1)}, f32[256,512]{1,0:T(8,128)S(1)}, f32[8,256,128]{2,1,0:T(8,128)S(1)}, bf...) custom-call(s32[4]{0:T(128)S(1)} %pad_add_fusion.refs_0_, ...), custom_call_target="tpu_custom_call" | custom-call | flops 10000000000 | bytes 1 | tf_op jit(solution)/shard_map/middle_kernel/pallas_call | solution.py:70
  99.1 1.1 leave_kernel.1
  100.3 1.2 collective-permute-start.21
  101.4 3.0 %collective-permute-start.22 = (f32[128,128]{1,0:T(8,128)S(1)}, f32[128,128]{1,0:T(8,128)S(1)}, u32[]{:S(2)}, u32[]{:S(2)}) collective-permute-start(f32[128,128]{1,0:T(8,128)S(1)} %get-tuple-element.114), channel_id=1, source_target_pairs={{0,16},{8,24},{16,0},{24,8},{1,17},{9,25},{17,1},{25,9},{2,18},{10... | collective-permute-start | bytes 196616 | tf_op jit(solution)/shard_map/ppermute | solution.py:860
  104.7 1.0 blend_kernel.1
  106.1 1.3 collective-permute-done.22.refs_3_
  107.4 1.3 collective-permute-done.23.refs_4_
  108.7 0.8 part_kernel.1
  109.7 3.0 %collective-permute-start.30 = (bf16[4,64,1024]{2,1,0:T(8,128)(2,1)S(1)}, bf16[4,64,1024]{2,1,0:T(8,128)(2,1)S(1)}, u32[]{:S(2)}, u32[]{:S(2)}) collective-permute-start(bf16[4,64,1024]{2,1,0:T(8,128)(2,1)S(1)} %get-tuple-element.132), channel_id=1, source_target_pairs={{0,16},{8,24},{16,0},{24,8},{1,17},{9,25},{17,1},{25,9},{2,18},{10... | collective-permute-start | bytes 1572872 | tf_op jit(solution)/shard_map/ppermute | solution.py:860
  112.7 1.2 collective-permute-start.31
  113.8 10.1 %last_kernel.1 = (f32[256,1024]{1,0:T(8,128)}, f32[256,512]{1,0:T(8,128)}, f32[8,256]{1,0:T(8,128)}, f32[8,256]{1,0:T(8,128)}) custom-call(s32[4]{0:T(128)S(1)} %pad_add_fusion.refs_0_, bf16[256,512]{1,0:T(8,128)(2,1)S(1)} %copy-done.7, f32[8,256]{1,0:T(8,128)S(1)} %get-tuple-element.79.refs_3_.refs_4_.refs_2_, f32[4,256,128]{2,1,0:T(8,128)S(1)} %copy-done.20, ...), custom_call_target="tpu_custom_call" | custom-call | flops 10000000000 | bytes 1 | tf_op jit(solution)/shard_map/last_kernel/pallas_call | solution.py:70
  123.9 0.7 copy-done.12
  124.6 2.5 %mix_kernel.1 = bf16[4,256,512]{2,1,0:T(8,128)(2,1)S(1)} custom-call(s32[4]{0:T(128)S(1)} %pad_add_fusion.refs_0_, bf16[256,1024]{1,0:T(8,128)(2,1)S(1)} %get-tuple-element.98.refs_2_.refs_1_, bf16[2048,1024]{1,0:T(8,128)(2,1)S(1)} %copy-done.14, f32[8,256]{1,0:T(8,128)S(1)} %copy-done.12), custom_call_target="tpu_custom_call" | custom-call | flops 5000000000 | bytes 1 | tf_op jit(solution)/shard_map/mix_kernel/pallas_call | solution.py:70
  127.2 1.8 %collective-permute-start.26 = (bf16[256,512]{1,0:T(8,128)(2,1)S(1)}, bf16[256,512]{1,0:T(8,128)(2,1)S(1)}, u32[]{:S(2)}, u32[]{:S(2)}) collective-permute-start(bf16[256,512]{1,0:T(8,128)(2,1)S(1)} %get-tuple-element.138), channel_id=1, source_target_pairs={{0,1},{1,2},{2,3},{3,0},{4,5},{5,6},{6,7},{7,4},{8,9},{9,10},{10,1... | collective-permute-start | bytes 786440 | tf_op jit(solution)/shard_map/ppermute | solution.py:860
  129.0 1.9 %collective-permute-start.28 = (bf16[256,512]{1,0:T(8,128)(2,1)S(1)}, bf16[256,512]{1,0:T(8,128)(2,1)S(1)}, u32[]{:S(2)}, u32[]{:S(2)}) collective-permute-start(bf16[256,512]{1,0:T(8,128)(2,1)S(1)} %get-tuple-element.139), channel_id=1, source_target_pairs={{0,3},{1,0},{2,1},{3,2},{4,7},{5,4},{6,5},{7,6},{8,11},{9,8},{10,9... | collective-permute-start | bytes 786440 | tf_op jit(solution)/shard_map/ppermute | solution.py:860
  130.9 5.5 %collective-permute-done.29.refs_2_ = bf16[4,64,1024]{2,1,0:T(8,128)(2,1)S(1)} collective-permute-done((bf16[4,64,1024]{2,1,0:T(8,128)(2,1)S(1)}, bf16[4,64,1024]{2,1,0:T(8,128)(2,1)S(1)}, u32[]{:S(2)}, u32[]{:S(2)}) %collective-permute-start.29) | collective-permute-done | bytes 524320 | tf_op jit(solution)/shard_map/ppermute | solution.py:860
  137.0 0.8 sum_kernel.1
  137.8 1.9 %collective-permute-start.32 = (bf16[64,1024]{1,0:T(8,128)(2,1)S(1)}, bf16[64,1024]{1,0:T(8,128)(2,1)S(1)}, u32[]{:S(2)}, u32[]{:S(2)}) collective-permute-start(bf16[64,1024]{1,0:T(8,128)(2,1)S(1)} %get-tuple-element.135), channel_id=1, source_target_pairs={{0,32},{32,64},{64,96},{96,0},{1,33},{33,65},{65,97},{97,1},{2,34}... | collective-permute-start | bytes 393224 | tf_op jit(solution)/shard_map/ppermute | solution.py:860
  139.8 2.6 %collective-permute-start.33 = (bf16[64,1024]{1,0:T(8,128)(2,1)S(1)}, bf16[64,1024]{1,0:T(8,128)(2,1)S(1)}, u32[]{:S(2)}, u32[]{:S(2)}) collective-permute-start(bf16[64,1024]{1,0:T(8,128)(2,1)S(1)} %get-tuple-element.136), channel_id=1, source_target_pairs={{0,64},{32,96},{64,0},{96,32},{1,65},{33,97},{65,1},{97,33},{2,66}... | collective-permute-start | bytes 393224 | tf_op jit(solution)/shard_map/ppermute | solution.py:860
  142.4 2.5 %collective-permute-start.34 = (bf16[64,1024]{1,0:T(8,128)(2,1)S(1)}, bf16[64,1024]{1,0:T(8,128)(2,1)S(1)}, u32[]{:S(2)}, u32[]{:S(2)}) collective-permute-start(bf16[64,1024]{1,0:T(8,128)(2,1)S(1)} %get-tuple-element.137), channel_id=1, source_target_pairs={{0,96},{32,0},{64,32},{96,64},{1,97},{33,1},{65,33},{97,65},{2,98}... | collective-permute-start | bytes 393224 | tf_op jit(solution)/shard_map/ppermute | solution.py:860
  144.9 0.8 fusion.2
  145.8 1.3 collective-permute-done.33
  147.5 0.9 broadcast_multiply_fusion
  (90 shorter events, 6.7 us)
Async XLA Ops:
  7.2 55.2 %all-gather.2.cloned.1.call-start = ((), (), s32[]{:S(2)}) async-start(), calls=%async_computation | async-start | bytes 4325376 | tf_op jit(solution)/shard_map/all_gather | solution.py:881
  9.6 29.4 %collective-permute-start.10 = (bf16[256,512]{1,0:T(8,128)(2,1)}, bf16[256,512]{1,0:T(8,128)(2,1)S(1)}, u32[]{:S(2)}, u32[]{:S(2)}) collective-permute-start(bf16[256,512]{1,0:T(8,128)(2,1)} %param.17), channel_id=1, source_target_pairs={{0,3},{1,0},{2,1},{3,2},{4,7},{5,4},{6,5},{7,6},{8,11},{9,8},{10,9... | collective-permute-start | bytes 786440 | tf_op jit(solution)/shard_map/ppermute | solution.py:860
  12.5 27.5 %collective-permute-start.12 = (bf16[256,512]{1,0:T(8,128)(2,1)}, bf16[256,512]{1,0:T(8,128)(2,1)S(1)}, u32[]{:S(2)}, u32[]{:S(2)}) collective-permute-start(bf16[256,512]{1,0:T(8,128)(2,1)} %param.17), channel_id=1, source_target_pairs={{0,1},{1,2},{2,3},{3,0},{4,5},{5,6},{6,7},{7,4},{8,9},{9,10},{10,1... | collective-permute-start | bytes 786440 | tf_op jit(solution)/shard_map/ppermute | solution.py:860
  12.5 27.5 %collective-permute-start.11 = (bf16[256,512]{1,0:T(8,128)(2,1)}, bf16[256,512]{1,0:T(8,128)(2,1)S(1)}, u32[]{:S(2)}, u32[]{:S(2)}) collective-permute-start(bf16[256,512]{1,0:T(8,128)(2,1)} %param.17), channel_id=1, source_target_pairs={{0,2},{1,3},{2,0},{3,1},{4,6},{5,7},{6,4},{7,5},{8,10},{9,11},{10,... | collective-permute-start | bytes 786440 | tf_op jit(solution)/shard_map/ppermute | solution.py:860
  14.8 1.0 copy-start
  15.9 0.9 copy-start.6
  16.8 0.7 copy-start.10
  17.5 0.7 copy-start.11
  28.7 3.9 %copy-start.15 = (bf16[8,256,256]{2,1,0:T(8,128)(2,1)}, bf16[8,256,256]{2,1,0:T(8,128)(2,1)S(1)}, u32[]{:S(2)}) copy-start(bf16[8,256,256]{2,1,0:T(8,128)(2,1)S(1)} %get-tuple-element.81.refs_5_.refs_9_) | copy-start | bytes 3145732
  28.7 3.9 %copy-start.17 = (bf16[8,256,256]{2,1,0:T(8,128)(2,1)}, bf16[8,256,256]{2,1,0:T(8,128)(2,1)S(1)}, u32[]{:S(2)}) copy-start(bf16[8,256,256]{2,1,0:T(8,128)(2,1)S(1)} %get-tuple-element.82.refs_6_.refs_10_) | copy-start | bytes 3145732
  28.7 3.9 %copy-start.19 = (f32[4,256,128]{2,1,0:T(8,128)}, f32[4,256,128]{2,1,0:T(8,128)S(1)}, u32[]{:S(2)}) copy-start(f32[4,256,128]{2,1,0:T(8,128)S(1)} %get-tuple-element.80.refs_4_.refs_5_.refs_3_) | copy-start | bytes 1572868
  28.7 3.9 %collective-permute-start = (bf16[4,272,128]{2,1,0:T(8,128)(2,1)S(1)}, bf16[4,272,128]{2,1,0:T(8,128)(2,1)S(1)}, u32[]{:S(2)}, u32[]{:S(2)}) collective-permute-start(bf16[4,272,128]{2,1,0:T(8,128)(2,1)S(1)} %get-tuple-element.74), channel_id=1, source_target_pairs={{0,4},{4,0},{1,5},{5,1},{2,6},{6,2},{3,7},{7,3},{8,12},{12,8},{9,1... | collective-permute-start | bytes 835592 | tf_op jit(solution)/shard_map/ppermute | solution.py:872
  28.8 1.2 copy-start.21
  29.9 10.8 %copy-start.25 = (bf16[256,512]{1,0:T(8,128)(2,1)S(1)}, bf16[256,512]{1,0:T(8,128)(2,1)}, u32[]{:S(2)}) copy-start(bf16[256,512]{1,0:T(8,128)(2,1)} %param.17) | copy-start | bytes 786436
  32.6 7.5 %copy-start.2 = (bf16[8,256,128]{2,1,0:T(8,128)(2,1)}, bf16[8,256,128]{2,1,0:T(8,128)(2,1)S(1)}, u32[]{:S(2)}) copy-start(bf16[8,256,128]{2,1,0:T(8,128)(2,1)S(1)} %get-tuple-element.96.refs_3_) | copy-start | bytes 1572868
  32.6 17.4 %copy-start.23 = (bf16[8,256,256]{2,1,0:T(8,128)(2,1)}, bf16[8,256,256]{2,1,0:T(8,128)(2,1)S(1)}, u32[]{:S(2)}) copy-start(bf16[8,256,256]{2,1,0:T(8,128)(2,1)S(1)} %get-tuple-element.110.refs_8_) | copy-start | bytes 3145732
  33.4 8.6 %collective-permute-start.1 = (bf16[272,128]{1,0:T(8,128)(2,1)S(1)}, bf16[272,128]{1,0:T(8,128)(2,1)S(1)}, u32[]{:S(2)}, u32[]{:S(2)}) collective-permute-start(bf16[272,128]{1,0:T(8,128)(2,1)S(1)} %get-tuple-element.76), channel_id=1, source_target_pairs={{0,8},{8,16},{16,24},{24,0},{1,9},{9,17},{17,25},{25,1},{2,10},{10... | collective-permute-start | bytes 208904 | tf_op jit(solution)/shard_map/ppermute | solution.py:860
  35.4 7.4 %collective-permute-start.2 = (bf16[272,128]{1,0:T(8,128)(2,1)S(1)}, bf16[272,128]{1,0:T(8,128)(2,1)S(1)}, u32[]{:S(2)}, u32[]{:S(2)}) collective-permute-start(bf16[272,128]{1,0:T(8,128)(2,1)S(1)} %get-tuple-element.77), channel_id=1, source_target_pairs={{0,16},{8,24},{16,0},{24,8},{1,17},{9,25},{17,1},{25,9},{2,18},{10... | collective-permute-start | bytes 208904 | tf_op jit(solution)/shard_map/ppermute | solution.py:860
  39.0 4.3 %collective-permute-start.3 = (bf16[272,128]{1,0:T(8,128)(2,1)S(1)}, bf16[272,128]{1,0:T(8,128)(2,1)S(1)}, u32[]{:S(2)}, u32[]{:S(2)}) collective-permute-start(bf16[272,128]{1,0:T(8,128)(2,1)S(1)} %get-tuple-element.78), channel_id=1, source_target_pairs={{0,24},{8,0},{16,8},{24,16},{1,25},{9,1},{17,9},{25,17},{2,26},{10... | collective-permute-start | bytes 208904 | tf_op jit(solution)/shard_map/ppermute | solution.py:860
  40.0 0.7 copy-start.26
  40.0 0.8 copy-start.27
  44.4 5.6 %copy-start.4 = (bf16[4,272,128]{2,1,0:T(8,128)(2,1)}, bf16[4,272,128]{2,1,0:T(8,128)(2,1)S(1)}, u32[]{:S(2)}) copy-start(bf16[4,272,128]{2,1,0:T(8,128)(2,1)S(1)} %get-tuple-element.88.refs_1_.refs_5_) | copy-start | bytes 835588
  44.4 6.2 %collective-permute-start.6 = (bf16[272,128]{1,0:T(8,128)(2,1)S(1)}, bf16[272,128]{1,0:T(8,128)(2,1)S(1)}, u32[]{:S(2)}, u32[]{:S(2)}) collective-permute-start(bf16[272,128]{1,0:T(8,128)(2,1)S(1)} %get-tuple-element.84), channel_id=1, source_target_pairs={{0,96},{32,0},{64,32},{96,64},{1,97},{33,1},{65,33},{97,65},{2,98}... | collective-permute-start | bytes 208904 | tf_op jit(solution)/shard_map/ppermute | solution.py:860
  47.5 7.2 %collective-permute-start.5 = (bf16[272,128]{1,0:T(8,128)(2,1)S(1)}, bf16[272,128]{1,0:T(8,128)(2,1)S(1)}, u32[]{:S(2)}, u32[]{:S(2)}) collective-permute-start(bf16[272,128]{1,0:T(8,128)(2,1)S(1)} %get-tuple-element.84), channel_id=1, source_target_pairs={{0,64},{32,96},{64,0},{96,32},{1,65},{33,97},{65,1},{97,33},{2,66}... | collective-permute-start | bytes 208904 | tf_op jit(solution)/shard_map/ppermute | solution.py:860
  48.1 7.3 %collective-permute-start.4 = (bf16[272,128]{1,0:T(8,128)(2,1)S(1)}, bf16[272,128]{1,0:T(8,128)(2,1)S(1)}, u32[]{:S(2)}, u32[]{:S(2)}) collective-permute-start(bf16[272,128]{1,0:T(8,128)(2,1)S(1)} %get-tuple-element.84), channel_id=1, source_target_pairs={{0,32},{32,64},{64,96},{96,0},{1,33},{33,65},{65,97},{97,1},{2,34}... | collective-permute-start | bytes 208904 | tf_op jit(solution)/shard_map/ppermute | solution.py:860
  57.1 0.6 copy-start.8
  57.7 9.6 %collective-permute-start.7 = (f32[128,128]{1,0:T(8,128)}, f32[128,128]{1,0:T(8,128)}, u32[]{:S(2)}, u32[]{:S(2)}) collective-permute-start(f32[128,128]{1,0:T(8,128)} %get-tuple-element.91), channel_id=1, source_target_pairs={{0,8},{8,16},{16,24},{24,0},{1,9},{9,17},{17,25},{25,1},{2,10},{10... | collective-permute-start | bytes 196616 | tf_op jit(solution)/shard_map/ppermute | solution.py:860
  58.9 8.4 %collective-permute-start.8 = (f32[128,128]{1,0:T(8,128)}, f32[128,128]{1,0:T(8,128)}, u32[]{:S(2)}, u32[]{:S(2)}) collective-permute-start(f32[128,128]{1,0:T(8,128)} %get-tuple-element.92), channel_id=1, source_target_pairs={{0,16},{8,24},{16,0},{24,8},{1,17},{9,25},{17,1},{25,9},{2,18},{10... | collective-permute-start | bytes 196616 | tf_op jit(solution)/shard_map/ppermute | solution.py:860
  61.8 5.5 %collective-permute-start.9 = (f32[128,128]{1,0:T(8,128)}, f32[128,128]{1,0:T(8,128)}, u32[]{:S(2)}, u32[]{:S(2)}) collective-permute-start(f32[128,128]{1,0:T(8,128)} %get-tuple-element.93), channel_id=1, source_target_pairs={{0,24},{8,0},{16,8},{24,16},{1,25},{9,1},{17,9},{25,17},{2,26},{10... | collective-permute-start | bytes 196616 | tf_op jit(solution)/shard_map/ppermute | solution.py:860
  62.4 2.2 %copy-start.13 = (bf16[2048,1024]{1,0:T(8,128)(2,1)S(1)}, bf16[2048,1024]{1,0:T(8,128)(2,1)}, u32[]{:S(2)}) copy-start(bf16[2048,1024]{1,0:T(8,128)(2,1)} %all-gather.2.cloned.1.call-done.refs_2_) | copy-start | bytes 12582916
  64.6 2.8 %copy-start.9 = (f32[128,128]{1,0:T(8,128)S(1)}, f32[128,128]{1,0:T(8,128)}, u32[]{:S(2)}) copy-start(f32[128,128]{1,0:T(8,128)} %copy-done.8) | copy-start | bytes 196612
  67.3 3.3 %copy-start.3 = (bf16[8,256,128]{2,1,0:T(8,128)(2,1)S(1)}, bf16[8,256,128]{2,1,0:T(8,128)(2,1)}, u32[]{:S(2)}) copy-start(bf16[8,256,128]{2,1,0:T(8,128)(2,1)} %copy-done.2) | copy-start | bytes 1572868
  69.0 1.6 %collective-permute-start.13 = (f32[4,128,128]{2,1,0:T(8,128)S(1)}, f32[4,128,128]{2,1,0:T(8,128)S(1)}, u32[]{:S(2)}, u32[]{:S(2)}) collective-permute-start(f32[4,128,128]{2,1,0:T(8,128)S(1)} %get-tuple-element.94), channel_id=1, source_target_pairs={{0,4},{4,0},{1,5},{5,1},{2,6},{6,2},{3,7},{7,3},{8,12},{12,8},{9,1... | collective-permute-start | bytes 786440 | tf_op jit(solution)/shard_map/ppermute | solution.py:872
  76.0 1.8 %collective-permute-start.14 = (f32[4,128,128]{2,1,0:T(8,128)S(1)}, f32[4,128,128]{2,1,0:T(8,128)S(1)}, u32[]{:S(2)}, u32[]{:S(2)}) collective-permute-start(f32[4,128,128]{2,1,0:T(8,128)S(1)} %get-tuple-element.101), channel_id=1, source_target_pairs={{0,4},{4,0},{1,5},{5,1},{2,6},{6,2},{3,7},{7,3},{8,12},{12,8},{9,1... | collective-permute-start | bytes 786440 | tf_op jit(solution)/shard_map/ppermute | solution.py:872
  77.8 11.3 %copy-start.5 = (bf16[4,272,128]{2,1,0:T(8,128)(2,1)S(1)}, bf16[4,272,128]{2,1,0:T(8,128)(2,1)}, u32[]{:S(2)}) copy-start(bf16[4,272,128]{2,1,0:T(8,128)(2,1)} %copy-done.4) | copy-start | bytes 835588
  77.8 16.5 %copy-start.1 = (bf16[256,1024]{1,0:T(8,128)(2,1)S(1)}, bf16[256,1024]{1,0:T(8,128)(2,1)}, u32[]{:S(2)}) copy-start(bf16[256,1024]{1,0:T(8,128)(2,1)} %refs_3_.3) | copy-start | bytes 1572868
  77.8 16.5 %copy-start.7 = (bf16[256,512]{1,0:T(8,128)(2,1)S(1)}, bf16[256,512]{1,0:T(8,128)(2,1)}, u32[]{:S(2)}) copy-start(bf16[256,512]{1,0:T(8,128)(2,1)} %refs_1_.7) | copy-start | bytes 786436
  77.8 16.5 %copy-start.16 = (bf16[8,256,256]{2,1,0:T(8,128)(2,1)S(1)}, bf16[8,256,256]{2,1,0:T(8,128)(2,1)}, u32[]{:S(2)}) copy-start(bf16[8,256,256]{2,1,0:T(8,128)(2,1)} %copy-done.15) | copy-start | bytes 3145732
  77.8 16.5 %copy-start.18 = (bf16[8,256,256]{2,1,0:T(8,128)(2,1)S(1)}, bf16[8,256,256]{2,1,0:T(8,128)(2,1)}, u32[]{:S(2)}) copy-start(bf16[8,256,256]{2,1,0:T(8,128)(2,1)} %copy-done.17) | copy-start | bytes 3145732
  77.8 16.5 %copy-start.20 = (f32[4,256,128]{2,1,0:T(8,128)S(1)}, f32[4,256,128]{2,1,0:T(8,128)}, u32[]{:S(2)}) copy-start(f32[4,256,128]{2,1,0:T(8,128)} %copy-done.19) | copy-start | bytes 1572868
  77.8 16.5 %copy-start.22 = (bf16[256,512]{1,0:T(8,128)(2,1)S(1)}, bf16[256,512]{1,0:T(8,128)(2,1)}, u32[]{:S(2)}) copy-start(bf16[256,512]{1,0:T(8,128)(2,1)} %refs_1_.6) | copy-start | bytes 786436
  77.8 16.5 %copy-start.24 = (bf16[8,256,256]{2,1,0:T(8,128)(2,1)S(1)}, bf16[8,256,256]{2,1,0:T(8,128)(2,1)}, u32[]{:S(2)}) copy-start(bf16[8,256,256]{2,1,0:T(8,128)(2,1)} %copy-done.23) | copy-start | bytes 3145732
  80.4 24.3 %collective-permute-start.24 = (bf16[4,4,64,1024]{3,2,1,0:T(8,128)(2,1)S(1)}, bf16[4,4,64,1024]{3,2,1,0:T(8,128)(2,1)S(1)}, u32[]{:S(2)}, u32[]{:S(2)}) collective-permute-start(bf16[4,4,64,1024]{3,2,1,0:T(8,128)(2,1)S(1)} %get-tuple-element.117), channel_id=1, source_target_pairs={{0,4},{4,0},{1,5},{5,1},{2,6},{6,2},{3,7},{7,3},{8,12},{12,8},{9,1... | collective-permute-start | bytes 6291464 | tf_op jit(solution)/shard_map/ppermute | solution.py:872
  81.4 5.6 %collective-permute-start.15 = (f32[128,128]{1,0:T(8,128)S(1)}, f32[128,128]{1,0:T(8,128)S(1)}, u32[]{:S(2)}, u32[]{:S(2)}) collective-permute-start(f32[128,128]{1,0:T(8,128)S(1)} %get-tuple-element.103), channel_id=1, source_target_pairs={{0,8},{8,16},{16,24},{24,0},{1,9},{9,17},{17,25},{25,1},{2,10},{10... | collective-permute-start | bytes 196616 | tf_op jit(solution)/shard_map/ppermute | solution.py:860
  82.9 5.8 %collective-permute-start.16 = (f32[128,128]{1,0:T(8,128)S(1)}, f32[128,128]{1,0:T(8,128)S(1)}, u32[]{:S(2)}, u32[]{:S(2)}) collective-permute-start(f32[128,128]{1,0:T(8,128)S(1)} %get-tuple-element.104), channel_id=1, source_target_pairs={{0,16},{8,24},{16,0},{24,8},{1,17},{9,25},{17,1},{25,9},{2,18},{10... | collective-permute-start | bytes 196616 | tf_op jit(solution)/shard_map/ppermute | solution.py:860
  83.9 5.2 %collective-permute-start.17 = (f32[128,128]{1,0:T(8,128)S(1)}, f32[128,128]{1,0:T(8,128)S(1)}, u32[]{:S(2)}, u32[]{:S(2)}) collective-permute-start(f32[128,128]{1,0:T(8,128)S(1)} %get-tuple-element.105), channel_id=1, source_target_pairs={{0,24},{8,0},{16,8},{24,16},{1,25},{9,1},{17,9},{25,17},{2,26},{10... | collective-permute-start | bytes 196616 | tf_op jit(solution)/shard_map/ppermute | solution.py:860
  90.3 8.8 %collective-permute-start.20 = (f32[128,128]{1,0:T(8,128)S(1)}, f32[128,128]{1,0:T(8,128)S(1)}, u32[]{:S(2)}, u32[]{:S(2)}) collective-permute-start(f32[128,128]{1,0:T(8,128)S(1)} %get-tuple-element.106.refs_3_), channel_id=1, source_target_pairs={{0,32},{32,64},{64,96},{96,0},{1,33},{33,65},{65,97},{97,1},{2,34}... | collective-permute-start | bytes 196616 | tf_op jit(solution)/shard_map/ppermute | solution.py:860
  90.6 8.5 %collective-permute-start.19 = (f32[128,128]{1,0:T(8,128)S(1)}, f32[128,128]{1,0:T(8,128)S(1)}, u32[]{:S(2)}, u32[]{:S(2)}) collective-permute-start(f32[128,128]{1,0:T(8,128)S(1)} %get-tuple-element.106.refs_3_), channel_id=1, source_target_pairs={{0,64},{32,96},{64,0},{96,32},{1,65},{33,97},{65,1},{97,33},{2,66}... | collective-permute-start | bytes 196616 | tf_op jit(solution)/shard_map/ppermute | solution.py:860
  94.2 4.9 %collective-permute-start.18 = (f32[128,128]{1,0:T(8,128)S(1)}, f32[128,128]{1,0:T(8,128)S(1)}, u32[]{:S(2)}, u32[]{:S(2)}) collective-permute-start(f32[128,128]{1,0:T(8,128)S(1)} %get-tuple-element.106.refs_3_), channel_id=1, source_target_pairs={{0,96},{32,0},{64,32},{96,64},{1,97},{33,1},{65,33},{97,65},{2,98}... | collective-permute-start | bytes 196616 | tf_op jit(solution)/shard_map/ppermute | solution.py:860
  100.3 5.9 %collective-permute-start.21 = (f32[128,128]{1,0:T(8,128)S(1)}, f32[128,128]{1,0:T(8,128)S(1)}, u32[]{:S(2)}, u32[]{:S(2)}) collective-permute-start(f32[128,128]{1,0:T(8,128)S(1)} %get-tuple-element.113), channel_id=1, source_target_pairs={{0,8},{8,16},{16,24},{24,0},{1,9},{9,17},{17,25},{25,1},{2,10},{10... | collective-permute-start | bytes 196616 | tf_op jit(solution)/shard_map/ppermute | solution.py:860
  101.4 6.0 %collective-permute-start.22 = (f32[128,128]{1,0:T(8,128)S(1)}, f32[128,128]{1,0:T(8,128)S(1)}, u32[]{:S(2)}, u32[]{:S(2)}) collective-permute-start(f32[128,128]{1,0:T(8,128)S(1)} %get-tuple-element.114), channel_id=1, source_target_pairs={{0,16},{8,24},{16,0},{24,8},{1,17},{9,25},{17,1},{25,9},{2,18},{10... | collective-permute-start | bytes 196616 | tf_op jit(solution)/shard_map/ppermute | solution.py:860
  104.5 4.3 %collective-permute-start.23 = (f32[128,128]{1,0:T(8,128)S(1)}, f32[128,128]{1,0:T(8,128)S(1)}, u32[]{:S(2)}, u32[]{:S(2)}) collective-permute-start(f32[128,128]{1,0:T(8,128)S(1)} %get-tuple-element.115), channel_id=1, source_target_pairs={{0,24},{8,0},{16,8},{24,16},{1,25},{9,1},{17,9},{25,17},{2,26},{10... | collective-permute-start | bytes 196616 | tf_op jit(solution)/shard_map/ppermute | solution.py:860
  109.5 4.3 %collective-permute-start.25 = (f32[4,128,128]{2,1,0:T(8,128)S(1)}, f32[4,128,128]{2,1,0:T(8,128)S(1)}, u32[]{:S(2)}, u32[]{:S(2)}) collective-permute-start(f32[4,128,128]{2,1,0:T(8,128)S(1)} %get-tuple-element.119), channel_id=1, source_target_pairs={{0,4},{4,0},{1,5},{5,1},{2,6},{6,2},{3,7},{7,3},{8,12},{12,8},{9,1... | collective-permute-start | bytes 786440 | tf_op jit(solution)/shard_map/ppermute | solution.py:872
  109.6 26.8 %collective-permute-start.29 = (bf16[4,64,1024]{2,1,0:T(8,128)(2,1)S(1)}, bf16[4,64,1024]{2,1,0:T(8,128)(2,1)S(1)}, u32[]{:S(2)}, u32[]{:S(2)}) collective-permute-start(bf16[4,64,1024]{2,1,0:T(8,128)(2,1)S(1)} %get-tuple-element.131), channel_id=1, source_target_pairs={{0,8},{8,16},{16,24},{24,0},{1,9},{9,17},{17,25},{25,1},{2,10},{10... | collective-permute-start | bytes 1572872 | tf_op jit(solution)/shard_map/ppermute | solution.py:860
  109.7 26.7 %collective-permute-start.30 = (bf16[4,64,1024]{2,1,0:T(8,128)(2,1)S(1)}, bf16[4,64,1024]{2,1,0:T(8,128)(2,1)S(1)}, u32[]{:S(2)}, u32[]{:S(2)}) collective-permute-start(bf16[4,64,1024]{2,1,0:T(8,128)(2,1)S(1)} %get-tuple-element.132), channel_id=1, source_target_pairs={{0,16},{8,24},{16,0},{24,8},{1,17},{9,25},{17,1},{25,9},{2,18},{10... | collective-permute-start | bytes 1572872 | tf_op jit(solution)/shard_map/ppermute | solution.py:860
  112.7 24.3 %collective-permute-start.31 = (bf16[4,64,1024]{2,1,0:T(8,128)(2,1)S(1)}, bf16[4,64,1024]{2,1,0:T(8,128)(2,1)S(1)}, u32[]{:S(2)}, u32[]{:S(2)}) collective-permute-start(bf16[4,64,1024]{2,1,0:T(8,128)(2,1)S(1)} %get-tuple-element.133), channel_id=1, source_target_pairs={{0,24},{8,0},{16,8},{24,16},{1,25},{9,1},{17,9},{25,17},{2,26},{10... | collective-permute-start | bytes 1572872 | tf_op jit(solution)/shard_map/ppermute | solution.py:860
  113.8 10.1 %copy-start.14 = (bf16[2048,1024]{1,0:T(8,128)(2,1)S(1)}, bf16[2048,1024]{1,0:T(8,128)(2,1)}, u32[]{:S(2)}) copy-start(bf16[2048,1024]{1,0:T(8,128)(2,1)} %all-gather.2.cloned.1.call-done.refs_2_) | copy-start | bytes 12582916
  123.9 0.7 copy-start.12
  127.2 15.2 %collective-permute-start.26 = (bf16[256,512]{1,0:T(8,128)(2,1)S(1)}, bf16[256,512]{1,0:T(8,128)(2,1)S(1)}, u32[]{:S(2)}, u32[]{:S(2)}) collective-permute-start(bf16[256,512]{1,0:T(8,128)(2,1)S(1)} %get-tuple-element.138), channel_id=1, source_target_pairs={{0,1},{1,2},{2,3},{3,0},{4,5},{5,6},{6,7},{7,4},{8,9},{9,10},{10,1... | collective-permute-start | bytes 786440 | tf_op jit(solution)/shard_map/ppermute | solution.py:860
  129.0 16.0 %collective-permute-start.28 = (bf16[256,512]{1,0:T(8,128)(2,1)S(1)}, bf16[256,512]{1,0:T(8,128)(2,1)S(1)}, u32[]{:S(2)}, u32[]{:S(2)}) collective-permute-start(bf16[256,512]{1,0:T(8,128)(2,1)S(1)} %get-tuple-element.139), channel_id=1, source_target_pairs={{0,3},{1,0},{2,1},{3,2},{4,7},{5,4},{6,5},{7,6},{8,11},{9,8},{10,9... | collective-permute-start | bytes 786440 | tf_op jit(solution)/shard_map/ppermute | solution.py:860
  136.4 8.6 %collective-permute-start.27 = (bf16[256,512]{1,0:T(8,128)(2,1)S(1)}, bf16[256,512]{1,0:T(8,128)(2,1)S(1)}, u32[]{:S(2)}, u32[]{:S(2)}) collective-permute-start(bf16[256,512]{1,0:T(8,128)(2,1)S(1)} %get-tuple-element.140), channel_id=1, source_target_pairs={{0,2},{1,3},{2,0},{3,1},{4,6},{5,7},{6,4},{7,5},{8,10},{9,11},{10,... | collective-permute-start | bytes 786440 | tf_op jit(solution)/shard_map/ppermute | solution.py:860
  137.8 8.0 %collective-permute-start.32 = (bf16[64,1024]{1,0:T(8,128)(2,1)S(1)}, bf16[64,1024]{1,0:T(8,128)(2,1)S(1)}, u32[]{:S(2)}, u32[]{:S(2)}) collective-permute-start(bf16[64,1024]{1,0:T(8,128)(2,1)S(1)} %get-tuple-element.135), channel_id=1, source_target_pairs={{0,32},{32,64},{64,96},{96,0},{1,33},{33,65},{65,97},{97,1},{2,34}... | collective-permute-start | bytes 393224 | tf_op jit(solution)/shard_map/ppermute | solution.py:860
  139.8 7.4 %collective-permute-start.33 = (bf16[64,1024]{1,0:T(8,128)(2,1)S(1)}, bf16[64,1024]{1,0:T(8,128)(2,1)S(1)}, u32[]{:S(2)}, u32[]{:S(2)}) collective-permute-start(bf16[64,1024]{1,0:T(8,128)(2,1)S(1)} %get-tuple-element.136), channel_id=1, source_target_pairs={{0,64},{32,96},{64,0},{96,32},{1,65},{33,97},{65,1},{97,33},{2,66}... | collective-permute-start | bytes 393224 | tf_op jit(solution)/shard_map/ppermute | solution.py:860
  142.4 5.1 %collective-permute-start.34 = (bf16[64,1024]{1,0:T(8,128)(2,1)S(1)}, bf16[64,1024]{1,0:T(8,128)(2,1)S(1)}, u32[]{:S(2)}, u32[]{:S(2)}) collective-permute-start(bf16[64,1024]{1,0:T(8,128)(2,1)S(1)} %get-tuple-element.137), channel_id=1, source_target_pairs={{0,96},{32,0},{64,32},{96,64},{1,97},{33,1},{65,33},{97,65},{2,98}... | collective-permute-start | bytes 393224 | tf_op jit(solution)/shard_map/ppermute | solution.py:860
Sparse Core Ops, SparseCore 0:
  10.8 50.8 all-gather.1

commit v4 on v3

--- a/solution.py
+++ b/solution.py
@@ -283,7 +283,7 @@
             xz_ref[h] = mm_tn(x_ref[h], tail).astype(BF)
 
 
-def attend_pass(place, query, key, cums, cols, inverse, wu):
+def attend_pass(place, query, key, cums, cols, inverse, wu, after):
     heads = 2 * KEYS
     return call(
         attend_kernel,
@@ -311,6 +311,7 @@
         (query, key, cums, cols, inverse, wu),
         LONG,
         prefetch=place,
+        after=after,
     )
 
 
@@ -741,7 +742,7 @@
         ],
         (wide_spec(2 * DK), wide_spec(DK), whole(cums), whole(cums)),
         (key, cums, cols, state, got, own, error, y, update, xz, dk0, dcc, dcr),
-        2 * LONG,
+        SHORT,
         prefetch=place,
         after=after,
     )
@@ -795,7 +796,7 @@
         ],
         (pl.BlockSpec((1, TOK, depth), lambda k, place: (k, 0, 0)),),
         (normed, weight),
-        LONG,
+        SHORT,
         prefetch=place,
         after=after,
     )[0]
@@ -838,21 +839,21 @@
     for y in range(NY):
         for z in range(NZ):
             total = mine_ref[y, z].astype(F32) + other_ref[y, z].astype(F32)
-            out_refs[z][y] = total.astype(BF)
+            out_refs[y][z] = total.astype(BF)
 
 
 def blend_pass(place, mine, other, after):
-    outs = (shape(NY, *mine.shape[2:], dtype=BF),) * NZ
+    outs = (shape(NZ, *mine.shape[2:], dtype=BF),) * NY
     return single(blend_kernel, outs, (mine, other), place, after, LONG)
 
 
 def sum_kernel(place_ref, *refs):
-    for y in range(NY):
-        refs[NZ + y][...] = sum(refs[z][y].astype(F32) for z in range(NZ)).astype(BF)
+    for z in range(NZ):
+        refs[NY + z][...] = sum(refs[y][z].astype(F32) for y in range(NY)).astype(BF)
 
 
 def sum_pass(place, parts, after):
-    outs = (shape(*parts[0].shape[1:], dtype=BF),) * NY
+    outs = (shape(*parts[0].shape[1:], dtype=BF),) * NZ
     return single(sum_kernel, outs, parts, place, after)
 
 
@@ -884,7 +885,9 @@
     sent, kept, inverse, wu, cums, cols = pre_pass(place, key, value, beta, decay)
     got = swap(sent)
     parts = spread(pair_pass(place, kept, got), "z", NZ)
-    attend, carried, local, xz = attend_pass(place, query, key, cums, cols, inverse, wu)
+    attend, carried, local, xz = attend_pass(
+        place, query, key, cums, cols, inverse, wu, (parts[0],)
+    )
     row, nx, bx, gx, total = prefix_pass(place, parts, (xz,))
     totals = [shift(total, "y", NY, k) for k in range(1, NY)]
     ns, gs = suffix_pass(place, row)
@@ -905,7 +908,7 @@
         place, query, key, value, cums, cols, state, back, attend, inverse, wu
     )
     laters = spread(leave_pass(place, totals, grads, ns, gs, suffixes, (dk0,)), "z", NZ)
-    sums = spread(blend_pass(place, mine, theirs, (grad_total,)), "z", NZ)
+    sums = spread(blend_pass(place, mine, theirs, (laters[0],)), "y", NY)
     gown, gsend = part_pass(place, laters, kept, got, dkept, dgot, (sums[0],))
     ggot = swap(gsend)
 
@@ -915,7 +918,7 @@
     mixes = mix_pass(place, normed, weight, (grad_beta,))
     mixed = scatter_stage([mixes[k] for k in range(NH)], "head", NH).astype(BF)
     sums = sum_pass(place, sums, (grad_beta,))
-    grad_weight = scatter_stage(sums, "y", NY)
+    grad_weight = scatter_stage(sums, "z", NZ)
     return (
         mixed,
         grad_query,

time: 156 us -> 156 us (level)
    ppermute x30, waiting for transfers between devices: 20.8 us -> 19.1 us  [shift(): lax.ppermute(array, axis, [(i, (i + step) % count) for i in range(count)])]
    unnamed x56 -> x64, local copies, waits for them, and re-layouts: 8.88 us -> 9.53 us
  transfers between devices with their start and end apart: 36 -> 36, of which waited for: 17 -> 19; matrix products, arithmetic and copies ran while one was open for 1% -> 1% of each run, Pallas kernels for 27% -> 28%
where the time goes in v4:
time: 156 us; the launch traced here: 155 us
  Pallas kernels  53 us (34%)
  starting transfers between devices  49 us (31%)
  waiting for transfers between devices  23.1 us (15%)
  between operations  15.2 us (10%)
  local copies, waits for them, and re-layouts  9.58 us (6%)
  other arithmetic  4.75 us (3%)
    pallas_call x19, Pallas kernels, call(): pl.pallas_call(run, out_shape=out_shape, compiler_params=pltpu.CompilerPa...  53 us
    ppermute x30, starting transfers between devices, shift(): lax.ppermute(array, axis, [(i, (i + step) % count) for i in range(count)])  47.6 us
    ppermute x30, waiting for transfers between devices, shift(): lax.ppermute(array, axis, [(i, (i + step) % count) for i in range(count)])  19.1 us
    unnamed x64, local copies, waits for them, and re-layouts  9.53 us
  transfers between devices with their start and end apart: 36, of which 19 were waited for; matrix products, arithmetic and copies ran while one was open for 1% of the time, Pallas kernels for 28%

profile of v4, /device:TPU:0, one launch (start us, length us, event | category | flops | bytes accessed | tf_op | source)
XLA Modules:
  0.0 154.6 jit_solution(15328322751016074024)
XLA Ops:
  7.9 1.7 %add_convert_fusion = bf16[64,1024]{1,0:T(8,128)(2,1)} fusion(bf16[64,1024]{1,0:T(8,128)(2,1)} %param.15, bf16[64,1024]{1,0:T(8,128)(2,1)} %param.14, f32[]{:T(128)} %bitcast.8, f32[]{:T(128)S(6)} %sub.4), kind=kLoop, calls=%fused_computation.10 | loop fusion | flops 393216 | bytes 393224 | tf_op jit(solution)/shard_map/convert_element_type | solution.py:881
  9.6 2.9 %collective-permute-start.10 = (bf16[256,512]{1,0:T(8,128)(2,1)}, bf16[256,512]{1,0:T(8,128)(2,1)S(1)}, u32[]{:S(2)}, u32[]{:S(2)}) collective-permute-start(bf16[256,512]{1,0:T(8,128)(2,1)} %param.17), channel_id=1, source_target_pairs={{0,3},{1,0},{2,1},{3,2},{4,7},{5,4},{6,5},{7,6},{8,11},{9,8},{10,9... | collective-permute-start | bytes 786440 | tf_op jit(solution)/shard_map/ppermute | solution.py:861
  12.5 2.3 %collective-permute-start.11 = (bf16[256,512]{1,0:T(8,128)(2,1)}, bf16[256,512]{1,0:T(8,128)(2,1)S(1)}, u32[]{:S(2)}, u32[]{:S(2)}) collective-permute-start(bf16[256,512]{1,0:T(8,128)(2,1)} %param.17), channel_id=1, source_target_pairs={{0,2},{1,3},{2,0},{3,1},{4,6},{5,7},{6,4},{7,5},{8,10},{9,11},{10,... | collective-permute-start | bytes 786440 | tf_op jit(solution)/shard_map/ppermute | solution.py:861
  14.9 0.9 copy-done.2
  15.8 1.0 copy-done.7
  18.3 10.4 %pre_kernel.1 = (bf16[4,272,128]{2,1,0:T(8,128)(2,1)S(1)}, bf16[4,272,128]{2,1,0:T(8,128)(2,1)S(1)}, bf16[8,256,256]{2,1,0:T(8,128)(2,1)S(1)}, bf16[8,256,256]{2...) custom-call(s32[4]{0:T(128)S(1)} %pad_add_fusion.refs_0_, bf16[256,512]{1,0:T(8,128)(2,1)S(1)} %copy-done.2, ...), custom_call_target="tpu_custom_call" | custom-call | flops 1000000 | bytes 1 | tf_op jit(solution)/shard_map/pre_kernel/pallas_call | solution.py:70
  28.9 1.3 pad_maximum_fusion.refs_1_
  30.4 0.8 pair_kernel.1
  31.2 2.0 %collective-permute-start.1 = (bf16[272,128]{1,0:T(8,128)(2,1)S(1)}, bf16[272,128]{1,0:T(8,128)(2,1)S(1)}, u32[]{:S(2)}, u32[]{:S(2)}) collective-permute-start(bf16[272,128]{1,0:T(8,128)(2,1)S(1)} %get-tuple-element.76), channel_id=1, source_target_pairs={{0,8},{8,16},{16,24},{24,0},{1,9},{9,17},{17,25},{25,1},{2,10},{10... | collective-permute-start | bytes 208904 | tf_op jit(solution)/shard_map/ppermute | solution.py:861
  33.2 3.6 %collective-permute-start.2 = (bf16[272,128]{1,0:T(8,128)(2,1)S(1)}, bf16[272,128]{1,0:T(8,128)(2,1)S(1)}, u32[]{:S(2)}, u32[]{:S(2)}) collective-permute-start(bf16[272,128]{1,0:T(8,128)(2,1)S(1)} %get-tuple-element.77), channel_id=1, source_target_pairs={{0,16},{8,24},{16,0},{24,8},{1,17},{9,25},{17,1},{25,9},{2,18},{10... | collective-permute-start | bytes 208904 | tf_op jit(solution)/shard_map/ppermute | solution.py:861
  36.8 1.0 collective-permute-start.3
  37.8 2.6 %attend_kernel.1 = (bf16[8,256,256]{2,1,0:T(8,128)(2,1)S(1)}, bf16[8,256,128]{2,1,0:T(8,128)(2,1)S(1)}, f32[8,256,128]{2,1,0:T(8,128)S(1)}, bf16[8,256,128]{2,1,0:T(8,128)(2,1)S(1)}) custom-call(s32[4]{0:T(128)S(1)} %pad_add_fusion.refs_0_, bf16[256,512]{1,0:T(8,128)(2,1)S(1)} %copy-done.28, bf16[256,512]{1,0:T(8,128)(2,1)S(1)} %copy-done.3, ...), custom_call_target="tpu_custom_call" | custom-call | flops 5000000000 | bytes 1 | tf_op jit(solution)/shard_map/attend_kernel/pallas_call | solution.py:70
  40.4 1.0 copy-done.30
  41.4 1.1 prefix_kernel.1
  42.5 3.1 %collective-permute-start.6 = (bf16[272,128]{1,0:T(8,128)(2,1)S(1)}, bf16[272,128]{1,0:T(8,128)(2,1)S(1)}, u32[]{:S(2)}, u32[]{:S(2)}) collective-permute-start(bf16[272,128]{1,0:T(8,128)(2,1)S(1)} %get-tuple-element.84), channel_id=1, source_target_pairs={{0,96},{32,0},{64,32},{96,64},{1,97},{33,1},{65,33},{97,65},{2,98}... | collective-permute-start | bytes 208904 | tf_op jit(solution)/shard_map/ppermute | solution.py:861
  46.2 1.0 collective-permute-start.4
  47.2 0.9 suffix_kernel.1
  48.1 1.2 collective-permute-done.6.refs_3_
  49.3 3.4 %collective-permute-done.5.refs_2_ = bf16[272,128]{1,0:T(8,128)(2,1)S(1)} collective-permute-done((bf16[272,128]{1,0:T(8,128)(2,1)S(1)}, bf16[272,128]{1,0:T(8,128)(2,1)S(1)}, u32[]{:S(2)}, u32[]{:S(2)}) %collective-permute-start.5) | collective-permute-done | bytes 69664 | tf_op jit(solution)/shard_map/ppermute | solution.py:861
  52.7 1.2 collective-permute-done.4.refs_1_
  53.9 1.7 %enter_kernel.1 = (f32[128,128]{1,0:T(8,128)S(1)}, f32[128,128]{1,0:T(8,128)}, f32[128,128]{1,0:T(8,128)}, f32[128,128]{1,0:T(8,128)}) custom-call(s32[4]{0:T(128)S(1)} %pad_add_fusion.refs_0_, bf16[272,128]{1,0:T(8,128)(2,1)S(1)} %collective-permute-done.4.refs_1_, bf16[272,128]{1,0:T(8,128)(2,1)S(1)} %collective-permute-done.5.refs_2_, ...), custom_call_target="tpu_custom_call" | custom-call | flops 1000000 | bytes 1 | tf_op jit(solution)/shard_map/enter_kernel/pallas_call | solution.py:70
  57.0 1.1 collective-permute-start.7
  58.1 2.2 %collective-permute-start.8 = (f32[128,128]{1,0:T(8,128)}, f32[128,128]{1,0:T(8,128)}, u32[]{:S(2)}, u32[]{:S(2)}) collective-permute-start(f32[128,128]{1,0:T(8,128)} %get-tuple-element.92), channel_id=1, source_target_pairs={{0,16},{8,24},{16,0},{24,8},{1,17},{9,25},{17,1},{25,9},{2,18},{10... | collective-permute-start | bytes 196616 | tf_op jit(solution)/shard_map/ppermute | solution.py:861
  60.8 1.2 all-gather.2.cloned.1.call-done.refs_2_
  62.0 2.2 %copy-done = bf16[2048,1024]{1,0:T(8,128)(2,1)S(1)} copy-done((bf16[2048,1024]{1,0:T(8,128)(2,1)S(1)}, bf16[2048,1024]{1,0:T(8,128)(2,1)}, u32[]{:S(2)}) %copy-start) | copy-done | bytes 4194328
  64.2 0.9 copy-done.5
  65.1 2.8 %back_kernel.1.refs_7_.refs_5_ = f32[256,1024]{1,0:T(8,128)S(1)} custom-call(s32[4]{0:T(128)S(1)} %pad_add_fusion.refs_0_, bf16[4,256,512]{2,1,0:T(8,128)(2,1)S(1)} %pad_maximum_fusion.refs_1_, bf16[2048,1024]{1,0:T(8,128)(2,1)S(1)} %copy-done, bf16[4,128,128]{2,1,0:T(8,128)(2,1)S(1)} %copy-done.5), custom_call_target="tpu_custom_call" | custom-call | flops 5000000000 | bytes 1 | tf_op jit(solution)/shard_map/back_kernel/pallas_call | solution.py:70
  67.9 1.7 %split_kernel.1 = (f32[4,128,128]{2,1,0:T(8,128)S(1)}, f32[4,128,128]{2,1,0:T(8,128)S(1)}) custom-call(s32[4]{0:T(128)S(1)} %pad_add_fusion.refs_0_, f32[128,128]{1,0:T(8,128)S(1)} %copy-done.20, f32[128,128]{1,0:T(8,128)} %collective-permute-done.7.refs_2_, f32[128,128]{1,0:T(8,128)} %collective-permute-done.8.refs_3_, ...), custom_call_target="tpu_custom_call" | custom-call | flops 1000000 | bytes 1 | tf_op jit(solution)/shard_map/split_kernel/pallas_call | solution.py:70
  69.9 1.3 collective-permute-done.13.refs_1_
  71.2 5.4 %norm_kernel.1 = (bf16[256,1024]{1,0:T(8,128)(2,1)S(1)}, bf16[8,128,128]{2,1,0:T(8,128)(2,1)S(1)}, f32[8,256,128]{2,1,0:T(8,128)S(1)}, f32[4,128,128]{2,1,0:T(8,128)S(1)}, f32[4,128,128]{2,1,0:T(8,128)S(1)}) custom-call(s32[4]{0:T(128)S(1)} %pad_add_fusion.refs_0_, f32[4,128,128]{2,1,0:T(8,128)S(1)} %collective-permute-done.13.refs_1_, ...), custom_call_target="tpu_custom_call" | custom-call | flops 1000000 | bytes 1 | tf_op jit(solution)/shard_map/norm_kernel/pallas_call | solution.py:70
  77.1 1.3 collective-permute-done.14.refs_4_.refs_3_.refs_8_
  78.4 2.6 %outer_kernel.1 = (bf16[4,4,64,1024]{3,2,1,0:T(8,128)(2,1)S(1)}, bf16[4,4,64,1024]{3,2,1,0:T(8,128)(2,1)S(1)}) custom-call(s32[4]{0:T(128)S(1)} %pad_add_fusion.refs_0_, bf16[4,256,512]{2,1,0:T(8,128)(2,1)S(1)} %pad_maximum_fusion.refs_1_, bf16[256,1024]{1,0:T(8,128)(2,1)S(1)} %get-tuple-element.98.refs_2_.refs_1_, ...), custom_call_target="tpu_custom_call" | custom-call | flops 5000000000 | bytes 1 | tf_op jit(solution)/shard_map/outer_kernel/pallas_call | solution.py:70
  81.4 0.8 join_kernel.1
  82.2 0.9 collective-permute-start.15
  83.0 2.4 %collective-permute-start.16 = (f32[128,128]{1,0:T(8,128)S(1)}, f32[128,128]{1,0:T(8,128)S(1)}, u32[]{:S(2)}, u32[]{:S(2)}) collective-permute-start(f32[128,128]{1,0:T(8,128)S(1)} %get-tuple-element.104), channel_id=1, source_target_pairs={{0,16},{8,24},{16,0},{24,8},{1,17},{9,25},{17,1},{25,9},{2,18},{10... | collective-permute-start | bytes 196616 | tf_op jit(solution)/shard_map/ppermute | solution.py:861
  85.5 1.1 collective-permute-start.17
  86.6 1.8 %collective-permute-done.15.refs_2_ = f32[128,128]{1,0:T(8,128)S(1)} collective-permute-done((f32[128,128]{1,0:T(8,128)S(1)}, f32[128,128]{1,0:T(8,128)S(1)}, u32[]{:S(2)}, u32[]{:S(2)}) %collective-permute-start.15) | collective-permute-done | bytes 65568 | tf_op jit(solution)/shard_map/ppermute | solution.py:861
  88.3 0.8 collective-permute-done.16.refs_3_
  89.9 1.3 later_kernel.1
  91.6 2.6 %collective-permute-start.19 = (f32[128,128]{1,0:T(8,128)S(1)}, f32[128,128]{1,0:T(8,128)S(1)}, u32[]{:S(2)}, u32[]{:S(2)}) collective-permute-start(f32[128,128]{1,0:T(8,128)S(1)} %get-tuple-element.106), channel_id=1, source_target_pairs={{0,64},{32,96},{64,0},{96,32},{1,65},{33,97},{65,1},{97,33},{2,66}... | collective-permute-start | bytes 196616 | tf_op jit(solution)/shard_map/ppermute | solution.py:861
  94.2 2.1 %collective-permute-start.18 = (f32[128,128]{1,0:T(8,128)S(1)}, f32[128,128]{1,0:T(8,128)S(1)}, u32[]{:S(2)}, u32[]{:S(2)}) collective-permute-start(f32[128,128]{1,0:T(8,128)S(1)} %get-tuple-element.106), channel_id=1, source_target_pairs={{0,96},{32,0},{64,32},{96,64},{1,97},{33,1},{65,33},{97,65},{2,98}... | collective-permute-start | bytes 196616 | tf_op jit(solution)/shard_map/ppermute | solution.py:861
  96.4 4.7 %middle_kernel.1 = (f32[256,512]{1,0:T(8,128)}, bf16[8,256,128]{2,1,0:T(8,128)(2,1)S(1)}, f32[256,512]{1,0:T(8,128)S(1)}, f32[8,256,128]{2,1,0:T(8,128)S(1)}, bf...) custom-call(s32[4]{0:T(128)S(1)} %pad_add_fusion.refs_0_, ...), custom_call_target="tpu_custom_call" | custom-call | flops 10000000000 | bytes 1 | tf_op jit(solution)/shard_map/middle_kernel/pallas_call | solution.py:70
  101.1 1.1 leave_kernel.1
  103.0 3.1 %collective-permute-start.22 = (f32[128,128]{1,0:T(8,128)S(1)}, f32[128,128]{1,0:T(8,128)S(1)}, u32[]{:S(2)}, u32[]{:S(2)}) collective-permute-start(f32[128,128]{1,0:T(8,128)S(1)} %get-tuple-element.114), channel_id=1, source_target_pairs={{0,16},{8,24},{16,0},{24,8},{1,17},{9,25},{17,1},{25,9},{2,18},{10... | collective-permute-start | bytes 196616 | tf_op jit(solution)/shard_map/ppermute | solution.py:861
  106.6 1.0 blend_kernel.1
  107.8 1.2 collective-permute-done.22.refs_3_
  109.0 1.3 collective-permute-done.23.refs_4_
  110.3 0.8 part_kernel.1
  111.2 1.3 collective-permute-start.30
  112.5 1.6 %collective-permute-start.31 = (bf16[4,64,1024]{2,1,0:T(8,128)(2,1)S(1)}, bf16[4,64,1024]{2,1,0:T(8,128)(2,1)S(1)}, u32[]{:S(2)}, u32[]{:S(2)}) collective-permute-start(bf16[4,64,1024]{2,1,0:T(8,128)(2,1)S(1)} %get-tuple-element.133), channel_id=1, source_target_pairs={{0,96},{32,0},{64,32},{96,64},{1,97},{33,1},{65,33},{97,65},{2,98}... | collective-permute-start | bytes 1572872 | tf_op jit(solution)/shard_map/ppermute | solution.py:861
  114.1 10.1 %last_kernel.1 = (f32[256,1024]{1,0:T(8,128)}, f32[256,512]{1,0:T(8,128)}, f32[8,256]{1,0:T(8,128)}, f32[8,256]{1,0:T(8,128)}) custom-call(s32[4]{0:T(128)S(1)} %pad_add_fusion.refs_0_, bf16[256,512]{1,0:T(8,128)(2,1)S(1)} %copy-done.3, f32[8,256]{1,0:T(8,128)S(1)} %get-tuple-element.79.refs_3_.refs_4_.refs_2_, f32[4,256,128]{2,1,0:T(8,128)S(1)} %copy-done.12, ...), custom_call_target="tpu_custom_call" | custom-call | flops 1000000 | bytes 1 | tf_op jit(solution)/shard_map/last_kernel/pallas_call | solution.py:70
  124.9 2.5 %mix_kernel.1 = bf16[4,256,512]{2,1,0:T(8,128)(2,1)S(1)} custom-call(s32[4]{0:T(128)S(1)} %pad_add_fusion.refs_0_, bf16[256,1024]{1,0:T(8,128)(2,1)S(1)} %get-tuple-element.98.refs_2_.refs_1_, bf16[2048,1024]{1,0:T(8,128)(2,1)S(1)} %copy-done.1, f32[8,256]{1,0:T(8,128)S(1)} %copy-done.21), custom_call_target="tpu_custom_call" | custom-call | flops 1000000 | bytes 1 | tf_op jit(solution)/shard_map/mix_kernel/pallas_call | solution.py:70
  127.4 1.6 %collective-permute-start.26 = (bf16[256,512]{1,0:T(8,128)(2,1)S(1)}, bf16[256,512]{1,0:T(8,128)(2,1)S(1)}, u32[]{:S(2)}, u32[]{:S(2)}) collective-permute-start(bf16[256,512]{1,0:T(8,128)(2,1)S(1)} %get-tuple-element.138), channel_id=1, source_target_pairs={{0,1},{1,2},{2,3},{3,0},{4,5},{5,6},{6,7},{7,4},{8,9},{9,10},{10,1... | collective-permute-start | bytes 786440 | tf_op jit(solution)/shard_map/ppermute | solution.py:861
  129.1 1.7 %collective-permute-start.28 = (bf16[256,512]{1,0:T(8,128)(2,1)S(1)}, bf16[256,512]{1,0:T(8,128)(2,1)S(1)}, u32[]{:S(2)}, u32[]{:S(2)}) collective-permute-start(bf16[256,512]{1,0:T(8,128)(2,1)S(1)} %get-tuple-element.139), channel_id=1, source_target_pairs={{0,3},{1,0},{2,1},{3,2},{4,7},{5,4},{6,5},{7,6},{8,11},{9,8},{10,9... | collective-permute-start | bytes 786440 | tf_op jit(solution)/shard_map/ppermute | solution.py:861
  131.1 2.6 %collective-permute-start.27 = (bf16[256,512]{1,0:T(8,128)(2,1)S(1)}, bf16[256,512]{1,0:T(8,128)(2,1)S(1)}, u32[]{:S(2)}, u32[]{:S(2)}) collective-permute-start(bf16[256,512]{1,0:T(8,128)(2,1)S(1)} %get-tuple-element.140), channel_id=1, source_target_pairs={{0,2},{1,3},{2,0},{3,1},{4,6},{5,7},{6,4},{7,5},{8,10},{9,11},{10,... | collective-permute-start | bytes 786440 | tf_op jit(solution)/shard_map/ppermute | solution.py:861
  133.7 2.6 %collective-permute-done.31.refs_4_ = bf16[4,64,1024]{2,1,0:T(8,128)(2,1)S(1)} collective-permute-done((bf16[4,64,1024]{2,1,0:T(8,128)(2,1)S(1)}, bf16[4,64,1024]{2,1,0:T(8,128)(2,1)S(1)}, u32[]{:S(2)}, u32[]{:S(2)}) %collective-permute-start.31) | collective-permute-done | bytes 524320 | tf_op jit(solution)/shard_map/ppermute | solution.py:861
  136.3 0.8 sum_kernel.1
  137.1 1.5 collective-permute-start.32
  138.6 1.8 %collective-permute-start.33 = (bf16[64,1024]{1,0:T(8,128)(2,1)S(1)}, bf16[64,1024]{1,0:T(8,128)(2,1)S(1)}, u32[]{:S(2)}, u32[]{:S(2)}) collective-permute-start(bf16[64,1024]{1,0:T(8,128)(2,1)S(1)} %get-tuple-element.136), channel_id=1, source_target_pairs={{0,16},{8,24},{16,0},{24,8},{1,17},{9,25},{17,1},{25,9},{2,18},{10... | collective-permute-start | bytes 393224 | tf_op jit(solution)/shard_map/ppermute | solution.py:861
  140.4 1.3 collective-permute-start.34
  141.7 1.8 %collective-permute-done.27 = bf16[256,512]{1,0:T(8,128)(2,1)S(1)} collective-permute-done((bf16[256,512]{1,0:T(8,128)(2,1)S(1)}, bf16[256,512]{1,0:T(8,128)(2,1)S(1)}, u32[]{:S(2)}, u32[]{:S(2)}) %collective-permute-start.27) | collective-permute-done | bytes 262176 | tf_op jit(solution)/shard_map/ppermute | solution.py:861
  143.5 0.8 fusion.2
  144.8 1.5 collective-permute-done.33
  146.8 0.9 broadcast_multiply_fusion
  (98 shorter events, 10.4 us)
Async XLA Ops:
  7.2 30.6 %copy-start.3 = (bf16[256,512]{1,0:T(8,128)(2,1)S(1)}, bf16[256,512]{1,0:T(8,128)(2,1)}, u32[]{:S(2)}) copy-start(bf16[256,512]{1,0:T(8,128)(2,1)} %refs_1_.7) | copy-start | bytes 786436
  7.2 54.8 %all-gather.2.cloned.1.call-start = ((), (), s32[]{:S(2)}) async-start(), calls=%async_computation | async-start | bytes 4325376 | tf_op jit(solution)/shard_map/all_gather | solution.py:882
  9.6 19.2 %collective-permute-start.10 = (bf16[256,512]{1,0:T(8,128)(2,1)}, bf16[256,512]{1,0:T(8,128)(2,1)S(1)}, u32[]{:S(2)}, u32[]{:S(2)}) collective-permute-start(bf16[256,512]{1,0:T(8,128)(2,1)} %param.17), channel_id=1, source_target_pairs={{0,3},{1,0},{2,1},{3,2},{4,7},{5,4},{6,5},{7,6},{8,11},{9,8},{10,9... | collective-permute-start | bytes 786440 | tf_op jit(solution)/shard_map/ppermute | solution.py:861
  12.5 16.3 %collective-permute-start.12 = (bf16[256,512]{1,0:T(8,128)(2,1)}, bf16[256,512]{1,0:T(8,128)(2,1)S(1)}, u32[]{:S(2)}, u32[]{:S(2)}) collective-permute-start(bf16[256,512]{1,0:T(8,128)(2,1)} %param.17), channel_id=1, source_target_pairs={{0,1},{1,2},{2,3},{3,0},{4,5},{5,6},{6,7},{7,4},{8,9},{9,10},{10,1... | collective-permute-start | bytes 786440 | tf_op jit(solution)/shard_map/ppermute | solution.py:861
  12.5 16.3 %collective-permute-start.11 = (bf16[256,512]{1,0:T(8,128)(2,1)}, bf16[256,512]{1,0:T(8,128)(2,1)S(1)}, u32[]{:S(2)}, u32[]{:S(2)}) collective-permute-start(bf16[256,512]{1,0:T(8,128)(2,1)} %param.17), channel_id=1, source_target_pairs={{0,2},{1,3},{2,0},{3,1},{4,6},{5,7},{6,4},{7,5},{8,10},{9,11},{10,... | collective-permute-start | bytes 786440 | tf_op jit(solution)/shard_map/ppermute | solution.py:861
  14.9 1.0 copy-start.2
  15.8 1.0 copy-start.7
  18.3 19.5 %copy-start.28 = (bf16[256,512]{1,0:T(8,128)(2,1)S(1)}, bf16[256,512]{1,0:T(8,128)(2,1)}, u32[]{:S(2)}) copy-start(bf16[256,512]{1,0:T(8,128)(2,1)} %refs_1_.6) | copy-start | bytes 786436
  28.7 11.6 %copy-start.11 = (f32[4,256,128]{2,1,0:T(8,128)}, f32[4,256,128]{2,1,0:T(8,128)S(1)}, u32[]{:S(2)}) copy-start(f32[4,256,128]{2,1,0:T(8,128)S(1)} %get-tuple-element.80.refs_4_.refs_5_.refs_3_) | copy-start | bytes 1572868
  28.7 11.6 %copy-start.24 = (bf16[8,256,256]{2,1,0:T(8,128)(2,1)}, bf16[8,256,256]{2,1,0:T(8,128)(2,1)S(1)}, u32[]{:S(2)}) copy-start(bf16[8,256,256]{2,1,0:T(8,128)(2,1)S(1)} %get-tuple-element.81.refs_5_.refs_9_) | copy-start | bytes 3145732
  28.7 11.6 %copy-start.26 = (bf16[8,256,256]{2,1,0:T(8,128)(2,1)}, bf16[8,256,256]{2,1,0:T(8,128)(2,1)S(1)}, u32[]{:S(2)}) copy-start(bf16[8,256,256]{2,1,0:T(8,128)(2,1)S(1)} %get-tuple-element.82.refs_6_.refs_10_) | copy-start | bytes 3145732
  28.7 1.6 %collective-permute-start = (bf16[4,272,128]{2,1,0:T(8,128)(2,1)S(1)}, bf16[4,272,128]{2,1,0:T(8,128)(2,1)S(1)}, u32[]{:S(2)}, u32[]{:S(2)}) collective-permute-start(bf16[4,272,128]{2,1,0:T(8,128)(2,1)S(1)} %get-tuple-element.74), channel_id=1, source_target_pairs={{0,4},{4,0},{1,5},{5,1},{2,6},{6,2},{3,7},{7,3},{8,12},{12,8},{9,1... | collective-permute-start | bytes 835592 | tf_op jit(solution)/shard_map/ppermute | solution.py:873
  31.2 10.1 %collective-permute-start.1 = (bf16[272,128]{1,0:T(8,128)(2,1)S(1)}, bf16[272,128]{1,0:T(8,128)(2,1)S(1)}, u32[]{:S(2)}, u32[]{:S(2)}) collective-permute-start(bf16[272,128]{1,0:T(8,128)(2,1)S(1)} %get-tuple-element.76), channel_id=1, source_target_pairs={{0,8},{8,16},{16,24},{24,0},{1,9},{9,17},{17,25},{25,1},{2,10},{10... | collective-permute-start | bytes 208904 | tf_op jit(solution)/shard_map/ppermute | solution.py:861
  33.2 8.2 %collective-permute-start.2 = (bf16[272,128]{1,0:T(8,128)(2,1)S(1)}, bf16[272,128]{1,0:T(8,128)(2,1)S(1)}, u32[]{:S(2)}, u32[]{:S(2)}) collective-permute-start(bf16[272,128]{1,0:T(8,128)(2,1)S(1)} %get-tuple-element.77), channel_id=1, source_target_pairs={{0,16},{8,24},{16,0},{24,8},{1,17},{9,25},{17,1},{25,9},{2,18},{10... | collective-permute-start | bytes 208904 | tf_op jit(solution)/shard_map/ppermute | solution.py:861
  36.8 4.6 %collective-permute-start.3 = (bf16[272,128]{1,0:T(8,128)(2,1)S(1)}, bf16[272,128]{1,0:T(8,128)(2,1)S(1)}, u32[]{:S(2)}, u32[]{:S(2)}) collective-permute-start(bf16[272,128]{1,0:T(8,128)(2,1)S(1)} %get-tuple-element.78), channel_id=1, source_target_pairs={{0,24},{8,0},{16,8},{24,16},{1,25},{9,1},{17,9},{25,17},{2,26},{10... | collective-permute-start | bytes 208904 | tf_op jit(solution)/shard_map/ppermute | solution.py:861
  40.4 1.0 copy-start.30
  41.3 6.8 %copy-start.9 = (bf16[8,256,128]{2,1,0:T(8,128)(2,1)}, bf16[8,256,128]{2,1,0:T(8,128)(2,1)S(1)}, u32[]{:S(2)}) copy-start(bf16[8,256,128]{2,1,0:T(8,128)(2,1)S(1)} %get-tuple-element.96.refs_3_) | copy-start | bytes 1572868
  42.5 5.7 %copy-start.17 = (bf16[4,272,128]{2,1,0:T(8,128)(2,1)}, bf16[4,272,128]{2,1,0:T(8,128)(2,1)S(1)}, u32[]{:S(2)}) copy-start(bf16[4,272,128]{2,1,0:T(8,128)(2,1)S(1)} %get-tuple-element.88.refs_1_.refs_5_) | copy-start | bytes 835588
  42.5 6.8 %collective-permute-start.6 = (bf16[272,128]{1,0:T(8,128)(2,1)S(1)}, bf16[272,128]{1,0:T(8,128)(2,1)S(1)}, u32[]{:S(2)}, u32[]{:S(2)}) collective-permute-start(bf16[272,128]{1,0:T(8,128)(2,1)S(1)} %get-tuple-element.84), channel_id=1, source_target_pairs={{0,96},{32,0},{64,32},{96,64},{1,97},{33,1},{65,33},{97,65},{2,98}... | collective-permute-start | bytes 208904 | tf_op jit(solution)/shard_map/ppermute | solution.py:861
  45.6 7.2 %collective-permute-start.5 = (bf16[272,128]{1,0:T(8,128)(2,1)S(1)}, bf16[272,128]{1,0:T(8,128)(2,1)S(1)}, u32[]{:S(2)}, u32[]{:S(2)}) collective-permute-start(bf16[272,128]{1,0:T(8,128)(2,1)S(1)} %get-tuple-element.84), channel_id=1, source_target_pairs={{0,64},{32,96},{64,0},{96,32},{1,65},{33,97},{65,1},{97,33},{2,66}... | collective-permute-start | bytes 208904 | tf_op jit(solution)/shard_map/ppermute | solution.py:861
  46.2 7.7 %collective-permute-start.4 = (bf16[272,128]{1,0:T(8,128)(2,1)S(1)}, bf16[272,128]{1,0:T(8,128)(2,1)S(1)}, u32[]{:S(2)}, u32[]{:S(2)}) collective-permute-start(bf16[272,128]{1,0:T(8,128)(2,1)S(1)} %get-tuple-element.84), channel_id=1, source_target_pairs={{0,32},{32,64},{64,96},{96,0},{1,33},{33,65},{65,97},{97,1},{2,34}... | collective-permute-start | bytes 208904 | tf_op jit(solution)/shard_map/ppermute | solution.py:861
  52.7 3.0 %copy-start.13 = (bf16[272,128]{1,0:T(8,128)(2,1)}, bf16[272,128]{1,0:T(8,128)(2,1)S(1)}, u32[]{:S(2)}) copy-start(bf16[272,128]{1,0:T(8,128)(2,1)S(1)} %collective-permute-done.5.refs_2_) | copy-start | bytes 208900
  53.9 3.0 %copy-start.15 = (bf16[272,128]{1,0:T(8,128)(2,1)}, bf16[272,128]{1,0:T(8,128)(2,1)S(1)}, u32[]{:S(2)}) copy-start(bf16[272,128]{1,0:T(8,128)(2,1)S(1)} %collective-permute-done.4.refs_1_) | copy-start | bytes 208900
  57.0 10.9 %collective-permute-start.7 = (f32[128,128]{1,0:T(8,128)}, f32[128,128]{1,0:T(8,128)}, u32[]{:S(2)}, u32[]{:S(2)}) collective-permute-start(f32[128,128]{1,0:T(8,128)} %get-tuple-element.91), channel_id=1, source_target_pairs={{0,8},{8,16},{16,24},{24,0},{1,9},{9,17},{17,25},{25,1},{2,10},{10... | collective-permute-start | bytes 196616 | tf_op jit(solution)/shard_map/ppermute | solution.py:861
  58.1 9.8 %collective-permute-start.8 = (f32[128,128]{1,0:T(8,128)}, f32[128,128]{1,0:T(8,128)}, u32[]{:S(2)}, u32[]{:S(2)}) collective-permute-start(f32[128,128]{1,0:T(8,128)} %get-tuple-element.92), channel_id=1, source_target_pairs={{0,16},{8,24},{16,0},{24,8},{1,17},{9,25},{17,1},{25,9},{2,18},{10... | collective-permute-start | bytes 196616 | tf_op jit(solution)/shard_map/ppermute | solution.py:861
  60.2 7.7 %collective-permute-start.9 = (f32[128,128]{1,0:T(8,128)}, f32[128,128]{1,0:T(8,128)}, u32[]{:S(2)}, u32[]{:S(2)}) collective-permute-start(f32[128,128]{1,0:T(8,128)} %get-tuple-element.93), channel_id=1, source_target_pairs={{0,24},{8,0},{16,8},{24,16},{1,25},{9,1},{17,9},{25,17},{2,26},{10... | collective-permute-start | bytes 196616 | tf_op jit(solution)/shard_map/ppermute | solution.py:861
  62.0 2.2 %copy-start = (bf16[2048,1024]{1,0:T(8,128)(2,1)S(1)}, bf16[2048,1024]{1,0:T(8,128)(2,1)}, u32[]{:S(2)}) copy-start(bf16[2048,1024]{1,0:T(8,128)(2,1)} %all-gather.2.cloned.1.call-done.refs_2_) | copy-start | bytes 12582916
  64.2 0.9 copy-start.5
  65.1 2.8 %copy-start.20 = (f32[128,128]{1,0:T(8,128)S(1)}, f32[128,128]{1,0:T(8,128)}, u32[]{:S(2)}) copy-start(f32[128,128]{1,0:T(8,128)} %copy-done.19) | copy-start | bytes 196612
  67.9 3.3 %copy-start.10 = (bf16[8,256,128]{2,1,0:T(8,128)(2,1)S(1)}, bf16[8,256,128]{2,1,0:T(8,128)(2,1)}, u32[]{:S(2)}) copy-start(bf16[8,256,128]{2,1,0:T(8,128)(2,1)} %copy-done.9) | copy-start | bytes 1572868
  69.6 1.6 %collective-permute-start.13 = (f32[4,128,128]{2,1,0:T(8,128)S(1)}, f32[4,128,128]{2,1,0:T(8,128)S(1)}, u32[]{:S(2)}, u32[]{:S(2)}) collective-permute-start(f32[4,128,128]{2,1,0:T(8,128)S(1)} %get-tuple-element.94), channel_id=1, source_target_pairs={{0,4},{4,0},{1,5},{5,1},{2,6},{6,2},{3,7},{7,3},{8,12},{12,8},{9,1... | collective-permute-start | bytes 786440 | tf_op jit(solution)/shard_map/ppermute | solution.py:873
  76.6 1.8 %collective-permute-start.14 = (f32[4,128,128]{2,1,0:T(8,128)S(1)}, f32[4,128,128]{2,1,0:T(8,128)S(1)}, u32[]{:S(2)}, u32[]{:S(2)}) collective-permute-start(f32[4,128,128]{2,1,0:T(8,128)S(1)} %get-tuple-element.101), channel_id=1, source_target_pairs={{0,4},{4,0},{1,5},{5,1},{2,6},{6,2},{3,7},{7,3},{8,12},{12,8},{9,1... | collective-permute-start | bytes 786440 | tf_op jit(solution)/shard_map/ppermute | solution.py:873
  78.4 11.5 %copy-start.18 = (bf16[4,272,128]{2,1,0:T(8,128)(2,1)S(1)}, bf16[4,272,128]{2,1,0:T(8,128)(2,1)}, u32[]{:S(2)}) copy-start(bf16[4,272,128]{2,1,0:T(8,128)(2,1)} %copy-done.17) | copy-start | bytes 835588
  78.4 17.9 %copy-start.8 = (bf16[256,1024]{1,0:T(8,128)(2,1)S(1)}, bf16[256,1024]{1,0:T(8,128)(2,1)}, u32[]{:S(2)}) copy-start(bf16[256,1024]{1,0:T(8,128)(2,1)} %refs_3_.3) | copy-start | bytes 1572868
  78.4 17.9 %copy-start.12 = (f32[4,256,128]{2,1,0:T(8,128)S(1)}, f32[4,256,128]{2,1,0:T(8,128)}, u32[]{:S(2)}) copy-start(f32[4,256,128]{2,1,0:T(8,128)} %copy-done.11) | copy-start | bytes 1572868
  78.4 17.9 %copy-start.25 = (bf16[8,256,256]{2,1,0:T(8,128)(2,1)S(1)}, bf16[8,256,256]{2,1,0:T(8,128)(2,1)}, u32[]{:S(2)}) copy-start(bf16[8,256,256]{2,1,0:T(8,128)(2,1)} %copy-done.24) | copy-start | bytes 3145732
  78.4 17.9 %copy-start.27 = (bf16[8,256,256]{2,1,0:T(8,128)(2,1)S(1)}, bf16[8,256,256]{2,1,0:T(8,128)(2,1)}, u32[]{:S(2)}) copy-start(bf16[8,256,256]{2,1,0:T(8,128)(2,1)} %copy-done.26) | copy-start | bytes 3145732
  78.4 17.9 %copy-start.29 = (bf16[256,512]{1,0:T(8,128)(2,1)S(1)}, bf16[256,512]{1,0:T(8,128)(2,1)}, u32[]{:S(2)}) copy-start(bf16[256,512]{1,0:T(8,128)(2,1)} %refs_1_.6) | copy-start | bytes 786436
  78.4 17.9 %copy-start.31 = (bf16[8,256,256]{2,1,0:T(8,128)(2,1)S(1)}, bf16[8,256,256]{2,1,0:T(8,128)(2,1)}, u32[]{:S(2)}) copy-start(bf16[8,256,256]{2,1,0:T(8,128)(2,1)} %copy-done.30) | copy-start | bytes 3145732
  81.0 25.5 %collective-permute-start.24 = (bf16[4,4,64,1024]{3,2,1,0:T(8,128)(2,1)S(1)}, bf16[4,4,64,1024]{3,2,1,0:T(8,128)(2,1)S(1)}, u32[]{:S(2)}, u32[]{:S(2)}) collective-permute-start(bf16[4,4,64,1024]{3,2,1,0:T(8,128)(2,1)S(1)} %get-tuple-element.117), channel_id=1, source_target_pairs={{0,4},{4,0},{1,5},{5,1},{2,6},{6,2},{3,7},{7,3},{8,12},{12,8},{9,1... | collective-permute-start | bytes 6291464 | tf_op jit(solution)/shard_map/ppermute | solution.py:873
  82.2 6.2 %collective-permute-start.15 = (f32[128,128]{1,0:T(8,128)S(1)}, f32[128,128]{1,0:T(8,128)S(1)}, u32[]{:S(2)}, u32[]{:S(2)}) collective-permute-start(f32[128,128]{1,0:T(8,128)S(1)} %get-tuple-element.103), channel_id=1, source_target_pairs={{0,8},{8,16},{16,24},{24,0},{1,9},{9,17},{17,25},{25,1},{2,10},{10... | collective-permute-start | bytes 196616 | tf_op jit(solution)/shard_map/ppermute | solution.py:861
  83.0 6.1 %collective-permute-start.16 = (f32[128,128]{1,0:T(8,128)S(1)}, f32[128,128]{1,0:T(8,128)S(1)}, u32[]{:S(2)}, u32[]{:S(2)}) collective-permute-start(f32[128,128]{1,0:T(8,128)S(1)} %get-tuple-element.104), channel_id=1, source_target_pairs={{0,16},{8,24},{16,0},{24,8},{1,17},{9,25},{17,1},{25,9},{2,18},{10... | collective-permute-start | bytes 196616 | tf_op jit(solution)/shard_map/ppermute | solution.py:861
  85.5 4.4 %collective-permute-start.17 = (f32[128,128]{1,0:T(8,128)S(1)}, f32[128,128]{1,0:T(8,128)S(1)}, u32[]{:S(2)}, u32[]{:S(2)}) collective-permute-start(f32[128,128]{1,0:T(8,128)S(1)} %get-tuple-element.105), channel_id=1, source_target_pairs={{0,24},{8,0},{16,8},{24,16},{1,25},{9,1},{17,9},{25,17},{2,26},{10... | collective-permute-start | bytes 196616 | tf_op jit(solution)/shard_map/ppermute | solution.py:861
  91.1 9.9 %collective-permute-start.20 = (f32[128,128]{1,0:T(8,128)S(1)}, f32[128,128]{1,0:T(8,128)S(1)}, u32[]{:S(2)}, u32[]{:S(2)}) collective-permute-start(f32[128,128]{1,0:T(8,128)S(1)} %get-tuple-element.106), channel_id=1, source_target_pairs={{0,32},{32,64},{64,96},{96,0},{1,33},{33,65},{65,97},{97,1},{2,34}... | collective-permute-start | bytes 196616 | tf_op jit(solution)/shard_map/ppermute | solution.py:861
  91.6 9.5 %collective-permute-start.19 = (f32[128,128]{1,0:T(8,128)S(1)}, f32[128,128]{1,0:T(8,128)S(1)}, u32[]{:S(2)}, u32[]{:S(2)}) collective-permute-start(f32[128,128]{1,0:T(8,128)S(1)} %get-tuple-element.106), channel_id=1, source_target_pairs={{0,64},{32,96},{64,0},{96,32},{1,65},{33,97},{65,1},{97,33},{2,66}... | collective-permute-start | bytes 196616 | tf_op jit(solution)/shard_map/ppermute | solution.py:861
  94.2 6.9 %collective-permute-start.18 = (f32[128,128]{1,0:T(8,128)S(1)}, f32[128,128]{1,0:T(8,128)S(1)}, u32[]{:S(2)}, u32[]{:S(2)}) collective-permute-start(f32[128,128]{1,0:T(8,128)S(1)} %get-tuple-element.106), channel_id=1, source_target_pairs={{0,96},{32,0},{64,32},{96,64},{1,97},{33,1},{65,33},{97,65},{2,98}... | collective-permute-start | bytes 196616 | tf_op jit(solution)/shard_map/ppermute | solution.py:861
  96.3 4.8 %copy-start.6 = (bf16[4,128,128]{2,1,0:T(8,128)(2,1)S(1)}, bf16[4,128,128]{2,1,0:T(8,128)(2,1)}, u32[]{:S(2)}) copy-start(bf16[4,128,128]{2,1,0:T(8,128)(2,1)} %copy-done.4) | copy-start | bytes 393220
  96.4 4.8 %copy-start.14 = (bf16[272,128]{1,0:T(8,128)(2,1)S(1)}, bf16[272,128]{1,0:T(8,128)(2,1)}, u32[]{:S(2)}) copy-start(bf16[272,128]{1,0:T(8,128)(2,1)} %copy-done.13) | copy-start | bytes 208900
  96.4 4.8 %copy-start.16 = (bf16[272,128]{1,0:T(8,128)(2,1)S(1)}, bf16[272,128]{1,0:T(8,128)(2,1)}, u32[]{:S(2)}) copy-start(bf16[272,128]{1,0:T(8,128)(2,1)} %copy-done.15) | copy-start | bytes 208900
  102.3 5.5 %collective-permute-start.21 = (f32[128,128]{1,0:T(8,128)S(1)}, f32[128,128]{1,0:T(8,128)S(1)}, u32[]{:S(2)}, u32[]{:S(2)}) collective-permute-start(f32[128,128]{1,0:T(8,128)S(1)} %get-tuple-element.113), channel_id=1, source_target_pairs={{0,8},{8,16},{16,24},{24,0},{1,9},{9,17},{17,25},{25,1},{2,10},{10... | collective-permute-start | bytes 196616 | tf_op jit(solution)/shard_map/ppermute | solution.py:861
  103.0 6.1 %collective-permute-start.22 = (f32[128,128]{1,0:T(8,128)S(1)}, f32[128,128]{1,0:T(8,128)S(1)}, u32[]{:S(2)}, u32[]{:S(2)}) collective-permute-start(f32[128,128]{1,0:T(8,128)S(1)} %get-tuple-element.114), channel_id=1, source_target_pairs={{0,16},{8,24},{16,0},{24,8},{1,17},{9,25},{17,1},{25,9},{2,18},{10... | collective-permute-start | bytes 196616 | tf_op jit(solution)/shard_map/ppermute | solution.py:861
  106.1 4.3 %collective-permute-start.23 = (f32[128,128]{1,0:T(8,128)S(1)}, f32[128,128]{1,0:T(8,128)S(1)}, u32[]{:S(2)}, u32[]{:S(2)}) collective-permute-start(f32[128,128]{1,0:T(8,128)S(1)} %get-tuple-element.115), channel_id=1, source_target_pairs={{0,24},{8,0},{16,8},{24,16},{1,25},{9,1},{17,9},{25,17},{2,26},{10... | collective-permute-start | bytes 196616 | tf_op jit(solution)/shard_map/ppermute | solution.py:861
  107.6 23.5 %collective-permute-start.29 = (bf16[4,64,1024]{2,1,0:T(8,128)(2,1)S(1)}, bf16[4,64,1024]{2,1,0:T(8,128)(2,1)S(1)}, u32[]{:S(2)}, u32[]{:S(2)}) collective-permute-start(bf16[4,64,1024]{2,1,0:T(8,128)(2,1)S(1)} %get-tuple-element.131), channel_id=1, source_target_pairs={{0,32},{32,64},{64,96},{96,0},{1,33},{33,65},{65,97},{97,1},{2,34}... | collective-permute-start | bytes 1572872 | tf_op jit(solution)/shard_map/ppermute | solution.py:861
  111.1 3.0 %collective-permute-start.25 = (f32[4,128,128]{2,1,0:T(8,128)S(1)}, f32[4,128,128]{2,1,0:T(8,128)S(1)}, u32[]{:S(2)}, u32[]{:S(2)}) collective-permute-start(f32[4,128,128]{2,1,0:T(8,128)S(1)} %get-tuple-element.119), channel_id=1, source_target_pairs={{0,4},{4,0},{1,5},{5,1},{2,6},{6,2},{3,7},{7,3},{8,12},{12,8},{9,1... | collective-permute-start | bytes 786440 | tf_op jit(solution)/shard_map/ppermute | solution.py:873
  111.2 22.5 %collective-permute-start.30 = (bf16[4,64,1024]{2,1,0:T(8,128)(2,1)S(1)}, bf16[4,64,1024]{2,1,0:T(8,128)(2,1)S(1)}, u32[]{:S(2)}, u32[]{:S(2)}) collective-permute-start(bf16[4,64,1024]{2,1,0:T(8,128)(2,1)S(1)} %get-tuple-element.132), channel_id=1, source_target_pairs={{0,64},{32,96},{64,0},{96,32},{1,65},{33,97},{65,1},{97,33},{2,66}... | collective-permute-start | bytes 1572872 | tf_op jit(solution)/shard_map/ppermute | solution.py:861
  112.5 23.8 %collective-permute-start.31 = (bf16[4,64,1024]{2,1,0:T(8,128)(2,1)S(1)}, bf16[4,64,1024]{2,1,0:T(8,128)(2,1)S(1)}, u32[]{:S(2)}, u32[]{:S(2)}) collective-permute-start(bf16[4,64,1024]{2,1,0:T(8,128)(2,1)S(1)} %get-tuple-element.133), channel_id=1, source_target_pairs={{0,96},{32,0},{64,32},{96,64},{1,97},{33,1},{65,33},{97,65},{2,98}... | collective-permute-start | bytes 1572872 | tf_op jit(solution)/shard_map/ppermute | solution.py:861
  114.1 10.1 %copy-start.1 = (bf16[2048,1024]{1,0:T(8,128)(2,1)S(1)}, bf16[2048,1024]{1,0:T(8,128)(2,1)}, u32[]{:S(2)}) copy-start(bf16[2048,1024]{1,0:T(8,128)(2,1)} %all-gather.2.cloned.1.call-done.refs_2_) | copy-start | bytes 12582916
  124.2 0.7 copy-start.21
  127.4 13.0 %collective-permute-start.26 = (bf16[256,512]{1,0:T(8,128)(2,1)S(1)}, bf16[256,512]{1,0:T(8,128)(2,1)S(1)}, u32[]{:S(2)}, u32[]{:S(2)}) collective-permute-start(bf16[256,512]{1,0:T(8,128)(2,1)S(1)} %get-tuple-element.138), channel_id=1, source_target_pairs={{0,1},{1,2},{2,3},{3,0},{4,5},{5,6},{6,7},{7,4},{8,9},{9,10},{10,1... | collective-permute-start | bytes 786440 | tf_op jit(solution)/shard_map/ppermute | solution.py:861
  129.1 12.6 %collective-permute-start.28 = (bf16[256,512]{1,0:T(8,128)(2,1)S(1)}, bf16[256,512]{1,0:T(8,128)(2,1)S(1)}, u32[]{:S(2)}, u32[]{:S(2)}) collective-permute-start(bf16[256,512]{1,0:T(8,128)(2,1)S(1)} %get-tuple-element.139), channel_id=1, source_target_pairs={{0,3},{1,0},{2,1},{3,2},{4,7},{5,4},{6,5},{7,6},{8,11},{9,8},{10,9... | collective-permute-start | bytes 786440 | tf_op jit(solution)/shard_map/ppermute | solution.py:861
  131.1 12.4 %collective-permute-start.27 = (bf16[256,512]{1,0:T(8,128)(2,1)S(1)}, bf16[256,512]{1,0:T(8,128)(2,1)S(1)}, u32[]{:S(2)}, u32[]{:S(2)}) collective-permute-start(bf16[256,512]{1,0:T(8,128)(2,1)S(1)} %get-tuple-element.140), channel_id=1, source_target_pairs={{0,2},{1,3},{2,0},{3,1},{4,6},{5,7},{6,4},{7,5},{8,10},{9,11},{10,... | collective-permute-start | bytes 786440 | tf_op jit(solution)/shard_map/ppermute | solution.py:861
  137.1 7.6 %collective-permute-start.32 = (bf16[64,1024]{1,0:T(8,128)(2,1)S(1)}, bf16[64,1024]{1,0:T(8,128)(2,1)S(1)}, u32[]{:S(2)}, u32[]{:S(2)}) collective-permute-start(bf16[64,1024]{1,0:T(8,128)(2,1)S(1)} %get-tuple-element.135), channel_id=1, source_target_pairs={{0,8},{8,16},{16,24},{24,0},{1,9},{9,17},{17,25},{25,1},{2,10},{10... | collective-permute-start | bytes 393224 | tf_op jit(solution)/shard_map/ppermute | solution.py:861
  138.6 7.6 %collective-permute-start.33 = (bf16[64,1024]{1,0:T(8,128)(2,1)S(1)}, bf16[64,1024]{1,0:T(8,128)(2,1)S(1)}, u32[]{:S(2)}, u32[]{:S(2)}) collective-permute-start(bf16[64,1024]{1,0:T(8,128)(2,1)S(1)} %get-tuple-element.136), channel_id=1, source_target_pairs={{0,16},{8,24},{16,0},{24,8},{1,17},{9,25},{17,1},{25,9},{2,18},{10... | collective-permute-start | bytes 393224 | tf_op jit(solution)/shard_map/ppermute | solution.py:861
  140.4 6.4 %collective-permute-start.34 = (bf16[64,1024]{1,0:T(8,128)(2,1)S(1)}, bf16[64,1024]{1,0:T(8,128)(2,1)S(1)}, u32[]{:S(2)}, u32[]{:S(2)}) collective-permute-start(bf16[64,1024]{1,0:T(8,128)(2,1)S(1)} %get-tuple-element.137), channel_id=1, source_target_pairs={{0,24},{8,0},{16,8},{24,16},{1,25},{9,1},{17,9},{25,17},{2,26},{10... | collective-permute-start | bytes 393224 | tf_op jit(solution)/shard_map/ppermute | solution.py:861
  (4 other events, 2.7 us)
Sparse Core Ops, SparseCore 0:
  10.8 51.1 all-gather.1

commit v5 on v4

--- a/solution.py
+++ b/solution.py
@@ -796,7 +796,7 @@
         ],
         (pl.BlockSpec((1, TOK, depth), lambda k, place: (k, 0, 0)),),
         (normed, weight),
-        SHORT,
+        LONG,
         prefetch=place,
         after=after,
     )[0]
@@ -902,7 +902,8 @@
     grad_parts = spread(join_pass(place, kept, got, dkept, dgot, ()), "z", NZ)
     mine, other = outer_pass(place, cot, normed, (dgot,))
     theirs = swap(other)
-    suffixes, grad_total, _ = later_pass(place, grad_parts, row, ())
+    mixes = mix_pass(place, normed, weight, (grad_parts[0],))
+    suffixes, grad_total, _ = later_pass(place, grad_parts, row, (mixes,))
     grads = [shift(grad_total, "y", NY, -k) for k in range(1, NY)]
     grad_query, update, dk0, error, y, dcc, dcr = middle_pass(
         place, query, key, value, cums, cols, state, back, attend, inverse, wu
@@ -915,7 +916,7 @@
     grad_value, grad_key, grad_beta, grad_decay = last_pass(
         place, key, cums, cols, state, ggot, gown, error, y, update, xz, dk0, dcc, dcr, ()
     )
-    mixes = mix_pass(place, normed, weight, (grad_beta,))
+    mixes, grad_beta = lax.optimization_barrier((mixes, grad_beta))
     mixed = scatter_stage([mixes[k] for k in range(NH)], "head", NH).astype(BF)
     sums = sum_pass(place, sums, (grad_beta,))
     grad_weight = scatter_stage(sums, "z", NZ)

time: 156 us -> 158 us (1.013)
  waiting for transfers between devices: 23.1 us -> 25.3 us
    ppermute x30, waiting for transfers between devices: 19.1 us -> 22.2 us  [shift(): lax.ppermute(array, axis, [(i, (i + step) % count) for i in range(count)])]
  transfers between devices with their start and end apart: 36 -> 36, of which waited for: 19 -> 13; matrix products, arithmetic and copies ran while one was open for 1% -> 1% of each run, Pallas kernels for 28% -> 28%
where the time goes in v5:
time: 158 us; the launch traced here: 157 us
  Pallas kernels  53 us (34%)
  starting transfers between devices  49 us (31%)
  waiting for transfers between devices  25.3 us (16%)
  between operations  15.2 us (10%)
  local copies, waits for them, and re-layouts  9.58 us (6%)
  other arithmetic  4.75 us (3%)
    pallas_call x19, Pallas kernels, call(): pl.pallas_call(run, out_shape=out_shape, compiler_params=pltpu.CompilerPa...  53 us
    ppermute x30, starting transfers between devices, shift(): lax.ppermute(array, axis, [(i, (i + step) % count) for i in range(count)])  48.1 us
    ppermute x30, waiting for transfers between devices, shift(): lax.ppermute(array, axis, [(i, (i + step) % count) for i in range(count)])  22.2 us
    unnamed x64, local copies, waits for them, and re-layouts  9.53 us
  transfers between devices with their start and end apart: 36, of which 13 were waited for; matrix products, arithmetic and copies ran while one was open for 1% of the time, Pallas kernels for 28%

profile of v5, /device:TPU:0, one launch (start us, length us, event | category | flops | bytes accessed | tf_op | source)
XLA Modules:
  0.0 156.8 jit_solution(5706972983144034796)
XLA Ops:
  7.9 1.7 %add_convert_fusion = bf16[64,1024]{1,0:T(8,128)(2,1)} fusion(bf16[64,1024]{1,0:T(8,128)(2,1)} %param.15, bf16[64,1024]{1,0:T(8,128)(2,1)} %param.14, f32[]{:T(128)} %bitcast.8, f32[]{:T(128)S(6)} %sub.4), kind=kLoop, calls=%fused_computation.9 | loop fusion | flops 393216 | bytes 393224 | tf_op jit(solution)/shard_map/convert_element_type | solution.py:881
  9.6 1.6 %collective-permute-start.12 = (bf16[256,512]{1,0:T(8,128)(2,1)}, bf16[256,512]{1,0:T(8,128)(2,1)S(1)}, u32[]{:S(2)}, u32[]{:S(2)}) collective-permute-start(bf16[256,512]{1,0:T(8,128)(2,1)} %param.17), channel_id=1, source_target_pairs={{0,1},{1,2},{2,3},{3,0},{4,5},{5,6},{6,7},{7,4},{8,9},{9,10},{10,1... | collective-permute-start | bytes 786440 | tf_op jit(solution)/shard_map/ppermute | solution.py:861
  11.3 2.7 %collective-permute-start.11 = (bf16[256,512]{1,0:T(8,128)(2,1)}, bf16[256,512]{1,0:T(8,128)(2,1)S(1)}, u32[]{:S(2)}, u32[]{:S(2)}) collective-permute-start(bf16[256,512]{1,0:T(8,128)(2,1)} %param.17), channel_id=1, source_target_pairs={{0,2},{1,3},{2,0},{3,1},{4,6},{5,7},{6,4},{7,5},{8,10},{9,11},{10,... | collective-permute-start | bytes 786440 | tf_op jit(solution)/shard_map/ppermute | solution.py:861
  14.0 1.4 collective-permute-start.10
  15.5 0.9 copy-done
  16.4 1.0 copy-done.5
  18.9 10.4 %pre_kernel.1 = (bf16[4,272,128]{2,1,0:T(8,128)(2,1)S(1)}, bf16[4,272,128]{2,1,0:T(8,128)(2,1)S(1)}, bf16[8,256,256]{2,1,0:T(8,128)(2,1)S(1)}, bf16[8,256,256]{2...) custom-call(s32[4]{0:T(128)S(1)} %pad_add_fusion.refs_0_, bf16[256,512]{1,0:T(8,128)(2,1)S(1)} %copy-done, ...), custom_call_target="tpu_custom_call" | custom-call | flops 1000000 | bytes 1 | tf_op jit(solution)/shard_map/pre_kernel/pallas_call | solution.py:70
  29.5 1.3 pad_maximum_fusion.refs_1_
  31.0 0.8 pair_kernel.1
  31.8 2.0 %collective-permute-start.1 = (bf16[272,128]{1,0:T(8,128)(2,1)S(1)}, bf16[272,128]{1,0:T(8,128)(2,1)S(1)}, u32[]{:S(2)}, u32[]{:S(2)}) collective-permute-start(bf16[272,128]{1,0:T(8,128)(2,1)S(1)} %get-tuple-element.78), channel_id=1, source_target_pairs={{0,8},{8,16},{16,24},{24,0},{1,9},{9,17},{17,25},{25,1},{2,10},{10... | collective-permute-start | bytes 208904 | tf_op jit(solution)/shard_map/ppermute | solution.py:861
  33.8 3.6 %collective-permute-start.2 = (bf16[272,128]{1,0:T(8,128)(2,1)S(1)}, bf16[272,128]{1,0:T(8,128)(2,1)S(1)}, u32[]{:S(2)}, u32[]{:S(2)}) collective-permute-start(bf16[272,128]{1,0:T(8,128)(2,1)S(1)} %get-tuple-element.79), channel_id=1, source_target_pairs={{0,16},{8,24},{16,0},{24,8},{1,17},{9,25},{17,1},{25,9},{2,18},{10... | collective-permute-start | bytes 208904 | tf_op jit(solution)/shard_map/ppermute | solution.py:861
  37.4 1.0 collective-permute-start.3
  38.4 2.6 %attend_kernel.1 = (bf16[8,256,256]{2,1,0:T(8,128)(2,1)S(1)}, bf16[8,256,128]{2,1,0:T(8,128)(2,1)S(1)}, f32[8,256,128]{2,1,0:T(8,128)S(1)}, bf16[8,256,128]{2,1,0:T(8,128)(2,1)S(1)}) custom-call(s32[4]{0:T(128)S(1)} %pad_add_fusion.refs_0_, bf16[256,512]{1,0:T(8,128)(2,1)S(1)} %copy-done.28, bf16[256,512]{1,0:T(8,128)(2,1)S(1)} %copy-done.1, ...), custom_call_target="tpu_custom_call" | custom-call | flops 5000000000 | bytes 1 | tf_op jit(solution)/shard_map/attend_kernel/pallas_call | solution.py:70
  41.0 1.0 copy-done.30
  42.0 1.1 prefix_kernel.1
  43.1 1.6 %collective-permute-start.4 = (bf16[272,128]{1,0:T(8,128)(2,1)S(1)}, bf16[272,128]{1,0:T(8,128)(2,1)S(1)}, u32[]{:S(2)}, u32[]{:S(2)}) collective-permute-start(bf16[272,128]{1,0:T(8,128)(2,1)S(1)} %get-tuple-element.86), channel_id=1, source_target_pairs={{0,32},{32,64},{64,96},{96,0},{1,33},{33,65},{65,97},{97,1},{2,34}... | collective-permute-start | bytes 208904 | tf_op jit(solution)/shard_map/ppermute | solution.py:861
  44.7 2.9 %collective-permute-start.5 = (bf16[272,128]{1,0:T(8,128)(2,1)S(1)}, bf16[272,128]{1,0:T(8,128)(2,1)S(1)}, u32[]{:S(2)}, u32[]{:S(2)}) collective-permute-start(bf16[272,128]{1,0:T(8,128)(2,1)S(1)} %get-tuple-element.86), channel_id=1, source_target_pairs={{0,64},{32,96},{64,0},{96,32},{1,65},{33,97},{65,1},{97,33},{2,66}... | collective-permute-start | bytes 208904 | tf_op jit(solution)/shard_map/ppermute | solution.py:861
  47.6 1.3 collective-permute-start.6
  49.0 0.9 suffix_kernel.1
  49.9 4.2 %collective-permute-done.5.refs_2_ = bf16[272,128]{1,0:T(8,128)(2,1)S(1)} collective-permute-done((bf16[272,128]{1,0:T(8,128)(2,1)S(1)}, bf16[272,128]{1,0:T(8,128)(2,1)S(1)}, u32[]{:S(2)}, u32[]{:S(2)}) %collective-permute-start.5) | collective-permute-done | bytes 69664 | tf_op jit(solution)/shard_map/ppermute | solution.py:861
  54.2 1.7 %enter_kernel.1 = (f32[128,128]{1,0:T(8,128)S(1)}, f32[128,128]{1,0:T(8,128)}, f32[128,128]{1,0:T(8,128)}, f32[128,128]{1,0:T(8,128)}) custom-call(s32[4]{0:T(128)S(1)} %pad_add_fusion.refs_0_, bf16[272,128]{1,0:T(8,128)(2,1)S(1)} %collective-permute-done.4.refs_1_, bf16[272,128]{1,0:T(8,128)(2,1)S(1)} %collective-permute-done.5.refs_2_, ...), custom_call_target="tpu_custom_call" | custom-call | flops 1000000 | bytes 1 | tf_op jit(solution)/shard_map/enter_kernel/pallas_call | solution.py:70
  57.2 1.0 collective-permute-start.7
  58.2 1.5 collective-permute-start.8
  59.7 1.2 collective-permute-start.9
  60.9 0.9 copy-done.3
  61.8 2.2 %copy-done.22 = bf16[2048,1024]{1,0:T(8,128)(2,1)S(1)} copy-done((bf16[2048,1024]{1,0:T(8,128)(2,1)S(1)}, bf16[2048,1024]{1,0:T(8,128)(2,1)}, u32[]{:S(2)}) %copy-start.22) | copy-done | bytes 4194328
  64.0 2.8 %back_kernel.1.refs_7_.refs_5_ = f32[256,1024]{1,0:T(8,128)S(1)} custom-call(s32[4]{0:T(128)S(1)} %pad_add_fusion.refs_0_, bf16[4,256,512]{2,1,0:T(8,128)(2,1)S(1)} %pad_maximum_fusion.refs_1_, bf16[2048,1024]{1,0:T(8,128)(2,1)S(1)} %copy-done.22, bf16[4,128,128]{2,1,0:T(8,128)(2,1)S(1)} %copy-done.3), custom_call_target="tpu_custom_call" | custom-call | flops 5000000000 | bytes 1 | tf_op jit(solution)/shard_map/back_kernel/pallas_call | solution.py:70
  66.8 1.7 %split_kernel.1 = (f32[4,128,128]{2,1,0:T(8,128)S(1)}, f32[4,128,128]{2,1,0:T(8,128)S(1)}) custom-call(s32[4]{0:T(128)S(1)} %pad_add_fusion.refs_0_, f32[128,128]{1,0:T(8,128)S(1)} %copy-done.18, f32[128,128]{1,0:T(8,128)} %collective-permute-done.7.refs_2_, f32[128,128]{1,0:T(8,128)} %collective-permute-done.8.refs_3_, ...), custom_call_target="tpu_custom_call" | custom-call | flops 1000000 | bytes 1 | tf_op jit(solution)/shard_map/split_kernel/pallas_call | solution.py:70
  68.6 1.5 collective-permute-done.13.refs_1_
  70.1 5.4 %norm_kernel.1 = (bf16[256,1024]{1,0:T(8,128)(2,1)S(1)}, bf16[8,128,128]{2,1,0:T(8,128)(2,1)S(1)}, f32[8,256,128]{2,1,0:T(8,128)S(1)}, f32[4,128,128]{2,1,0:T(8,128)S(1)}, f32[4,128,128]{2,1,0:T(8,128)S(1)}) custom-call(s32[4]{0:T(128)S(1)} %pad_add_fusion.refs_0_, f32[4,128,128]{2,1,0:T(8,128)S(1)} %collective-permute-done.13.refs_1_, ...), custom_call_target="tpu_custom_call" | custom-call | flops 1000000 | bytes 1 | tf_op jit(solution)/shard_map/norm_kernel/pallas_call | solution.py:70
  75.9 1.4 collective-permute-done.14.refs_4_.refs_3_.refs_8_
  77.3 2.6 %outer_kernel.1 = (bf16[4,4,64,1024]{3,2,1,0:T(8,128)(2,1)S(1)}, bf16[4,4,64,1024]{3,2,1,0:T(8,128)(2,1)S(1)}) custom-call(s32[4]{0:T(128)S(1)} %pad_add_fusion.refs_0_, bf16[4,256,512]{2,1,0:T(8,128)(2,1)S(1)} %pad_maximum_fusion.refs_1_, bf16[256,1024]{1,0:T(8,128)(2,1)S(1)} %get-tuple-element.100.refs_1_.refs_2_, ...), custom_call_target="tpu_custom_call" | custom-call | flops 5000000000 | bytes 1 | tf_op jit(solution)/shard_map/outer_kernel/pallas_call | solution.py:70
  80.1 0.8 join_kernel.1
  80.9 1.0 collective-permute-start.15
  81.8 2.6 %collective-permute-start.16 = (f32[128,128]{1,0:T(8,128)S(1)}, f32[128,128]{1,0:T(8,128)S(1)}, u32[]{:S(2)}, u32[]{:S(2)}) collective-permute-start(f32[128,128]{1,0:T(8,128)S(1)} %get-tuple-element.106), channel_id=1, source_target_pairs={{0,16},{8,24},{16,0},{24,8},{1,17},{9,25},{17,1},{25,9},{2,18},{10... | collective-permute-start | bytes 196616 | tf_op jit(solution)/shard_map/ppermute | solution.py:861
  84.4 1.6 %collective-permute-start.17 = (f32[128,128]{1,0:T(8,128)S(1)}, f32[128,128]{1,0:T(8,128)S(1)}, u32[]{:S(2)}, u32[]{:S(2)}) collective-permute-start(f32[128,128]{1,0:T(8,128)S(1)} %get-tuple-element.107), channel_id=1, source_target_pairs={{0,24},{8,0},{16,8},{24,16},{1,25},{9,1},{17,9},{25,17},{2,26},{10... | collective-permute-start | bytes 196616 | tf_op jit(solution)/shard_map/ppermute | solution.py:861
  86.1 2.5 %mix_kernel.1.refs_6_ = bf16[4,256,512]{2,1,0:T(8,128)(2,1)S(1)} custom-call(s32[4]{0:T(128)S(1)} %pad_add_fusion.refs_0_, bf16[256,1024]{1,0:T(8,128)(2,1)S(1)} %get-tuple-element.100.refs_1_.refs_2_, bf16[2048,1024]{1,0:T(8,128)(2,1)S(1)} %copy-done.23, f32[128,128]{1,0:T(8,128)S(1)} %get-tuple-element.103.refs_3_.refs_1_), custom_call_target="tpu_custom_call" | custom-call | flops 5000000000 | bytes 1 | tf_op jit(solution)/shard_map/mix_kernel/pallas_call | solution.py:70
  88.7 1.3 later_kernel.1
  90.0 2.4 %collective-permute-start.18 = (f32[128,128]{1,0:T(8,128)S(1)}, f32[128,128]{1,0:T(8,128)S(1)}, u32[]{:S(2)}, u32[]{:S(2)}) collective-permute-start(f32[128,128]{1,0:T(8,128)S(1)} %get-tuple-element.108), channel_id=1, source_target_pairs={{0,96},{32,0},{64,32},{96,64},{1,97},{33,1},{65,33},{97,65},{2,98}... | collective-permute-start | bytes 196616 | tf_op jit(solution)/shard_map/ppermute | solution.py:861
  92.4 1.7 %collective-permute-start.19 = (f32[128,128]{1,0:T(8,128)S(1)}, f32[128,128]{1,0:T(8,128)S(1)}, u32[]{:S(2)}, u32[]{:S(2)}) collective-permute-start(f32[128,128]{1,0:T(8,128)S(1)} %get-tuple-element.108), channel_id=1, source_target_pairs={{0,64},{32,96},{64,0},{96,32},{1,65},{33,97},{65,1},{97,33},{2,66}... | collective-permute-start | bytes 196616 | tf_op jit(solution)/shard_map/ppermute | solution.py:861
  94.3 4.7 %middle_kernel.1 = (f32[256,512]{1,0:T(8,128)}, bf16[8,256,128]{2,1,0:T(8,128)(2,1)S(1)}, f32[256,512]{1,0:T(8,128)S(1)}, f32[8,256,128]{2,1,0:T(8,128)S(1)}, bf...) custom-call(s32[4]{0:T(128)S(1)} %pad_add_fusion.refs_0_, ...), custom_call_target="tpu_custom_call" | custom-call | flops 10000000000 | bytes 1 | tf_op jit(solution)/shard_map/middle_kernel/pallas_call | solution.py:70
  99.6 1.1 leave_kernel.1
  100.8 1.0 collective-permute-start.21
  101.8 2.9 %collective-permute-start.22 = (f32[128,128]{1,0:T(8,128)S(1)}, f32[128,128]{1,0:T(8,128)S(1)}, u32[]{:S(2)}, u32[]{:S(2)}) collective-permute-start(f32[128,128]{1,0:T(8,128)S(1)} %get-tuple-element.116), channel_id=1, source_target_pairs={{0,16},{8,24},{16,0},{24,8},{1,17},{9,25},{17,1},{25,9},{2,18},{10... | collective-permute-start | bytes 196616 | tf_op jit(solution)/shard_map/ppermute | solution.py:861
  104.8 1.0 blend_kernel.1
  105.8 1.5 collective-permute-start.29
  107.6 1.3 collective-permute-done.23.refs_4_
  108.9 0.8 part_kernel.1
  109.8 1.9 %collective-permute-start.30 = (bf16[4,64,1024]{2,1,0:T(8,128)(2,1)S(1)}, bf16[4,64,1024]{2,1,0:T(8,128)(2,1)S(1)}, u32[]{:S(2)}, u32[]{:S(2)}) collective-permute-start(bf16[4,64,1024]{2,1,0:T(8,128)(2,1)S(1)} %get-tuple-element.136), channel_id=1, source_target_pairs={{0,64},{32,96},{64,0},{96,32},{1,65},{33,97},{65,1},{97,33},{2,66}... | collective-permute-start | bytes 1572872 | tf_op jit(solution)/shard_map/ppermute | solution.py:861
  111.7 2.0 %collective-permute-start.31 = (bf16[4,64,1024]{2,1,0:T(8,128)(2,1)S(1)}, bf16[4,64,1024]{2,1,0:T(8,128)(2,1)S(1)}, u32[]{:S(2)}, u32[]{:S(2)}) collective-permute-start(bf16[4,64,1024]{2,1,0:T(8,128)(2,1)S(1)} %get-tuple-element.137), channel_id=1, source_target_pairs={{0,96},{32,0},{64,32},{96,64},{1,97},{33,1},{65,33},{97,65},{2,98}... | collective-permute-start | bytes 1572872 | tf_op jit(solution)/shard_map/ppermute | solution.py:861
  113.7 10.1 %last_kernel.1 = (f32[256,1024]{1,0:T(8,128)}, f32[256,512]{1,0:T(8,128)}, f32[8,256]{1,0:T(8,128)}, f32[8,256]{1,0:T(8,128)}) custom-call(s32[4]{0:T(128)S(1)} %pad_add_fusion.refs_0_, bf16[256,512]{1,0:T(8,128)(2,1)S(1)} %copy-done.1, f32[8,256]{1,0:T(8,128)S(1)} %get-tuple-element.81.refs_3_.refs_4_.refs_2_, f32[4,256,128]{2,1,0:T(8,128)S(1)} %copy-done.10, ...), custom_call_target="tpu_custom_call" | custom-call | flops 1000000 | bytes 1 | tf_op jit(solution)/shard_map/last_kernel/pallas_call | solution.py:70
  123.8 2.4 %collective-permute-start.28 = (bf16[256,512]{1,0:T(8,128)(2,1)S(1)}, bf16[256,512]{1,0:T(8,128)(2,1)S(1)}, u32[]{:S(2)}, u32[]{:S(2)}) collective-permute-start(bf16[256,512]{1,0:T(8,128)(2,1)S(1)} %get-tuple-element.143), channel_id=1, source_target_pairs={{0,3},{1,0},{2,1},{3,2},{4,7},{5,4},{6,5},{7,6},{8,11},{9,8},{10,9... | collective-permute-start | bytes 786440 | tf_op jit(solution)/shard_map/ppermute | solution.py:861
  126.9 1.2 collective-permute-start.26
  128.1 2.6 %collective-permute-done.30.refs_3_ = bf16[4,64,1024]{2,1,0:T(8,128)(2,1)S(1)} collective-permute-done((bf16[4,64,1024]{2,1,0:T(8,128)(2,1)S(1)}, bf16[4,64,1024]{2,1,0:T(8,128)(2,1)S(1)}, u32[]{:S(2)}, u32[]{:S(2)}) %collective-permute-start.30) | collective-permute-done | bytes 524320 | tf_op jit(solution)/shard_map/ppermute | solution.py:861
  130.7 6.2 %collective-permute-done.31.refs_4_ = bf16[4,64,1024]{2,1,0:T(8,128)(2,1)S(1)} collective-permute-done((bf16[4,64,1024]{2,1,0:T(8,128)(2,1)S(1)}, bf16[4,64,1024]{2,1,0:T(8,128)(2,1)S(1)}, u32[]{:S(2)}, u32[]{:S(2)}) %collective-permute-start.31) | collective-permute-done | bytes 524320 | tf_op jit(solution)/shard_map/ppermute | solution.py:861
  136.9 0.7 copy-done.21
  137.6 0.8 sum_kernel.1
  138.4 1.7 %collective-permute-start.34 = (bf16[64,1024]{1,0:T(8,128)(2,1)S(1)}, bf16[64,1024]{1,0:T(8,128)(2,1)S(1)}, u32[]{:S(2)}, u32[]{:S(2)}) collective-permute-start(bf16[64,1024]{1,0:T(8,128)(2,1)S(1)} %get-tuple-element.141), channel_id=1, source_target_pairs={{0,24},{8,0},{16,8},{24,16},{1,25},{9,1},{17,9},{25,17},{2,26},{10... | collective-permute-start | bytes 393224 | tf_op jit(solution)/shard_map/ppermute | solution.py:861
  140.0 0.7 collective-permute-start.33
  141.4 0.8 fusion.2
  142.2 2.6 %collective-permute-done.34 = bf16[64,1024]{1,0:T(8,128)(2,1)S(1)} collective-permute-done((bf16[64,1024]{1,0:T(8,128)(2,1)S(1)}, bf16[64,1024]{1,0:T(8,128)(2,1)S(1)}, u32[]{:S(2)}, u32[]{:S(2)}) %collective-permute-start.34) | collective-permute-done | bytes 131104 | tf_op jit(solution)/shard_map/ppermute | solution.py:861
  144.9 2.9 %collective-permute-done.33 = bf16[64,1024]{1,0:T(8,128)(2,1)S(1)} collective-permute-done((bf16[64,1024]{1,0:T(8,128)(2,1)S(1)}, bf16[64,1024]{1,0:T(8,128)(2,1)S(1)}, u32[]{:S(2)}, u32[]{:S(2)}) %collective-permute-start.33) | collective-permute-done | bytes 131104 | tf_op jit(solution)/shard_map/ppermute | solution.py:861
  147.7 1.4 collective-permute-done.32
  149.1 0.9 broadcast_multiply_fusion
  (98 shorter events, 6.5 us)
Async XLA Ops:
  7.2 31.2 %copy-start.1 = (bf16[256,512]{1,0:T(8,128)(2,1)S(1)}, bf16[256,512]{1,0:T(8,128)(2,1)}, u32[]{:S(2)}) copy-start(bf16[256,512]{1,0:T(8,128)(2,1)} %refs_1_.7) | copy-start | bytes 786436
  7.2 53.7 %all-gather.2.cloned.1.call-start = ((), (), s32[]{:S(2)}) async-start(), calls=%async_computation | async-start | bytes 4325376 | tf_op jit(solution)/shard_map/all_gather | solution.py:882
  9.6 19.8 %collective-permute-start.12 = (bf16[256,512]{1,0:T(8,128)(2,1)}, bf16[256,512]{1,0:T(8,128)(2,1)S(1)}, u32[]{:S(2)}, u32[]{:S(2)}) collective-permute-start(bf16[256,512]{1,0:T(8,128)(2,1)} %param.17), channel_id=1, source_target_pairs={{0,1},{1,2},{2,3},{3,0},{4,5},{5,6},{6,7},{7,4},{8,9},{9,10},{10,1... | collective-permute-start | bytes 786440 | tf_op jit(solution)/shard_map/ppermute | solution.py:861
  11.3 18.2 %collective-permute-start.11 = (bf16[256,512]{1,0:T(8,128)(2,1)}, bf16[256,512]{1,0:T(8,128)(2,1)S(1)}, u32[]{:S(2)}, u32[]{:S(2)}) collective-permute-start(bf16[256,512]{1,0:T(8,128)(2,1)} %param.17), channel_id=1, source_target_pairs={{0,2},{1,3},{2,0},{3,1},{4,6},{5,7},{6,4},{7,5},{8,10},{9,11},{10,... | collective-permute-start | bytes 786440 | tf_op jit(solution)/shard_map/ppermute | solution.py:861
  14.0 15.5 %collective-permute-start.10 = (bf16[256,512]{1,0:T(8,128)(2,1)}, bf16[256,512]{1,0:T(8,128)(2,1)S(1)}, u32[]{:S(2)}, u32[]{:S(2)}) collective-permute-start(bf16[256,512]{1,0:T(8,128)(2,1)} %param.17), channel_id=1, source_target_pairs={{0,3},{1,0},{2,1},{3,2},{4,7},{5,4},{6,5},{7,6},{8,11},{9,8},{10,9... | collective-permute-start | bytes 786440 | tf_op jit(solution)/shard_map/ppermute | solution.py:861
  15.5 1.0 copy-start
  16.4 1.0 copy-start.5
  18.9 19.5 %copy-start.28 = (bf16[256,512]{1,0:T(8,128)(2,1)S(1)}, bf16[256,512]{1,0:T(8,128)(2,1)}, u32[]{:S(2)}) copy-start(bf16[256,512]{1,0:T(8,128)(2,1)} %refs_1_.6) | copy-start | bytes 786436
  29.3 11.6 %copy-start.9 = (f32[4,256,128]{2,1,0:T(8,128)}, f32[4,256,128]{2,1,0:T(8,128)S(1)}, u32[]{:S(2)}) copy-start(f32[4,256,128]{2,1,0:T(8,128)S(1)} %get-tuple-element.82.refs_4_.refs_5_.refs_3_) | copy-start | bytes 1572868
  29.3 11.6 %copy-start.24 = (bf16[8,256,256]{2,1,0:T(8,128)(2,1)}, bf16[8,256,256]{2,1,0:T(8,128)(2,1)S(1)}, u32[]{:S(2)}) copy-start(bf16[8,256,256]{2,1,0:T(8,128)(2,1)S(1)} %get-tuple-element.83.refs_5_.refs_9_) | copy-start | bytes 3145732
  29.3 11.6 %copy-start.26 = (bf16[8,256,256]{2,1,0:T(8,128)(2,1)}, bf16[8,256,256]{2,1,0:T(8,128)(2,1)S(1)}, u32[]{:S(2)}) copy-start(bf16[8,256,256]{2,1,0:T(8,128)(2,1)S(1)} %get-tuple-element.84.refs_6_.refs_10_) | copy-start | bytes 3145732
  29.4 1.6 %collective-permute-start = (bf16[4,272,128]{2,1,0:T(8,128)(2,1)S(1)}, bf16[4,272,128]{2,1,0:T(8,128)(2,1)S(1)}, u32[]{:S(2)}, u32[]{:S(2)}) collective-permute-start(bf16[4,272,128]{2,1,0:T(8,128)(2,1)S(1)} %get-tuple-element.76), channel_id=1, source_target_pairs={{0,4},{4,0},{1,5},{5,1},{2,6},{6,2},{3,7},{7,3},{8,12},{12,8},{9,1... | collective-permute-start | bytes 835592 | tf_op jit(solution)/shard_map/ppermute | solution.py:873
  31.8 10.1 %collective-permute-start.1 = (bf16[272,128]{1,0:T(8,128)(2,1)S(1)}, bf16[272,128]{1,0:T(8,128)(2,1)S(1)}, u32[]{:S(2)}, u32[]{:S(2)}) collective-permute-start(bf16[272,128]{1,0:T(8,128)(2,1)S(1)} %get-tuple-element.78), channel_id=1, source_target_pairs={{0,8},{8,16},{16,24},{24,0},{1,9},{9,17},{17,25},{25,1},{2,10},{10... | collective-permute-start | bytes 208904 | tf_op jit(solution)/shard_map/ppermute | solution.py:861
  33.8 8.2 %collective-permute-start.2 = (bf16[272,128]{1,0:T(8,128)(2,1)S(1)}, bf16[272,128]{1,0:T(8,128)(2,1)S(1)}, u32[]{:S(2)}, u32[]{:S(2)}) collective-permute-start(bf16[272,128]{1,0:T(8,128)(2,1)S(1)} %get-tuple-element.79), channel_id=1, source_target_pairs={{0,16},{8,24},{16,0},{24,8},{1,17},{9,25},{17,1},{25,9},{2,18},{10... | collective-permute-start | bytes 208904 | tf_op jit(solution)/shard_map/ppermute | solution.py:861
  37.4 4.6 %collective-permute-start.3 = (bf16[272,128]{1,0:T(8,128)(2,1)S(1)}, bf16[272,128]{1,0:T(8,128)(2,1)S(1)}, u32[]{:S(2)}, u32[]{:S(2)}) collective-permute-start(bf16[272,128]{1,0:T(8,128)(2,1)S(1)} %get-tuple-element.80), channel_id=1, source_target_pairs={{0,24},{8,0},{16,8},{24,16},{1,25},{9,1},{17,9},{25,17},{2,26},{10... | collective-permute-start | bytes 208904 | tf_op jit(solution)/shard_map/ppermute | solution.py:861
  41.0 1.0 copy-start.30
  41.9 8.0 %copy-start.7 = (bf16[8,256,128]{2,1,0:T(8,128)(2,1)}, bf16[8,256,128]{2,1,0:T(8,128)(2,1)S(1)}, u32[]{:S(2)}) copy-start(bf16[8,256,128]{2,1,0:T(8,128)(2,1)S(1)} %get-tuple-element.98.refs_3_) | copy-start | bytes 1572868
  43.1 6.9 %copy-start.15 = (bf16[4,272,128]{2,1,0:T(8,128)(2,1)}, bf16[4,272,128]{2,1,0:T(8,128)(2,1)S(1)}, u32[]{:S(2)}) copy-start(bf16[4,272,128]{2,1,0:T(8,128)(2,1)S(1)} %get-tuple-element.90.refs_1_.refs_5_) | copy-start | bytes 835588
  43.1 6.9 %collective-permute-start.4 = (bf16[272,128]{1,0:T(8,128)(2,1)S(1)}, bf16[272,128]{1,0:T(8,128)(2,1)S(1)}, u32[]{:S(2)}, u32[]{:S(2)}) collective-permute-start(bf16[272,128]{1,0:T(8,128)(2,1)S(1)} %get-tuple-element.86), channel_id=1, source_target_pairs={{0,32},{32,64},{64,96},{96,0},{1,33},{33,65},{65,97},{97,1},{2,34}... | collective-permute-start | bytes 208904 | tf_op jit(solution)/shard_map/ppermute | solution.py:861
  44.7 9.4 %collective-permute-start.5 = (bf16[272,128]{1,0:T(8,128)(2,1)S(1)}, bf16[272,128]{1,0:T(8,128)(2,1)S(1)}, u32[]{:S(2)}, u32[]{:S(2)}) collective-permute-start(bf16[272,128]{1,0:T(8,128)(2,1)S(1)} %get-tuple-element.86), channel_id=1, source_target_pairs={{0,64},{32,96},{64,0},{96,32},{1,65},{33,97},{65,1},{97,33},{2,66}... | collective-permute-start | bytes 208904 | tf_op jit(solution)/shard_map/ppermute | solution.py:861
  47.6 6.5 %collective-permute-start.6 = (bf16[272,128]{1,0:T(8,128)(2,1)S(1)}, bf16[272,128]{1,0:T(8,128)(2,1)S(1)}, u32[]{:S(2)}, u32[]{:S(2)}) collective-permute-start(bf16[272,128]{1,0:T(8,128)(2,1)S(1)} %get-tuple-element.86), channel_id=1, source_target_pairs={{0,96},{32,0},{64,32},{96,64},{1,97},{33,1},{65,33},{97,65},{2,98}... | collective-permute-start | bytes 208904 | tf_op jit(solution)/shard_map/ppermute | solution.py:861
  54.2 1.7 %copy-start.11 = (bf16[272,128]{1,0:T(8,128)(2,1)}, bf16[272,128]{1,0:T(8,128)(2,1)S(1)}, u32[]{:S(2)}) copy-start(bf16[272,128]{1,0:T(8,128)(2,1)S(1)} %collective-permute-done.5.refs_2_) | copy-start | bytes 208900
  54.2 3.0 %copy-start.13 = (bf16[272,128]{1,0:T(8,128)(2,1)}, bf16[272,128]{1,0:T(8,128)(2,1)S(1)}, u32[]{:S(2)}) copy-start(bf16[272,128]{1,0:T(8,128)(2,1)S(1)} %collective-permute-done.6.refs_3_) | copy-start | bytes 208900
  57.2 9.6 %collective-permute-start.7 = (f32[128,128]{1,0:T(8,128)}, f32[128,128]{1,0:T(8,128)}, u32[]{:S(2)}, u32[]{:S(2)}) collective-permute-start(f32[128,128]{1,0:T(8,128)} %get-tuple-element.93), channel_id=1, source_target_pairs={{0,8},{8,16},{16,24},{24,0},{1,9},{9,17},{17,25},{25,1},{2,10},{10... | collective-permute-start | bytes 196616 | tf_op jit(solution)/shard_map/ppermute | solution.py:861
  58.2 8.6 %collective-permute-start.8 = (f32[128,128]{1,0:T(8,128)}, f32[128,128]{1,0:T(8,128)}, u32[]{:S(2)}, u32[]{:S(2)}) collective-permute-start(f32[128,128]{1,0:T(8,128)} %get-tuple-element.94), channel_id=1, source_target_pairs={{0,16},{8,24},{16,0},{24,8},{1,17},{9,25},{17,1},{25,9},{2,18},{10... | collective-permute-start | bytes 196616 | tf_op jit(solution)/shard_map/ppermute | solution.py:861
  59.7 7.1 %collective-permute-start.9 = (f32[128,128]{1,0:T(8,128)}, f32[128,128]{1,0:T(8,128)}, u32[]{:S(2)}, u32[]{:S(2)}) collective-permute-start(f32[128,128]{1,0:T(8,128)} %get-tuple-element.95), channel_id=1, source_target_pairs={{0,24},{8,0},{16,8},{24,16},{1,25},{9,1},{17,9},{25,17},{2,26},{10... | collective-permute-start | bytes 196616 | tf_op jit(solution)/shard_map/ppermute | solution.py:861
  60.9 0.9 copy-start.3
  61.8 2.2 %copy-start.22 = (bf16[2048,1024]{1,0:T(8,128)(2,1)S(1)}, bf16[2048,1024]{1,0:T(8,128)(2,1)}, u32[]{:S(2)}) copy-start(bf16[2048,1024]{1,0:T(8,128)(2,1)} %all-gather.2.cloned.1.call-done.refs_2_) | copy-start | bytes 12582916
  64.0 2.8 %copy-start.18 = (f32[128,128]{1,0:T(8,128)S(1)}, f32[128,128]{1,0:T(8,128)}, u32[]{:S(2)}) copy-start(f32[128,128]{1,0:T(8,128)} %copy-done.17) | copy-start | bytes 196612
  66.8 3.3 %copy-start.8 = (bf16[8,256,128]{2,1,0:T(8,128)(2,1)S(1)}, bf16[8,256,128]{2,1,0:T(8,128)(2,1)}, u32[]{:S(2)}) copy-start(bf16[8,256,128]{2,1,0:T(8,128)(2,1)} %copy-done.7) | copy-start | bytes 1572868
  68.5 1.6 %collective-permute-start.13 = (f32[4,128,128]{2,1,0:T(8,128)S(1)}, f32[4,128,128]{2,1,0:T(8,128)S(1)}, u32[]{:S(2)}, u32[]{:S(2)}) collective-permute-start(f32[4,128,128]{2,1,0:T(8,128)S(1)} %get-tuple-element.96), channel_id=1, source_target_pairs={{0,4},{4,0},{1,5},{5,1},{2,6},{6,2},{3,7},{7,3},{8,12},{12,8},{9,1... | collective-permute-start | bytes 786440 | tf_op jit(solution)/shard_map/ppermute | solution.py:873
  75.5 1.8 %collective-permute-start.14 = (f32[4,128,128]{2,1,0:T(8,128)S(1)}, f32[4,128,128]{2,1,0:T(8,128)S(1)}, u32[]{:S(2)}, u32[]{:S(2)}) collective-permute-start(f32[4,128,128]{2,1,0:T(8,128)S(1)} %get-tuple-element.102), channel_id=1, source_target_pairs={{0,4},{4,0},{1,5},{5,1},{2,6},{6,2},{3,7},{7,3},{8,12},{12,8},{9,1... | collective-permute-start | bytes 786440 | tf_op jit(solution)/shard_map/ppermute | solution.py:873
  77.3 8.7 %copy-start.23 = (bf16[2048,1024]{1,0:T(8,128)(2,1)S(1)}, bf16[2048,1024]{1,0:T(8,128)(2,1)}, u32[]{:S(2)}) copy-start(bf16[2048,1024]{1,0:T(8,128)(2,1)} %all-gather.2.cloned.1.call-done.refs_2_) | copy-start | bytes 12582916
  79.9 24.9 %collective-permute-start.24 = (bf16[4,4,64,1024]{3,2,1,0:T(8,128)(2,1)S(1)}, bf16[4,4,64,1024]{3,2,1,0:T(8,128)(2,1)S(1)}, u32[]{:S(2)}, u32[]{:S(2)}) collective-permute-start(bf16[4,4,64,1024]{3,2,1,0:T(8,128)(2,1)S(1)} %get-tuple-element.119), channel_id=1, source_target_pairs={{0,4},{4,0},{1,5},{5,1},{2,6},{6,2},{3,7},{7,3},{8,12},{12,8},{9,1... | collective-permute-start | bytes 6291464 | tf_op jit(solution)/shard_map/ppermute | solution.py:873
  80.9 7.7 %collective-permute-start.15 = (f32[128,128]{1,0:T(8,128)S(1)}, f32[128,128]{1,0:T(8,128)S(1)}, u32[]{:S(2)}, u32[]{:S(2)}) collective-permute-start(f32[128,128]{1,0:T(8,128)S(1)} %get-tuple-element.105), channel_id=1, source_target_pairs={{0,8},{8,16},{16,24},{24,0},{1,9},{9,17},{17,25},{25,1},{2,10},{10... | collective-permute-start | bytes 196616 | tf_op jit(solution)/shard_map/ppermute | solution.py:861
  81.8 6.8 %collective-permute-start.16 = (f32[128,128]{1,0:T(8,128)S(1)}, f32[128,128]{1,0:T(8,128)S(1)}, u32[]{:S(2)}, u32[]{:S(2)}) collective-permute-start(f32[128,128]{1,0:T(8,128)S(1)} %get-tuple-element.106), channel_id=1, source_target_pairs={{0,16},{8,24},{16,0},{24,8},{1,17},{9,25},{17,1},{25,9},{2,18},{10... | collective-permute-start | bytes 196616 | tf_op jit(solution)/shard_map/ppermute | solution.py:861
  84.4 4.3 %collective-permute-start.17 = (f32[128,128]{1,0:T(8,128)S(1)}, f32[128,128]{1,0:T(8,128)S(1)}, u32[]{:S(2)}, u32[]{:S(2)}) collective-permute-start(f32[128,128]{1,0:T(8,128)S(1)} %get-tuple-element.107), channel_id=1, source_target_pairs={{0,24},{8,0},{16,8},{24,16},{1,25},{9,1},{17,9},{25,17},{2,26},{10... | collective-permute-start | bytes 196616 | tf_op jit(solution)/shard_map/ppermute | solution.py:861
  86.0 2.7 %copy-start.16 = (bf16[4,272,128]{2,1,0:T(8,128)(2,1)S(1)}, bf16[4,272,128]{2,1,0:T(8,128)(2,1)}, u32[]{:S(2)}) copy-start(bf16[4,272,128]{2,1,0:T(8,128)(2,1)} %copy-done.15) | copy-start | bytes 835588
  86.0 8.2 %copy-start.6 = (bf16[256,1024]{1,0:T(8,128)(2,1)S(1)}, bf16[256,1024]{1,0:T(8,128)(2,1)}, u32[]{:S(2)}) copy-start(bf16[256,1024]{1,0:T(8,128)(2,1)} %refs_3_.3) | copy-start | bytes 1572868
  86.0 8.2 %copy-start.10 = (f32[4,256,128]{2,1,0:T(8,128)S(1)}, f32[4,256,128]{2,1,0:T(8,128)}, u32[]{:S(2)}) copy-start(f32[4,256,128]{2,1,0:T(8,128)} %copy-done.9) | copy-start | bytes 1572868
  86.0 8.2 %copy-start.25 = (bf16[8,256,256]{2,1,0:T(8,128)(2,1)S(1)}, bf16[8,256,256]{2,1,0:T(8,128)(2,1)}, u32[]{:S(2)}) copy-start(bf16[8,256,256]{2,1,0:T(8,128)(2,1)} %copy-done.24) | copy-start | bytes 3145732
  86.0 8.2 %copy-start.27 = (bf16[8,256,256]{2,1,0:T(8,128)(2,1)S(1)}, bf16[8,256,256]{2,1,0:T(8,128)(2,1)}, u32[]{:S(2)}) copy-start(bf16[8,256,256]{2,1,0:T(8,128)(2,1)} %copy-done.26) | copy-start | bytes 3145732
  86.1 8.2 %copy-start.29 = (bf16[256,512]{1,0:T(8,128)(2,1)S(1)}, bf16[256,512]{1,0:T(8,128)(2,1)}, u32[]{:S(2)}) copy-start(bf16[256,512]{1,0:T(8,128)(2,1)} %refs_1_.6) | copy-start | bytes 786436
  86.1 8.2 %copy-start.31 = (bf16[8,256,256]{2,1,0:T(8,128)(2,1)S(1)}, bf16[8,256,256]{2,1,0:T(8,128)(2,1)}, u32[]{:S(2)}) copy-start(bf16[8,256,256]{2,1,0:T(8,128)(2,1)} %copy-done.30) | copy-start | bytes 3145732
  90.0 9.0 %collective-permute-start.18 = (f32[128,128]{1,0:T(8,128)S(1)}, f32[128,128]{1,0:T(8,128)S(1)}, u32[]{:S(2)}, u32[]{:S(2)}) collective-permute-start(f32[128,128]{1,0:T(8,128)S(1)} %get-tuple-element.108), channel_id=1, source_target_pairs={{0,96},{32,0},{64,32},{96,64},{1,97},{33,1},{65,33},{97,65},{2,98}... | collective-permute-start | bytes 196616 | tf_op jit(solution)/shard_map/ppermute | solution.py:861
  92.4 6.6 %collective-permute-start.19 = (f32[128,128]{1,0:T(8,128)S(1)}, f32[128,128]{1,0:T(8,128)S(1)}, u32[]{:S(2)}, u32[]{:S(2)}) collective-permute-start(f32[128,128]{1,0:T(8,128)S(1)} %get-tuple-element.108), channel_id=1, source_target_pairs={{0,64},{32,96},{64,0},{96,32},{1,65},{33,97},{65,1},{97,33},{2,66}... | collective-permute-start | bytes 196616 | tf_op jit(solution)/shard_map/ppermute | solution.py:861
  94.1 5.5 %collective-permute-start.20 = (f32[128,128]{1,0:T(8,128)S(1)}, f32[128,128]{1,0:T(8,128)S(1)}, u32[]{:S(2)}, u32[]{:S(2)}) collective-permute-start(f32[128,128]{1,0:T(8,128)S(1)} %get-tuple-element.108), channel_id=1, source_target_pairs={{0,32},{32,64},{64,96},{96,0},{1,33},{33,65},{65,97},{97,1},{2,34}... | collective-permute-start | bytes 196616 | tf_op jit(solution)/shard_map/ppermute | solution.py:861
  94.2 5.4 %copy-start.4 = (bf16[4,128,128]{2,1,0:T(8,128)(2,1)S(1)}, bf16[4,128,128]{2,1,0:T(8,128)(2,1)}, u32[]{:S(2)}) copy-start(bf16[4,128,128]{2,1,0:T(8,128)(2,1)} %copy-done.2) | copy-start | bytes 393220
  94.2 5.4 %copy-start.12 = (bf16[272,128]{1,0:T(8,128)(2,1)S(1)}, bf16[272,128]{1,0:T(8,128)(2,1)}, u32[]{:S(2)}) copy-start(bf16[272,128]{1,0:T(8,128)(2,1)} %copy-done.11) | copy-start | bytes 208900
  94.3 5.4 %copy-start.14 = (bf16[272,128]{1,0:T(8,128)(2,1)S(1)}, bf16[272,128]{1,0:T(8,128)(2,1)}, u32[]{:S(2)}) copy-start(bf16[272,128]{1,0:T(8,128)(2,1)} %copy-done.13) | copy-start | bytes 208900
  100.8 6.6 %collective-permute-start.21 = (f32[128,128]{1,0:T(8,128)S(1)}, f32[128,128]{1,0:T(8,128)S(1)}, u32[]{:S(2)}, u32[]{:S(2)}) collective-permute-start(f32[128,128]{1,0:T(8,128)S(1)} %get-tuple-element.115), channel_id=1, source_target_pairs={{0,8},{8,16},{16,24},{24,0},{1,9},{9,17},{17,25},{25,1},{2,10},{10... | collective-permute-start | bytes 196616 | tf_op jit(solution)/shard_map/ppermute | solution.py:861
  101.8 5.9 %collective-permute-start.22 = (f32[128,128]{1,0:T(8,128)S(1)}, f32[128,128]{1,0:T(8,128)S(1)}, u32[]{:S(2)}, u32[]{:S(2)}) collective-permute-start(f32[128,128]{1,0:T(8,128)S(1)} %get-tuple-element.116), channel_id=1, source_target_pairs={{0,16},{8,24},{16,0},{24,8},{1,17},{9,25},{17,1},{25,9},{2,18},{10... | collective-permute-start | bytes 196616 | tf_op jit(solution)/shard_map/ppermute | solution.py:861
  104.7 4.3 %collective-permute-start.23 = (f32[128,128]{1,0:T(8,128)S(1)}, f32[128,128]{1,0:T(8,128)S(1)}, u32[]{:S(2)}, u32[]{:S(2)}) collective-permute-start(f32[128,128]{1,0:T(8,128)S(1)} %get-tuple-element.117), channel_id=1, source_target_pairs={{0,24},{8,0},{16,8},{24,16},{1,25},{9,1},{17,9},{25,17},{2,26},{10... | collective-permute-start | bytes 196616 | tf_op jit(solution)/shard_map/ppermute | solution.py:861
  105.8 21.1 %collective-permute-start.29 = (bf16[4,64,1024]{2,1,0:T(8,128)(2,1)S(1)}, bf16[4,64,1024]{2,1,0:T(8,128)(2,1)S(1)}, u32[]{:S(2)}, u32[]{:S(2)}) collective-permute-start(bf16[4,64,1024]{2,1,0:T(8,128)(2,1)S(1)} %get-tuple-element.135), channel_id=1, source_target_pairs={{0,32},{32,64},{64,96},{96,0},{1,33},{33,65},{65,97},{97,1},{2,34}... | collective-permute-start | bytes 1572872 | tf_op jit(solution)/shard_map/ppermute | solution.py:861
  109.7 4.0 %collective-permute-start.25 = (f32[4,128,128]{2,1,0:T(8,128)S(1)}, f32[4,128,128]{2,1,0:T(8,128)S(1)}, u32[]{:S(2)}, u32[]{:S(2)}) collective-permute-start(f32[4,128,128]{2,1,0:T(8,128)S(1)} %get-tuple-element.121), channel_id=1, source_target_pairs={{0,4},{4,0},{1,5},{5,1},{2,6},{6,2},{3,7},{7,3},{8,12},{12,8},{9,1... | collective-permute-start | bytes 786440 | tf_op jit(solution)/shard_map/ppermute | solution.py:873
  109.8 20.9 %collective-permute-start.30 = (bf16[4,64,1024]{2,1,0:T(8,128)(2,1)S(1)}, bf16[4,64,1024]{2,1,0:T(8,128)(2,1)S(1)}, u32[]{:S(2)}, u32[]{:S(2)}) collective-permute-start(bf16[4,64,1024]{2,1,0:T(8,128)(2,1)S(1)} %get-tuple-element.136), channel_id=1, source_target_pairs={{0,64},{32,96},{64,0},{96,32},{1,65},{33,97},{65,1},{97,33},{2,66}... | collective-permute-start | bytes 1572872 | tf_op jit(solution)/shard_map/ppermute | solution.py:861
  111.7 25.2 %collective-permute-start.31 = (bf16[4,64,1024]{2,1,0:T(8,128)(2,1)S(1)}, bf16[4,64,1024]{2,1,0:T(8,128)(2,1)S(1)}, u32[]{:S(2)}, u32[]{:S(2)}) collective-permute-start(bf16[4,64,1024]{2,1,0:T(8,128)(2,1)S(1)} %get-tuple-element.137), channel_id=1, source_target_pairs={{0,96},{32,0},{64,32},{96,64},{1,97},{33,1},{65,33},{97,65},{2,98}... | collective-permute-start | bytes 1572872 | tf_op jit(solution)/shard_map/ppermute | solution.py:861
  123.8 16.9 %collective-permute-start.28 = (bf16[256,512]{1,0:T(8,128)(2,1)S(1)}, bf16[256,512]{1,0:T(8,128)(2,1)S(1)}, u32[]{:S(2)}, u32[]{:S(2)}) collective-permute-start(bf16[256,512]{1,0:T(8,128)(2,1)S(1)} %get-tuple-element.143), channel_id=1, source_target_pairs={{0,3},{1,0},{2,1},{3,2},{4,7},{5,4},{6,5},{7,6},{8,11},{9,8},{10,9... | collective-permute-start | bytes 786440 | tf_op jit(solution)/shard_map/ppermute | solution.py:861
  126.3 15.1 %collective-permute-start.27 = (bf16[256,512]{1,0:T(8,128)(2,1)S(1)}, bf16[256,512]{1,0:T(8,128)(2,1)S(1)}, u32[]{:S(2)}, u32[]{:S(2)}) collective-permute-start(bf16[256,512]{1,0:T(8,128)(2,1)S(1)} %get-tuple-element.144), channel_id=1, source_target_pairs={{0,2},{1,3},{2,0},{3,1},{4,6},{5,7},{6,4},{7,5},{8,10},{9,11},{10,... | collective-permute-start | bytes 786440 | tf_op jit(solution)/shard_map/ppermute | solution.py:861
  126.9 14.5 %collective-permute-start.26 = (bf16[256,512]{1,0:T(8,128)(2,1)S(1)}, bf16[256,512]{1,0:T(8,128)(2,1)S(1)}, u32[]{:S(2)}, u32[]{:S(2)}) collective-permute-start(bf16[256,512]{1,0:T(8,128)(2,1)S(1)} %get-tuple-element.142), channel_id=1, source_target_pairs={{0,1},{1,2},{2,3},{3,0},{4,5},{5,6},{6,7},{7,4},{8,9},{9,10},{10,1... | collective-permute-start | bytes 786440 | tf_op jit(solution)/shard_map/ppermute | solution.py:861
  136.9 0.7 copy-start.21
  138.4 6.5 %collective-permute-start.34 = (bf16[64,1024]{1,0:T(8,128)(2,1)S(1)}, bf16[64,1024]{1,0:T(8,128)(2,1)S(1)}, u32[]{:S(2)}, u32[]{:S(2)}) collective-permute-start(bf16[64,1024]{1,0:T(8,128)(2,1)S(1)} %get-tuple-element.141), channel_id=1, source_target_pairs={{0,24},{8,0},{16,8},{24,16},{1,25},{9,1},{17,9},{25,17},{2,26},{10... | collective-permute-start | bytes 393224 | tf_op jit(solution)/shard_map/ppermute | solution.py:861
  140.0 7.7 %collective-permute-start.33 = (bf16[64,1024]{1,0:T(8,128)(2,1)S(1)}, bf16[64,1024]{1,0:T(8,128)(2,1)S(1)}, u32[]{:S(2)}, u32[]{:S(2)}) collective-permute-start(bf16[64,1024]{1,0:T(8,128)(2,1)S(1)} %get-tuple-element.140), channel_id=1, source_target_pairs={{0,16},{8,24},{16,0},{24,8},{1,17},{9,25},{17,1},{25,9},{2,18},{10... | collective-permute-start | bytes 393224 | tf_op jit(solution)/shard_map/ppermute | solution.py:861
  140.8 8.4 %collective-permute-start.32 = (bf16[64,1024]{1,0:T(8,128)(2,1)S(1)}, bf16[64,1024]{1,0:T(8,128)(2,1)S(1)}, u32[]{:S(2)}, u32[]{:S(2)}) collective-permute-start(bf16[64,1024]{1,0:T(8,128)(2,1)S(1)} %get-tuple-element.139), channel_id=1, source_target_pairs={{0,8},{8,16},{16,24},{24,0},{1,9},{9,17},{17,25},{25,1},{2,10},{10... | collective-permute-start | bytes 393224 | tf_op jit(solution)/shard_map/ppermute | solution.py:861
  (4 other events, 2.7 us)
Sparse Core Ops, SparseCore 0:
  10.8 49.7 all-gather.1

commit v6 on v5

--- a/solution.py
+++ b/solution.py
@@ -836,25 +836,33 @@
 
 
 def blend_kernel(place_ref, mine_ref, other_ref, *out_refs):
+    wide = mine_ref.shape[3] // 2
     for y in range(NY):
         for z in range(NZ):
-            total = mine_ref[y, z].astype(F32) + other_ref[y, z].astype(F32)
-            out_refs[y][z] = total.astype(BF)
+            total = (mine_ref[y, z].astype(F32) + other_ref[y, z].astype(F32)).astype(BF)
+            out_refs[z][y] = total[:, :wide]
+            out_refs[NZ + y][z] = total[:, wide:]
 
 
 def blend_pass(place, mine, other, after):
-    outs = (shape(NZ, *mine.shape[2:], dtype=BF),) * NY
-    return single(blend_kernel, outs, (mine, other), place, after, LONG)
+    rows, cols = mine.shape[2:]
+    outs = (shape(NY, rows, cols // 2, dtype=BF),) * NZ + (shape(NZ, rows, cols // 2, dtype=BF),) * NY
+    parts = single(blend_kernel, outs, (mine, other), place, after, LONG)
+    return parts[:NZ], parts[NZ:]
 
 
 def sum_kernel(place_ref, *refs):
+    ins, outs = refs[: NZ + NY], refs[NZ + NY :]
+    for y in range(NY):
+        outs[y][...] = sum(ins[z][y].astype(F32) for z in range(NZ)).astype(BF)
     for z in range(NZ):
-        refs[NY + z][...] = sum(refs[y][z].astype(F32) for y in range(NY)).astype(BF)
-
-
-def sum_pass(place, parts, after):
-    outs = (shape(*parts[0].shape[1:], dtype=BF),) * NZ
-    return single(sum_kernel, outs, parts, place, after)
+        outs[NY + z][...] = sum(ins[NZ + y][z].astype(F32) for y in range(NY)).astype(BF)
+
+
+def sum_pass(place, left, right, after):
+    outs = (shape(*left[0].shape[1:], dtype=BF),) * (NY + NZ)
+    parts = single(sum_kernel, outs, (*left, *right), place, after)
+    return parts[:NY], parts[NY:]
 
 
 def shift(array, axis, count, step):
@@ -909,8 +917,9 @@
         place, query, key, value, cums, cols, state, back, attend, inverse, wu
     )
     laters = spread(leave_pass(place, totals, grads, ns, gs, suffixes, (dk0,)), "z", NZ)
-    sums = spread(blend_pass(place, mine, theirs, (laters[0],)), "y", NY)
-    gown, gsend = part_pass(place, laters, kept, got, dkept, dgot, (sums[0],))
+    left, right = blend_pass(place, mine, theirs, (laters[0],))
+    left, right = spread(left, "z", NZ), spread(right, "y", NY)
+    gown, gsend = part_pass(place, laters, kept, got, dkept, dgot, (left[0],))
     ggot = swap(gsend)
 
     grad_value, grad_key, grad_beta, grad_decay = last_pass(
@@ -918,8 +927,9 @@
     )
     mixes, grad_beta = lax.optimization_barrier((mixes, grad_beta))
     mixed = scatter_stage([mixes[k] for k in range(NH)], "head", NH).astype(BF)
-    sums = sum_pass(place, sums, (grad_beta,))
-    grad_weight = scatter_stage(sums, "z", NZ)
+    left, right = sum_pass(place, left, right, (grad_beta,))
+    left, right = scatter_stage(left, "y", NY), scatter_stage(right, "z", NZ)
+    grad_weight = jnp.concatenate([left, right], axis=-1)
     return (
         mixed,
         grad_query,

time: 158 us -> 165 us (1.044)
  starting transfers between devices: 49 us -> 55.4 us
    ppermute x30 -> x36, starting transfers between devices: 48.1 us -> 54.5 us  [shift(): lax.ppermute(array, axis, [(i, (i + step) % count) for i in range(count)])]
    ppermute x30 -> x36, waiting for transfers between devices: 22.2 us -> 23.3 us  [shift(): lax.ppermute(array, axis, [(i, (i + step) % count) for i in range(count)])]
  transfers between devices with their start and end apart: 36 -> 42, of which waited for: 13 -> 16; matrix products, arithmetic and copies ran while one was open for 1% -> 1% of each run, Pallas kernels for 28% -> 25%
where the time goes in v6:
time: 165 us
  starting transfers between devices  55.4 us (34%)
  Pallas kernels  53.1 us (32%)
  waiting for transfers between devices  26.5 us (16%)
  between operations  15.2 us (9%)
  local copies, waits for them, and re-layouts  9.57 us (6%)
  other arithmetic  4.8 us (3%)
    ppermute x36, starting transfers between devices, shift(): lax.ppermute(array, axis, [(i, (i + step) % count) for i in range(count)])  54.5 us
    pallas_call x19, Pallas kernels, call(): pl.pallas_call(run, out_shape=out_shape, compiler_params=pltpu.CompilerPa...  53.1 us
    ppermute x36, waiting for transfers between devices, shift(): lax.ppermute(array, axis, [(i, (i + step) % count) for i in range(count)])  23.3 us
    unnamed x64, local copies, waits for them, and re-layouts  9.52 us
  transfers between devices with their start and end apart: 42, of which 16 were waited for; matrix products, arithmetic and copies ran while one was open for 1% of the time, Pallas kernels for 25%

profile of v6, /device:TPU:0, one launch (start us, length us, event | category | flops | bytes accessed | tf_op | source)
XLA Modules:
  0.0 164.6 jit_solution(17151371690142328027)
XLA Ops:
  7.9 1.7 %add_convert_fusion = bf16[64,1024]{1,0:T(8,128)(2,1)} fusion(bf16[64,1024]{1,0:T(8,128)(2,1)} %param.15, bf16[64,1024]{1,0:T(8,128)(2,1)} %param.14, f32[]{:T(128)} %bitcast.8, f32[]{:T(128)S(6)} %sub.4), kind=kLoop, calls=%fused_computation.9 | loop fusion | flops 393216 | bytes 393224 | tf_op jit(solution)/shard_map/convert_element_type | solution.py:889
  9.6 1.6 collective-permute-start.12
  11.3 2.7 %collective-permute-start.11 = (bf16[256,512]{1,0:T(8,128)(2,1)}, bf16[256,512]{1,0:T(8,128)(2,1)S(1)}, u32[]{:S(2)}, u32[]{:S(2)}) collective-permute-start(bf16[256,512]{1,0:T(8,128)(2,1)} %param.17), channel_id=1, source_target_pairs={{0,2},{1,3},{2,0},{3,1},{4,6},{5,7},{6,4},{7,5},{8,10},{9,11},{10,... | collective-permute-start | bytes 786440 | tf_op jit(solution)/shard_map/ppermute | solution.py:869
  14.0 1.4 collective-permute-start.10
  15.5 0.9 copy-done
  16.4 1.0 copy-done.5
  18.9 10.4 %pre_kernel.1 = (bf16[4,272,128]{2,1,0:T(8,128)(2,1)S(1)}, bf16[4,272,128]{2,1,0:T(8,128)(2,1)S(1)}, bf16[8,256,256]{2,1,0:T(8,128)(2,1)S(1)}, bf16[8,256,256]{2...) custom-call(s32[4]{0:T(128)S(1)} %pad_add_fusion.refs_0_, bf16[256,512]{1,0:T(8,128)(2,1)S(1)} %copy-done, ...), custom_call_target="tpu_custom_call" | custom-call | flops 1000000 | bytes 1 | tf_op jit(solution)/shard_map/pre_kernel/pallas_call | solution.py:70
  29.5 1.3 pad_maximum_fusion.refs_1_
  31.0 0.8 pair_kernel.1
  31.8 2.0 %collective-permute-start.1 = (bf16[272,128]{1,0:T(8,128)(2,1)S(1)}, bf16[272,128]{1,0:T(8,128)(2,1)S(1)}, u32[]{:S(2)}, u32[]{:S(2)}) collective-permute-start(bf16[272,128]{1,0:T(8,128)(2,1)S(1)} %get-tuple-element.86), channel_id=1, source_target_pairs={{0,8},{8,16},{16,24},{24,0},{1,9},{9,17},{17,25},{25,1},{2,10},{10... | collective-permute-start | bytes 208904 | tf_op jit(solution)/shard_map/ppermute | solution.py:869
  33.8 3.6 %collective-permute-start.2 = (bf16[272,128]{1,0:T(8,128)(2,1)S(1)}, bf16[272,128]{1,0:T(8,128)(2,1)S(1)}, u32[]{:S(2)}, u32[]{:S(2)}) collective-permute-start(bf16[272,128]{1,0:T(8,128)(2,1)S(1)} %get-tuple-element.87), channel_id=1, source_target_pairs={{0,16},{8,24},{16,0},{24,8},{1,17},{9,25},{17,1},{25,9},{2,18},{10... | collective-permute-start | bytes 208904 | tf_op jit(solution)/shard_map/ppermute | solution.py:869
  37.4 1.0 collective-permute-start.3
  38.4 2.6 %attend_kernel.1 = (bf16[8,256,256]{2,1,0:T(8,128)(2,1)S(1)}, bf16[8,256,128]{2,1,0:T(8,128)(2,1)S(1)}, f32[8,256,128]{2,1,0:T(8,128)S(1)}, bf16[8,256,128]{2,1,0:T(8,128)(2,1)S(1)}) custom-call(s32[4]{0:T(128)S(1)} %pad_add_fusion.refs_0_, bf16[256,512]{1,0:T(8,128)(2,1)S(1)} %copy-done.28, bf16[256,512]{1,0:T(8,128)(2,1)S(1)} %copy-done.1, ...), custom_call_target="tpu_custom_call" | custom-call | flops 5000000000 | bytes 1 | tf_op jit(solution)/shard_map/attend_kernel/pallas_call | solution.py:70
  41.0 1.0 copy-done.30
  42.0 1.1 prefix_kernel.1
  43.1 1.6 %collective-permute-start.4 = (bf16[272,128]{1,0:T(8,128)(2,1)S(1)}, bf16[272,128]{1,0:T(8,128)(2,1)S(1)}, u32[]{:S(2)}, u32[]{:S(2)}) collective-permute-start(bf16[272,128]{1,0:T(8,128)(2,1)S(1)} %get-tuple-element.94), channel_id=1, source_target_pairs={{0,32},{32,64},{64,96},{96,0},{1,33},{33,65},{65,97},{97,1},{2,34}... | collective-permute-start | bytes 208904 | tf_op jit(solution)/shard_map/ppermute | solution.py:869
  44.7 2.9 %collective-permute-start.5 = (bf16[272,128]{1,0:T(8,128)(2,1)S(1)}, bf16[272,128]{1,0:T(8,128)(2,1)S(1)}, u32[]{:S(2)}, u32[]{:S(2)}) collective-permute-start(bf16[272,128]{1,0:T(8,128)(2,1)S(1)} %get-tuple-element.94), channel_id=1, source_target_pairs={{0,64},{32,96},{64,0},{96,32},{1,65},{33,97},{65,1},{97,33},{2,66}... | collective-permute-start | bytes 208904 | tf_op jit(solution)/shard_map/ppermute | solution.py:869
  47.6 1.3 collective-permute-start.6
  49.0 0.9 suffix_kernel.1
  49.9 4.2 %collective-permute-done.5.refs_2_ = bf16[272,128]{1,0:T(8,128)(2,1)S(1)} collective-permute-done((bf16[272,128]{1,0:T(8,128)(2,1)S(1)}, bf16[272,128]{1,0:T(8,128)(2,1)S(1)}, u32[]{:S(2)}, u32[]{:S(2)}) %collective-permute-start.5) | collective-permute-done | bytes 69664 | tf_op jit(solution)/shard_map/ppermute | solution.py:869
  54.2 1.8 %enter_kernel.1 = (f32[128,128]{1,0:T(8,128)S(1)}, f32[128,128]{1,0:T(8,128)}, f32[128,128]{1,0:T(8,128)}, f32[128,128]{1,0:T(8,128)}) custom-call(s32[4]{0:T(128)S(1)} %pad_add_fusion.refs_0_, bf16[272,128]{1,0:T(8,128)(2,1)S(1)} %collective-permute-done.4.refs_1_, bf16[272,128]{1,0:T(8,128)(2,1)S(1)} %collective-permute-done.5.refs_2_, ...), custom_call_target="tpu_custom_call" | custom-call | flops 1000000 | bytes 1 | tf_op jit(solution)/shard_map/enter_kernel/pallas_call | solution.py:70
  57.2 1.0 collective-permute-start.7
  58.2 1.5 collective-permute-start.8
  59.7 1.2 collective-permute-start.9
  60.9 0.9 copy-done.3
  61.8 2.2 %copy-done.22 = bf16[2048,1024]{1,0:T(8,128)(2,1)S(1)} copy-done((bf16[2048,1024]{1,0:T(8,128)(2,1)S(1)}, bf16[2048,1024]{1,0:T(8,128)(2,1)}, u32[]{:S(2)}) %copy-start.22) | copy-done | bytes 4194328
  64.0 2.7 %back_kernel.1.refs_7_.refs_5_ = f32[256,1024]{1,0:T(8,128)S(1)} custom-call(s32[4]{0:T(128)S(1)} %pad_add_fusion.refs_0_, bf16[4,256,512]{2,1,0:T(8,128)(2,1)S(1)} %pad_maximum_fusion.refs_1_, bf16[2048,1024]{1,0:T(8,128)(2,1)S(1)} %copy-done.22, bf16[4,128,128]{2,1,0:T(8,128)(2,1)S(1)} %copy-done.3), custom_call_target="tpu_custom_call" | custom-call | flops 5000000000 | bytes 1 | tf_op jit(solution)/shard_map/back_kernel/pallas_call | solution.py:70
  66.8 1.7 %split_kernel.1 = (f32[4,128,128]{2,1,0:T(8,128)S(1)}, f32[4,128,128]{2,1,0:T(8,128)S(1)}) custom-call(s32[4]{0:T(128)S(1)} %pad_add_fusion.refs_0_, f32[128,128]{1,0:T(8,128)S(1)} %copy-done.18, f32[128,128]{1,0:T(8,128)} %collective-permute-done.7.refs_2_, f32[128,128]{1,0:T(8,128)} %collective-permute-done.8.refs_3_, ...), custom_call_target="tpu_custom_call" | custom-call | flops 1000000 | bytes 1 | tf_op jit(solution)/shard_map/split_kernel/pallas_call | solution.py:70
  68.6 1.5 collective-permute-done.13.refs_1_
  70.1 5.4 %norm_kernel.1 = (bf16[256,1024]{1,0:T(8,128)(2,1)S(1)}, bf16[8,128,128]{2,1,0:T(8,128)(2,1)S(1)}, f32[8,256,128]{2,1,0:T(8,128)S(1)}, f32[4,128,128]{2,1,0:T(8,128)S(1)}, f32[4,128,128]{2,1,0:T(8,128)S(1)}) custom-call(s32[4]{0:T(128)S(1)} %pad_add_fusion.refs_0_, f32[4,128,128]{2,1,0:T(8,128)S(1)} %collective-permute-done.13.refs_1_, ...), custom_call_target="tpu_custom_call" | custom-call | flops 1000000 | bytes 1 | tf_op jit(solution)/shard_map/norm_kernel/pallas_call | solution.py:70
  75.9 1.4 collective-permute-done.14.refs_4_.refs_3_.refs_8_
  77.3 2.6 %outer_kernel.1 = (bf16[4,4,64,1024]{3,2,1,0:T(8,128)(2,1)S(1)}, bf16[4,4,64,1024]{3,2,1,0:T(8,128)(2,1)S(1)}) custom-call(s32[4]{0:T(128)S(1)} %pad_add_fusion.refs_0_, bf16[4,256,512]{2,1,0:T(8,128)(2,1)S(1)} %pad_maximum_fusion.refs_1_, bf16[256,1024]{1,0:T(8,128)(2,1)S(1)} %get-tuple-element.108.refs_1_.refs_2_, ...), custom_call_target="tpu_custom_call" | custom-call | flops 5000000000 | bytes 1 | tf_op jit(solution)/shard_map/outer_kernel/pallas_call | solution.py:70
  80.9 1.0 collective-permute-start.15
  81.9 2.6 %collective-permute-start.16 = (f32[128,128]{1,0:T(8,128)S(1)}, f32[128,128]{1,0:T(8,128)S(1)}, u32[]{:S(2)}, u32[]{:S(2)}) collective-permute-start(f32[128,128]{1,0:T(8,128)S(1)} %get-tuple-element.114), channel_id=1, source_target_pairs={{0,16},{8,24},{16,0},{24,8},{1,17},{9,25},{17,1},{25,9},{2,18},{10... | collective-permute-start | bytes 196616 | tf_op jit(solution)/shard_map/ppermute | solution.py:869
  84.4 1.6 collective-permute-start.17
  86.1 2.5 %mix_kernel.1.refs_6_ = bf16[4,256,512]{2,1,0:T(8,128)(2,1)S(1)} custom-call(s32[4]{0:T(128)S(1)} %pad_add_fusion.refs_0_, bf16[256,1024]{1,0:T(8,128)(2,1)S(1)} %get-tuple-element.108.refs_1_.refs_2_, bf16[2048,1024]{1,0:T(8,128)(2,1)S(1)} %copy-done.23, f32[128,128]{1,0:T(8,128)S(1)} %get-tuple-element.111.refs_3_.refs_1_), custom_call_target="tpu_custom_call" | custom-call | flops 5000000000 | bytes 1 | tf_op jit(solution)/shard_map/mix_kernel/pallas_call | solution.py:70
  88.7 1.3 later_kernel.1
  90.0 2.4 %collective-permute-start.18 = (f32[128,128]{1,0:T(8,128)S(1)}, f32[128,128]{1,0:T(8,128)S(1)}, u32[]{:S(2)}, u32[]{:S(2)}) collective-permute-start(f32[128,128]{1,0:T(8,128)S(1)} %get-tuple-element.116), channel_id=1, source_target_pairs={{0,96},{32,0},{64,32},{96,64},{1,97},{33,1},{65,33},{97,65},{2,98}... | collective-permute-start | bytes 196616 | tf_op jit(solution)/shard_map/ppermute | solution.py:869
  92.4 1.7 %collective-permute-start.19 = (f32[128,128]{1,0:T(8,128)S(1)}, f32[128,128]{1,0:T(8,128)S(1)}, u32[]{:S(2)}, u32[]{:S(2)}) collective-permute-start(f32[128,128]{1,0:T(8,128)S(1)} %get-tuple-element.116), channel_id=1, source_target_pairs={{0,64},{32,96},{64,0},{96,32},{1,65},{33,97},{65,1},{97,33},{2,66}... | collective-permute-start | bytes 196616 | tf_op jit(solution)/shard_map/ppermute | solution.py:869
  94.3 4.7 %middle_kernel.1 = (f32[256,512]{1,0:T(8,128)}, bf16[8,256,128]{2,1,0:T(8,128)(2,1)S(1)}, f32[256,512]{1,0:T(8,128)S(1)}, f32[8,256,128]{2,1,0:T(8,128)S(1)}, bf...) custom-call(s32[4]{0:T(128)S(1)} %pad_add_fusion.refs_0_, ...), custom_call_target="tpu_custom_call" | custom-call | flops 10000000000 | bytes 1 | tf_op jit(solution)/shard_map/middle_kernel/pallas_call | solution.py:70
  99.6 1.1 leave_kernel.1
  100.8 1.0 collective-permute-start.21
  101.8 2.9 %collective-permute-start.22 = (f32[128,128]{1,0:T(8,128)S(1)}, f32[128,128]{1,0:T(8,128)S(1)}, u32[]{:S(2)}, u32[]{:S(2)}) collective-permute-start(f32[128,128]{1,0:T(8,128)S(1)} %get-tuple-element.124), channel_id=1, source_target_pairs={{0,16},{8,24},{16,0},{24,8},{1,17},{9,25},{17,1},{25,9},{2,18},{10... | collective-permute-start | bytes 196616 | tf_op jit(solution)/shard_map/ppermute | solution.py:869
  104.8 1.0 blend_kernel.1
  106.3 1.3 collective-permute-done.22.refs_3_
  107.6 1.3 collective-permute-done.23.refs_4_
  108.9 0.8 part_kernel.1
  110.1 2.8 %collective-permute-start.30 = (bf16[4,64,512]{2,1,0:T(8,128)(2,1)S(1)}, bf16[4,64,512]{2,1,0:T(8,128)(2,1)S(1)}, u32[]{:S(2)}, u32[]{:S(2)}) collective-permute-start(bf16[4,64,512]{2,1,0:T(8,128)(2,1)S(1)} %get-tuple-element.144), channel_id=1, source_target_pairs={{0,16},{8,24},{16,0},{24,8},{1,17},{9,25},{17,1},{25,9},{2,18},{10... | collective-permute-start | bytes 786440 | tf_op jit(solution)/shard_map/ppermute | solution.py:869
  113.0 1.1 collective-permute-start.31
  114.0 1.1 collective-permute-start.32
  115.2 2.9 %collective-permute-start.33 = (bf16[4,64,512]{2,1,0:T(8,128)(2,1)S(1)}, bf16[4,64,512]{2,1,0:T(8,128)(2,1)S(1)}, u32[]{:S(2)}, u32[]{:S(2)}) collective-permute-start(bf16[4,64,512]{2,1,0:T(8,128)(2,1)S(1)} %get-tuple-element.148), channel_id=1, source_target_pairs={{0,64},{32,96},{64,0},{96,32},{1,65},{33,97},{65,1},{97,33},{2,66}... | collective-permute-start | bytes 786440 | tf_op jit(solution)/shard_map/ppermute | solution.py:869
  118.1 7.3 %collective-permute-done.29.refs_2_ = bf16[4,64,512]{2,1,0:T(8,128)(2,1)S(1)} collective-permute-done((bf16[4,64,512]{2,1,0:T(8,128)(2,1)S(1)}, bf16[4,64,512]{2,1,0:T(8,128)(2,1)S(1)}, u32[]{:S(2)}, u32[]{:S(2)}) %collective-permute-start.29) | collective-permute-done | bytes 262176 | tf_op jit(solution)/shard_map/ppermute | solution.py:869
  125.4 2.6 %collective-permute-start.34 = (bf16[4,64,512]{2,1,0:T(8,128)(2,1)S(1)}, bf16[4,64,512]{2,1,0:T(8,128)(2,1)S(1)}, u32[]{:S(2)}, u32[]{:S(2)}) collective-permute-start(bf16[4,64,512]{2,1,0:T(8,128)(2,1)S(1)} %get-tuple-element.149), channel_id=1, source_target_pairs={{0,96},{32,0},{64,32},{96,64},{1,97},{33,1},{65,33},{97,65},{2,98}... | collective-permute-start | bytes 786440 | tf_op jit(solution)/shard_map/ppermute | solution.py:869
  128.0 10.1 %last_kernel.1 = (f32[256,1024]{1,0:T(8,128)}, f32[256,512]{1,0:T(8,128)}, f32[8,256]{1,0:T(8,128)}, f32[8,256]{1,0:T(8,128)}) custom-call(s32[4]{0:T(128)S(1)} %pad_add_fusion.refs_0_, bf16[256,512]{1,0:T(8,128)(2,1)S(1)} %copy-done.1, f32[8,256]{1,0:T(8,128)S(1)} %get-tuple-element.89.refs_3_.refs_4_.refs_2_, f32[4,256,128]{2,1,0:T(8,128)S(1)} %copy-done.10, ...), custom_call_target="tpu_custom_call" | custom-call | flops 1000000 | bytes 1 | tf_op jit(solution)/shard_map/last_kernel/pallas_call | solution.py:70
  138.8 0.8 sum_kernel.1
  139.8 1.9 %collective-permute-start.38 = (bf16[64,512]{1,0:T(8,128)(2,1)S(1)}, bf16[64,512]{1,0:T(8,128)(2,1)S(1)}, u32[]{:S(2)}, u32[]{:S(2)}) collective-permute-start(bf16[64,512]{1,0:T(8,128)(2,1)S(1)} %get-tuple-element.155), channel_id=1, source_target_pairs={{0,8},{8,16},{16,24},{24,0},{1,9},{9,17},{17,25},{25,1},{2,10},{10... | collective-permute-start | bytes 196616 | tf_op jit(solution)/shard_map/ppermute | solution.py:869
  141.8 2.9 %collective-permute-start.28 = (bf16[256,512]{1,0:T(8,128)(2,1)S(1)}, bf16[256,512]{1,0:T(8,128)(2,1)S(1)}, u32[]{:S(2)}, u32[]{:S(2)}) collective-permute-start(bf16[256,512]{1,0:T(8,128)(2,1)S(1)} %get-tuple-element.159), channel_id=1, source_target_pairs={{0,3},{1,0},{2,1},{3,2},{4,7},{5,4},{6,5},{7,6},{8,11},{9,8},{10,9... | collective-permute-start | bytes 786440 | tf_op jit(solution)/shard_map/ppermute | solution.py:869
  145.5 1.0 collective-permute-start.36
  147.2 2.1 %collective-permute-done.37 = bf16[64,512]{1,0:T(8,128)(2,1)S(1)} collective-permute-done((bf16[64,512]{1,0:T(8,128)(2,1)S(1)}, bf16[64,512]{1,0:T(8,128)(2,1)S(1)}, u32[]{:S(2)}, u32[]{:S(2)}) %collective-permute-start.37) | collective-permute-done | bytes 65568 | tf_op jit(solution)/shard_map/ppermute | solution.py:869
  149.3 1.3 collective-permute-start.26
  151.3 0.8 collective-permute-done.35
  152.1 0.8 fusion.3
  153.0 3.9 %collective-permute-done.26 = bf16[256,512]{1,0:T(8,128)(2,1)S(1)} collective-permute-done((bf16[256,512]{1,0:T(8,128)(2,1)S(1)}, bf16[256,512]{1,0:T(8,128)(2,1)S(1)}, u32[]{:S(2)}, u32[]{:S(2)}) %collective-permute-start.26) | collective-permute-done | bytes 262176 | tf_op jit(solution)/shard_map/ppermute | solution.py:869
  156.9 0.8 fusion.2
  (112 shorter events, 9.6 us)
Async XLA Ops:
  7.2 31.2 %copy-start.1 = (bf16[256,512]{1,0:T(8,128)(2,1)S(1)}, bf16[256,512]{1,0:T(8,128)(2,1)}, u32[]{:S(2)}) copy-start(bf16[256,512]{1,0:T(8,128)(2,1)} %refs_1_.7) | copy-start | bytes 786436
  7.2 53.7 %all-gather.2.cloned.1.call-start = ((), (), s32[]{:S(2)}) async-start(), calls=%async_computation | async-start | bytes 4325376 | tf_op jit(solution)/shard_map/all_gather | solution.py:890
  9.6 19.8 %collective-permute-start.12 = (bf16[256,512]{1,0:T(8,128)(2,1)}, bf16[256,512]{1,0:T(8,128)(2,1)S(1)}, u32[]{:S(2)}, u32[]{:S(2)}) collective-permute-start(bf16[256,512]{1,0:T(8,128)(2,1)} %param.17), channel_id=1, source_target_pairs={{0,1},{1,2},{2,3},{3,0},{4,5},{5,6},{6,7},{7,4},{8,9},{9,10},{10,1... | collective-permute-start | bytes 786440 | tf_op jit(solution)/shard_map/ppermute | solution.py:869
  11.3 18.2 %collective-permute-start.11 = (bf16[256,512]{1,0:T(8,128)(2,1)}, bf16[256,512]{1,0:T(8,128)(2,1)S(1)}, u32[]{:S(2)}, u32[]{:S(2)}) collective-permute-start(bf16[256,512]{1,0:T(8,128)(2,1)} %param.17), channel_id=1, source_target_pairs={{0,2},{1,3},{2,0},{3,1},{4,6},{5,7},{6,4},{7,5},{8,10},{9,11},{10,... | collective-permute-start | bytes 786440 | tf_op jit(solution)/shard_map/ppermute | solution.py:869
  14.0 15.5 %collective-permute-start.10 = (bf16[256,512]{1,0:T(8,128)(2,1)}, bf16[256,512]{1,0:T(8,128)(2,1)S(1)}, u32[]{:S(2)}, u32[]{:S(2)}) collective-permute-start(bf16[256,512]{1,0:T(8,128)(2,1)} %param.17), channel_id=1, source_target_pairs={{0,3},{1,0},{2,1},{3,2},{4,7},{5,4},{6,5},{7,6},{8,11},{9,8},{10,9... | collective-permute-start | bytes 786440 | tf_op jit(solution)/shard_map/ppermute | solution.py:869
  18.9 19.5 %copy-start.28 = (bf16[256,512]{1,0:T(8,128)(2,1)S(1)}, bf16[256,512]{1,0:T(8,128)(2,1)}, u32[]{:S(2)}) copy-start(bf16[256,512]{1,0:T(8,128)(2,1)} %refs_1_.6) | copy-start | bytes 786436
  29.3 11.6 %copy-start.9 = (f32[4,256,128]{2,1,0:T(8,128)}, f32[4,256,128]{2,1,0:T(8,128)S(1)}, u32[]{:S(2)}) copy-start(f32[4,256,128]{2,1,0:T(8,128)S(1)} %get-tuple-element.90.refs_4_.refs_5_.refs_3_) | copy-start | bytes 1572868
  29.3 11.6 %copy-start.24 = (bf16[8,256,256]{2,1,0:T(8,128)(2,1)}, bf16[8,256,256]{2,1,0:T(8,128)(2,1)S(1)}, u32[]{:S(2)}) copy-start(bf16[8,256,256]{2,1,0:T(8,128)(2,1)S(1)} %get-tuple-element.91.refs_5_.refs_9_) | copy-start | bytes 3145732
  29.3 11.6 %copy-start.26 = (bf16[8,256,256]{2,1,0:T(8,128)(2,1)}, bf16[8,256,256]{2,1,0:T(8,128)(2,1)S(1)}, u32[]{:S(2)}) copy-start(bf16[8,256,256]{2,1,0:T(8,128)(2,1)S(1)} %get-tuple-element.92.refs_6_.refs_10_) | copy-start | bytes 3145732
  29.4 1.6 collective-permute-start
  31.8 10.1 %collective-permute-start.1 = (bf16[272,128]{1,0:T(8,128)(2,1)S(1)}, bf16[272,128]{1,0:T(8,128)(2,1)S(1)}, u32[]{:S(2)}, u32[]{:S(2)}) collective-permute-start(bf16[272,128]{1,0:T(8,128)(2,1)S(1)} %get-tuple-element.86), channel_id=1, source_target_pairs={{0,8},{8,16},{16,24},{24,0},{1,9},{9,17},{17,25},{25,1},{2,10},{10... | collective-permute-start | bytes 208904 | tf_op jit(solution)/shard_map/ppermute | solution.py:869
  33.8 8.2 %collective-permute-start.2 = (bf16[272,128]{1,0:T(8,128)(2,1)S(1)}, bf16[272,128]{1,0:T(8,128)(2,1)S(1)}, u32[]{:S(2)}, u32[]{:S(2)}) collective-permute-start(bf16[272,128]{1,0:T(8,128)(2,1)S(1)} %get-tuple-element.87), channel_id=1, source_target_pairs={{0,16},{8,24},{16,0},{24,8},{1,17},{9,25},{17,1},{25,9},{2,18},{10... | collective-permute-start | bytes 208904 | tf_op jit(solution)/shard_map/ppermute | solution.py:869
  37.4 4.6 %collective-permute-start.3 = (bf16[272,128]{1,0:T(8,128)(2,1)S(1)}, bf16[272,128]{1,0:T(8,128)(2,1)S(1)}, u32[]{:S(2)}, u32[]{:S(2)}) collective-permute-start(bf16[272,128]{1,0:T(8,128)(2,1)S(1)} %get-tuple-element.88), channel_id=1, source_target_pairs={{0,24},{8,0},{16,8},{24,16},{1,25},{9,1},{17,9},{25,17},{2,26},{10... | collective-permute-start | bytes 208904 | tf_op jit(solution)/shard_map/ppermute | solution.py:869
  41.9 8.0 %copy-start.7 = (bf16[8,256,128]{2,1,0:T(8,128)(2,1)}, bf16[8,256,128]{2,1,0:T(8,128)(2,1)S(1)}, u32[]{:S(2)}) copy-start(bf16[8,256,128]{2,1,0:T(8,128)(2,1)S(1)} %get-tuple-element.106.refs_3_) | copy-start | bytes 1572868
  43.1 6.9 %copy-start.15 = (bf16[4,272,128]{2,1,0:T(8,128)(2,1)}, bf16[4,272,128]{2,1,0:T(8,128)(2,1)S(1)}, u32[]{:S(2)}) copy-start(bf16[4,272,128]{2,1,0:T(8,128)(2,1)S(1)} %get-tuple-element.98.refs_1_.refs_5_) | copy-start | bytes 835588
  43.1 6.9 %collective-permute-start.4 = (bf16[272,128]{1,0:T(8,128)(2,1)S(1)}, bf16[272,128]{1,0:T(8,128)(2,1)S(1)}, u32[]{:S(2)}, u32[]{:S(2)}) collective-permute-start(bf16[272,128]{1,0:T(8,128)(2,1)S(1)} %get-tuple-element.94), channel_id=1, source_target_pairs={{0,32},{32,64},{64,96},{96,0},{1,33},{33,65},{65,97},{97,1},{2,34}... | collective-permute-start | bytes 208904 | tf_op jit(solution)/shard_map/ppermute | solution.py:869
  44.7 9.4 %collective-permute-start.5 = (bf16[272,128]{1,0:T(8,128)(2,1)S(1)}, bf16[272,128]{1,0:T(8,128)(2,1)S(1)}, u32[]{:S(2)}, u32[]{:S(2)}) collective-permute-start(bf16[272,128]{1,0:T(8,128)(2,1)S(1)} %get-tuple-element.94), channel_id=1, source_target_pairs={{0,64},{32,96},{64,0},{96,32},{1,65},{33,97},{65,1},{97,33},{2,66}... | collective-permute-start | bytes 208904 | tf_op jit(solution)/shard_map/ppermute | solution.py:869
  47.6 6.5 %collective-permute-start.6 = (bf16[272,128]{1,0:T(8,128)(2,1)S(1)}, bf16[272,128]{1,0:T(8,128)(2,1)S(1)}, u32[]{:S(2)}, u32[]{:S(2)}) collective-permute-start(bf16[272,128]{1,0:T(8,128)(2,1)S(1)} %get-tuple-element.94), channel_id=1, source_target_pairs={{0,96},{32,0},{64,32},{96,64},{1,97},{33,1},{65,33},{97,65},{2,98}... | collective-permute-start | bytes 208904 | tf_op jit(solution)/shard_map/ppermute | solution.py:869
  54.2 3.1 %copy-start.13 = (bf16[272,128]{1,0:T(8,128)(2,1)}, bf16[272,128]{1,0:T(8,128)(2,1)S(1)}, u32[]{:S(2)}) copy-start(bf16[272,128]{1,0:T(8,128)(2,1)S(1)} %collective-permute-done.6.refs_3_) | copy-start | bytes 208900
  57.2 9.6 %collective-permute-start.7 = (f32[128,128]{1,0:T(8,128)}, f32[128,128]{1,0:T(8,128)}, u32[]{:S(2)}, u32[]{:S(2)}) collective-permute-start(f32[128,128]{1,0:T(8,128)} %get-tuple-element.101), channel_id=1, source_target_pairs={{0,8},{8,16},{16,24},{24,0},{1,9},{9,17},{17,25},{25,1},{2,10},{10... | collective-permute-start | bytes 196616 | tf_op jit(solution)/shard_map/ppermute | solution.py:869
  58.2 8.6 %collective-permute-start.8 = (f32[128,128]{1,0:T(8,128)}, f32[128,128]{1,0:T(8,128)}, u32[]{:S(2)}, u32[]{:S(2)}) collective-permute-start(f32[128,128]{1,0:T(8,128)} %get-tuple-element.102), channel_id=1, source_target_pairs={{0,16},{8,24},{16,0},{24,8},{1,17},{9,25},{17,1},{25,9},{2,18},{10... | collective-permute-start | bytes 196616 | tf_op jit(solution)/shard_map/ppermute | solution.py:869
  59.7 7.1 %collective-permute-start.9 = (f32[128,128]{1,0:T(8,128)}, f32[128,128]{1,0:T(8,128)}, u32[]{:S(2)}, u32[]{:S(2)}) collective-permute-start(f32[128,128]{1,0:T(8,128)} %get-tuple-element.103), channel_id=1, source_target_pairs={{0,24},{8,0},{16,8},{24,16},{1,25},{9,1},{17,9},{25,17},{2,26},{10... | collective-permute-start | bytes 196616 | tf_op jit(solution)/shard_map/ppermute | solution.py:869
  61.8 2.2 %copy-start.22 = (bf16[2048,1024]{1,0:T(8,128)(2,1)S(1)}, bf16[2048,1024]{1,0:T(8,128)(2,1)}, u32[]{:S(2)}) copy-start(bf16[2048,1024]{1,0:T(8,128)(2,1)} %all-gather.2.cloned.1.call-done.refs_2_) | copy-start | bytes 12582916
  64.0 2.8 %copy-start.18 = (f32[128,128]{1,0:T(8,128)S(1)}, f32[128,128]{1,0:T(8,128)}, u32[]{:S(2)}) copy-start(f32[128,128]{1,0:T(8,128)} %copy-done.17) | copy-start | bytes 196612
  66.8 3.3 %copy-start.8 = (bf16[8,256,128]{2,1,0:T(8,128)(2,1)S(1)}, bf16[8,256,128]{2,1,0:T(8,128)(2,1)}, u32[]{:S(2)}) copy-start(bf16[8,256,128]{2,1,0:T(8,128)(2,1)} %copy-done.7) | copy-start | bytes 1572868
  68.5 1.6 collective-permute-start.13
  75.5 1.8 %collective-permute-start.14 = (f32[4,128,128]{2,1,0:T(8,128)S(1)}, f32[4,128,128]{2,1,0:T(8,128)S(1)}, u32[]{:S(2)}, u32[]{:S(2)}) collective-permute-start(f32[4,128,128]{2,1,0:T(8,128)S(1)} %get-tuple-element.110), channel_id=1, source_target_pairs={{0,4},{4,0},{1,5},{5,1},{2,6},{6,2},{3,7},{7,3},{8,12},{12,8},{9,1... | collective-permute-start | bytes 786440 | tf_op jit(solution)/shard_map/ppermute | solution.py:881
  77.3 8.7 %copy-start.23 = (bf16[2048,1024]{1,0:T(8,128)(2,1)S(1)}, bf16[2048,1024]{1,0:T(8,128)(2,1)}, u32[]{:S(2)}) copy-start(bf16[2048,1024]{1,0:T(8,128)(2,1)} %all-gather.2.cloned.1.call-done.refs_2_) | copy-start | bytes 12582916
  79.9 24.9 %collective-permute-start.24 = (bf16[4,4,64,1024]{3,2,1,0:T(8,128)(2,1)S(1)}, bf16[4,4,64,1024]{3,2,1,0:T(8,128)(2,1)S(1)}, u32[]{:S(2)}, u32[]{:S(2)}) collective-permute-start(bf16[4,4,64,1024]{3,2,1,0:T(8,128)(2,1)S(1)} %get-tuple-element.127), channel_id=1, source_target_pairs={{0,4},{4,0},{1,5},{5,1},{2,6},{6,2},{3,7},{7,3},{8,12},{12,8},{9,1... | collective-permute-start | bytes 6291464 | tf_op jit(solution)/shard_map/ppermute | solution.py:881
  80.9 7.7 %collective-permute-start.15 = (f32[128,128]{1,0:T(8,128)S(1)}, f32[128,128]{1,0:T(8,128)S(1)}, u32[]{:S(2)}, u32[]{:S(2)}) collective-permute-start(f32[128,128]{1,0:T(8,128)S(1)} %get-tuple-element.113), channel_id=1, source_target_pairs={{0,8},{8,16},{16,24},{24,0},{1,9},{9,17},{17,25},{25,1},{2,10},{10... | collective-permute-start | bytes 196616 | tf_op jit(solution)/shard_map/ppermute | solution.py:869
  81.9 6.8 %collective-permute-start.16 = (f32[128,128]{1,0:T(8,128)S(1)}, f32[128,128]{1,0:T(8,128)S(1)}, u32[]{:S(2)}, u32[]{:S(2)}) collective-permute-start(f32[128,128]{1,0:T(8,128)S(1)} %get-tuple-element.114), channel_id=1, source_target_pairs={{0,16},{8,24},{16,0},{24,8},{1,17},{9,25},{17,1},{25,9},{2,18},{10... | collective-permute-start | bytes 196616 | tf_op jit(solution)/shard_map/ppermute | solution.py:869
  84.4 4.3 %collective-permute-start.17 = (f32[128,128]{1,0:T(8,128)S(1)}, f32[128,128]{1,0:T(8,128)S(1)}, u32[]{:S(2)}, u32[]{:S(2)}) collective-permute-start(f32[128,128]{1,0:T(8,128)S(1)} %get-tuple-element.115), channel_id=1, source_target_pairs={{0,24},{8,0},{16,8},{24,16},{1,25},{9,1},{17,9},{25,17},{2,26},{10... | collective-permute-start | bytes 196616 | tf_op jit(solution)/shard_map/ppermute | solution.py:869
  86.1 2.7 %copy-start.16 = (bf16[4,272,128]{2,1,0:T(8,128)(2,1)S(1)}, bf16[4,272,128]{2,1,0:T(8,128)(2,1)}, u32[]{:S(2)}) copy-start(bf16[4,272,128]{2,1,0:T(8,128)(2,1)} %copy-done.15) | copy-start | bytes 835588
  86.1 8.2 %copy-start.6 = (bf16[256,1024]{1,0:T(8,128)(2,1)S(1)}, bf16[256,1024]{1,0:T(8,128)(2,1)}, u32[]{:S(2)}) copy-start(bf16[256,1024]{1,0:T(8,128)(2,1)} %refs_3_.3) | copy-start | bytes 1572868
  86.1 8.2 %copy-start.10 = (f32[4,256,128]{2,1,0:T(8,128)S(1)}, f32[4,256,128]{2,1,0:T(8,128)}, u32[]{:S(2)}) copy-start(f32[4,256,128]{2,1,0:T(8,128)} %copy-done.9) | copy-start | bytes 1572868
  86.1 8.2 %copy-start.25 = (bf16[8,256,256]{2,1,0:T(8,128)(2,1)S(1)}, bf16[8,256,256]{2,1,0:T(8,128)(2,1)}, u32[]{:S(2)}) copy-start(bf16[8,256,256]{2,1,0:T(8,128)(2,1)} %copy-done.24) | copy-start | bytes 3145732
  86.1 8.2 %copy-start.27 = (bf16[8,256,256]{2,1,0:T(8,128)(2,1)S(1)}, bf16[8,256,256]{2,1,0:T(8,128)(2,1)}, u32[]{:S(2)}) copy-start(bf16[8,256,256]{2,1,0:T(8,128)(2,1)} %copy-done.26) | copy-start | bytes 3145732
  86.1 8.2 %copy-start.29 = (bf16[256,512]{1,0:T(8,128)(2,1)S(1)}, bf16[256,512]{1,0:T(8,128)(2,1)}, u32[]{:S(2)}) copy-start(bf16[256,512]{1,0:T(8,128)(2,1)} %refs_1_.6) | copy-start | bytes 786436
  86.1 8.2 %copy-start.31 = (bf16[8,256,256]{2,1,0:T(8,128)(2,1)S(1)}, bf16[8,256,256]{2,1,0:T(8,128)(2,1)}, u32[]{:S(2)}) copy-start(bf16[8,256,256]{2,1,0:T(8,128)(2,1)} %copy-done.30) | copy-start | bytes 3145732
  90.0 9.0 %collective-permute-start.18 = (f32[128,128]{1,0:T(8,128)S(1)}, f32[128,128]{1,0:T(8,128)S(1)}, u32[]{:S(2)}, u32[]{:S(2)}) collective-permute-start(f32[128,128]{1,0:T(8,128)S(1)} %get-tuple-element.116), channel_id=1, source_target_pairs={{0,96},{32,0},{64,32},{96,64},{1,97},{33,1},{65,33},{97,65},{2,98}... | collective-permute-start | bytes 196616 | tf_op jit(solution)/shard_map/ppermute | solution.py:869
  92.4 6.7 %collective-permute-start.19 = (f32[128,128]{1,0:T(8,128)S(1)}, f32[128,128]{1,0:T(8,128)S(1)}, u32[]{:S(2)}, u32[]{:S(2)}) collective-permute-start(f32[128,128]{1,0:T(8,128)S(1)} %get-tuple-element.116), channel_id=1, source_target_pairs={{0,64},{32,96},{64,0},{96,32},{1,65},{33,97},{65,1},{97,33},{2,66}... | collective-permute-start | bytes 196616 | tf_op jit(solution)/shard_map/ppermute | solution.py:869
  94.1 5.5 %collective-permute-start.20 = (f32[128,128]{1,0:T(8,128)S(1)}, f32[128,128]{1,0:T(8,128)S(1)}, u32[]{:S(2)}, u32[]{:S(2)}) collective-permute-start(f32[128,128]{1,0:T(8,128)S(1)} %get-tuple-element.116), channel_id=1, source_target_pairs={{0,32},{32,64},{64,96},{96,0},{1,33},{33,65},{65,97},{97,1},{2,34}... | collective-permute-start | bytes 196616 | tf_op jit(solution)/shard_map/ppermute | solution.py:869
  94.3 5.4 %copy-start.4 = (bf16[4,128,128]{2,1,0:T(8,128)(2,1)S(1)}, bf16[4,128,128]{2,1,0:T(8,128)(2,1)}, u32[]{:S(2)}) copy-start(bf16[4,128,128]{2,1,0:T(8,128)(2,1)} %copy-done.2) | copy-start | bytes 393220
  94.3 5.3 %copy-start.12 = (bf16[272,128]{1,0:T(8,128)(2,1)S(1)}, bf16[272,128]{1,0:T(8,128)(2,1)}, u32[]{:S(2)}) copy-start(bf16[272,128]{1,0:T(8,128)(2,1)} %copy-done.11) | copy-start | bytes 208900
  94.3 5.3 %copy-start.14 = (bf16[272,128]{1,0:T(8,128)(2,1)S(1)}, bf16[272,128]{1,0:T(8,128)(2,1)}, u32[]{:S(2)}) copy-start(bf16[272,128]{1,0:T(8,128)(2,1)} %copy-done.13) | copy-start | bytes 208900
  100.8 5.5 %collective-permute-start.21 = (f32[128,128]{1,0:T(8,128)S(1)}, f32[128,128]{1,0:T(8,128)S(1)}, u32[]{:S(2)}, u32[]{:S(2)}) collective-permute-start(f32[128,128]{1,0:T(8,128)S(1)} %get-tuple-element.123), channel_id=1, source_target_pairs={{0,8},{8,16},{16,24},{24,0},{1,9},{9,17},{17,25},{25,1},{2,10},{10... | collective-permute-start | bytes 196616 | tf_op jit(solution)/shard_map/ppermute | solution.py:869
  101.8 5.9 %collective-permute-start.22 = (f32[128,128]{1,0:T(8,128)S(1)}, f32[128,128]{1,0:T(8,128)S(1)}, u32[]{:S(2)}, u32[]{:S(2)}) collective-permute-start(f32[128,128]{1,0:T(8,128)S(1)} %get-tuple-element.124), channel_id=1, source_target_pairs={{0,16},{8,24},{16,0},{24,8},{1,17},{9,25},{17,1},{25,9},{2,18},{10... | collective-permute-start | bytes 196616 | tf_op jit(solution)/shard_map/ppermute | solution.py:869
  104.7 4.3 %collective-permute-start.23 = (f32[128,128]{1,0:T(8,128)S(1)}, f32[128,128]{1,0:T(8,128)S(1)}, u32[]{:S(2)}, u32[]{:S(2)}) collective-permute-start(f32[128,128]{1,0:T(8,128)S(1)} %get-tuple-element.125), channel_id=1, source_target_pairs={{0,24},{8,0},{16,8},{24,16},{1,25},{9,1},{17,9},{25,17},{2,26},{10... | collective-permute-start | bytes 196616 | tf_op jit(solution)/shard_map/ppermute | solution.py:869
  109.7 5.5 %collective-permute-start.25 = (f32[4,128,128]{2,1,0:T(8,128)S(1)}, f32[4,128,128]{2,1,0:T(8,128)S(1)}, u32[]{:S(2)}, u32[]{:S(2)}) collective-permute-start(f32[4,128,128]{2,1,0:T(8,128)S(1)} %get-tuple-element.129), channel_id=1, source_target_pairs={{0,4},{4,0},{1,5},{5,1},{2,6},{6,2},{3,7},{7,3},{8,12},{12,8},{9,1... | collective-permute-start | bytes 786440 | tf_op jit(solution)/shard_map/ppermute | solution.py:881
  109.8 15.6 %collective-permute-start.29 = (bf16[4,64,512]{2,1,0:T(8,128)(2,1)S(1)}, bf16[4,64,512]{2,1,0:T(8,128)(2,1)S(1)}, u32[]{:S(2)}, u32[]{:S(2)}) collective-permute-start(bf16[4,64,512]{2,1,0:T(8,128)(2,1)S(1)} %get-tuple-element.143), channel_id=1, source_target_pairs={{0,8},{8,16},{16,24},{24,0},{1,9},{9,17},{17,25},{25,1},{2,10},{10... | collective-permute-start | bytes 786440 | tf_op jit(solution)/shard_map/ppermute | solution.py:869
  110.1 27.9 %collective-permute-start.30 = (bf16[4,64,512]{2,1,0:T(8,128)(2,1)S(1)}, bf16[4,64,512]{2,1,0:T(8,128)(2,1)S(1)}, u32[]{:S(2)}, u32[]{:S(2)}) collective-permute-start(bf16[4,64,512]{2,1,0:T(8,128)(2,1)S(1)} %get-tuple-element.144), channel_id=1, source_target_pairs={{0,16},{8,24},{16,0},{24,8},{1,17},{9,25},{17,1},{25,9},{2,18},{10... | collective-permute-start | bytes 786440 | tf_op jit(solution)/shard_map/ppermute | solution.py:869
  113.0 25.1 %collective-permute-start.31 = (bf16[4,64,512]{2,1,0:T(8,128)(2,1)S(1)}, bf16[4,64,512]{2,1,0:T(8,128)(2,1)S(1)}, u32[]{:S(2)}, u32[]{:S(2)}) collective-permute-start(bf16[4,64,512]{2,1,0:T(8,128)(2,1)S(1)} %get-tuple-element.145), channel_id=1, source_target_pairs={{0,24},{8,0},{16,8},{24,16},{1,25},{9,1},{17,9},{25,17},{2,26},{10... | collective-permute-start | bytes 786440 | tf_op jit(solution)/shard_map/ppermute | solution.py:869
  114.0 24.0 %collective-permute-start.32 = (bf16[4,64,512]{2,1,0:T(8,128)(2,1)S(1)}, bf16[4,64,512]{2,1,0:T(8,128)(2,1)S(1)}, u32[]{:S(2)}, u32[]{:S(2)}) collective-permute-start(bf16[4,64,512]{2,1,0:T(8,128)(2,1)S(1)} %get-tuple-element.147), channel_id=1, source_target_pairs={{0,32},{32,64},{64,96},{96,0},{1,33},{33,65},{65,97},{97,1},{2,34}... | collective-permute-start | bytes 786440 | tf_op jit(solution)/shard_map/ppermute | solution.py:869
  115.2 22.9 %collective-permute-start.33 = (bf16[4,64,512]{2,1,0:T(8,128)(2,1)S(1)}, bf16[4,64,512]{2,1,0:T(8,128)(2,1)S(1)}, u32[]{:S(2)}, u32[]{:S(2)}) collective-permute-start(bf16[4,64,512]{2,1,0:T(8,128)(2,1)S(1)} %get-tuple-element.148), channel_id=1, source_target_pairs={{0,64},{32,96},{64,0},{96,32},{1,65},{33,97},{65,1},{97,33},{2,66}... | collective-permute-start | bytes 786440 | tf_op jit(solution)/shard_map/ppermute | solution.py:869
  125.4 12.7 %collective-permute-start.34 = (bf16[4,64,512]{2,1,0:T(8,128)(2,1)S(1)}, bf16[4,64,512]{2,1,0:T(8,128)(2,1)S(1)}, u32[]{:S(2)}, u32[]{:S(2)}) collective-permute-start(bf16[4,64,512]{2,1,0:T(8,128)(2,1)S(1)} %get-tuple-element.149), channel_id=1, source_target_pairs={{0,96},{32,0},{64,32},{96,64},{1,97},{33,1},{65,33},{97,65},{2,98}... | collective-permute-start | bytes 786440 | tf_op jit(solution)/shard_map/ppermute | solution.py:869
  139.6 5.4 %collective-permute-start.40 = (bf16[64,512]{1,0:T(8,128)(2,1)S(1)}, bf16[64,512]{1,0:T(8,128)(2,1)S(1)}, u32[]{:S(2)}, u32[]{:S(2)}) collective-permute-start(bf16[64,512]{1,0:T(8,128)(2,1)S(1)} %get-tuple-element.157), channel_id=1, source_target_pairs={{0,24},{8,0},{16,8},{24,16},{1,25},{9,1},{17,9},{25,17},{2,26},{10... | collective-permute-start | bytes 196616 | tf_op jit(solution)/shard_map/ppermute | solution.py:869
  139.7 5.8 %collective-permute-start.39 = (bf16[64,512]{1,0:T(8,128)(2,1)S(1)}, bf16[64,512]{1,0:T(8,128)(2,1)S(1)}, u32[]{:S(2)}, u32[]{:S(2)}) collective-permute-start(bf16[64,512]{1,0:T(8,128)(2,1)S(1)} %get-tuple-element.156), channel_id=1, source_target_pairs={{0,16},{8,24},{16,0},{24,8},{1,17},{9,25},{17,1},{25,9},{2,18},{10... | collective-permute-start | bytes 196616 | tf_op jit(solution)/shard_map/ppermute | solution.py:869
  139.8 6.8 %collective-permute-start.38 = (bf16[64,512]{1,0:T(8,128)(2,1)S(1)}, bf16[64,512]{1,0:T(8,128)(2,1)S(1)}, u32[]{:S(2)}, u32[]{:S(2)}) collective-permute-start(bf16[64,512]{1,0:T(8,128)(2,1)S(1)} %get-tuple-element.155), channel_id=1, source_target_pairs={{0,8},{8,16},{16,24},{24,0},{1,9},{9,17},{17,25},{25,1},{2,10},{10... | collective-permute-start | bytes 196616 | tf_op jit(solution)/shard_map/ppermute | solution.py:869
  141.8 11.2 %collective-permute-start.28 = (bf16[256,512]{1,0:T(8,128)(2,1)S(1)}, bf16[256,512]{1,0:T(8,128)(2,1)S(1)}, u32[]{:S(2)}, u32[]{:S(2)}) collective-permute-start(bf16[256,512]{1,0:T(8,128)(2,1)S(1)} %get-tuple-element.159), channel_id=1, source_target_pairs={{0,3},{1,0},{2,1},{3,2},{4,7},{5,4},{6,5},{7,6},{8,11},{9,8},{10,9... | collective-permute-start | bytes 786440 | tf_op jit(solution)/shard_map/ppermute | solution.py:869
  144.7 8.3 %collective-permute-start.27 = (bf16[256,512]{1,0:T(8,128)(2,1)S(1)}, bf16[256,512]{1,0:T(8,128)(2,1)S(1)}, u32[]{:S(2)}, u32[]{:S(2)}) collective-permute-start(bf16[256,512]{1,0:T(8,128)(2,1)S(1)} %get-tuple-element.160), channel_id=1, source_target_pairs={{0,2},{1,3},{2,0},{3,1},{4,6},{5,7},{6,4},{7,5},{8,10},{9,11},{10,... | collective-permute-start | bytes 786440 | tf_op jit(solution)/shard_map/ppermute | solution.py:869
  145.0 4.3 %collective-permute-start.37 = (bf16[64,512]{1,0:T(8,128)(2,1)S(1)}, bf16[64,512]{1,0:T(8,128)(2,1)S(1)}, u32[]{:S(2)}, u32[]{:S(2)}) collective-permute-start(bf16[64,512]{1,0:T(8,128)(2,1)S(1)} %get-tuple-element.153), channel_id=1, source_target_pairs={{0,96},{32,0},{64,32},{96,64},{1,97},{33,1},{65,33},{97,65},{2,98}... | collective-permute-start | bytes 196616 | tf_op jit(solution)/shard_map/ppermute | solution.py:869
  145.5 5.8 %collective-permute-start.36 = (bf16[64,512]{1,0:T(8,128)(2,1)S(1)}, bf16[64,512]{1,0:T(8,128)(2,1)S(1)}, u32[]{:S(2)}, u32[]{:S(2)}) collective-permute-start(bf16[64,512]{1,0:T(8,128)(2,1)S(1)} %get-tuple-element.152), channel_id=1, source_target_pairs={{0,64},{32,96},{64,0},{96,32},{1,65},{33,97},{65,1},{97,33},{2,66}... | collective-permute-start | bytes 196616 | tf_op jit(solution)/shard_map/ppermute | solution.py:869
  146.6 5.5 %collective-permute-start.35 = (bf16[64,512]{1,0:T(8,128)(2,1)S(1)}, bf16[64,512]{1,0:T(8,128)(2,1)S(1)}, u32[]{:S(2)}, u32[]{:S(2)}) collective-permute-start(bf16[64,512]{1,0:T(8,128)(2,1)S(1)} %get-tuple-element.151), channel_id=1, source_target_pairs={{0,32},{32,64},{64,96},{96,0},{1,33},{33,65},{65,97},{97,1},{2,34}... | collective-permute-start | bytes 196616 | tf_op jit(solution)/shard_map/ppermute | solution.py:869
  149.3 7.6 %collective-permute-start.26 = (bf16[256,512]{1,0:T(8,128)(2,1)S(1)}, bf16[256,512]{1,0:T(8,128)(2,1)S(1)}, u32[]{:S(2)}, u32[]{:S(2)}) collective-permute-start(bf16[256,512]{1,0:T(8,128)(2,1)S(1)} %get-tuple-element.158), channel_id=1, source_target_pairs={{0,1},{1,2},{2,3},{3,0},{4,5},{5,6},{6,7},{7,4},{8,9},{9,10},{10,1... | collective-permute-start | bytes 786440 | tf_op jit(solution)/shard_map/ppermute | solution.py:869
  (10 other events, 9.0 us)
Sparse Core Ops, SparseCore 0:
  10.8 49.7 all-gather.1
